TPU v7x, 32 devices: a whole 2x2x4 slice. The times are simulated.
32 devices in a mesh: fsdp: 2 (over x), ctx: 4 (over z), tp: 4 (over y, core).
Axes of the slice: x: 2, y: 2, z: 4, core: 2. Of those that a mesh axis runs over, the one named last changes fastest.
Arguments:
- block_input: bfloat16 [2, 2048, 2048], P('fsdp', 'ctx'), may hold values from -6 to 6
- segment_ids: int32 [2, 2048], P('fsdp'), may hold values from 0 to 4, as said below
- attention_gain: bfloat16 [2048], P('fsdp'), may hold values from 0.25 to 1.75
- query_weight: bfloat16 [2048, 2048], P('fsdp', 'tp'), may hold values from -0.125 to 0.125
- key_weight: bfloat16 [2048, 512], P('fsdp', 'tp'), may hold values from -0.125 to 0.125
- value_weight: bfloat16 [2048, 512], P('fsdp', 'tp'), may hold values from -0.125 to 0.125
- out_weight: bfloat16 [2048, 2048], P('tp', 'fsdp'), may hold values from -0.5 to 0.5
- feed_gain: bfloat16 [2048], P('fsdp'), may hold values from 0.25 to 1.75
- gate_weight: bfloat16 [2048, 8192], P('fsdp', 'tp'), may hold values from -0.125 to 0.125
- up_weight: bfloat16 [2048, 8192], P('fsdp', 'tp'), may hold values from -0.125 to 0.125
- down_weight: bfloat16 [8192, 2048], P('tp', 'fsdp'), may hold values from -0.0625 to 0.0625
- cotangent: bfloat16 [2, 2048, 2048], P('fsdp', 'ctx'), may hold values from -6 to 6
Outputs:
- block_out: bfloat16 [2, 2048, 2048], P('fsdp', 'ctx')
- input_grad: bfloat16 [2, 2048, 2048], P('fsdp', 'ctx')
- attention_gain_grad: float32 [2048], P('fsdp')
- query_grad: float32 [2048, 2048], P('fsdp', 'tp')
- key_grad: float32 [2048, 512], P('fsdp', 'tp')
- value_grad: float32 [2048, 512], P('fsdp', 'tp')
- out_weight_grad: float32 [2048, 2048], P('tp', 'fsdp')
- feed_gain_grad: float32 [2048], P('fsdp')
- gate_grad: float32 [2048, 8192], P('fsdp', 'tp')
- up_grad: float32 [2048, 8192], P('fsdp', 'tp')
- down_grad: float32 [8192, 2048], P('tp', 'fsdp')
Inputs may be any that keep to these rules, and one draw needn't show every extreme that they name: `segment_ids`: along each sequence the ids never fall and begin at 0; id 4 is the padding, which ends every sequence.
All inputs are finite; a program needn't handle non-finite values.
Results may differ from a plain program's by a relative error of at most 0.014.
Values may be sent and summed in bfloat16 or wider, within the bound.
A program may use at most 256 MiB of HBM per device.

v0:
```python
import jax
import jax.numpy as jnp
from jax import lax
from jax.sharding import PartitionSpec as P

HD = 64
WINDOW = 1024


NORM_EPS = 1e-05
ROPE_BASE = 500000.0
MASK_FILL = -1e30


def dot_rows(matrix, other_side):
    return jnp.dot(matrix, other_side, preferred_element_type=jnp.float32)


def dot_back(matrix, other_side):
    return lax.dot_general(
        matrix, other_side, (((1,), (1,)), ((), ())), preferred_element_type=jnp.float32
    )


def dot_outer(matrix, other_side):
    return lax.dot_general(
        matrix, other_side, (((0,), (0,)), ((), ())), preferred_element_type=jnp.float32
    )


def doc_positions(segments):
    seq_count, seq_length = segments.shape
    index_grid = jnp.broadcast_to(jnp.arange(seq_length, dtype=jnp.int32)[None, :], segments.shape)
    begins = jnp.concatenate(
        [jnp.ones((seq_count, 1), dtype=bool), segments[:, 1:] != segments[:, :-1]], axis=1
    )
    return index_grid - lax.cummax(jnp.where(begins, index_grid, 0), axis=1)


def rope_tables(positions, head_size):
    half_size = head_size // 2
    frequency = ROPE_BASE ** (-(jnp.arange(half_size, dtype=jnp.float32) * 2.0 / head_size))
    angles = positions.astype(jnp.float32)[..., None] * frequency
    return (jnp.cos(angles), jnp.sin(angles))


def rotate(vectors, cosine, sine_val):
    half_size = vectors.shape[-1] // 2
    front_half = vectors[..., :half_size]
    back_half = vectors[..., half_size:]
    cosine_wide = cosine[..., None, :]
    sine_wide = sine_val[..., None, :]
    return jnp.concatenate(
        [
            front_half * cosine_wide - back_half * sine_wide,
            back_half * cosine_wide + front_half * sine_wide,
        ],
        axis=-1,
    )


def unrotate(vectors, cosine, sine_val):
    half_size = vectors.shape[-1] // 2
    front_half = vectors[..., :half_size]
    back_half = vectors[..., half_size:]
    cosine_wide = cosine[..., None, :]
    sine_wide = sine_val[..., None, :]
    return jnp.concatenate(
        [
            front_half * cosine_wide + back_half * sine_wide,
            back_half * cosine_wide - front_half * sine_wide,
        ],
        axis=-1,
    )


def row_scale_of(values):
    return lax.rsqrt(jnp.mean(values * values, axis=-1, keepdims=True) + NORM_EPS)


def norm_back(grad_hidden, gain_full, normed, row_scale, residual_grad):
    grad_normed = grad_hidden * gain_full.astype(jnp.float32)
    return residual_grad + row_scale * (
        grad_normed - normed * jnp.mean(grad_normed * normed, axis=-1, keepdims=True)
    )


def shards(
    block_input,
    segment_ids,
    attention_gain,
    query_weight,
    key_weight,
    value_weight,
    out_weight,
    feed_gain,
    gate_weight,
    up_weight,
    down_weight,
    cotangent,
):
    seq_dev, span_len, width = block_input.shape
    total_rows = seq_dev * span_len
    half_rows = total_rows // 2
    seq_length = segment_ids.shape[1]
    head_size = HD
    local_heads = query_weight.shape[1] // head_size
    local_kv = key_weight.shape[1] // head_size
    group_size = local_heads // local_kv
    score_scale = head_size ** (-0.5)

    def fetch_attention():
        return (
            lax.all_gather(attention_gain, "fsdp", axis=0, tiled=True),
            lax.all_gather(query_weight, "fsdp", axis=0, tiled=True),
            lax.all_gather(key_weight, "fsdp", axis=0, tiled=True),
            lax.all_gather(value_weight, "fsdp", axis=0, tiled=True),
            lax.all_gather(out_weight, "fsdp", axis=1, tiled=True),
        )

    def fetch_feed():
        return (
            lax.all_gather(feed_gain, "fsdp", axis=0, tiled=True),
            lax.all_gather(gate_weight, "fsdp", axis=0, tiled=True),
            lax.all_gather(up_weight, "fsdp", axis=0, tiled=True),
            lax.all_gather(down_weight, "fsdp", axis=1, tiled=True),
        )

    span_start = lax.axis_index("ctx") * span_len
    positions = lax.dynamic_slice_in_dim(doc_positions(segment_ids), span_start, span_len, 1)
    seg_query = lax.dynamic_slice_in_dim(segment_ids, span_start, span_len, 1)
    cosine, sine_val = rope_tables(positions, head_size)
    query_index = span_start + jnp.arange(span_len, dtype=jnp.int32)
    distance = query_index[:, None] - jnp.arange(seq_length, dtype=jnp.int32)[None, :]
    allowed = (seg_query[:, :, None] == segment_ids[:, None, :]) & (
        (distance >= 0) & (distance < WINDOW)
    )[None]
    allowed = allowed[:, None, None]
    gain_full, query_full, key_full, value_full, outproj_full = fetch_attention()
    inputs = block_input.reshape(total_rows, width).astype(jnp.float32)
    scale_a = row_scale_of(inputs)
    normed_a = inputs * scale_a
    hidden_a = (normed_a * gain_full.astype(jnp.float32)).astype(jnp.bfloat16)
    query_raw = dot_rows(hidden_a, query_full).reshape(seq_dev, span_len, local_heads, head_size)
    key_raw = dot_rows(hidden_a, key_full).reshape(seq_dev, span_len, local_kv, head_size)
    value_raw = dot_rows(hidden_a, value_full)
    query_rot = (
        rotate(query_raw, cosine, sine_val)
        .astype(jnp.bfloat16)
        .reshape(seq_dev, span_len, local_kv, group_size, head_size)
    )
    key_rot = (
        rotate(key_raw, cosine, sine_val)
        .astype(jnp.bfloat16)
        .reshape(seq_dev, span_len, local_kv * head_size)
    )
    value_low = value_raw.astype(jnp.bfloat16).reshape(seq_dev, span_len, local_kv * head_size)
    keys_all, values_all = (
        lax.all_gather(key_rot, "ctx", axis=1, tiled=True),
        lax.all_gather(value_low, "ctx", axis=1, tiled=True),
    )
    keys_all = keys_all.reshape(seq_dev, seq_length, local_kv, head_size)
    values_all = values_all.reshape(seq_dev, seq_length, local_kv, head_size)
    scores = (
        jnp.einsum("sckgd,slkd->skgcl", query_rot, keys_all, preferred_element_type=jnp.float32)
        * score_scale
    )
    scores = jnp.where(allowed, scores, MASK_FILL)
    row_max = jnp.max(scores, axis=-1, keepdims=True)
    exponent = jnp.exp(scores - row_max)
    row_total = jnp.sum(exponent, axis=-1, keepdims=True)
    weights_low = (exponent / row_total).astype(jnp.bfloat16)
    mixed = jnp.einsum(
        "skgcl,slkd->sckgd", weights_low, values_all, preferred_element_type=jnp.float32
    )
    mixed_low = mixed.reshape(total_rows, local_heads * head_size).astype(jnp.bfloat16)
    branch_a = lax.psum(dot_rows(mixed_low, outproj_full), "tp")
    middle = inputs + branch_a
    outputs = []
    stored = []
    for micro_batch in range(2):
        rows_in = middle[micro_batch * half_rows : (micro_batch + 1) * half_rows]
        feed_gain_full, gate_full, up_full, down_full = fetch_feed()
        scale_m = row_scale_of(rows_in)
        normed_m = rows_in * scale_m
        hidden_m = (normed_m * feed_gain_full.astype(jnp.float32)).astype(jnp.bfloat16)
        gate_value = dot_rows(hidden_m, gate_full)
        up_value = dot_rows(hidden_m, up_full)
        activated = (jax.nn.silu(gate_value) * up_value).astype(jnp.bfloat16)
        branch_m = lax.psum(dot_rows(activated, down_full).astype(jnp.bfloat16), "tp").astype(
            jnp.float32
        )
        outputs.append(rows_in + branch_m)
        stored.append((scale_m, normed_m, hidden_m))
    block_out = (
        jnp.concatenate(outputs, axis=0).astype(jnp.bfloat16).reshape(seq_dev, span_len, width)
    )
    grad_rows = cotangent.reshape(total_rows, width)
    feed_width = gate_weight.shape[1]
    feed_gain_acc = jnp.zeros((width,), jnp.float32)
    gate_acc = jnp.zeros((width, feed_width), jnp.float32)
    up_acc = jnp.zeros((width, feed_width), jnp.float32)
    down_acc = jnp.zeros((feed_width, width), jnp.float32)
    middle_grads = []
    for micro_batch in range(2):
        rows_grad = grad_rows[micro_batch * half_rows : (micro_batch + 1) * half_rows]
        feed_gain_full, gate_full, up_full, down_full = fetch_feed()
        scale_m, normed_m, hidden_m = stored[micro_batch]
        gate_value = dot_rows(hidden_m, gate_full)
        up_value = dot_rows(hidden_m, up_full)
        activated = (jax.nn.silu(gate_value) * up_value).astype(jnp.bfloat16)
        down_acc = down_acc + dot_outer(activated, rows_grad)
        grad_act = dot_back(rows_grad, down_full)
        sigmoid_gate = jax.nn.sigmoid(gate_value)
        grad_gate_rows = (
            grad_act * up_value * sigmoid_gate * (1.0 + gate_value * (1.0 - sigmoid_gate))
        ).astype(jnp.bfloat16)
        grad_up_rows = (grad_act * gate_value * sigmoid_gate).astype(jnp.bfloat16)
        gate_acc = gate_acc + dot_outer(hidden_m, grad_gate_rows)
        up_acc = up_acc + dot_outer(hidden_m, grad_up_rows)
        grad_hidden_m = lax.psum(
            dot_back(grad_gate_rows, gate_full) + dot_back(grad_up_rows, up_full), "tp"
        )
        feed_gain_acc = feed_gain_acc + jnp.sum(grad_hidden_m * normed_m, axis=0)
        middle_grads.append(
            norm_back(
                grad_hidden_m, feed_gain_full, normed_m, scale_m, rows_grad.astype(jnp.float32)
            )
        )
    grad_middle = jnp.concatenate(middle_grads, axis=0)
    gain_full, query_full, key_full, value_full, outproj_full = fetch_attention()
    grad_branch = grad_middle.astype(jnp.bfloat16)
    outproj_acc = dot_outer(mixed_low, grad_branch)
    grad_mixed = (
        dot_back(grad_branch, outproj_full)
        .astype(jnp.bfloat16)
        .reshape(seq_dev, span_len, local_kv, group_size, head_size)
    )
    scores = (
        jnp.einsum("sckgd,slkd->skgcl", query_rot, keys_all, preferred_element_type=jnp.float32)
        * score_scale
    )
    scores = jnp.where(allowed, scores, MASK_FILL)
    probs_full = jnp.exp(scores - row_max) / row_total
    probs_low = probs_full.astype(jnp.bfloat16)
    grad_values = jnp.einsum(
        "skgcl,sckgd->slkd", probs_low, grad_mixed, preferred_element_type=jnp.float32
    )
    grad_probs = jnp.einsum(
        "sckgd,slkd->skgcl", grad_mixed, values_all, preferred_element_type=jnp.float32
    )
    row_spread = jnp.sum(probs_full * grad_probs, axis=-1, keepdims=True)
    grad_scores = (probs_full * (grad_probs - row_spread)).astype(jnp.bfloat16)
    grad_query = (
        jnp.einsum("skgcl,slkd->sckgd", grad_scores, keys_all, preferred_element_type=jnp.float32)
        * score_scale
    )
    grad_keys = (
        jnp.einsum("skgcl,sckgd->slkd", grad_scores, query_rot, preferred_element_type=jnp.float32)
        * score_scale
    )
    key_sum, value_sum = (
        lax.psum_scatter(
            grad_keys.reshape(seq_dev, seq_length, local_kv * head_size),
            "ctx",
            scatter_dimension=1,
            tiled=True,
        ),
        lax.psum_scatter(
            grad_values.reshape(seq_dev, seq_length, local_kv * head_size),
            "ctx",
            scatter_dimension=1,
            tiled=True,
        ),
    )
    grad_query_raw = (
        unrotate(grad_query.reshape(seq_dev, span_len, local_heads, head_size), cosine, sine_val)
        .astype(jnp.bfloat16)
        .reshape(total_rows, local_heads * head_size)
    )
    grad_key_raw = (
        unrotate(key_sum.reshape(seq_dev, span_len, local_kv, head_size), cosine, sine_val)
        .astype(jnp.bfloat16)
        .reshape(total_rows, local_kv * head_size)
    )
    grad_value_raw = value_sum.astype(jnp.bfloat16).reshape(total_rows, local_kv * head_size)
    query_acc = dot_outer(hidden_a, grad_query_raw)
    key_acc = dot_outer(hidden_a, grad_key_raw)
    value_acc = dot_outer(hidden_a, grad_value_raw)
    grad_hidden_a = lax.psum(
        dot_back(grad_query_raw, query_full)
        + dot_back(grad_key_raw, key_full)
        + dot_back(grad_value_raw, value_full),
        "tp",
    )
    attention_gain_acc = jnp.sum(grad_hidden_a * normed_a, axis=0)
    grad_inputs = norm_back(grad_hidden_a, gain_full, normed_a, scale_a, grad_middle)
    input_grad = grad_inputs.astype(jnp.bfloat16).reshape(seq_dev, span_len, width)
    gradients = (
        attention_gain_acc,
        query_acc,
        key_acc,
        value_acc,
        outproj_acc,
        feed_gain_acc,
        gate_acc,
        up_acc,
        down_acc,
    )
    halves = (
        lax.psum_scatter(gradients[0], "fsdp", scatter_dimension=0, tiled=True),
        lax.psum_scatter(gradients[1], "fsdp", scatter_dimension=0, tiled=True),
        lax.psum_scatter(gradients[2], "fsdp", scatter_dimension=0, tiled=True),
        lax.psum_scatter(gradients[3], "fsdp", scatter_dimension=0, tiled=True),
        lax.psum_scatter(gradients[4], "fsdp", scatter_dimension=1, tiled=True),
        lax.psum_scatter(gradients[5], "fsdp", scatter_dimension=0, tiled=True),
        lax.psum_scatter(gradients[6], "fsdp", scatter_dimension=0, tiled=True),
        lax.psum_scatter(gradients[7], "fsdp", scatter_dimension=0, tiled=True),
        lax.psum_scatter(gradients[8], "fsdp", scatter_dimension=1, tiled=True),
    )
    pieces = (
        lax.psum_scatter(halves[0], "ctx", scatter_dimension=0, tiled=True),
        lax.psum_scatter(halves[1], "ctx", scatter_dimension=0, tiled=True),
        lax.psum_scatter(halves[2], "ctx", scatter_dimension=0, tiled=True),
        lax.psum_scatter(halves[3], "ctx", scatter_dimension=0, tiled=True),
        lax.psum_scatter(halves[4], "ctx", scatter_dimension=1, tiled=True),
        lax.psum_scatter(halves[5], "ctx", scatter_dimension=0, tiled=True),
        lax.psum_scatter(halves[6], "ctx", scatter_dimension=0, tiled=True),
        lax.psum_scatter(halves[7], "ctx", scatter_dimension=0, tiled=True),
        lax.psum_scatter(halves[8], "ctx", scatter_dimension=1, tiled=True),
    )
    owned_grads = (
        lax.all_gather(pieces[0], "ctx", axis=0, tiled=True),
        lax.all_gather(pieces[1], "ctx", axis=0, tiled=True),
        lax.all_gather(pieces[2], "ctx", axis=0, tiled=True),
        lax.all_gather(pieces[3], "ctx", axis=0, tiled=True),
        lax.all_gather(pieces[4], "ctx", axis=1, tiled=True),
        lax.all_gather(pieces[5], "ctx", axis=0, tiled=True),
        lax.all_gather(pieces[6], "ctx", axis=0, tiled=True),
        lax.all_gather(pieces[7], "ctx", axis=0, tiled=True),
        lax.all_gather(pieces[8], "ctx", axis=1, tiled=True),
    )
    return (
        block_out,
        input_grad,
        owned_grads[0],
        owned_grads[1],
        owned_grads[2],
        owned_grads[3],
        owned_grads[4],
        owned_grads[5],
        owned_grads[6],
        owned_grads[7],
        owned_grads[8],
    )


def solution(mesh):
    in_specs = (
        P("fsdp", "ctx", None),
        P("fsdp", None),
        P("fsdp"),
        P("fsdp", "tp"),
        P("fsdp", "tp"),
        P("fsdp", "tp"),
        P("tp", "fsdp"),
        P("fsdp"),
        P("fsdp", "tp"),
        P("fsdp", "tp"),
        P("tp", "fsdp"),
        P("fsdp", "ctx", None),
    )
    out_specs = (
        P("fsdp", "ctx", None),
        P("fsdp", "ctx", None),
        P("fsdp"),
        P("fsdp", "tp"),
        P("fsdp", "tp"),
        P("fsdp", "tp"),
        P("tp", "fsdp"),
        P("fsdp"),
        P("fsdp", "tp"),
        P("fsdp", "tp"),
        P("tp", "fsdp"),
    )
    return jax.shard_map(shards, mesh=mesh, in_specs=in_specs, out_specs=out_specs, check_vma=False)
```

profile of v0, /device:TPU:0, one launch (start us, length us, event | category | flops | bytes accessed | tf_op | source)
XLA Modules:
  0.0 2822.8 jit_solution(17238292315016920190)
XLA Ops:
  9.2 10.2 all_gather.78
  25.2 16.3 all-gather
  53.3 17.0 all_gather.81
  79.5 13.6 fusion.5
  93.1 14.4 fusion.4
  107.6 15.3 fusion.53
  134.6 77.9 %all-reduce.13.cloned.1.call-done = f32[512,2048]{1,0:T(8,128)} async-done(((f32[512,2048]{1,0:T(8,128)}), f32[512,2048]{1,0:T(8,128)}) %all-reduce.13.cloned.1.call-update) | async-done | bytes 4194320 | tf_op jit(solution)/shard_map/psum | solution.py:177
  217.8 100.4 %all-gather.18.cloned.1.call-done = bf16[2048,2048]{1,0:T(8,128)(2,1)} async-done(((bf16[1024,2048]{1,0:T(8,128)(2,1)}), bf16[2048,2048]{1,0:T(8,128)(2,1)}) %all-gather.18.cloned.1.call-update) | async-done | bytes 8388624 | tf_op jit(solution)/shard_map/all_gather | solution.py:124
  325.2 98.5 %all-gather.20.cloned.1.call-done = bf16[2048,2048]{1,0:T(8,128)(2,1)} async-done(((bf16[1024,2048]{1,0:T(8,128)(2,1)}), bf16[2048,2048]{1,0:T(8,128)(2,1)}) %all-gather.20.cloned.1.call-update) | async-done | bytes 8388624 | tf_op jit(solution)/shard_map/all_gather | solution.py:125
  423.7 7.2 fusion.99
  438.4 90.8 %all-gather.22.cloned.1.call-done = bf16[2048,2048]{1,0:T(8,128)(2,1)} async-done(((bf16[2048,1024]{1,0:T(8,128)(2,1)}), bf16[2048,2048]{1,0:T(8,128)(2,1)}) %all-gather.22.cloned.1.call-update) | async-done | bytes 8388624 | tf_op jit(solution)/shard_map/all_gather | solution.py:126
  529.2 9.0 multiply_convert_fusion
  558.4 7.3 convolution_add_fusion.3
  584.3 70.9 %all-reduce.17.cloned.1.call-done = (f32[256,2048]{1,0:T(8,128)}, f32[256,2048]{1,0:T(8,128)}) async-done(((f32[256,2048]{1,0:T(8,128)}, f32[256,2048]{1,0:T(8,128)}), (f32[256,2048]{1,0:T(8,128)}, f32[256,2048]{1,0:T(8,128)})) %all-reduce.17.cloned.1.call-update) | async-done | bytes 4194320 | tf_op jit(solution)/shard_map/psum | solution.py:221
  660.3 49.7 %all-reduce.19.cloned.1.call-done = (bf16[256,2048]{1,0:T(8,128)(2,1)}, bf16[256,2048]{1,0:T(8,128)(2,1)}) async-done(((bf16[256,2048]{1,0:T(8,128)(2,1)}, bf16[256,2048]{1,0:T(8,128)(2,1)}), (bf16[256,2048]{1,0:T(8,128)(2,1)}, bf16[256,2048]{1,0:T(8,128)(2,1)})) %all-reduce.19.cloned.1.call-update) | async-done | bytes 2097168 | tf_op jit(solution)/shard_map/psum | solution.py:190
  718.8 24.4 fusion
  743.2 28.3 %fusion.6 = bf16[2,4,512,2048]{2,3,1,0:T(8,128)(2,1)} fusion(f32[2,2048,512,4]{2,1,3,0:T(8,128)} %get-tuple-element.54, f32[2,4,512]{2,1,0:T(4,128)S(1)} %get-tuple-element.53, f32[2,4,512]{2,1,0:T(4,128)S(1)} %fusion.4, f32[2,4,512]{2,1,0:T(4,128)S(1)} %get-tuple-element.51, f32[2,2048,512,4]{2,1,3,0:T(8,128)} %get-tuple-element.52, ...), kind=kLoop, calls=%fused_computation.10 | loop fusion | flops 58720256 | bytes 84983808 | tf_op jit(solution)/shard_map/reshape.63
  771.5 11.9 fusion.34
  783.5 15.2 fusion.7
  799.2 9.2 convolution_multiply_fusion
  823.6 9.6 convolution_add_fusion.2
  837.4 10.0 convolution_add_fusion.1
  851.4 9.9 convolution_add_fusion
  867.4 27.3 reduce-scatter.21.cloned.1.call-done
  894.8 57.0 %reduce-scatter.33.cloned.1.call-done = f32[512,1024]{1,0:T(8,128)} async-done(((f32[512,2048]{1,0:T(8,128)}), f32[512,1024]{1,0:T(8,128)}) %reduce-scatter.33.cloned.1.call-update) | async-done | bytes 2097168 | tf_op jit(solution)/shard_map/reduce_scatter | solution.py:315
  951.8 191.5 %reduce-scatter.37.cloned.1.call-done = f32[1024,2048]{1,0:T(8,128)} async-done(((f32[2048,2048]{1,0:T(8,128)}), f32[1024,2048]{1,0:T(8,128)}) %reduce-scatter.37.cloned.1.call-update) | async-done | bytes 8388624 | tf_op jit(solution)/shard_map/reduce_scatter | solution.py:317
  1143.4 191.2 %reduce-scatter.41.cloned.1.call-done = f32[1024,2048]{1,0:T(8,128)} async-done(((f32[2048,2048]{1,0:T(8,128)}), f32[1024,2048]{1,0:T(8,128)}) %reduce-scatter.41.cloned.1.call-update) | async-done | bytes 8388624 | tf_op jit(solution)/shard_map/reduce_scatter | solution.py:318
  1334.7 191.3 %reduce-scatter.45.cloned.1.call-done = f32[2048,1024]{1,0:T(8,128)} async-done(((f32[2048,2048]{1,0:T(8,128)}), f32[2048,1024]{1,0:T(8,128)}) %reduce-scatter.45.cloned.1.call-update) | async-done | bytes 8388624 | tf_op jit(solution)/shard_map/reduce_scatter | solution.py:319
  1533.9 15.1 reduce-scatter.25.cloned.1.call-done
  1549.1 23.0 reduce-scatter.29.cloned.1.call-done
  1572.3 46.0 %reduce-scatter.23.cloned.1.call-done = f32[256,512]{1,0:T(8,128)} async-done(((f32[1024,512]{1,0:T(8,128)}), f32[256,512]{1,0:T(8,128)}) %reduce-scatter.23.cloned.1.call-update) | async-done | bytes 524304 | tf_op jit(solution)/shard_map/reduce_scatter | solution.py:323
  1618.3 45.6 %reduce-scatter.35.cloned.1.call-done = f32[512,256]{1,0:T(8,128)} async-done(((f32[512,1024]{1,0:T(8,128)}), f32[512,256]{1,0:T(8,128)}) %reduce-scatter.35.cloned.1.call-update) | async-done | bytes 524304 | tf_op jit(solution)/shard_map/reduce_scatter | solution.py:326
  1663.9 146.0 %reduce-scatter.39.cloned.1.call-done = f32[256,2048]{1,0:T(8,128)} async-done(((f32[1024,2048]{1,0:T(8,128)}), f32[256,2048]{1,0:T(8,128)}) %reduce-scatter.39.cloned.1.call-update) | async-done | bytes 2097168 | tf_op jit(solution)/shard_map/reduce_scatter | solution.py:328
  1810.0 147.5 %reduce-scatter.43.cloned.1.call-done = f32[256,2048]{1,0:T(8,128)} async-done(((f32[1024,2048]{1,0:T(8,128)}), f32[256,2048]{1,0:T(8,128)}) %reduce-scatter.43.cloned.1.call-update) | async-done | bytes 2097168 | tf_op jit(solution)/shard_map/reduce_scatter | solution.py:329
  1957.5 147.5 %reduce-scatter.47.cloned.1.call-done = f32[2048,256]{1,0:T(8,128)} async-done(((f32[2048,1024]{1,0:T(8,128)}), f32[2048,256]{1,0:T(8,128)}) %reduce-scatter.47.cloned.1.call-update) | async-done | bytes 2097168 | tf_op jit(solution)/shard_map/reduce_scatter | solution.py:330
  2110.4 83.9 %all-reduce.15.cloned.1.call-done = f32[512,2048]{1,0:T(8,128)} async-done(((f32[512,2048]{1,0:T(8,128)}), f32[512,2048]{1,0:T(8,128)}) %all-reduce.15.cloned.1.call-update) | async-done | bytes 4194320 | tf_op jit(solution)/shard_map/psum | solution.py:290
  2197.5 8.1 all-reduce.6
  2205.7 12.4 all-reduce.5
  2218.1 7.6 all-gather.1
  2225.8 9.7 all-gather.2
  2241.4 18.6 all_gather.90
  2259.9 19.9 all_gather.91
  2279.9 15.4 all-gather.24.cloned.1.call-done
  2295.3 46.8 %all-gather.26.cloned.1.call-done = f32[512,1024]{1,0:T(8,128)} async-done(((f32[512,256]{1,0:T(8,128)}), f32[512,1024]{1,0:T(8,128)}) %all-gather.26.cloned.1.call-update) | async-done | bytes 2097168 | tf_op jit(solution)/shard_map/all_gather | solution.py:337
  2342.1 150.0 %all-gather.28.cloned.1.call-done = f32[1024,2048]{1,0:T(8,128)} async-done(((f32[256,2048]{1,0:T(8,128)}), f32[1024,2048]{1,0:T(8,128)}) %all-gather.28.cloned.1.call-update) | async-done | bytes 8388624 | tf_op jit(solution)/shard_map/all_gather | solution.py:339
  2492.1 149.6 %all-gather.30.cloned.1.call-done = f32[1024,2048]{1,0:T(8,128)} async-done(((f32[256,2048]{1,0:T(8,128)}), f32[1024,2048]{1,0:T(8,128)}) %all-gather.30.cloned.1.call-update) | async-done | bytes 8388624 | tf_op jit(solution)/shard_map/all_gather | solution.py:340
  2641.7 149.4 %all-gather.32.cloned.1.call-done = f32[2048,1024]{1,0:T(8,128)} async-done(((f32[2048,256]{1,0:T(8,128)}), f32[2048,1024]{1,0:T(8,128)}) %all-gather.32.cloned.1.call-update) | async-done | bytes 8388624 | tf_op jit(solution)/shard_map/all_gather | solution.py:341
  2807.3 8.4 copy.76
  (271 shorter events, 180.4 us)
Async XLA Ops:
  7.2 65.2 %all-gather.14.cloned.1.call-start = ((), (), s32[]{:S(2)}) async-start(), calls=%async_computation.16 | async-start | bytes 3145728 | tf_op jit(solution)/shard_map/all_gather | solution.py:115
  7.9 114.9 %all-gather.16.cloned.1.call-start = ((), (), s32[]{:S(2)}) async-start(), calls=%async_computation.17 | async-start | bytes 3145728 | tf_op jit(solution)/shard_map/all_gather | solution.py:118
  8.7 203.9 %all-reduce.13.cloned.1.call-start = ((), (), s32[]{:S(2)}) async-start(), calls=%async_computation.18 | async-start | bytes 8388608 | tf_op jit(solution)/shard_map/psum | solution.py:177
  23.9 52.4 %copy-start.37 = (f32[2048]{0:T(1024)}, f32[2048]{0:T(1024)S(1)}, u32[]{:S(2)}) copy-start(f32[2048]{0:T(1024)S(1)} %convert_element_type.187) | copy-start | bytes 24580
  23.9 20.1 copy-start.39
  24.4 27.8 copy-start.42
  51.1 19.3 copy-start.12
  53.2 26.0 copy-start.22
  53.3 26.0 copy-start.24
  53.3 23.0 copy-start.43
  127.9 190.3 %all-gather.18.cloned.1.call-start = ((), (), s32[]{:S(2)}) async-start(), calls=%async_computation.19 | async-start | bytes 12582912 | tf_op jit(solution)/shard_map/all_gather | solution.py:124
  128.5 295.2 %all-gather.20.cloned.1.call-start = ((), (), s32[]{:S(2)}) async-start(), calls=%async_computation.20 | async-start | bytes 12582912 | tf_op jit(solution)/shard_map/all_gather | solution.py:125
  129.1 400.1 %all-gather.22.cloned.1.call-start = ((), (), s32[]{:S(2)}) async-start(), calls=%async_computation.21 | async-start | bytes 12582912 | tf_op jit(solution)/shard_map/all_gather | solution.py:126
  129.7 525.6 %all-reduce.17.cloned.1.call-start = ((), (), s32[]{:S(2)}) async-start(), calls=%async_computation.44 | async-start | bytes 8388608 | tf_op jit(solution)/shard_map/psum | solution.py:221
  217.7 205.9 %copy-start.3 = (bf16[256,2048]{1,0:T(8,128)(2,1)}, bf16[256,2048]{1,0:T(8,128)(2,1)S(1)}, u32[]{:S(2)}) copy-start(bf16[256,2048]{1,0:T(8,128)(2,1)S(1)} %get-tuple-element.32) | copy-start | bytes 3145732
  217.8 216.9 %copy-start.7 = (bf16[256,2048]{1,0:T(8,128)(2,1)}, bf16[256,2048]{1,0:T(8,128)(2,1)S(1)}, u32[]{:S(2)}) copy-start(bf16[256,2048]{1,0:T(8,128)(2,1)S(1)} %get-tuple-element.31) | copy-start | bytes 3145732
  538.2 20.2 copy-start.26
  569.4 140.6 %all-reduce.19.cloned.1.call-start = ((), (), s32[]{:S(2)}) async-start(), calls=%async_computation.45 | async-start | bytes 4194304 | tf_op jit(solution)/shard_map/psum | solution.py:190
  584.1 277.3 %reduce-scatter.17.cloned.1.call-start = ((), (), s32[]{:S(2)}) async-start(), calls=%async_computation.22 | async-start | bytes 1310720 | tf_op jit(solution)/shard_map/reduce_scatter | solution.py:263
  718.8 24.4 copy-start.50
  743.1 28.3 %copy-start.29 = (bf16[1,512,8,32]{1,3,2,0:T(8,128)(2,1)S(1)}, bf16[1,512,8,32]{1,3,2,0:T(8,128)(2,1)}, u32[]{:S(2)}) copy-start(bf16[1,512,8,32]{1,3,2,0:T(8,128)(2,1)} %copy-done.28) | copy-start | bytes 786436
  743.2 28.3 %copy-start.31 = (bf16[1,512,8,32]{1,3,2,0:T(8,128)(2,1)S(1)}, bf16[1,512,8,32]{1,3,2,0:T(8,128)(2,1)}, u32[]{:S(2)}) copy-start(bf16[1,512,8,32]{1,3,2,0:T(8,128)(2,1)} %copy-done.30) | copy-start | bytes 786436
  783.4 81.0 %reduce-scatter.19.cloned.1.call-start = ((), (), s32[]{:S(2)}) async-start(), calls=%async_computation.23 | async-start | bytes 1310720 | tf_op jit(solution)/shard_map/reduce_scatter | solution.py:269
  798.8 95.9 %reduce-scatter.21.cloned.1.call-start = ((), (), s32[]{:S(2)}) async-start(), calls=%async_computation.25 | async-start | bytes 6291456 | tf_op jit(solution)/shard_map/reduce_scatter | solution.py:312
  813.0 138.8 %reduce-scatter.33.cloned.1.call-start = ((), (), s32[]{:S(2)}) async-start(), calls=%async_computation.32 | async-start | bytes 6291456 | tf_op jit(solution)/shard_map/reduce_scatter | solution.py:315
  819.5 323.8 %reduce-scatter.37.cloned.1.call-start = ((), (), s32[]{:S(2)}) async-start(), calls=%async_computation.35 | async-start | bytes 25165824 | tf_op jit(solution)/shard_map/reduce_scatter | solution.py:317
  833.2 501.4 %reduce-scatter.41.cloned.1.call-start = ((), (), s32[]{:S(2)}) async-start(), calls=%async_computation.38 | async-start | bytes 25165824 | tf_op jit(solution)/shard_map/reduce_scatter | solution.py:318
  847.4 678.6 %reduce-scatter.45.cloned.1.call-start = ((), (), s32[]{:S(2)}) async-start(), calls=%async_computation.41 | async-start | bytes 25165824 | tf_op jit(solution)/shard_map/reduce_scatter | solution.py:319
  861.3 687.8 %reduce-scatter.25.cloned.1.call-start = ((), (), s32[]{:S(2)}) async-start(), calls=%async_computation.28 | async-start | bytes 1572864 | tf_op jit(solution)/shard_map/reduce_scatter | solution.py:313
  864.4 707.8 %reduce-scatter.29.cloned.1.call-start = ((), (), s32[]{:S(2)}) async-start(), calls=%async_computation.30 | async-start | bytes 1572864 | tf_op jit(solution)/shard_map/reduce_scatter | solution.py:314
  867.4 750.8 %reduce-scatter.23.cloned.1.call-start = ((), (), s32[]{:S(2)}) async-start(), calls=%async_computation.26 | async-start | bytes 2621440 | tf_op jit(solution)/shard_map/reduce_scatter | solution.py:323
  894.7 769.1 %reduce-scatter.35.cloned.1.call-start = ((), (), s32[]{:S(2)}) async-start(), calls=%async_computation.33 | async-start | bytes 2621440 | tf_op jit(solution)/shard_map/reduce_scatter | solution.py:326
  951.8 858.1 %reduce-scatter.39.cloned.1.call-start = ((), (), s32[]{:S(2)}) async-start(), calls=%async_computation.36 | async-start | bytes 10485760 | tf_op jit(solution)/shard_map/reduce_scatter | solution.py:328
  1143.4 814.1 %reduce-scatter.43.cloned.1.call-start = ((), (), s32[]{:S(2)}) async-start(), calls=%async_computation.39 | async-start | bytes 10485760 | tf_op jit(solution)/shard_map/reduce_scatter | solution.py:329
  1334.7 770.4 %reduce-scatter.47.cloned.1.call-start = ((), (), s32[]{:S(2)}) async-start(), calls=%async_computation.42 | async-start | bytes 10485760 | tf_op jit(solution)/shard_map/reduce_scatter | solution.py:330
  1526.1 668.2 %all-reduce.15.cloned.1.call-start = ((), (), s32[]{:S(2)}) async-start(), calls=%async_computation.24 | async-start | bytes 8388608 | tf_op jit(solution)/shard_map/psum | solution.py:290
  1533.9 707.5 %reduce-scatter.27.cloned.1.call-start = ((), (), s32[]{:S(2)}) async-start(), calls=%async_computation.29 | async-start | bytes 655360 | tf_op jit(solution)/shard_map/reduce_scatter | solution.py:324
  1549.1 556.0 %copy-start.53 = (u32[32]{0:T(128)S(1)}, u32[32]{0:T(128)}, u32[]{:S(2)}) copy-start(u32[32]{0:T(128)} %constant.62) | copy-start | bytes 388
  1549.1 556.6 %copy-start.52 = (u32[32]{0:T(128)S(1)}, u32[32]{0:T(128)}, u32[]{:S(2)}) copy-start(u32[32]{0:T(128)} %constant.66) | copy-start | bytes 388
  1549.1 558.5 %copy-start.45 = (f32[2048]{0:T(1024)S(1)}, f32[2048]{0:T(1024)}, u32[]{:S(2)}) copy-start(f32[2048]{0:T(1024)} %get-tuple-element.15) | copy-start | bytes 24580
  1549.1 558.5 %copy-start.46 = (f32[2048]{0:T(1024)S(1)}, f32[2048]{0:T(1024)}, u32[]{:S(2)}) copy-start(f32[2048]{0:T(1024)} %get-tuple-element.18) | copy-start | bytes 24580
  1549.1 558.5 %copy-start.14 = (bf16[1,256,2048]{2,1,0:T(8,128)(2,1)S(1)}, bf16[1,256,2048]{2,1,0:T(8,128)(2,1)}, u32[]{:S(2)}) copy-start(bf16[1,256,2048]{2,1,0:T(8,128)(2,1)} %get-tuple-element.33) | copy-start | bytes 3145732
  1549.1 710.9 %reduce-scatter.31.cloned.1.call-start = ((), (), s32[]{:S(2)}) async-start(), calls=%async_computation.31 | async-start | bytes 655360 | tf_op jit(solution)/shard_map/reduce_scatter | solution.py:325
  1572.2 723.1 %all-gather.24.cloned.1.call-start = ((), (), s32[]{:S(2)}) async-start(), calls=%async_computation.27 | async-start | bytes 2621440 | tf_op jit(solution)/shard_map/all_gather | solution.py:334
  1618.2 723.9 %all-gather.26.cloned.1.call-start = ((), (), s32[]{:S(2)}) async-start(), calls=%async_computation.34 | async-start | bytes 2621440 | tf_op jit(solution)/shard_map/all_gather | solution.py:337
  1663.9 828.3 %all-gather.28.cloned.1.call-start = ((), (), s32[]{:S(2)}) async-start(), calls=%async_computation.37 | async-start | bytes 10485760 | tf_op jit(solution)/shard_map/all_gather | solution.py:339
  1809.9 831.8 %all-gather.30.cloned.1.call-start = ((), (), s32[]{:S(2)}) async-start(), calls=%async_computation.40 | async-start | bytes 10485760 | tf_op jit(solution)/shard_map/all_gather | solution.py:340
  1957.5 833.6 %all-gather.32.cloned.1.call-start = ((), (), s32[]{:S(2)}) async-start(), calls=%async_computation.43 | async-start | bytes 10485760 | tf_op jit(solution)/shard_map/all_gather | solution.py:341
  (42 other events, 293.8 us)
Sparse Core Ops, SparseCore 0:
  9.6 37.6 all-gather.13
  48.8 33.5 all-gather.15
  128.0 84.4 all-reduce.12
  214.0 104.1 all-gather.17
  319.6 103.9 all-gather.19
  425.1 103.9 all-gather.21
  569.5 85.6 all-reduce.16
  658.2 51.6 all-reduce.18
  783.5 27.1 reduce-scatter.16
  812.9 25.7 reduce-scatter.18
  841.7 52.9 reduce-scatter.20
  897.4 54.3 reduce-scatter.32
  954.2 189.1 reduce-scatter.36
  1145.5 189.1 reduce-scatter.40
  1336.9 189.0 reduce-scatter.44
  1528.7 20.3 reduce-scatter.24
  1551.8 20.3 reduce-scatter.28
  1574.3 43.8 reduce-scatter.22
  1620.6 43.1 reduce-scatter.34
  1666.1 143.7 reduce-scatter.38
  1812.2 145.1 reduce-scatter.42
  1959.8 145.1 reduce-scatter.46
  2108.0 86.2 all-reduce.14
  2196.5 21.9 reduce-scatter.26
  2220.8 20.3 reduce-scatter.30
  2242.8 52.4 all-gather.23
  2296.8 45.2 all-gather.25
  2343.8 148.3 all-gather.27
  2493.8 147.8 all-gather.29
  2643.2 147.8 all-gather.31
where the time goes:
time: 2830 us; the launch traced here: 2820 us
  waiting for transfers between devices  2320 us (82%)
  matrix products  237 us (8%)
  blocking collectives  136 us (5%)
  other arithmetic  76.7 us (3%)
  local copies, waits for them, and re-layouts  38.3 us (1%)
    reduce_scatter x1, waiting for transfers between devices, shards(): lax.psum_scatter(gradients[6], 'fsdp', scatter_dimension=0, tiled=True)  191 us
    reduce_scatter x1, waiting for transfers between devices, shards(): lax.psum_scatter(gradients[8], 'fsdp', scatter_dimension=1, tiled=True)  191 us
    reduce_scatter x1, waiting for transfers between devices, shards(): lax.psum_scatter(gradients[7], 'fsdp', scatter_dimension=0, tiled=True)  191 us
    all_gather x1, waiting for transfers between devices, shards(): lax.all_gather(pieces[6], 'ctx', axis=0, tiled=True)  150 us
    all_gather x1, waiting for transfers between devices, shards(): lax.all_gather(pieces[7], 'ctx', axis=0, tiled=True)  150 us
    all_gather x1, waiting for transfers between devices, shards(): lax.all_gather(pieces[8], 'ctx', axis=1, tiled=True)  149 us
    reduce_scatter x1, waiting for transfers between devices, shards(): lax.psum_scatter(halves[7], 'ctx', scatter_dimension=0, tiled=True)  148 us
    reduce_scatter x1, waiting for transfers between devices, shards(): lax.psum_scatter(halves[8], 'ctx', scatter_dimension=1, tiled=True)  148 us
  transfers between devices with their start and end apart: 30, of which 24 were waited for; matrix products, arithmetic and copies ran while one was open for 7% of the time, Pallas kernels for 0%

commit v1 on v0

v1 whole, which is shorter than its diff:
```python
import functools

import jax
import jax.numpy as jnp
from jax import lax
from jax.experimental import pallas as pl
from jax.experimental.pallas import tpu as pltpu
from jax.sharding import PartitionSpec as P

HD = 64
WINDOW = 1024
NORM_EPS = 1e-05
ROPE_BASE = 500000.0
MASK_FILL = -1e30
LANES = 128
F32 = jnp.float32
BF16 = jnp.bfloat16


def dot_rows(matrix, other_side):
    return jnp.dot(matrix, other_side, preferred_element_type=F32)


def dot_back(matrix, other_side):
    return lax.dot_general(matrix, other_side, (((1,), (1,)), ((), ())), preferred_element_type=F32)


def dot_outer(matrix, other_side):
    return lax.dot_general(matrix, other_side, (((0,), (0,)), ((), ())), preferred_element_type=F32)


def tie(*values):
    return lax.optimization_barrier(values)


def take(array, start, size, axis):
    return lax.dynamic_slice_in_dim(array, start, size, axis)


def doc_positions(segments):
    seq_count, seq_length = segments.shape
    index_grid = jnp.broadcast_to(jnp.arange(seq_length, dtype=jnp.int32)[None, :], segments.shape)
    begins = jnp.concatenate(
        [jnp.ones((seq_count, 1), dtype=bool), segments[:, 1:] != segments[:, :-1]], axis=1
    )
    return index_grid - lax.cummax(jnp.where(begins, index_grid, 0), axis=1)


def rope_tables(positions):
    half_size = HD // 2
    frequency = ROPE_BASE ** (-(jnp.arange(half_size, dtype=F32) * 2.0 / HD))
    angles = positions.astype(F32)[:, None] * frequency
    cosine, sine = jnp.cos(angles), jnp.sin(angles)
    return jnp.concatenate([cosine] * 4, axis=1), jnp.concatenate([-sine, sine] * 2, axis=1)


def rotate(vectors, cosine, signed_sine):
    width = vectors.shape[1]
    half = HD // 2
    ahead = jnp.concatenate([vectors[:, half:], vectors[:, :half]], axis=1)
    behind = jnp.concatenate([vectors[:, -half:], vectors[:, :-half]], axis=1)
    first = (jnp.arange(width) % HD < half)[None, :]
    reps = width // LANES
    return vectors * jnp.tile(cosine, (1, reps)) + jnp.where(first, ahead, behind) * jnp.tile(
        signed_sine, (1, reps)
    )


def row_scale_of(values):
    return lax.rsqrt(jnp.mean(values * values, axis=-1, keepdims=True) + NORM_EPS)


def norm_back(grad_hidden, gain, normed, row_scale, residual_grad):
    grad_normed = grad_hidden * gain
    return residual_grad + row_scale * (
        grad_normed - normed * jnp.mean(grad_normed * normed, axis=-1, keepdims=True)
    )


def attend_forward_body(lead, heads, group, q_ref, kv_ref, qseg_ref, kseg_ref, mixed_ref, lse_ref):
    block = q_ref.shape[1]
    reach = kseg_ref.shape[-1]
    start = pl.multiple_of(pl.program_id(1) * block, block)
    window = kv_ref.at[0, pl.ds(start, reach), :]
    distance = (
        lax.broadcasted_iota(jnp.int32, (block, reach), 0)
        + lead
        - lax.broadcasted_iota(jnp.int32, (block, reach), 1)
    )
    allowed = (qseg_ref[0] == kseg_ref[0, 0]) & (distance >= 0) & (distance < WINDOW)
    bias = jnp.where(allowed, 0.0, MASK_FILL)
    lane = lax.broadcasted_iota(jnp.int32, (block, LANES), 1)
    log_sums = jnp.zeros((block, LANES), F32)
    kv_width = heads // group * HD
    outs = []
    for head in range(heads):
        shared = head // group * HD
        keys = window[:, shared : shared + HD]
        values = window[:, kv_width + shared : kv_width + shared + HD]
        scores = dot_back(q_ref[0, :, head * HD : (head + 1) * HD], keys) + bias
        row_max = jnp.max(scores, axis=-1, keepdims=True)
        exponent = jnp.exp(scores - row_max)
        row_total = jnp.sum(exponent, axis=-1, keepdims=True)
        probs = (exponent * (1.0 / row_total)).astype(BF16)
        outs.append(dot_rows(probs, values))
        log_sums = jnp.where(lane == head, row_max + jnp.log(row_total), log_sums)
    mixed_ref[0] = jnp.concatenate(outs, axis=1).astype(BF16)
    lse_ref[0] = log_sums


def attend_backward_body(
    lead, heads, group, q_ref, kv_ref, grad_ref, lse_ref, qseg_ref, kseg_ref, dq_ref, dkv_ref
):
    block = q_ref.shape[1]
    reach = block + lead
    step = pl.program_id(1)
    start = pl.multiple_of(step * block, block)
    window = kv_ref.at[0, pl.ds(start, reach), :]

    @pl.when(step == 0)
    def _():
        dkv_ref[...] = jnp.zeros_like(dkv_ref)

    distance = (
        lax.broadcasted_iota(jnp.int32, (reach, block), 1)
        + lead
        - lax.broadcasted_iota(jnp.int32, (reach, block), 0)
    )
    same = kseg_ref[0, pl.ds(start, reach), :] == qseg_ref[0]
    bias = jnp.where(same & (distance >= 0) & (distance < WINDOW), 0.0, MASK_FILL)
    kv_width = heads // group * HD
    key_grads, value_grads, query_grads = [], [], []
    for shared in range(heads // group):
        keys = window[:, shared * HD : (shared + 1) * HD]
        values = window[:, kv_width + shared * HD : kv_width + (shared + 1) * HD]
        key_sum = value_sum = None
        for member in range(group):
            head = shared * group + member
            query = q_ref[0, :, head * HD : (head + 1) * HD]
            grad = grad_ref[0, :, head * HD : (head + 1) * HD]
            probs = jnp.exp(dot_back(keys, query) + bias - lse_ref[0, head : head + 1, :])
            grad_probs = dot_back(values, grad)
            spread = jnp.sum(probs * grad_probs, axis=0, keepdims=True)
            grad_scores = (probs * (grad_probs - spread)).astype(BF16)
            value_part = dot_rows(probs.astype(BF16), grad)
            key_part = dot_rows(grad_scores, query)
            query_grads.append(dot_outer(grad_scores, keys) * HD**-0.5)
            value_sum = value_part if value_sum is None else value_sum + value_part
            key_sum = key_part if key_sum is None else key_sum + key_part
        key_grads.append(key_sum)
        value_grads.append(value_sum)
    dq_ref[0] = jnp.concatenate(query_grads, axis=1)
    dkv_ref[0, pl.ds(start, reach), :] += jnp.concatenate(key_grads + value_grads, axis=1)


def attention_plan(span, window):
    blocks_back = -(-(window - 1) // span)
    base = (blocks_back * span - (window - 1)) // LANES * LANES
    return blocks_back, base, blocks_back * span - base


def key_tiles(key_segments, base, lead, block, span):
    return jnp.stack(
        [
            key_segments[:, base + at : base + at + block + lead]
            for at in range(0, span, block)
        ],
        axis=1,
    )[:, :, None, :]


def attend_forward(query, keys_values, query_segments, key_segments, base, lead, group):
    seqs, span, width = query.shape
    block = min(LANES, span)
    heads = width // HD
    reach = block + lead
    keys_used = keys_values[:, base:]
    return pl.pallas_call(
        functools.partial(attend_forward_body, lead, heads, group),
        grid=(seqs, span // block),
        in_specs=[
            pl.BlockSpec((1, block, width), lambda s, i: (s, i, 0)),
            pl.BlockSpec((1,) + keys_used.shape[1:], lambda s, i: (s, 0, 0)),
            pl.BlockSpec((1, block, 1), lambda s, i: (s, i, 0)),
            pl.BlockSpec((1, 1, 1, reach), lambda s, i: (s, i, 0, 0)),
        ],
        out_specs=[
            pl.BlockSpec((1, block, width), lambda s, i: (s, i, 0)),
            pl.BlockSpec((1, block, LANES), lambda s, i: (s, i, 0)),
        ],
        out_shape=[
            jax.ShapeDtypeStruct(query.shape, BF16),
            jax.ShapeDtypeStruct((seqs, span, LANES), F32),
        ],
        compiler_params=pltpu.CompilerParams(vmem_limit_bytes=40 << 20),
        cost_estimate=pl.CostEstimate(
            flops=4 * seqs * span * reach * width, bytes_accessed=4 << 20, transcendentals=0
        ),
        name="attend_forward",
    )(query, keys_used, query_segments[:, :, None], key_tiles(key_segments, base, lead, block, span))


def attend_backward(
    query, keys_values, grad_mixed, log_sums, query_segments, key_segments, base, lead, group
):
    seqs, span, width = query.shape
    block = min(LANES, span)
    heads = width // HD
    reach = block + lead
    keys_used = keys_values[:, base:]
    whole_keys = pl.BlockSpec((1,) + keys_used.shape[1:], lambda s, i: (s, 0, 0))
    rows = pl.BlockSpec((1, block, width), lambda s, i: (s, i, 0))
    grad_query, grad_keys_values = pl.pallas_call(
        functools.partial(attend_backward_body, lead, heads, group),
        grid=(seqs, span // block),
        in_specs=[
            rows,
            whole_keys,
            rows,
            pl.BlockSpec((1, heads, block), lambda s, i: (s, 0, i)),
            pl.BlockSpec((1, 1, block), lambda s, i: (s, 0, i)),
            pl.BlockSpec((1, keys_used.shape[1], 1), lambda s, i: (s, 0, 0)),
        ],
        out_specs=[rows, whole_keys],
        out_shape=[
            jax.ShapeDtypeStruct(query.shape, F32),
            jax.ShapeDtypeStruct(keys_used.shape, F32),
        ],
        compiler_params=pltpu.CompilerParams(vmem_limit_bytes=40 << 20),
        cost_estimate=pl.CostEstimate(
            flops=10 * seqs * span * reach * width, bytes_accessed=6 << 20, transcendentals=0
        ),
        name="attend_backward",
    )(
        query,
        keys_used,
        grad_mixed,
        log_sums,
        query_segments[:, None, :],
        key_segments[:, base:, None],
    )
    return grad_query, jnp.pad(grad_keys_values, ((0, 0), (base, 0), (0, 0)))


def swap(value, axis, size, bit):
    return lax.ppermute(value, axis, [(i, i ^ bit) for i in range(size)])


def shift(value, axis, size, by):
    if abs(by) >= size:
        return jnp.zeros_like(value)
    return lax.ppermute(
        value, axis, [(i, i + by) for i in range(size) if 0 <= i + by < size]
    )


class Lane:
    def __init__(self, move, depth=2):
        self.move, self.depth, self.done = move, depth, []

    def send(self, value):
        if len(self.done) >= self.depth:
            value, self.done[-self.depth] = tie(value, self.done[-self.depth])
        self.done.append(self.move(value))
        return len(self.done) - 1

    def get(self, at):
        return self.done[at]


class LineSum:
    def __init__(self, axis):
        self.axis = axis
        index = lax.axis_index(axis)
        self.edge = (index == 0) | (index == 3)
        self.partial = None
        self.total = None
        self.outs = []

    def add(self, own):
        total, self.total = self.total, None
        if own is not None and total is not None and own.shape == total.shape:
            out_first = jnp.where(self.edge, own, total)
            sends = [out_first]
        else:
            sends = [v for v in (own, total) if v is not None]
        if self.partial is not None:
            sends.append(self.partial)
        sends = list(tie(*sends)) if len(sends) > 1 else sends
        partial = sends.pop() if self.partial is not None else None
        inward, outward = [(0, 1), (3, 2)], [(1, 0), (2, 3)]
        got_in = got_out = middle = None
        if len(sends) == 1 and own is not None and total is not None:
            got_in = got_out = lax.ppermute(sends[0], self.axis, inward + outward)
        else:
            if own is not None:
                got_in = lax.ppermute(sends.pop(0), self.axis, inward)
            if total is not None:
                got_out = lax.ppermute(sends.pop(0), self.axis, outward)
        if partial is not None:
            middle = lax.ppermute(partial, self.axis, [(1, 2), (2, 1)])
        got = [v for v in (got_in if got_in is not None else got_out, middle) if v is not None]
        if len(got) == 2:
            first, middle = tie(*got)
            if got_in is not None:
                got_out = first if got_out is got_in else got_out
                got_in = first
            else:
                got_out = first
        if total is not None:
            self.outs.append(jnp.where(self.edge, got_out, total).astype(F32))
        if partial is not None:
            self.total = (partial.astype(F32) + middle.astype(F32)).astype(BF16)
        self.partial = None
        if own is not None:
            self.partial = (own.astype(F32) + got_in.astype(F32)).astype(BF16)

    def finish(self):
        while self.partial is not None or self.total is not None:
            self.add(None)
        return self.outs


class WholeSum:
    def __init__(self, axis):
        self.axis, self.outs = axis, []

    def add(self, own):
        self.outs.append(lax.psum(own.astype(F32), self.axis))

    def finish(self):
        return self.outs


def shards(
    sizes,
    block_input,
    segment_ids,
    attention_gain,
    query_weight,
    key_weight,
    value_weight,
    out_weight,
    feed_gain,
    gate_weight,
    up_weight,
    down_weight,
    cotangent,
):
    shard_count, ctx_count, tp_count = sizes
    seqs, span, width = block_input.shape
    rows = seqs * span
    seq_length = segment_ids.shape[1]
    half = width // 2
    part = half // 2
    q_width = query_weight.shape[1]
    kv_width = key_weight.shape[1]
    feed_width = gate_weight.shape[1]
    group = q_width // kv_width
    shard, ctx, tp = (lax.axis_index(name) for name in ("fsdp", "ctx", "tp"))
    odd = ctx % 2
    sibling = tp % 2

    own_at = shard * half
    near_at = (1 - shard) * half + odd * part
    far_at = (1 - shard) * half + (1 - odd) * part

    def to_local(value):
        return jnp.concatenate(
            [
                take(value, own_at, half, 1),
                take(value, near_at, part, 1),
                take(value, far_at, part, 1),
            ],
            axis=1,
        )

    def other_half(value):
        return jnp.concatenate(
            [
                take(value, half + odd * part, part, 1),
                take(value, half + (1 - odd) * part, part, 1),
            ],
            axis=1,
        )

    def from_local(value):
        own, other = value[:, :half], other_half(value)
        return jnp.where(
            shard == 0,
            jnp.concatenate([own, other], axis=1),
            jnp.concatenate([other, own], axis=1),
        )

    fsdp_lane = Lane(lambda value: swap(value, "fsdp", shard_count, 1))

    def fetch(weight, axis):
        at = fsdp_lane.send(take(weight, odd * part, part, axis))
        return lambda: (fsdp_lane.get(at), swap(fsdp_lane.get(at), "ctx", ctx_count, 1))

    def swap_half(value):
        mine = take(value, sibling * (rows // 2), rows // 2, 0)
        at = fsdp_lane.send(mine)

        def land():
            got = fsdp_lane.get(at)
            other = swap(got, "tp", tp_count, 1)
            return jnp.where(
                sibling == 0,
                jnp.concatenate([got, other], axis=0),
                jnp.concatenate([other, got], axis=0),
            )

        return land

    def tp_sum(first, second):
        if tp_count != 4:
            whole = jnp.where(
                sibling == 0,
                jnp.concatenate([second, first], axis=0),
                jnp.concatenate([first, second], axis=0),
            )
            return lax.psum(whole, "tp")
        chip = (second + swap(first.astype(BF16), "tp", tp_count, 1).astype(F32)).astype(BF16)
        total = (chip.astype(F32) + swap(chip, "tp", tp_count, 2).astype(F32)).astype(BF16)
        other = swap(total, "tp", tp_count, 1)
        return jnp.where(
            sibling == 0,
            jnp.concatenate([total, other], axis=0),
            jnp.concatenate([other, total], axis=0),
        ).astype(F32)

    def row_halves(value):
        return (
            take(value, (1 - sibling) * (rows // 2), rows // 2, 0),
            take(value, sibling * (rows // 2), rows // 2, 0),
        )

    gains_own = jnp.stack([attention_gain, feed_gain])
    gains_other = swap(gains_own, "fsdp", shard_count, 1)
    gains = jnp.concatenate(
        [gains_own, take(gains_other, odd * part, part, 1), take(gains_other, (1 - odd) * part, part, 1)],
        axis=1,
    ).astype(F32)
    gain_a, gain_m = gains[0:1], gains[1:2]

    qkv_own = jnp.concatenate([query_weight, key_weight, value_weight], axis=1)
    qkv_fetch = fetch(qkv_own, 0)
    out_fetch = fetch(out_weight, 1)
    feed_cuts = 2
    feed_part = feed_width // feed_cuts
    feed_fetch = []
    for cut in range(feed_cuts):
        columns = slice(cut * feed_part, (cut + 1) * feed_part)
        feed_fetch.append((fetch(gate_weight[:, columns], 0), fetch(up_weight[:, columns], 0)))

    span_start = ctx * span
    positions = take(doc_positions(segment_ids), span_start, span, 1).reshape(rows)
    query_segments = take(segment_ids, span_start, span, 1)
    cosine, sine = rope_tables(positions)
    blocks_back, base, lead = attention_plan(span, WINDOW)
    key_segments = take(
        jnp.pad(segment_ids, ((0, 0), (blocks_back * span, 0)), constant_values=-1),
        span_start,
        (blocks_back + 1) * span,
        1,
    )

    inputs = to_local(block_input.reshape(rows, width)).astype(F32)
    grad_rows = to_local(cotangent.reshape(rows, width))
    scale_a = row_scale_of(inputs)
    normed_a = inputs * scale_a
    hidden_a = (normed_a * gain_a).astype(BF16)

    def dot_pieces(matrix, own, pieces):
        near, far = pieces
        return (
            dot_rows(matrix[:, :half], own)
            + dot_rows(matrix[:, half : half + part], near)
            + dot_rows(matrix[:, half + part :], far)
        )

    def back_pieces(matrix, own, pieces):
        near, far = pieces
        return jnp.concatenate(
            [dot_back(matrix, own), dot_back(matrix, near), dot_back(matrix, far)], axis=1
        )

    qkv_pieces = qkv_fetch()
    qkv = dot_pieces(hidden_a, qkv_own, qkv_pieces)
    key_low = rotate(qkv[:, q_width : q_width + kv_width], cosine, sine).astype(BF16)
    value_low = qkv[:, q_width + kv_width :].astype(BF16)
    keys_values = jnp.concatenate([key_low, value_low], axis=1).reshape(seqs, span, 2 * kv_width)
    keys_values = jnp.concatenate(
        [shift(keys_values, "ctx", ctx_count, back) for back in range(blocks_back, 0, -1)]
        + [keys_values],
        axis=1,
    )
    query_low = (rotate(qkv[:, :q_width], cosine, sine).astype(BF16) * HD**-0.5).reshape(
        seqs, span, q_width
    )
    mixed, log_sums = attend_forward(
        query_low, keys_values, query_segments, key_segments, base, lead, group
    )
    mixed_low = mixed.reshape(rows, q_width)
    out_pieces = out_fetch()

    def out_project(matrix):
        return jnp.concatenate(
            [dot_rows(matrix, out_weight)] + [dot_rows(matrix, piece) for piece in out_pieces],
            axis=1,
        )

    branch_a = tp_sum(*(out_project(value) for value in row_halves(mixed_low)))
    middle = inputs + branch_a

    scale_m = row_scale_of(middle)
    normed_m = middle * scale_m
    hidden_m = (normed_m * gain_m).astype(BF16)
    feed_pieces = [(gate(), up()) for gate, up in feed_fetch]
    gate_cuts, up_cuts, act_cuts, act_other = [], [], [], []
    for cut in range(feed_cuts):
        columns = slice(cut * feed_part, (cut + 1) * feed_part)
        gate_value = dot_pieces(hidden_m, gate_weight[:, columns], feed_pieces[cut][0])
        up_value = dot_pieces(hidden_m, up_weight[:, columns], feed_pieces[cut][1])
        activated = (jax.nn.silu(gate_value) * up_value).astype(BF16)
        gate_cuts.append(gate_value)
        up_cuts.append(up_value)
        act_cuts.append(activated)

    grad_land = swap_half(other_half(grad_rows))
    act_at = [fsdp_lane.send(act_cuts[0])]
    down_fetch = [fetch(down_weight[:feed_part], 1)]
    act_at.append(fsdp_lane.send(act_cuts[1]))
    down_fetch.append(fetch(down_weight[feed_part:], 1))
    hidden_m_land = swap_half(other_half(hidden_m))

    line = [LineSum("ctx") if ctx_count == 4 else WholeSum("ctx") for _ in range(2)]
    made = []

    def reduce_over_ctx(own):
        at = len(made)
        made.append(own)
        line[at % 2].add(own)

    grad_own, grad_other = grad_rows[:, :half], grad_land()
    for cut in range(feed_cuts):
        other = fsdp_lane.get(act_at[cut])
        for piece in range(2):
            columns = slice(piece * feed_part // 2, (piece + 1) * feed_part // 2)
            reduce_over_ctx(
                (
                    dot_outer(act_cuts[cut][:, columns], grad_own)
                    + dot_outer(other[:, columns], grad_other)
                ).astype(BF16)
            )

    down_pieces = [land() for land in down_fetch]
    grad_gate_cuts, grad_up_cuts, gate_at, up_at = [], [], [], []
    for cut in range(feed_cuts):
        columns = slice(cut * feed_part, (cut + 1) * feed_part)
        near, far = down_pieces[cut]
        grad_act = (
            dot_back(grad_rows[:, :half], down_weight[columns])
            + dot_back(grad_rows[:, half : half + part], near)
            + dot_back(grad_rows[:, half + part :], far)
        )
        gate_value, up_value = gate_cuts[cut], up_cuts[cut]
        sigmoid_gate = jax.nn.sigmoid(gate_value)
        grad_gate = (
            grad_act * up_value * sigmoid_gate * (1.0 + gate_value * (1.0 - sigmoid_gate))
        ).astype(BF16)
        grad_up = (grad_act * gate_value * sigmoid_gate).astype(BF16)
        gate_at.append(fsdp_lane.send(grad_gate))
        up_at.append(fsdp_lane.send(grad_up))
        grad_gate_cuts.append(grad_gate)
        grad_up_cuts.append(grad_up)

    def feed_back(which):
        total = None
        for cut in range(feed_cuts):
            columns = slice(cut * feed_part, (cut + 1) * feed_part)
            gate_rows = row_halves(grad_gate_cuts[cut])[which]
            up_rows = row_halves(grad_up_cuts[cut])[which]
            value = back_pieces(gate_rows, gate_weight[:, columns], feed_pieces[cut][0])
            value += back_pieces(up_rows, up_weight[:, columns], feed_pieces[cut][1])
            total = value if total is None else total + value
        return total

    grad_hidden_m = tp_sum(feed_back(0), feed_back(1))
    feed_gain_part = jnp.sum(grad_hidden_m * normed_m, axis=0)
    grad_middle = norm_back(grad_hidden_m, gain_m, normed_m, scale_m, grad_rows.astype(F32))
    grad_branch = grad_middle.astype(BF16)

    hidden_own, hidden_other = hidden_m[:, :half], hidden_m_land()
    for cut in range(feed_cuts):
        for own, at in ((grad_gate_cuts[cut], gate_at[cut]), (grad_up_cuts[cut], up_at[cut])):
            other = fsdp_lane.get(at)
            for piece in range(2):
                columns = slice(piece * part, (piece + 1) * part)
                reduce_over_ctx(
                    (
                        dot_outer(hidden_own[:, columns], own)
                        + dot_outer(hidden_other[:, columns], other)
                    ).astype(BF16)
                )

    def down_project(which):
        total = None
        for cut in range(feed_cuts):
            act_rows = row_halves(act_cuts[cut])[which]
            columns = slice(cut * feed_part, (cut + 1) * feed_part)
            value = jnp.concatenate(
                [dot_rows(act_rows, down_weight[columns])]
                + [dot_rows(act_rows, piece) for piece in down_pieces[cut]],
                axis=1,
            )
            total = value if total is None else total + value
        return total

    branch_m = tp_sum(down_project(0), down_project(1))
    block_out = from_local((middle + branch_m).astype(BF16)).reshape(seqs, span, width)

    grad_mixed = (
        dot_back(grad_branch[:, :half], out_weight)
        + dot_back(grad_branch[:, half : half + part], out_pieces[0])
        + dot_back(grad_branch[:, half + part :], out_pieces[1])
    ).astype(BF16)
    branch_land = swap_half(other_half(grad_branch))
    mixed_at = fsdp_lane.send(mixed_low)
    hidden_a_land = swap_half(other_half(hidden_a))
    grad_query, grad_keys_values = attend_backward(
        query_low,
        keys_values,
        grad_mixed.reshape(seqs, span, q_width),
        jnp.swapaxes(log_sums, 1, 2)[:, : q_width // HD],
        query_segments,
        key_segments,
        base,
        lead,
        group,
    )
    kv_sum = grad_keys_values[:, blocks_back * span :]
    for back in range(1, blocks_back + 1):
        at = (blocks_back - back) * span
        kv_sum = kv_sum + shift(
            grad_keys_values[:, at : at + span].astype(BF16), "ctx", ctx_count, -back
        ).astype(F32)
    kv_sum = kv_sum.reshape(rows, 2 * kv_width)
    grad_qkv = jnp.concatenate(
        [
            rotate(grad_query.reshape(rows, q_width), cosine, -sine),
            rotate(kv_sum[:, :kv_width], cosine, -sine),
            kv_sum[:, kv_width:],
        ],
        axis=1,
    ).astype(BF16)
    qkv_at = fsdp_lane.send(grad_qkv)
    grad_hidden_a = tp_sum(
        *(back_pieces(value, qkv_own, qkv_pieces) for value in row_halves(grad_qkv))
    )
    attention_gain_part = jnp.sum(grad_hidden_a * normed_a, axis=0)
    input_grad = norm_back(grad_hidden_a, gain_a, normed_a, scale_a, grad_middle)
    input_grad = from_local(input_grad.astype(BF16)).reshape(seqs, span, width)

    reduce_over_ctx(
        (
            dot_outer(mixed_low, grad_branch[:, :half])
            + dot_outer(fsdp_lane.get(mixed_at), branch_land())
        ).astype(BF16)
    )
    own, other = grad_qkv, fsdp_lane.get(qkv_at)
    hidden_own, hidden_other = hidden_a[:, :half], hidden_a_land()

    def qkv_grad(columns, rows_at):
        return (
            dot_outer(hidden_own[:, rows_at], own[:, columns])
            + dot_outer(hidden_other[:, rows_at], other[:, columns])
        ).astype(BF16)

    row_cuts = [slice(0, part), slice(part, half)]
    reduce_over_ctx(
        jnp.concatenate([qkv_grad(slice(0, q_width), cut) for cut in row_cuts], axis=1)
    )
    reduce_over_ctx(
        jnp.concatenate([qkv_grad(slice(q_width, None), cut) for cut in row_cuts], axis=1)
    )

    gain_parts = jnp.stack([attention_gain_part, feed_gain_part])
    gain_other = swap(other_half(gain_parts), "fsdp", shard_count, 1)
    gain_sums = lax.psum(gain_parts[:, :half] + gain_other, "ctx")

    outs = [line_sum.finish() for line_sum in line]
    sums = [outs[at % 2][at // 2] for at in range(len(made))]
    down_grad = jnp.concatenate(sums[:4], axis=0)
    gate_up = []
    for which in range(2):
        gate_up.append(
            jnp.concatenate(
                [
                    jnp.concatenate(sums[at : at + 2], axis=0)
                    for at in (4 + 2 * which, 8 + 2 * which)
                ],
                axis=1,
            )
        )
    out_grad, q_sum, kv_sum = sums[12:]
    query_grad = jnp.concatenate([q_sum[:, :q_width], q_sum[:, q_width:]], axis=0)
    kv_grad = jnp.concatenate([kv_sum[:, : 2 * kv_width], kv_sum[:, 2 * kv_width :]], axis=0)
    return (
        block_out,
        input_grad,
        gain_sums[0],
        query_grad,
        kv_grad[:, :kv_width],
        kv_grad[:, kv_width:],
        out_grad,
        gain_sums[1],
        gate_up[0],
        gate_up[1],
        down_grad,
    )


def solution(mesh):
    sizes = tuple(mesh.shape[name] for name in ("fsdp", "ctx", "tp"))
    in_specs = (
        P("fsdp", "ctx", None),
        P("fsdp", None),
        P("fsdp"),
        P("fsdp", "tp"),
        P("fsdp", "tp"),
        P("fsdp", "tp"),
        P("tp", "fsdp"),
        P("fsdp"),
        P("fsdp", "tp"),
        P("fsdp", "tp"),
        P("tp", "fsdp"),
        P("fsdp", "ctx", None),
    )
    out_specs = (
        P("fsdp", "ctx", None),
        P("fsdp", "ctx", None),
        P("fsdp"),
        P("fsdp", "tp"),
        P("fsdp", "tp"),
        P("fsdp", "tp"),
        P("tp", "fsdp"),
        P("fsdp"),
        P("fsdp", "tp"),
        P("fsdp", "tp"),
        P("tp", "fsdp"),
    )
    return jax.shard_map(
        functools.partial(shards, sizes),
        mesh=mesh,
        in_specs=in_specs,
        out_specs=out_specs,
        check_vma=False,
    )
```

time: 2830 us -> 919 us (0.32)
  waiting for transfers between devices: 2320 us -> 253 us
  starting transfers between devices: 2.19 us -> 160 us
  blocking collectives: 136 us -> 12.2 us
  other arithmetic: 76.7 us -> 179 us
  matrix products: 237 us -> 181 us
  local copies, waits for them, and re-layouts: 38.3 us -> 81.2 us
  Pallas kernels: 0 us -> 38.3 us
    reduce_scatter x16 -> x0, waiting for transfers between devices: 1230 us -> none  [the longest x1 191 us: shards(): lax.psum_scatter(gradients[6], 'fsdp', scatter_dimension=0, tiled=True)]
    all_gather x10 -> x0, waiting for transfers between devices: 801 us -> none  [the longest x1 150 us: shards(): lax.all_gather(pieces[6], 'ctx', axis=0, tiled=True)]
    psum x4 -> x0, waiting for transfers between devices: 282 us -> none  [the longest x1 83.9 us: shards(): lax.psum(dot_back(grad_query_raw, query_full) + dot_back(grad_key_raw, ke...]
    ppermute x0 -> x85, waiting for transfers between devices: none -> 253 us  [the longest x46 158 us: swap(): return lax.ppermute(value, axis, [(i, i ^ bit) for i in range(size)])]
    ppermute x0 -> x85, starting transfers between devices: none -> 160 us  [the longest x10 58.2 us: add(): got_in = got_out = lax.ppermute(sends[0], self.axis, inward + outward)]
    all_gather x10 -> x0, blocking collectives: 116 us -> none  [the longest x1 19.9 us: shards(): lax.all_gather(pieces[3], 'ctx', axis=0, tiled=True)]
    dot_general x16 -> x33, matrix products: 134 us -> 44.6 us  [dot_rows(): return jnp.dot(matrix, other_side, preferred_element_type=F32)]
    convert_element_type x6 -> x41, other arithmetic: 0.49 us -> 84.7 us  [the longest x15 23.1 us: add(): self.partial = (own.astype(F32) + got_in.astype(F32)).astype(BF16)]
  transfers between devices with their start and end apart: 30 -> 85, of which waited for: 24 -> 24; matrix products, arithmetic and copies ran while one was open for 7% -> 47% of each run, Pallas kernels for 0% -> 4%
where the time goes in v1:
time: 919 us; the launch traced here: 909 us
  waiting for transfers between devices  253 us (28%)
  matrix products  181 us (20%)
  other arithmetic  179 us (19%)
  starting transfers between devices  160 us (17%)
  local copies, waits for them, and re-layouts  81.2 us (9%)
  Pallas kernels  38.3 us (4%)
  blocking collectives  12.2 us (1%)
    ppermute x46, waiting for transfers between devices, swap(): return lax.ppermute(value, axis, [(i, i ^ bit) for i in range(size)])  158 us
    dot_general x39, matrix products, dot_back(): lax.dot_general(matrix, other_side, (((1,), (1,)), ((), ())), preferred_e...  77.5 us
    dot_general x34, matrix products, dot_outer(): lax.dot_general(matrix, other_side, (((0,), (0,)), ((), ())), preferred_e...  58.6 us
    ppermute x10, starting transfers between devices, add(): got_in = got_out = lax.ppermute(sends[0], self.axis, inward + outward)  58.2 us
    unnamed x293, local copies, waits for them, and re-layouts  45.6 us
    dot_general x33, matrix products, dot_rows(): return jnp.dot(matrix, other_side, preferred_element_type=F32)  44.6 us
    ppermute x5, waiting for transfers between devices, add(): got_in = lax.ppermute(sends.pop(0), self.axis, inward)  43.1 us
    ppermute x46, starting transfers between devices, swap(): return lax.ppermute(value, axis, [(i, i ^ bit) for i in range(size)])  37.1 us
  transfers between devices with their start and end apart: 85, of which 24 were waited for; matrix products, arithmetic and copies ran while one was open for 47% of the time, Pallas kernels for 4%

profile of v1, /device:TPU:0, one launch (start us, length us, event | category | flops | bytes accessed | tf_op | source)
XLA Modules:
  0.0 908.5 jit_solution(10928872920513225069)
XLA Ops:
  15.9 4.2 fusion.358
  42.1 9.5 %collective-permute-done.2 = bf16[512,768]{1,0:T(8,128)(2,1)S(1)} collective-permute-done((bf16[512,768]{1,0:T(8,128)(2,1)}, bf16[512,768]{1,0:T(8,128)(2,1)S(1)}, u32[]{:S(2)}, u32[]{:S(2)}) %collective-permute-start.2) | collective-permute-done | bytes 786464 | tf_op jit(solution)/shard_map/ppermute | solution.py:246
  57.8 4.5 collective-permute-start.3
  63.7 3.9 collective-permute-done.4
  71.2 17.3 %attend_forward.1 = (bf16[1,512,512]{2,1,0:T(8,128)(2,1)S(1)}, f32[1,512,128]{2,1,0:T(8,128)S(1)}) custom-call(bf16[1,512,512]{2,1,0:T(8,128)(2,1)S(1)} %multiply_bitcast_fusion.q_ref, bf16[1,1536,256]{2,1,0:T(8,128)(2,1)S(1)} %pad_maximum_fusion.6.kv_ref, s32[1,512,1]{2,1,0:T(8,128)S(1)} %copy.94.qseg_ref, s32[1,4,1,1152]{3,2,1,0:T(1,128)S(1)} %add_bitcast_fusion.1.kseg_ref), custom_call_target="tpu_custom_call" | custom-call | flops 1207959552 | bytes 4194304 | tf_op jit(solution)/shard_map/attend_forward/pallas_call | solution.py:178
  106.3 35.5 %collective-permute-done.14 = bf16[512,1024]{1,0:T(8,128)(2,1)} collective-permute-done((bf16[512,1024]{1,0:T(8,128)(2,1)}, bf16[512,1024]{1,0:T(8,128)(2,1)}, u32[]{:S(2)}, u32[]{:S(2)}) %collective-permute-start.14) | collective-permute-done | bytes 1048608 | tf_op jit(solution)/shard_map/ppermute | solution.py:246
  144.5 4.2 fusion.340
  150.2 6.6 collective-permute-done.15
  163.0 4.3 fusion.336
  171.9 7.4 collective-permute-done.19
  179.3 19.6 %collective-permute-done.16 = bf16[1024,512]{1,0:T(8,128)(2,1)} collective-permute-done((bf16[1024,512]{1,0:T(8,128)(2,1)}, bf16[1024,512]{1,0:T(8,128)(2,1)}, u32[]{:S(2)}, u32[]{:S(2)}) %collective-permute-start.16) | collective-permute-done | bytes 1048608 | tf_op jit(solution)/shard_map/ppermute | solution.py:246
  204.7 4.4 multiply_convert_fusion
  231.2 30.5 %collective-permute-done.18 = bf16[512,1024]{1,0:T(8,128)(2,1)S(1)} collective-permute-done((bf16[512,1024]{1,0:T(8,128)(2,1)}, bf16[512,1024]{1,0:T(8,128)(2,1)S(1)}, u32[]{:S(2)}, u32[]{:S(2)}) %collective-permute-start.18) | collective-permute-done | bytes 1048608 | tf_op jit(solution)/shard_map/ppermute | solution.py:246
  264.7 19.2 %collective-permute-done.17 = bf16[1024,512]{1,0:T(8,128)(2,1)S(1)} collective-permute-done((bf16[1024,512]{1,0:T(8,128)(2,1)}, bf16[1024,512]{1,0:T(8,128)(2,1)S(1)}, u32[]{:S(2)}, u32[]{:S(2)}) %collective-permute-start.17) | collective-permute-done | bytes 1048608 | tf_op jit(solution)/shard_map/ppermute | solution.py:246
  323.9 11.6 %collective-permute-done.22 = bf16[1024,512]{1,0:T(8,128)(2,1)S(1)} collective-permute-done((bf16[1024,512]{1,0:T(8,128)(2,1)S(1)}, bf16[1024,512]{1,0:T(8,128)(2,1)S(1)}, u32[]{:S(2)}, u32[]{:S(2)}) %collective-permute-start.22) | collective-permute-done | bytes 1048608 | tf_op jit(solution)/shard_map/ppermute | solution.py:246
  359.2 3.9 fusion.27
  393.3 7.0 collective-permute-done.49
  404.7 4.7 collective-permute-start.50
  414.2 8.5 collective-permute-done.66
  427.6 7.2 collective-permute-done.42
  435.4 8.6 collective-permute-done.50
  444.0 4.4 collective-permute-start.67
  450.7 19.1 %collective-permute-done.67 = bf16[512,1024]{0,1:T(8,128)(2,1)S(1)} collective-permute-done((bf16[512,1024]{0,1:T(8,128)(2,1)S(1)}, bf16[512,1024]{0,1:T(8,128)(2,1)S(1)}, u32[]{:S(2)}, u32[]{:S(2)}) %collective-permute-start.67) | collective-permute-done | bytes 1048608 | tf_op jit(solution)/shard_map/ppermute | solution.py:297
  476.5 5.1 collective-permute-start.52
  495.4 5.3 add_convert_fusion
  503.4 4.2 fusion.10
  507.7 6.8 fusion.335
  517.4 21.0 %attend_backward.1 = (f32[1,512,512]{2,1,0:T(8,128)S(1)}, f32[1,1536,256]{2,1,0:T(8,128)S(1)}) custom-call(bf16[1,512,512]{2,1,0:T(8,128)(2,1)S(1)} %multiply_bitcast_fusion.q_ref, bf16[1,1536,256]{2,1,0:T(8,128)(2,1)S(1)} %pad_maximum_fusion.6.kv_ref, bf16[1,512,512]{2,1,0:T(8,128)(2,1)S(1)} %fusion.32.grad_ref, f32[1,8,512]{2,1,0:T(8,128)S(1)} %slice.416.lse_ref, ...), custom_call_target="tpu_custom_call" | custom-call | flops 3019898880 | bytes 6291456 | tf_op jit(solution)/shard_map/attend_backward/pallas_call | solution.py:213
  548.0 4.8 fusion.13
  571.8 5.1 collective-permute-start.71
  601.2 5.9 collective-permute-done.45
  615.7 5.5 collective-permute-start.56
  626.6 3.9 maximum_convert_fusion.2
  634.3 9.3 %copy.129 = f32[2048,1024]{1,0:T(8,128)} copy(f32[2048,1024]{0,1:T(8,128)} %maximum_convert_fusion.2) | data formatting | bytes 16777216
  671.2 11.4 %collective-permute-start.75 = (bf16[512,1024]{0,1:T(8,128)(2,1)S(1)}, bf16[512,1024]{0,1:T(8,128)(2,1)S(1)}, u32[]{:S(2)}, u32[]{:S(2)}) collective-permute-start(bf16[512,1024]{0,1:T(8,128)(2,1)S(1)} %get-tuple-element.186), channel_id=1, source_target_pairs={{0,4},{12,8},{4,0},{8,12},{1,5},{13,9},{5,1},{9,13},{2,6},{14,10},... | collective-permute-start | bytes 3145736 | tf_op jit(solution)/shard_map/ppermute | solution.py:294
  687.0 5.4 collective-permute-done.58
  695.2 11.3 %collective-permute-start.60 = (bf16[512,1024]{0,1:T(8,128)(2,1)}, bf16[512,1024]{0,1:T(8,128)(2,1)}, u32[]{:S(2)}, u32[]{:S(2)}) collective-permute-start(bf16[512,1024]{0,1:T(8,128)(2,1)} %broadcast_select_fusion.17), channel_id=1, source_target_pairs={{0,4},{12,8},{4,0},{8,12},{1,5},{13,9},{5,1},{9,13},{2,6},{14,10},... | collective-permute-start | bytes 3145736 | tf_op jit(solution)/shard_map/ppermute | solution.py:294
  708.1 6.8 collective-permute-done.75
  718.4 11.3 %collective-permute-start.77 = (bf16[512,1024]{0,1:T(8,128)(2,1)}, bf16[512,1024]{0,1:T(8,128)(2,1)}, u32[]{:S(2)}, u32[]{:S(2)}) collective-permute-start(bf16[512,1024]{0,1:T(8,128)(2,1)} %get-tuple-element.190), channel_id=1, source_target_pairs={{0,4},{12,8},{4,0},{8,12},{1,5},{13,9},{5,1},{9,13},{2,6},{14,10},... | collective-permute-start | bytes 3145736 | tf_op jit(solution)/shard_map/ppermute | solution.py:294
  739.4 9.9 %fusion.9 = bf16[512,2048]{1,0:T(8,128)(2,1)S(1)} fusion(f32[512]{0:T(512)S(1)} %broadcast_multiply_fusion, f32[2048]{0:T(1024)S(1)} %bitcast.207, f32[512]{0:T(512)S(1)} %copy-done.138, f32[512]{0:T(512)S(1)} %broadcast_multiply_fusion.1, f32[2048]{0:T(1024)S(1)} %bitcast.204, f32[512]{0:T(512)S(1)} %add_rsqrt_fusion, ...), kind=kLoop, calls=%fused_computation.15 | loop fusion | flops 58720256 | bytes 12607489 | tf_op jit(solution)/shard_map/convert_element_type | solution.py:664
  753.2 12.2 %psum.7 = f32[2,1024]{1,0:T(2,128)S(1)} all-reduce(f32[2,1024]{1,0:T(2,128)S(1)} %fusion.313), channel_id=1, replica_groups=mesh['fsdp'=2,'ctx'=4,'tp'=4] {'ctx'}, use_global_device_ids=true, to_apply=%region_8.9 | all-reduce | flops 2048 | bytes 16384 | tf_op jit(solution)/shard_map/psum | solution.py:691
  780.0 13.0 %collective-permute-start.79 = (bf16[512,512]{0,1:T(8,128)(2,1)}, bf16[512,512]{0,1:T(8,128)(2,1)}, u32[]{:S(2)}, u32[]{:S(2)}) collective-permute-start(bf16[512,512]{0,1:T(8,128)(2,1)} %pad_maximum_fusion.9), channel_id=1, source_target_pairs={{0,4},{12,8},{1,5},{13,9},{2,6},{14,10},{3,7},{15,11},{16,20},{28,... | collective-permute-start | bytes 1572872 | tf_op jit(solution)/shard_map/ppermute | solution.py:297
  798.1 17.5 %maximum_convert_fusion = f32[1024,2048]{0,1:T(8,128)} fusion(bf16[512,1024]{0,1:T(8,128)(2,1)S(1)} %broadcast_select_fusion.8, bf16[512,1024]{0,1:T(8,128)(2,1)S(1)} %broadcast_select_fusion.9, bf16[512,1024]{0,1:T(8,128)(2,1)S(1)} %broadcast_select_fusion.10, bf16[512,1024]{0,1:T(8,128)(2,1)S(1)} %copy-done.76), kind=kLoop, calls=%fused_computation.24 | loop fusion | flops 16777216 | bytes 12582912 | tf_op jit(solution)/shard_map/concatenate | solution.py:699
  815.6 9.2 %copy.127 = f32[1024,2048]{1,0:T(8,128)} copy(f32[1024,2048]{0,1:T(8,128)} %maximum_convert_fusion) | data formatting | bytes 16777216
  837.5 15.5 %collective-permute-done.84 = bf16[512,1024]{0,1:T(8,128)(2,1)S(1)} collective-permute-done((bf16[512,1024]{0,1:T(8,128)(2,1)}, bf16[512,1024]{0,1:T(8,128)(2,1)S(1)}, u32[]{:S(2)}, u32[]{:S(2)}) %collective-permute-start.84) | collective-permute-done | bytes 1048608 | tf_op jit(solution)/shard_map/ppermute | solution.py:299
  853.2 17.5 %maximum_convert_fusion.1 = f32[1024,2048]{0,1:T(8,128)} fusion(bf16[512,1024]{0,1:T(8,128)(2,1)S(1)} %broadcast_select_fusion.4, bf16[512,1024]{0,1:T(8,128)(2,1)S(1)} %broadcast_select_fusion.5, bf16[512,1024]{0,1:T(8,128)(2,1)S(1)} %copy-done.77, bf16[512,1024]{0,1:T(8,128)(2,1)S(1)} %copy-done.78), kind=kLoop, calls=%fused_computation.25 | loop fusion | flops 16777216 | bytes 12582912 | tf_op jit(solution)/shard_map/concatenate | solution.py:699
  870.7 9.1 %copy.128 = f32[1024,2048]{1,0:T(8,128)} copy(f32[1024,2048]{0,1:T(8,128)} %maximum_convert_fusion.1) | data formatting | bytes 16777216
  883.2 14.8 %collective-permute-done.64 = bf16[512,1024]{0,1:T(8,128)(2,1)} collective-permute-done((bf16[512,1024]{0,1:T(8,128)(2,1)S(1)}, bf16[512,1024]{0,1:T(8,128)(2,1)}, u32[]{:S(2)}, u32[]{:S(2)}) %collective-permute-start.64) | collective-permute-done | bytes 1048608 | tf_op jit(solution)/shard_map/ppermute | solution.py:299
  (679 shorter events, 416.8 us)
Async XLA Ops:
  38.3 51.8 %collective-permute-start.6 = (bf16[512,512]{1,0:T(8,128)(2,1)}, bf16[512,512]{1,0:T(8,128)(2,1)S(1)}, u32[]{:S(2)}, u32[]{:S(2)}) collective-permute-start(bf16[512,512]{1,0:T(8,128)(2,1)} %collective-permute-done.5), channel_id=1, source_target_pairs={{0,4},{4,0},{8,12},{12,8},{1,5},{5,1},{9,13},{13,9},{2,6},{6,2},{1... | collective-permute-start | bytes 1572872 | tf_op jit(solution)/shard_map/ppermute | solution.py:246
  39.8 55.6 %collective-permute-start.10 = (bf16[512,1024]{1,0:T(8,128)(2,1)S(1)}, bf16[512,1024]{1,0:T(8,128)(2,1)}, u32[]{:S(2)}, u32[]{:S(2)}) collective-permute-start(bf16[512,1024]{1,0:T(8,128)(2,1)S(1)} %copy-done.120), channel_id=1, source_target_pairs={{0,16},{16,0},{1,17},{17,1},{2,18},{18,2},{3,19},{19,3},{4,20},{20... | collective-permute-start | bytes 3145736 | tf_op jit(solution)/shard_map/ppermute | solution.py:246
  94.9 53.8 %collective-permute-start.12 = (bf16[512,1024]{1,0:T(8,128)(2,1)}, bf16[512,1024]{1,0:T(8,128)(2,1)}, u32[]{:S(2)}, u32[]{:S(2)}) collective-permute-start(bf16[512,1024]{1,0:T(8,128)(2,1)} %get-tuple-element.112), channel_id=1, source_target_pairs={{0,16},{16,0},{1,17},{17,1},{2,18},{18,2},{3,19},{19,3},{4,20},{20... | collective-permute-start | bytes 3145736 | tf_op jit(solution)/shard_map/ppermute | solution.py:246
  95.4 46.4 %collective-permute-start.14 = (bf16[512,1024]{1,0:T(8,128)(2,1)}, bf16[512,1024]{1,0:T(8,128)(2,1)}, u32[]{:S(2)}, u32[]{:S(2)}) collective-permute-start(bf16[512,1024]{1,0:T(8,128)(2,1)} %constant_dynamic-slice_fusion.16), channel_id=1, source_target_pairs={{0,16},{16,0},{1,17},{17,1},{2,18},{18,2},{3,19},{19,3},{4,20},{20... | collective-permute-start | bytes 3145736 | tf_op jit(solution)/shard_map/ppermute | solution.py:246
  100.4 56.9 %collective-permute-start.8 = (bf16[256,2048]{1,0:T(8,128)(2,1)}, bf16[256,2048]{1,0:T(8,128)(2,1)}, u32[]{:S(2)}, u32[]{:S(2)}) collective-permute-start(bf16[256,2048]{1,0:T(8,128)(2,1)} %fusion.19), channel_id=1, source_target_pairs={{0,2},{1,3},{2,0},{3,1},{4,6},{5,7},{6,4},{7,5},{8,10},{9,11},{10,... | collective-permute-start | bytes 3145736 | tf_op jit(solution)/shard_map/ppermute | solution.py:246
  156.8 42.1 %collective-permute-start.16 = (bf16[1024,512]{1,0:T(8,128)(2,1)}, bf16[1024,512]{1,0:T(8,128)(2,1)}, u32[]{:S(2)}, u32[]{:S(2)}) collective-permute-start(bf16[1024,512]{1,0:T(8,128)(2,1)} %constant_dynamic-slice_fusion.13), channel_id=1, source_target_pairs={{0,16},{16,0},{1,17},{17,1},{2,18},{18,2},{3,19},{19,3},{4,20},{20... | collective-permute-start | bytes 3145736 | tf_op jit(solution)/shard_map/ppermute | solution.py:246
  160.2 40.7 %collective-permute-start.9 = (bf16[256,2048]{1,0:T(8,128)(2,1)}, bf16[256,2048]{1,0:T(8,128)(2,1)}, u32[]{:S(2)}, u32[]{:S(2)}) collective-permute-start(bf16[256,2048]{1,0:T(8,128)(2,1)} %add_convert_fusion.45), channel_id=1, source_target_pairs={{0,1},{1,0},{2,3},{3,2},{4,5},{5,4},{6,7},{7,6},{8,9},{9,8},{10,11... | collective-permute-start | bytes 3145736 | tf_op jit(solution)/shard_map/ppermute | solution.py:246
  168.1 56.8 %collective-permute-start.13 = (bf16[512,1024]{1,0:T(8,128)(2,1)}, bf16[512,1024]{1,0:T(8,128)(2,1)}, u32[]{:S(2)}, u32[]{:S(2)}) collective-permute-start(bf16[512,1024]{1,0:T(8,128)(2,1)} %collective-permute-done.12), channel_id=1, source_target_pairs={{0,4},{4,0},{8,12},{12,8},{1,5},{5,1},{9,13},{13,9},{2,6},{6,2},{1... | collective-permute-start | bytes 3145736 | tf_op jit(solution)/shard_map/ppermute | solution.py:246
  168.1 52.7 %collective-permute-start.11 = (bf16[512,1024]{1,0:T(8,128)(2,1)}, bf16[512,1024]{1,0:T(8,128)(2,1)}, u32[]{:S(2)}, u32[]{:S(2)}) collective-permute-start(bf16[512,1024]{1,0:T(8,128)(2,1)} %collective-permute-done.10), channel_id=1, source_target_pairs={{0,4},{4,0},{8,12},{12,8},{1,5},{5,1},{9,13},{13,9},{2,6},{6,2},{1... | collective-permute-start | bytes 3145736 | tf_op jit(solution)/shard_map/ppermute | solution.py:246
  179.3 83.3 %collective-permute-start.20 = (bf16[512,1024]{1,0:T(8,128)(2,1)}, bf16[512,1024]{1,0:T(8,128)(2,1)S(1)}, u32[]{:S(2)}, u32[]{:S(2)}) collective-permute-start(bf16[512,1024]{1,0:T(8,128)(2,1)} %collective-permute-done.19), channel_id=1, source_target_pairs={{0,4},{4,0},{8,12},{12,8},{1,5},{5,1},{9,13},{13,9},{2,6},{6,2},{1... | collective-permute-start | bytes 3145736 | tf_op jit(solution)/shard_map/ppermute | solution.py:246
  198.8 62.9 %collective-permute-start.18 = (bf16[512,1024]{1,0:T(8,128)(2,1)}, bf16[512,1024]{1,0:T(8,128)(2,1)S(1)}, u32[]{:S(2)}, u32[]{:S(2)}) collective-permute-start(bf16[512,1024]{1,0:T(8,128)(2,1)} %collective-permute-done.14), channel_id=1, source_target_pairs={{0,4},{4,0},{8,12},{12,8},{1,5},{5,1},{9,13},{13,9},{2,6},{6,2},{1... | collective-permute-start | bytes 3145736 | tf_op jit(solution)/shard_map/ppermute | solution.py:246
  201.0 170.9 %collective-permute-start.48 = (bf16[256,1024]{1,0:T(8,128)(2,1)}, bf16[256,1024]{1,0:T(8,128)(2,1)}, u32[]{:S(2)}, u32[]{:S(2)}) collective-permute-start(bf16[256,1024]{1,0:T(8,128)(2,1)} %collective-permute-done.15), channel_id=1, source_target_pairs={{0,1},{1,0},{2,3},{3,2},{4,5},{5,4},{6,7},{7,6},{8,9},{9,8},{10,11... | collective-permute-start | bytes 1572872 | tf_op jit(solution)/shard_map/ppermute | solution.py:246
  220.9 62.9 %collective-permute-start.17 = (bf16[1024,512]{1,0:T(8,128)(2,1)}, bf16[1024,512]{1,0:T(8,128)(2,1)S(1)}, u32[]{:S(2)}, u32[]{:S(2)}) collective-permute-start(bf16[1024,512]{1,0:T(8,128)(2,1)} %collective-permute-done.16), channel_id=1, source_target_pairs={{0,4},{4,0},{8,12},{12,8},{1,5},{5,1},{9,13},{13,9},{2,6},{6,2},{1... | collective-permute-start | bytes 3145736 | tf_op jit(solution)/shard_map/ppermute | solution.py:246
  225.0 83.7 %collective-permute-start.21 = (bf16[1024,512]{1,0:T(8,128)(2,1)S(1)}, bf16[1024,512]{1,0:T(8,128)(2,1)S(1)}, u32[]{:S(2)}, u32[]{:S(2)}) collective-permute-start(bf16[1024,512]{1,0:T(8,128)(2,1)S(1)} %copy-done.125), channel_id=1, source_target_pairs={{0,16},{16,0},{1,17},{17,1},{2,18},{18,2},{3,19},{19,3},{4,20},{20... | collective-permute-start | bytes 3145736 | tf_op jit(solution)/shard_map/ppermute | solution.py:246
  308.7 54.9 %collective-permute-start.35 = (bf16[512,1024]{1,0:T(8,128)(2,1)S(1)}, bf16[512,1024]{1,0:T(8,128)(2,1)S(1)}, u32[]{:S(2)}, u32[]{:S(2)}) collective-permute-start(bf16[512,1024]{1,0:T(8,128)(2,1)S(1)} %get-tuple-element.123), channel_id=1, source_target_pairs={{0,16},{16,0},{1,17},{17,1},{2,18},{18,2},{3,19},{19,3},{4,20},{20... | collective-permute-start | bytes 3145736 | tf_op jit(solution)/shard_map/ppermute | solution.py:246
  310.2 55.0 %collective-permute-start.40 = (bf16[512,1024]{1,0:T(8,128)(2,1)S(1)}, bf16[512,1024]{1,0:T(8,128)(2,1)}, u32[]{:S(2)}, u32[]{:S(2)}) collective-permute-start(bf16[512,1024]{1,0:T(8,128)(2,1)S(1)} %get-tuple-element.127), channel_id=1, source_target_pairs={{0,16},{16,0},{1,17},{17,1},{2,18},{18,2},{3,19},{19,3},{4,20},{20... | collective-permute-start | bytes 3145736 | tf_op jit(solution)/shard_map/ppermute | solution.py:246
  346.1 43.1 %collective-permute-start.23 = (bf16[256,2048]{1,0:T(8,128)(2,1)}, bf16[256,2048]{1,0:T(8,128)(2,1)}, u32[]{:S(2)}, u32[]{:S(2)}) collective-permute-start(bf16[256,2048]{1,0:T(8,128)(2,1)} %fusion.22), channel_id=1, source_target_pairs={{0,1},{1,0},{2,3},{3,2},{4,5},{5,4},{6,7},{7,6},{8,9},{9,8},{10,11... | collective-permute-start | bytes 3145736 | tf_op jit(solution)/shard_map/ppermute | solution.py:246
  363.1 47.1 %collective-permute-start.26 = (bf16[256,2048]{1,0:T(8,128)(2,1)}, bf16[256,2048]{1,0:T(8,128)(2,1)}, u32[]{:S(2)}, u32[]{:S(2)}) collective-permute-start(bf16[256,2048]{1,0:T(8,128)(2,1)} %fusion.27), channel_id=1, source_target_pairs={{0,1},{1,0},{2,3},{3,2},{4,5},{5,4},{6,7},{7,6},{8,9},{9,8},{10,11... | collective-permute-start | bytes 3145736 | tf_op jit(solution)/shard_map/ppermute | solution.py:246
  380.1 42.6 %collective-permute-start.66 = (bf16[512,1024]{0,1:T(8,128)(2,1)S(1)}, bf16[512,1024]{0,1:T(8,128)(2,1)}, u32[]{:S(2)}, u32[]{:S(2)}) collective-permute-start(bf16[512,1024]{0,1:T(8,128)(2,1)S(1)} %add_convert_fusion.15), channel_id=1, source_target_pairs={{0,4},{12,8},{1,5},{13,9},{2,6},{14,10},{3,7},{15,11},{16,20},{28,... | collective-permute-start | bytes 3145736 | tf_op jit(solution)/shard_map/ppermute | solution.py:297
  391.7 57.5 %collective-permute-start.24 = (bf16[256,2048]{1,0:T(8,128)(2,1)S(1)}, bf16[256,2048]{1,0:T(8,128)(2,1)S(1)}, u32[]{:S(2)}, u32[]{:S(2)}) collective-permute-start(bf16[256,2048]{1,0:T(8,128)(2,1)S(1)} %fusion.21), channel_id=1, source_target_pairs={{0,2},{1,3},{2,0},{3,1},{4,6},{5,7},{6,4},{7,5},{8,10},{9,11},{10,... | collective-permute-start | bytes 3145736 | tf_op jit(solution)/shard_map/ppermute | solution.py:246
  404.7 39.3 %collective-permute-start.50 = (bf16[512,1024]{0,1:T(8,128)(2,1)S(1)}, bf16[512,1024]{0,1:T(8,128)(2,1)S(1)}, u32[]{:S(2)}, u32[]{:S(2)}) collective-permute-start(bf16[512,1024]{0,1:T(8,128)(2,1)S(1)} %add_convert_fusion.37), channel_id=1, source_target_pairs={{0,4},{12,8},{1,5},{13,9},{2,6},{14,10},{3,7},{15,11},{16,20},{28,... | collective-permute-start | bytes 3145736 | tf_op jit(solution)/shard_map/ppermute | solution.py:297
  409.4 39.0 %collective-permute-start.51 = (bf16[512,1024]{0,1:T(8,128)(2,1)S(1)}, bf16[512,1024]{0,1:T(8,128)(2,1)S(1)}, u32[]{:S(2)}, u32[]{:S(2)}) collective-permute-start(bf16[512,1024]{0,1:T(8,128)(2,1)S(1)} %add_convert_fusion.35), channel_id=1, source_target_pairs={{4,8},{8,4},{5,9},{9,5},{6,10},{10,6},{7,11},{11,7},{20,24},{24,20... | collective-permute-start | bytes 3145736 | tf_op jit(solution)/shard_map/ppermute | solution.py:301
  412.7 37.5 %collective-permute-start.27 = (bf16[256,2048]{1,0:T(8,128)(2,1)S(1)}, bf16[256,2048]{1,0:T(8,128)(2,1)S(1)}, u32[]{:S(2)}, u32[]{:S(2)}) collective-permute-start(bf16[256,2048]{1,0:T(8,128)(2,1)S(1)} %fusion.25), channel_id=1, source_target_pairs={{0,2},{1,3},{2,0},{3,1},{4,6},{5,7},{6,4},{7,5},{8,10},{9,11},{10,... | collective-permute-start | bytes 3145736 | tf_op jit(solution)/shard_map/ppermute | solution.py:246
  434.8 49.9 %collective-permute-start.36 = (bf16[512,1024]{1,0:T(8,128)(2,1)S(1)}, bf16[512,1024]{1,0:T(8,128)(2,1)S(1)}, u32[]{:S(2)}, u32[]{:S(2)}) collective-permute-start(bf16[512,1024]{1,0:T(8,128)(2,1)S(1)} %get-tuple-element.124), channel_id=1, source_target_pairs={{0,16},{16,0},{1,17},{17,1},{2,18},{18,2},{3,19},{19,3},{4,20},{20... | collective-permute-start | bytes 3145736 | tf_op jit(solution)/shard_map/ppermute | solution.py:246
  449.2 38.7 %collective-permute-start.43 = (bf16[512,1024]{1,0:T(8,128)(2,1)S(1)}, bf16[512,1024]{1,0:T(8,128)(2,1)S(1)}, u32[]{:S(2)}, u32[]{:S(2)}) collective-permute-start(bf16[512,1024]{1,0:T(8,128)(2,1)S(1)} %get-tuple-element.130), channel_id=1, source_target_pairs={{0,16},{16,0},{1,17},{17,1},{2,18},{18,2},{3,19},{19,3},{4,20},{20... | collective-permute-start | bytes 3145736 | tf_op jit(solution)/shard_map/ppermute | solution.py:246
  476.5 76.3 %collective-permute-start.52 = (bf16[512,1024]{0,1:T(8,128)(2,1)}, bf16[512,1024]{0,1:T(8,128)(2,1)}, u32[]{:S(2)}, u32[]{:S(2)}) collective-permute-start(bf16[512,1024]{0,1:T(8,128)(2,1)} %get-tuple-element.145), channel_id=1, source_target_pairs={{0,4},{12,8},{4,0},{8,12},{1,5},{13,9},{5,1},{9,13},{2,6},{14,10},... | collective-permute-start | bytes 3145736 | tf_op jit(solution)/shard_map/ppermute | solution.py:294
  484.7 69.6 %collective-permute-start.53 = (bf16[512,1024]{0,1:T(8,128)(2,1)}, bf16[512,1024]{0,1:T(8,128)(2,1)}, u32[]{:S(2)}, u32[]{:S(2)}) collective-permute-start(bf16[512,1024]{0,1:T(8,128)(2,1)} %add_convert_fusion.33), channel_id=1, source_target_pairs={{4,8},{8,4},{5,9},{9,5},{6,10},{10,6},{7,11},{11,7},{20,24},{24,20... | collective-permute-start | bytes 3145736 | tf_op jit(solution)/shard_map/ppermute | solution.py:301
  487.9 73.8 %collective-permute-start.69 = (bf16[512,1024]{0,1:T(8,128)(2,1)}, bf16[512,1024]{0,1:T(8,128)(2,1)}, u32[]{:S(2)}, u32[]{:S(2)}) collective-permute-start(bf16[512,1024]{0,1:T(8,128)(2,1)} %get-tuple-element.174), channel_id=1, source_target_pairs={{0,4},{12,8},{4,0},{8,12},{1,5},{13,9},{5,1},{9,13},{2,6},{14,10},... | collective-permute-start | bytes 3145736 | tf_op jit(solution)/shard_map/ppermute | solution.py:294
  493.8 69.5 %collective-permute-start.70 = (bf16[512,1024]{0,1:T(8,128)(2,1)}, bf16[512,1024]{0,1:T(8,128)(2,1)}, u32[]{:S(2)}, u32[]{:S(2)}) collective-permute-start(bf16[512,1024]{0,1:T(8,128)(2,1)} %add_convert_fusion.12), channel_id=1, source_target_pairs={{4,8},{8,4},{5,9},{9,5},{6,10},{10,6},{7,11},{11,7},{20,24},{24,20... | collective-permute-start | bytes 3145736 | tf_op jit(solution)/shard_map/ppermute | solution.py:301
  502.9 92.4 %collective-permute-start.44 = (bf16[512,1024]{1,0:T(8,128)(2,1)S(1)}, bf16[512,1024]{1,0:T(8,128)(2,1)}, u32[]{:S(2)}, u32[]{:S(2)}) collective-permute-start(bf16[512,1024]{1,0:T(8,128)(2,1)S(1)} %get-tuple-element.131), channel_id=1, source_target_pairs={{0,16},{16,0},{1,17},{17,1},{2,18},{18,2},{3,19},{19,3},{4,20},{20... | collective-permute-start | bytes 3145736 | tf_op jit(solution)/shard_map/ppermute | solution.py:246
  563.3 43.9 %collective-permute-start.54 = (bf16[512,1024]{0,1:T(8,128)(2,1)S(1)}, bf16[512,1024]{0,1:T(8,128)(2,1)S(1)}, u32[]{:S(2)}, u32[]{:S(2)}) collective-permute-start(bf16[512,1024]{0,1:T(8,128)(2,1)S(1)} %get-tuple-element.149), channel_id=1, source_target_pairs={{0,4},{12,8},{4,0},{8,12},{1,5},{13,9},{5,1},{9,13},{2,6},{14,10},... | collective-permute-start | bytes 3145736 | tf_op jit(solution)/shard_map/ppermute | solution.py:294
  570.9 36.8 %collective-permute-start.55 = (bf16[512,1024]{0,1:T(8,128)(2,1)S(1)}, bf16[512,1024]{0,1:T(8,128)(2,1)S(1)}, u32[]{:S(2)}, u32[]{:S(2)}) collective-permute-start(bf16[512,1024]{0,1:T(8,128)(2,1)S(1)} %add_convert_fusion.31), channel_id=1, source_target_pairs={{4,8},{8,4},{5,9},{9,5},{6,10},{10,6},{7,11},{11,7},{20,24},{24,20... | collective-permute-start | bytes 3145736 | tf_op jit(solution)/shard_map/ppermute | solution.py:301
  571.8 42.3 %collective-permute-start.71 = (bf16[512,1024]{0,1:T(8,128)(2,1)S(1)}, bf16[512,1024]{0,1:T(8,128)(2,1)S(1)}, u32[]{:S(2)}, u32[]{:S(2)}) collective-permute-start(bf16[512,1024]{0,1:T(8,128)(2,1)S(1)} %get-tuple-element.178), channel_id=1, source_target_pairs={{0,4},{12,8},{4,0},{8,12},{1,5},{13,9},{5,1},{9,13},{2,6},{14,10},... | collective-permute-start | bytes 3145736 | tf_op jit(solution)/shard_map/ppermute | solution.py:294
  607.1 36.5 %collective-permute-start.31 = (bf16[256,2048]{1,0:T(8,128)(2,1)}, bf16[256,2048]{1,0:T(8,128)(2,1)}, u32[]{:S(2)}, u32[]{:S(2)}) collective-permute-start(bf16[256,2048]{1,0:T(8,128)(2,1)} %pad_maximum_fusion.4), channel_id=1, source_target_pairs={{0,1},{1,0},{2,3},{3,2},{4,5},{5,4},{6,7},{7,6},{8,9},{9,8},{10,11... | collective-permute-start | bytes 3145736 | tf_op jit(solution)/shard_map/ppermute | solution.py:246
  614.2 36.5 %collective-permute-start.46 = (bf16[512,768]{1,0:T(8,128)(2,1)}, bf16[512,768]{1,0:T(8,128)(2,1)}, u32[]{:S(2)}, u32[]{:S(2)}) collective-permute-start(bf16[512,768]{1,0:T(8,128)(2,1)} %pad_maximum_fusion.7), channel_id=1, source_target_pairs={{0,16},{16,0},{1,17},{17,1},{2,18},{18,2},{3,19},{19,3},{4,20},{20... | collective-permute-start | bytes 2359304 | tf_op jit(solution)/shard_map/ppermute | solution.py:246
  615.7 43.4 %collective-permute-start.56 = (bf16[512,1024]{0,1:T(8,128)(2,1)}, bf16[512,1024]{0,1:T(8,128)(2,1)}, u32[]{:S(2)}, u32[]{:S(2)}) collective-permute-start(bf16[512,1024]{0,1:T(8,128)(2,1)} %get-tuple-element.153), channel_id=1, source_target_pairs={{0,4},{12,8},{4,0},{8,12},{1,5},{13,9},{5,1},{9,13},{2,6},{14,10},... | collective-permute-start | bytes 3145736 | tf_op jit(solution)/shard_map/ppermute | solution.py:294
  671.2 43.6 %collective-permute-start.75 = (bf16[512,1024]{0,1:T(8,128)(2,1)S(1)}, bf16[512,1024]{0,1:T(8,128)(2,1)S(1)}, u32[]{:S(2)}, u32[]{:S(2)}) collective-permute-start(bf16[512,1024]{0,1:T(8,128)(2,1)S(1)} %get-tuple-element.186), channel_id=1, source_target_pairs={{0,4},{12,8},{4,0},{8,12},{1,5},{13,9},{5,1},{9,13},{2,6},{14,10},... | collective-permute-start | bytes 3145736 | tf_op jit(solution)/shard_map/ppermute | solution.py:294
  686.9 48.9 %collective-permute-start.33 = (bf16[256,2048]{1,0:T(8,128)(2,1)S(1)}, bf16[256,2048]{1,0:T(8,128)(2,1)S(1)}, u32[]{:S(2)}, u32[]{:S(2)}) collective-permute-start(bf16[256,2048]{1,0:T(8,128)(2,1)S(1)} %add_convert_fusion.42), channel_id=1, source_target_pairs={{0,1},{1,0},{2,3},{3,2},{4,5},{5,4},{6,7},{7,6},{8,9},{9,8},{10,11... | collective-permute-start | bytes 3145736 | tf_op jit(solution)/shard_map/ppermute | solution.py:246
  695.2 70.8 %collective-permute-start.60 = (bf16[512,1024]{0,1:T(8,128)(2,1)}, bf16[512,1024]{0,1:T(8,128)(2,1)}, u32[]{:S(2)}, u32[]{:S(2)}) collective-permute-start(bf16[512,1024]{0,1:T(8,128)(2,1)} %broadcast_select_fusion.17), channel_id=1, source_target_pairs={{0,4},{12,8},{4,0},{8,12},{1,5},{13,9},{5,1},{9,13},{2,6},{14,10},... | collective-permute-start | bytes 3145736 | tf_op jit(solution)/shard_map/ppermute | solution.py:294
  706.5 59.5 %collective-permute-start.61 = (bf16[512,1024]{0,1:T(8,128)(2,1)}, bf16[512,1024]{0,1:T(8,128)(2,1)}, u32[]{:S(2)}, u32[]{:S(2)}) collective-permute-start(bf16[512,1024]{0,1:T(8,128)(2,1)} %add_convert_fusion.25), channel_id=1, source_target_pairs={{4,8},{8,4},{5,9},{9,5},{6,10},{10,6},{7,11},{11,7},{20,24},{24,20... | collective-permute-start | bytes 3145736 | tf_op jit(solution)/shard_map/ppermute | solution.py:301
  718.4 56.2 %collective-permute-start.77 = (bf16[512,1024]{0,1:T(8,128)(2,1)}, bf16[512,1024]{0,1:T(8,128)(2,1)}, u32[]{:S(2)}, u32[]{:S(2)}) collective-permute-start(bf16[512,1024]{0,1:T(8,128)(2,1)} %get-tuple-element.190), channel_id=1, source_target_pairs={{0,4},{12,8},{4,0},{8,12},{1,5},{13,9},{5,1},{9,13},{2,6},{14,10},... | collective-permute-start | bytes 3145736 | tf_op jit(solution)/shard_map/ppermute | solution.py:294
  729.7 44.8 %collective-permute-start.78 = (bf16[512,1024]{0,1:T(8,128)(2,1)}, bf16[512,1024]{0,1:T(8,128)(2,1)}, u32[]{:S(2)}, u32[]{:S(2)}) collective-permute-start(bf16[512,1024]{0,1:T(8,128)(2,1)} %add_convert_fusion.4), channel_id=1, source_target_pairs={{4,8},{8,4},{5,9},{9,5},{6,10},{10,6},{7,11},{11,7},{20,24},{24,20... | collective-permute-start | bytes 3145736 | tf_op jit(solution)/shard_map/ppermute | solution.py:301
  771.3 54.8 %collective-permute-start.62 = (bf16[512,1024]{0,1:T(8,128)(2,1)}, bf16[512,1024]{0,1:T(8,128)(2,1)}, u32[]{:S(2)}, u32[]{:S(2)}) collective-permute-start(bf16[512,1024]{0,1:T(8,128)(2,1)} %add_convert_fusion.24), channel_id=1, source_target_pairs={{4,0},{8,12},{5,1},{9,13},{6,2},{10,14},{7,3},{11,15},{20,16},{24,... | collective-permute-start | bytes 3145736 | tf_op jit(solution)/shard_map/ppermute | solution.py:299
  772.7 53.4 %collective-permute-start.63 = (bf16[512,1024]{0,1:T(8,128)(2,1)}, bf16[512,1024]{0,1:T(8,128)(2,1)}, u32[]{:S(2)}, u32[]{:S(2)}) collective-permute-start(bf16[512,1024]{0,1:T(8,128)(2,1)} %add_convert_fusion.23), channel_id=1, source_target_pairs={{4,8},{8,4},{5,9},{9,5},{6,10},{10,6},{7,11},{11,7},{20,24},{24,20... | collective-permute-start | bytes 3145736 | tf_op jit(solution)/shard_map/ppermute | solution.py:301
  780.0 46.1 %collective-permute-start.79 = (bf16[512,512]{0,1:T(8,128)(2,1)}, bf16[512,512]{0,1:T(8,128)(2,1)}, u32[]{:S(2)}, u32[]{:S(2)}) collective-permute-start(bf16[512,512]{0,1:T(8,128)(2,1)} %pad_maximum_fusion.9), channel_id=1, source_target_pairs={{0,4},{12,8},{1,5},{13,9},{2,6},{14,10},{3,7},{15,11},{16,20},{28,... | collective-permute-start | bytes 1572872 | tf_op jit(solution)/shard_map/ppermute | solution.py:297
  830.0 49.9 %collective-permute-start.81 = (bf16[512,1024]{0,1:T(8,128)(2,1)S(1)}, bf16[512,1024]{0,1:T(8,128)(2,1)}, u32[]{:S(2)}, u32[]{:S(2)}) collective-permute-start(bf16[512,1024]{0,1:T(8,128)(2,1)S(1)} %add_convert_fusion.1), channel_id=1, source_target_pairs={{4,0},{8,12},{5,1},{9,13},{6,2},{10,14},{7,3},{11,15},{20,16},{24,... | collective-permute-start | bytes 3145736 | tf_op jit(solution)/shard_map/ppermute | solution.py:299
  833.1 65.0 %collective-permute-start.64 = (bf16[512,1024]{0,1:T(8,128)(2,1)S(1)}, bf16[512,1024]{0,1:T(8,128)(2,1)}, u32[]{:S(2)}, u32[]{:S(2)}) collective-permute-start(bf16[512,1024]{0,1:T(8,128)(2,1)S(1)} %add_convert_fusion.22), channel_id=1, source_target_pairs={{4,0},{8,12},{5,1},{9,13},{6,2},{10,14},{7,3},{11,15},{20,16},{24,... | collective-permute-start | bytes 3145736 | tf_op jit(solution)/shard_map/ppermute | solution.py:299
  834.4 45.4 %collective-permute-start.82 = (bf16[512,512]{0,1:T(8,128)(2,1)}, bf16[512,512]{0,1:T(8,128)(2,1)}, u32[]{:S(2)}, u32[]{:S(2)}) collective-permute-start(bf16[512,512]{0,1:T(8,128)(2,1)} %add_convert_fusion.47), channel_id=1, source_target_pairs={{4,8},{8,4},{5,9},{9,5},{6,10},{10,6},{7,11},{11,7},{20,24},{24,20... | collective-permute-start | bytes 1572872 | tf_op jit(solution)/shard_map/ppermute | solution.py:301
  (179 other events, 3011.0 us)

commit v2 on v1

v2 whole, which is shorter than its diff:
```python
import functools

import jax
import jax.numpy as jnp
from jax import lax
from jax.experimental import pallas as pl
from jax.experimental.pallas import tpu as pltpu
from jax.sharding import PartitionSpec as P

HD = 64
WINDOW = 1024
NORM_EPS = 1e-05
ROPE_BASE = 500000.0
MASK_FILL = -1e30
LANES = 128
F32 = jnp.float32
BF16 = jnp.bfloat16


def dot_rows(matrix, other_side):
    return jnp.dot(matrix, other_side, preferred_element_type=F32)


def dot_back(matrix, other_side):
    return lax.dot_general(matrix, other_side, (((1,), (1,)), ((), ())), preferred_element_type=F32)


def dot_outer(matrix, other_side):
    return lax.dot_general(matrix, other_side, (((0,), (0,)), ((), ())), preferred_element_type=F32)


def tie(*values):
    return lax.optimization_barrier(values)


def take(array, start, size, axis):
    return lax.dynamic_slice_in_dim(array, start, size, axis)


def doc_positions(segments):
    seq_count, seq_length = segments.shape
    index_grid = jnp.broadcast_to(jnp.arange(seq_length, dtype=jnp.int32)[None, :], segments.shape)
    begins = jnp.concatenate(
        [jnp.ones((seq_count, 1), dtype=bool), segments[:, 1:] != segments[:, :-1]], axis=1
    )
    return index_grid - lax.cummax(jnp.where(begins, index_grid, 0), axis=1)


def rope_tables(positions):
    half_size = HD // 2
    frequency = ROPE_BASE ** (-(jnp.arange(half_size, dtype=F32) * 2.0 / HD))
    angles = positions.astype(F32)[:, None] * frequency
    cosine, sine = jnp.cos(angles), jnp.sin(angles)
    return jnp.concatenate([cosine] * 4, axis=1), jnp.concatenate([-sine, sine] * 2, axis=1)


def rotate(vectors, cosine, signed_sine):
    width = vectors.shape[1]
    half = HD // 2
    ahead = jnp.concatenate([vectors[:, half:], vectors[:, :half]], axis=1)
    behind = jnp.concatenate([vectors[:, -half:], vectors[:, :-half]], axis=1)
    first = (jnp.arange(width) % HD < half)[None, :]
    reps = width // LANES
    return vectors * jnp.tile(cosine, (1, reps)) + jnp.where(first, ahead, behind) * jnp.tile(
        signed_sine, (1, reps)
    )


def row_scale_of(values):
    return lax.rsqrt(jnp.mean(values * values, axis=-1, keepdims=True) + NORM_EPS)


def norm_back(grad_hidden, gain, normed, row_scale, residual_grad):
    grad_normed = grad_hidden * gain
    return residual_grad + row_scale * (
        grad_normed - normed * jnp.mean(grad_normed * normed, axis=-1, keepdims=True)
    )


def attend_forward_body(lead, heads, group, q_ref, kv_ref, qseg_ref, kseg_ref, mixed_ref, lse_ref):
    block = q_ref.shape[1]
    reach = kseg_ref.shape[-1]
    start = pl.multiple_of(pl.program_id(1) * block, block)
    window = kv_ref.at[0, pl.ds(start, reach), :]
    distance = (
        lax.broadcasted_iota(jnp.int32, (block, reach), 0)
        + lead
        - lax.broadcasted_iota(jnp.int32, (block, reach), 1)
    )
    allowed = (qseg_ref[0] == kseg_ref[0, 0]) & (distance >= 0) & (distance < WINDOW)
    bias = jnp.where(allowed, 0.0, MASK_FILL)
    lane = lax.broadcasted_iota(jnp.int32, (block, LANES), 1)
    log_sums = jnp.zeros((block, LANES), F32)
    kv_width = heads // group * HD
    outs = []
    for head in range(heads):
        shared = head // group * HD
        keys = window[:, shared : shared + HD]
        values = window[:, kv_width + shared : kv_width + shared + HD]
        scores = dot_back(q_ref[0, :, head * HD : (head + 1) * HD], keys) + bias
        row_max = jnp.max(scores, axis=-1, keepdims=True)
        exponent = jnp.exp(scores - row_max)
        row_total = jnp.sum(exponent, axis=-1, keepdims=True)
        probs = (exponent * (1.0 / row_total)).astype(BF16)
        outs.append(dot_rows(probs, values))
        log_sums = jnp.where(lane == head, row_max + jnp.log(row_total), log_sums)
    mixed_ref[0] = jnp.concatenate(outs, axis=1).astype(BF16)
    lse_ref[0] = log_sums


def attend_backward_body(
    lead, heads, group, q_ref, kv_ref, grad_ref, lse_ref, qseg_ref, kseg_ref, dq_ref, dkv_ref
):
    block = q_ref.shape[1]
    reach = block + lead
    step = pl.program_id(1)
    start = pl.multiple_of(step * block, block)
    window = kv_ref.at[0, pl.ds(start, reach), :]

    @pl.when(step == 0)
    def _():
        dkv_ref[...] = jnp.zeros_like(dkv_ref)

    distance = (
        lax.broadcasted_iota(jnp.int32, (reach, block), 1)
        + lead
        - lax.broadcasted_iota(jnp.int32, (reach, block), 0)
    )
    same = kseg_ref[0, pl.ds(start, reach), :] == qseg_ref[0]
    bias = jnp.where(same & (distance >= 0) & (distance < WINDOW), 0.0, MASK_FILL)
    query_grad, keys_grad = backward_tile(
        heads,
        group,
        lambda head: q_ref[0, :, head * HD : (head + 1) * HD],
        lambda head: grad_ref[0, :, head * HD : (head + 1) * HD],
        lambda head: lse_ref[0, head : head + 1, :],
        lambda at: window[:, at * HD : (at + 1) * HD],
        bias,
    )
    dq_ref[0] = query_grad
    dkv_ref[0, pl.ds(start, reach), :] += keys_grad


def backward_tile(heads, group, query_of, grad_of, log_sum_of, window_of, bias):
    key_grads, value_grads, query_grads = [], [], []
    shared_heads = heads // group
    for shared in range(shared_heads):
        keys, values = window_of(shared), window_of(shared_heads + shared)
        key_sum = value_sum = None
        for member in range(group):
            head = shared * group + member
            query, grad = query_of(head), grad_of(head)
            probs = jnp.exp(dot_back(keys, query) + bias - log_sum_of(head))
            grad_probs = dot_back(values, grad)
            spread = jnp.sum(probs * grad_probs, axis=0, keepdims=True)
            grad_scores = (probs * (grad_probs - spread)).astype(BF16)
            value_part = dot_rows(probs.astype(BF16), grad)
            key_part = dot_rows(grad_scores, query)
            query_grads.append(dot_outer(grad_scores, keys) * HD**-0.5)
            value_sum = value_part if value_sum is None else value_sum + value_part
            key_sum = key_part if key_sum is None else key_sum + key_part
        key_grads.append(key_sum)
        value_grads.append(value_sum)
    return jnp.concatenate(query_grads, axis=1), jnp.concatenate(key_grads + value_grads, axis=1)


def attention_plan(span, window):
    blocks_back = -(-(window - 1) // span)
    base = (blocks_back * span - (window - 1)) // LANES * LANES
    return blocks_back, base, blocks_back * span - base


def key_tiles(key_segments, base, lead, block, span):
    return jnp.stack(
        [
            key_segments[:, base + at : base + at + block + lead]
            for at in range(0, span, block)
        ],
        axis=1,
    )[:, :, None, :]


def attend_forward(query, keys_values, query_segments, key_segments, base, lead, group):
    seqs, span, width = query.shape
    block = min(LANES, span)
    heads = width // HD
    reach = block + lead
    keys_used = keys_values[:, base:]
    return pl.pallas_call(
        functools.partial(attend_forward_body, lead, heads, group),
        grid=(seqs, span // block),
        in_specs=[
            pl.BlockSpec((1, block, width), lambda s, i: (s, i, 0)),
            pl.BlockSpec((1,) + keys_used.shape[1:], lambda s, i: (s, 0, 0)),
            pl.BlockSpec((1, block, 1), lambda s, i: (s, i, 0)),
            pl.BlockSpec((1, 1, 1, reach), lambda s, i: (s, i, 0, 0)),
        ],
        out_specs=[
            pl.BlockSpec((1, block, width), lambda s, i: (s, i, 0)),
            pl.BlockSpec((1, block, LANES), lambda s, i: (s, i, 0)),
        ],
        out_shape=[
            jax.ShapeDtypeStruct(query.shape, BF16),
            jax.ShapeDtypeStruct((seqs, span, LANES), F32),
        ],
        compiler_params=pltpu.CompilerParams(vmem_limit_bytes=40 << 20),
        cost_estimate=pl.CostEstimate(
            flops=70 * seqs * span * reach * width, bytes_accessed=4 << 20, transcendentals=0
        ),
        name="attend_forward",
    )(query, keys_used, query_segments[:, :, None], key_tiles(key_segments, base, lead, block, span))


def attend_backward(
    query, keys_values, grad_mixed, log_sums, query_segments, key_segments, base, lead, group
):
    seqs, span, width = query.shape
    block = min(LANES, span)
    heads = width // HD
    reach = block + lead
    keys_used = keys_values[:, base:]
    whole_keys = pl.BlockSpec((1,) + keys_used.shape[1:], lambda s, i: (s, 0, 0))
    rows = pl.BlockSpec((1, block, width), lambda s, i: (s, i, 0))
    grad_query, grad_keys_values = pl.pallas_call(
        functools.partial(attend_backward_body, lead, heads, group),
        grid=(seqs, span // block),
        in_specs=[
            rows,
            whole_keys,
            rows,
            pl.BlockSpec((1, heads, block), lambda s, i: (s, 0, i)),
            pl.BlockSpec((1, 1, block), lambda s, i: (s, 0, i)),
            pl.BlockSpec((1, keys_used.shape[1], 1), lambda s, i: (s, 0, 0)),
        ],
        out_specs=[rows, whole_keys],
        out_shape=[
            jax.ShapeDtypeStruct(query.shape, F32),
            jax.ShapeDtypeStruct(keys_used.shape, F32),
        ],
        compiler_params=pltpu.CompilerParams(vmem_limit_bytes=40 << 20),
        cost_estimate=pl.CostEstimate(
            flops=85 * seqs * span * reach * width, bytes_accessed=6 << 20, transcendentals=0
        ),
        name="attend_backward",
    )(
        query,
        keys_used,
        grad_mixed,
        log_sums,
        query_segments[:, None, :],
        key_segments[:, base:, None],
    )
    return grad_query, jnp.pad(grad_keys_values, ((0, 0), (base, 0), (0, 0)))


def whole(array):
    return pl.BlockSpec(array.shape, lambda *at: (0,) * array.ndim)


def kernel_cost(flops, moved):
    return pl.CostEstimate(flops=flops, bytes_accessed=moved, transcendentals=0)


def feed_forward_body(sizes, hidden_ref, *refs):
    count = len(sizes)
    gate_refs, up_refs = refs[:count], refs[count : 2 * count]
    gate_ref, up_ref, act_ref = refs[2 * count :]

    def project(pieces):
        total, at = None, 0
        for size, piece in zip(sizes, pieces):
            value = dot_rows(hidden_ref[:, at : at + size], piece[...])
            total = value if total is None else total + value
            at += size
        return total

    gate_value, up_value = project(gate_refs), project(up_refs)
    gate_ref[...] = gate_value
    up_ref[...] = up_value
    act_ref[...] = (gate_value * jax.nn.sigmoid(gate_value) * up_value).astype(BF16)


def feed_forward(hidden, gate_pieces, up_pieces, cut, columns):
    rows = hidden.shape[0]
    tile = min(512, columns)
    steps = columns // tile
    own = lambda w: pl.BlockSpec((w.shape[0], tile), lambda i: (0, cut * steps + i))
    rest = lambda w: pl.BlockSpec((w.shape[0], tile), lambda i: (0, i))
    specs = [own(gate_pieces[0])] + [rest(w) for w in gate_pieces[1:]]
    out = pl.BlockSpec((rows, tile), lambda i: (0, i))
    return pl.pallas_call(
        functools.partial(feed_forward_body, tuple(w.shape[0] for w in gate_pieces)),
        grid=(steps,),
        in_specs=[whole(hidden)] + specs + specs,
        out_specs=[out] * 3,
        out_shape=[
            jax.ShapeDtypeStruct((rows, columns), F32),
            jax.ShapeDtypeStruct((rows, columns), F32),
            jax.ShapeDtypeStruct((rows, columns), BF16),
        ],
        compiler_params=pltpu.CompilerParams(vmem_limit_bytes=40 << 20),
        cost_estimate=kernel_cost(6 * rows * columns * hidden.shape[1], 8 << 20),
        name="feed_forward",
    )(hidden, *gate_pieces, *up_pieces)


def feed_backward_body(sizes, grad_ref, *refs):
    count = len(sizes)
    gate_ref, up_ref, grad_gate_ref, grad_up_ref = refs[count:]
    grad_act, at = None, 0
    for size, piece in zip(sizes, refs[:count]):
        value = dot_back(grad_ref[:, at : at + size], piece[...])
        grad_act = value if grad_act is None else grad_act + value
        at += size
    gate_value = gate_ref[...]
    sigmoid_gate = jax.nn.sigmoid(gate_value)
    grad_up = grad_act * sigmoid_gate
    grad_gate_ref[...] = (
        grad_up * up_ref[...] * (1.0 + gate_value * (1.0 - sigmoid_gate))
    ).astype(BF16)
    grad_up_ref[...] = (grad_up * gate_value).astype(BF16)


def feed_backward(grad, down_pieces, gate_value, up_value, cut):
    rows, columns = gate_value.shape
    tile = min(512, columns)
    steps = columns // tile
    own = lambda w: pl.BlockSpec((tile, w.shape[1]), lambda i: (cut * steps + i, 0))
    rest = lambda w: pl.BlockSpec((tile, w.shape[1]), lambda i: (i, 0))
    out = pl.BlockSpec((rows, tile), lambda i: (0, i))
    return pl.pallas_call(
        functools.partial(feed_backward_body, tuple(w.shape[1] for w in down_pieces)),
        grid=(steps,),
        in_specs=[whole(grad), own(down_pieces[0])]
        + [rest(w) for w in down_pieces[1:]]
        + [out, out],
        out_specs=[out] * 2,
        out_shape=[jax.ShapeDtypeStruct((rows, columns), BF16)] * 2,
        compiler_params=pltpu.CompilerParams(vmem_limit_bytes=40 << 20),
        cost_estimate=kernel_cost(4 * rows * columns * grad.shape[1], 8 << 20),
        name="feed_backward",
    )(grad, *down_pieces, gate_value, up_value)


def project_body(cuts, steps, terms, pieces, transposed, sibling_ref, *refs):
    first_ref, second_ref, total_ref = refs[-3:]
    step = pl.program_id(0)
    lefts = refs[: cuts * terms]
    weights = refs[cuts * terms : -3]

    @pl.when(step == 0)
    def _():
        total_ref[...] = jnp.zeros_like(total_ref)

    for cut in range(cuts):

        @pl.when(step // steps == cut)
        def _():
            at = 0
            for piece in range(pieces):
                value = None
                for term in range(terms):
                    left = lefts[cut * terms + term][...]
                    weight = weights[(cut * terms + term) * pieces + piece][...]
                    part = dot_back(left, weight) if transposed else dot_rows(left, weight)
                    value = part if value is None else value + part
                total_ref[:, at : at + value.shape[1]] += value
                at += value.shape[1]

    @pl.when(step == cuts * steps - 1)
    def _():
        half = total_ref.shape[0] // 2
        mine = pl.multiple_of(sibling_ref[0] * half, half)
        theirs = pl.multiple_of((1 - sibling_ref[0]) * half, half)
        first_ref[...] = total_ref[pl.ds(theirs, half), :].astype(BF16)
        second_ref[...] = total_ref[pl.ds(mine, half), :]


def project(sibling, lefts, weights, width, transposed):
    cuts, terms, pieces = len(lefts), len(lefts[0]), len(weights[0][0])
    rows, columns = lefts[0][0].shape
    tile = min(512, columns)
    steps = columns // tile
    in_specs = [pl.BlockSpec(memory_space=pltpu.SMEM)]
    operands = []

    def clipped(cut):
        return lambda i: jnp.clip(i - cut * steps, 0, steps - 1)

    for cut in range(cuts):
        for left in lefts[cut]:
            in_specs.append(pl.BlockSpec((rows, tile), lambda i, f=clipped(cut): (0, f(i))))
            operands.append(left)
    for cut in range(cuts):
        for term in weights[cut]:
            for piece, weight in enumerate(term):
                offset = cut * steps if piece == 0 else 0
                if transposed:
                    spec = pl.BlockSpec(
                        (weight.shape[0], tile), lambda i, f=clipped(cut), o=offset: (0, o + f(i))
                    )
                else:
                    spec = pl.BlockSpec(
                        (tile, weight.shape[1]), lambda i, f=clipped(cut), o=offset: (o + f(i), 0)
                    )
                in_specs.append(spec)
                operands.append(weight)
    half_rows = jax.ShapeDtypeStruct((rows // 2, width), BF16)
    return pl.pallas_call(
        functools.partial(project_body, cuts, steps, terms, pieces, transposed),
        grid=(cuts * steps,),
        in_specs=in_specs,
        out_specs=[whole(half_rows)] * 2,
        out_shape=[half_rows, jax.ShapeDtypeStruct((rows // 2, width), F32)],
        scratch_shapes=[pltpu.VMEM((rows, width), F32)],
        compiler_params=pltpu.CompilerParams(vmem_limit_bytes=48 << 20),
        cost_estimate=kernel_cost(3 * terms * rows * columns * cuts * width, 16 << 20),
        name="project",
    )(sibling.reshape(1), *operands)


CHUNK_ROWS, CHUNK_COLUMNS = 256, 1024


def outer_sum_body(split, groups, left_ref, left_other_ref, *refs):
    out_ref = refs[-1]
    rights, others = refs[:groups], refs[groups : 2 * groups]
    blocks = left_ref.shape[1] // CHUNK_ROWS
    for group in range(groups):

        def emit():
            for block in range(blocks):
                rows = slice(block * CHUNK_ROWS, (block + 1) * CHUNK_ROWS)
                value = dot_outer(left_ref[:, rows], rights[group][...])
                value += dot_outer(left_other_ref[:, rows], others[group][...])
                width = value.shape[1]
                out_ref[0, :, block * width : (block + 1) * width] = value.astype(BF16)

        if groups == 1:
            emit()
        else:
            pl.when(pl.program_id(0) // split == group)(emit)


def outer_sum(pool, at, count, left, left_other, rights, rights_other):
    groups = len(rights)
    rows = left.shape[0]
    columns = CHUNK_ROWS * CHUNK_COLUMNS // rights[0].shape[1]
    split = left.shape[1] // columns
    left_spec = pl.BlockSpec((rows, columns), lambda i: (0, lax.rem(i, split)))
    operands = (left, left_other, *rights, *rights_other)
    in_specs = [left_spec] * 2 + [whole(value) for value in operands[2:]]
    aliases = {}
    if pool is not None:
        operands += (pool,)
        in_specs.append(pl.BlockSpec(memory_space=pl.ANY))
        aliases = {len(operands) - 1: 0}
    return pl.pallas_call(
        functools.partial(outer_sum_body, split, groups),
        grid=(split * groups,),
        in_specs=in_specs,
        out_specs=pl.BlockSpec((1, CHUNK_ROWS, CHUNK_COLUMNS), lambda i: (at + i, 0, 0)),
        out_shape=jax.ShapeDtypeStruct((count, CHUNK_ROWS, CHUNK_COLUMNS), BF16),
        input_output_aliases=aliases,
        compiler_params=pltpu.CompilerParams(vmem_limit_bytes=48 << 20),
        cost_estimate=kernel_cost(
            4 * split * groups * rows * CHUNK_ROWS * CHUNK_COLUMNS, 4 << 20
        ),
        name="outer_sum",
    )(*operands)


def widen_body(starts, pool_ref, *out_refs):
    step = pl.program_id(0)
    value = pool_ref[0].astype(F32)
    last = len(starts) - 1
    for at, start in enumerate(starts):
        stop = starts[at + 1] if at < last else pl.num_programs(0)

        @pl.when((step >= start) & (step < stop))
        def _():
            if at < last - 1:
                out_refs[at][...] = value
            elif at == last - 1:
                half = CHUNK_COLUMNS // 2
                out_refs[at][:CHUNK_ROWS] = value[:, :half]
                out_refs[at][CHUNK_ROWS:] = value[:, half:]
            else:
                width = out_refs[at].shape[1]
                for block in range(CHUNK_COLUMNS // (2 * width)):
                    rows = slice(block * CHUNK_ROWS, (block + 1) * CHUNK_ROWS)
                    left = 2 * block * width
                    out_refs[at][rows] = value[:, left : left + width]
                    out_refs[at + 1][rows] = value[:, left + width : left + 2 * width]


def widen(pool, starts, shapes):
    specs = []
    for at, shape in enumerate(shapes):
        which = min(at, len(starts) - 1)
        start = starts[which]
        stop = starts[which + 1] if which + 1 < len(starts) else pool.shape[0]
        size = stop - start
        block = (shape[0] * shape[1] // (size * CHUNK_COLUMNS), CHUNK_COLUMNS)
        if which == len(starts) - 1:
            block = shape
        elif which == len(starts) - 2:
            block = (2 * CHUNK_ROWS, shape[1])
        down = shape[0] // block[0]

        def place(i, start=start, size=size, down=down):
            k = jnp.clip(i - start, 0, size - 1)
            return lax.rem(k, down), k // down

        specs.append(pl.BlockSpec(block, place))
    return pl.pallas_call(
        functools.partial(widen_body, starts),
        grid=(pool.shape[0],),
        in_specs=[pl.BlockSpec((1, CHUNK_ROWS, CHUNK_COLUMNS), lambda i: (i, 0, 0))],
        out_specs=specs,
        out_shape=[jax.ShapeDtypeStruct(shape, F32) for shape in shapes],
        compiler_params=pltpu.CompilerParams(vmem_limit_bytes=48 << 20),
        cost_estimate=kernel_cost(1, 45 << 20),
        name="widen",
    )(pool)


def tail_body(plan, *refs):
    heads, group, lead, ready, starts, count = plan
    (
        pool_in, gate_refs, up_refs, hidden_m_ref, hidden_m_send, hidden_a_ref, hidden_a_send,
        branch_ref, branch_send, mixed_ref, out_refs, query_ref, keys_ref, log_ref,
        query_seg_ref, key_seg_ref, cosine_ref, sine_ref, qkv_refs, inputs_ref, scale_ref,
        gain_ref, grad_middle_ref,
        pool_ref, sum_ref, near_ref, across_ref, grad_ref, gain_out_ref,
        gate_land, up_land, hidden_m_land, hidden_a_land, branch_land, mixed_land, qkv_land,
        grad_mixed_ref, dq_ref, dkv_ref, kv_send, kv_land, qkv_grad_ref,
        first_ref, second_ref, core_land, chip_ref, y_land, total_ref, other_ref,
        own_buf, near_buf, part_buf, across_buf, total_buf, piece_buf,
        x_send, x_recv, tp_send, tp_recv, kv_send_sem, kv_recv_sem,
        send_sem, land_sem, cross_send, cross_land, keep_sem, load_sem, piece_sem,
    ) = refs
    rows, width = inputs_ref.shape
    half, part = width // 2, width // 4
    half_rows = rows // 2
    mesh_id = pl.DeviceIdType.MESH
    shard, ctx, tp = (lax.axis_index(name) for name in ("fsdp", "ctx", "tp"))
    sibling = lax.rem(tp, 2)
    core = tp + 1 - 2 * sibling
    across_y = lax.rem(tp + 2, 4)
    partner = 1 - shard
    pair = ctx + 1 - 2 * lax.rem(ctx, 2)
    across = 3 - ctx
    is_end = (ctx == 0) | (ctx == 3)
    is_middle = jnp.logical_not(is_end)

    kv_land[...] = jnp.zeros_like(kv_land)
    dkv_ref[...] = jnp.zeros_like(dkv_ref)

    barrier = pltpu.get_barrier_semaphore()
    others = [{"fsdp": partner}, {"tp": core}, {"tp": across_y}]
    others += [{"ctx": lax.rem(ctx + step, 4)} for step in (1, 2, 3)]
    for other in others:
        pl.semaphore_signal(barrier, inc=1, device_id=other, device_id_type=mesh_id)
    pl.semaphore_wait(barrier, len(others))

    def x_copy(at, source, land):
        return pltpu.make_async_remote_copy(
            src_ref=source, dst_ref=land, send_sem=x_send.at[at], recv_sem=x_recv.at[at],
            device_id={"fsdp": partner}, device_id_type=mesh_id,
        )

    cuts = len(gate_refs)
    gate_copies = [x_copy(i, gate_refs[i], gate_land[i]) for i in range(cuts)]
    up_copies = [x_copy(cuts + i, up_refs[i], up_land[i]) for i in range(cuts)]
    hidden_m_copy = x_copy(2 * cuts, hidden_m_send, hidden_m_land)
    branch_copy = x_copy(2 * cuts + 1, branch_send, branch_land)
    mixed_copy = x_copy(2 * cuts + 2, mixed_ref, mixed_land)
    hidden_a_copy = x_copy(2 * cuts + 3, hidden_a_send, hidden_a_land)
    qkv_copy = x_copy(2 * cuts + 4, qkv_grad_ref, qkv_land)
    queue = gate_copies + [hidden_m_copy] + up_copies
    queue += [branch_copy, mixed_copy, qkv_copy, hidden_a_copy]

    def send_next(first, last):
        for at in range(first, last):
            if at >= 2:
                queue[at - 2].wait_send()
            queue[at].start()

    def to_pair(source, land, k):
        return pltpu.make_async_remote_copy(
            src_ref=source, dst_ref=land.at[k], send_sem=send_sem.at[k],
            recv_sem=land_sem.at[k], device_id={"ctx": pair}, device_id_type=mesh_id,
        )

    def inward_copy(k):
        return to_pair(pool_ref.at[k], near_ref, k)

    def outward_copy(k):
        return to_pair(total_buf.at[lax.rem(k, 2)], sum_ref, k)

    def cross_copy(k):
        return pltpu.make_async_remote_copy(
            src_ref=part_buf.at[lax.rem(k, 4)], dst_ref=across_ref.at[k],
            send_sem=cross_send.at[k], recv_sem=cross_land.at[k],
            device_id={"ctx": across}, device_id_type=mesh_id,
        )

    def keep_copy(k):
        return pltpu.make_async_copy(total_buf.at[lax.rem(k, 2)], sum_ref.at[k], keep_sem.at[k])

    def load(source, buffer, at):
        return pltpu.make_async_copy(source, buffer, load_sem.at[at])

    lag = 2

    def inward(k):
        inward_copy(k).wait_recv()
        loads = [load(pool_ref.at[k], own_buf, 0), load(near_ref.at[k], near_buf, 1)]
        for copy in loads:
            copy.start()
        for copy in loads:
            copy.wait()
        part_buf[lax.rem(k, 4)] = (own_buf[...].astype(F32) + near_buf[...].astype(F32)).astype(
            BF16
        )
        cross_copy(k).start()

    def outward(k, reuse):
        cross_copy(k).wait_recv()
        copy = load(across_ref.at[k], across_buf, 2)
        copy.start()
        if reuse:
            keep_copy(k - 2).wait()
            outward_copy(k - 2).wait_send()
        copy.wait()
        total_buf[lax.rem(k, 2)] = (
            part_buf[lax.rem(k, 4)].astype(F32) + across_buf[...].astype(F32)
        ).astype(BF16)
        cross_copy(k).wait_send()
        outward_copy(k).start()
        keep_copy(k).start()

    ahead = 2

    def send_piece(k, carry):
        inward_copy(k).wait_send()

        @pl.when(k + ahead < count)
        def _():
            inward_copy(k + ahead).start()

        return carry

    def pump(first, last):
        @pl.when(is_end)
        def _():
            lax.fori_loop(min(first, count), min(last, count), send_piece, 0)

        @pl.when(is_middle)
        def _():
            k = first
            while k < min(last, lag + 2):
                inward(jnp.int32(k))
                if k >= lag:
                    outward(jnp.int32(k - lag), False)
                k += 1
            if k < min(last, count):

                def both(at, carry):
                    inward(at)
                    outward(at - lag, True)
                    return carry

                lax.fori_loop(k, min(last, count), both, 0)
            k = max(k, count)
            while k < last:
                outward(jnp.int32(k - lag), True)
                k += 1

    @pl.when(is_end)
    def _():
        for k in range(ahead):
            inward_copy(jnp.int32(k)).start()

    send_next(0, 2)

    grad_mixed = None
    at = 0
    for piece in out_refs:
        value = dot_back(branch_ref[:, at : at + piece.shape[1]], piece[...])
        grad_mixed = value if grad_mixed is None else grad_mixed + value
        at += piece.shape[1]
    grad_mixed_ref[...] = grad_mixed.astype(BF16)

    tile = log_ref.shape[2]
    tiles = rows // tile
    reach = tile + lead

    def attend(step, carry):
        start = pl.multiple_of(step * tile, tile)
        distance = (
            lax.broadcasted_iota(jnp.int32, (reach, tile), 1)
            + lead
            - lax.broadcasted_iota(jnp.int32, (reach, tile), 0)
        )
        same = key_seg_ref[pl.ds(start, reach), :] == query_seg_ref[step]
        bias = jnp.where(same & (distance >= 0) & (distance < WINDOW), 0.0, MASK_FILL)
        query_grad, keys_grad = backward_tile(
            heads,
            group,
            lambda head: query_ref[pl.ds(start, tile), head * HD : (head + 1) * HD],
            lambda head: grad_mixed_ref[pl.ds(start, tile), head * HD : (head + 1) * HD],
            lambda head: log_ref[step, head : head + 1, :],
            lambda at: keys_ref[pl.ds(start, reach), at * HD : (at + 1) * HD],
            bias,
        )
        dq_ref[pl.ds(start, tile), :] = query_grad
        dkv_ref[pl.ds(start, reach), :] += keys_grad
        return carry

    lax.fori_loop(0, tiles, attend, 0)
    pump(0, 2)
    send_next(2, 3)

    for back in (1, 2):
        kv_send[back - 1] = dkv_ref[(2 - back) * rows : (3 - back) * rows, :].astype(BF16)

    def kv_copy(back):
        return pltpu.make_async_remote_copy(
            src_ref=kv_send.at[back - 1], dst_ref=kv_land.at[back - 1],
            send_sem=kv_send_sem.at[back - 1], recv_sem=kv_recv_sem.at[back - 1],
            device_id={"ctx": lax.rem(ctx + 4 - back, 4)}, device_id_type=mesh_id,
        )

    for back in (1, 2):

        @pl.when(ctx >= back)
        def _():
            kv_copy(back).start()

    pump(2, 3)
    for back in (1, 2):

        @pl.when(ctx + back < 4)
        def _():
            kv_copy(back).wait_recv()

    send_next(3, 4)
    kv_width = dkv_ref.shape[1] // 2
    q_width = dq_ref.shape[1]
    cosine, sine = cosine_ref[...], sine_ref[...]
    front = lax.rem(lax.broadcasted_iota(jnp.int32, (rows, LANES), 1), HD) < HD // 2

    def unrotate(value):
        swapped = jnp.where(
            front, pltpu.roll(value, LANES - HD // 2, 1), pltpu.roll(value, HD // 2, 1)
        )
        return (value * cosine - swapped * sine).astype(BF16)

    for at in range(0, q_width, LANES):
        qkv_grad_ref[:, at : at + LANES] = unrotate(dq_ref[:, at : at + LANES])
    kv_sum = dkv_ref[2 * rows :, :]
    for back in range(2):
        kv_sum = kv_sum + kv_land[back].astype(F32)
    for at in range(0, kv_width, LANES):
        qkv_grad_ref[:, q_width + at : q_width + at + LANES] = unrotate(
            kv_sum[:, at : at + LANES]
        )
    qkv_grad_ref[:, q_width + kv_width :] = kv_sum[:, kv_width:].astype(BF16)

    def tp_copy(at, source, land, target):
        return pltpu.make_async_remote_copy(
            src_ref=source, dst_ref=land, send_sem=tp_send.at[at], recv_sem=tp_recv.at[at],
            device_id={"tp": target}, device_id_type=mesh_id,
        )

    first_copy = tp_copy(0, first_ref, core_land, core)
    y_copy = tp_copy(1, chip_ref, y_land, across_y)
    total_copy = tp_copy(2, total_ref, other_ref, core)
    theirs = pl.multiple_of((1 - sibling) * half_rows, half_rows)
    mine = pl.multiple_of(sibling * half_rows, half_rows)

    def back_project(start, store):
        at = 0
        for piece in qkv_refs:
            size = piece.shape[0]
            store(at, size, dot_back(qkv_grad_ref[pl.ds(start, half_rows), :], piece[...]))
            at += size

    def store_first(at, size, value):
        first_ref[:, at : at + size] = value.astype(BF16)

    def store_second(at, size, value):
        second_ref[:, at : at + size] = value

    back_project(theirs, store_first)
    first_copy.start()
    back_project(mine, store_second)
    pump(3, 5)
    first_copy.wait_recv()
    chip_ref[...] = (second_ref[...] + core_land[...].astype(F32)).astype(BF16)
    y_copy.start()
    pump(5, 6)
    send_next(4, 5)

    def piece_copy(slot, k):
        return pltpu.make_async_copy(piece_buf.at[slot], pool_ref.at[k], piece_sem.at[slot])

    def put(first, values):
        for at, make in enumerate(values):
            slot = at % 2
            if at >= 2:
                piece_copy(slot, first + at - 2).wait()
            piece_buf[slot] = make()
            piece_copy(slot, first + at).start()
        for at in range(max(0, len(values) - 2), len(values)):
            piece_copy(at % 2, first + at).wait()

    def outer(left, left_other, right, right_other, block):
        columns = slice(block * CHUNK_ROWS, (block + 1) * CHUNK_ROWS)
        return (
            dot_outer(left[:, columns], right[...]) + dot_outer(left_other[:, columns], right_other[...])
        ).astype(BF16)

    def feed_pieces(rights, rights_other):
        return [
            functools.partial(outer, hidden_m_ref, hidden_m_land, right, right_other, block)
            for right, right_other in zip(rights, rights_other)
            for block in range(half // CHUNK_ROWS)
        ]

    for copy in gate_copies + [hidden_m_copy]:
        copy.wait_recv()
    put(starts[1], feed_pieces(gate_refs, gate_land))
    pump(6, 7)

    y_copy.wait_recv()
    total_ref[...] = (chip_ref[...].astype(F32) + y_land[...].astype(F32)).astype(BF16)
    total_copy.start()
    gain = gain_ref[...]
    near_at = pl.multiple_of((1 - shard) * half + lax.rem(ctx, 2) * part, part)
    far_at = pl.multiple_of((1 - shard) * half + (1 - lax.rem(ctx, 2)) * part, part)
    own_at = pl.multiple_of(shard * half, half)
    step_rows = 64

    def norm_rows(source, base):
        def body(step, total):
            at = pl.multiple_of(step * step_rows, step_rows)
            here = pl.ds(pl.multiple_of(base + at, step_rows), step_rows)
            scale = scale_ref[here, :]
            normed = inputs_ref[here, :].astype(F32) * scale
            hidden = source[pl.ds(at, step_rows), :].astype(F32)
            grad = hidden * gain
            mean = jnp.sum(grad * normed, axis=-1, keepdims=True) * (1.0 / width)
            value = (grad_middle_ref[here, :] + scale * (grad - normed * mean)).astype(BF16)
            grad_ref[here, pl.ds(own_at, half)] = value[:, :half]
            grad_ref[here, pl.ds(near_at, part)] = value[:, half : half + part]
            grad_ref[here, pl.ds(far_at, part)] = value[:, half + part :]
            return total + jnp.sum(hidden * normed, axis=0, keepdims=True)

        return lax.fori_loop(0, half_rows // step_rows, body, jnp.zeros((1, width), F32))

    gain_sum = norm_rows(total_ref, mine)
    pump(7, 8)
    send_next(5, 6)
    total_copy.wait_recv()
    gain_out_ref[...] = gain_sum + norm_rows(other_ref, theirs)
    pump(8, 10)
    send_next(6, 7)
    for copy in up_copies:
        copy.wait_recv()
    put(starts[2], feed_pieces(up_refs, up_land))
    pump(10, 12)
    send_next(7, 8)
    pump(12, 14)
    send_next(8, len(queue))
    branch_copy.wait_recv()
    mixed_copy.wait_recv()
    put(
        starts[3],
        [
            functools.partial(
                outer, mixed_ref, mixed_land, branch_ref.at[:, :half], branch_land, block
            )
            for block in range(q_width // CHUNK_ROWS)
        ],
    )
    pump(14, 17)
    hidden_a_copy.wait_recv()
    qkv_copy.wait_recv()

    def side_by_side(first, number, columns):
        return jnp.concatenate(
            [
                outer(
                    hidden_a_ref, hidden_a_land, qkv_grad_ref.at[:, columns],
                    qkv_land.at[:, columns], block,
                )
                for block in range(first, first + number)
            ],
            axis=1,
        )

    q_blocks = CHUNK_COLUMNS // q_width
    put(
        starts[4],
        [
            functools.partial(side_by_side, first, q_blocks, slice(0, q_width))
            for first in range(0, half // CHUNK_ROWS, q_blocks)
        ]
        + [
            functools.partial(
                side_by_side, 0, half // CHUNK_ROWS, slice(q_width, q_width + 2 * kv_width)
            )
        ],
    )
    pump(17, count + lag)

    for copy in queue[-2:] + [first_copy, y_copy, total_copy]:
        copy.wait_send()
    for back in (1, 2):

        @pl.when(ctx >= back)
        def _():
            kv_copy(back).wait_send()

    @pl.when(is_middle)
    def _():
        for k in (count - 2, count - 1):
            outward_copy(jnp.int32(k)).wait_send()
            keep_copy(jnp.int32(k)).wait()

    @pl.when(is_end)
    def _():
        def close(k, carry):
            to_pair(pool_ref.at[k], sum_ref, k).wait_recv()
            return carry

        lax.fori_loop(0, count, close, 0)


def flat_call(body, groups, **call):
    flat, tree = jax.tree.flatten(groups, is_leaf=lambda x: isinstance(x, tuple) and len(x) == 2 and isinstance(x[1], pl.BlockSpec))
    arrays, specs = [x[0] for x in flat], [x[1] for x in flat]

    def unflatten(*refs):
        body(*jax.tree.unflatten(tree, refs[: len(flat)]), *refs[len(flat) :])

    return pl.pallas_call(unflatten, in_specs=specs, **call)(*arrays)


def tail(plan, pool, v):
    heads, group, lead, ready, starts, count = plan
    rows, width = v["inputs"].shape
    half = width // 2
    q_width, kv_width = v["query"].shape[1], v["keys_values"].shape[1] // 2
    qkv_width = q_width + 2 * kv_width
    piece = (CHUNK_ROWS, CHUNK_COLUMNS)
    cuts, feed_part = len(v["grad_gate"]), v["grad_gate"][0].shape[1]

    def near(value):
        return (value, pl.BlockSpec(memory_space=pltpu.VMEM))

    def far(value):
        return (value, pl.BlockSpec(memory_space=pl.ANY))

    operands = [
        far(pool),
        [near(value) for value in v["grad_gate"]],
        [near(value) for value in v["grad_up"]],
        near(v["hidden_m"]), far(v["hidden_m_send"]),
        near(v["hidden_a"]), far(v["hidden_a_send"]),
        near(v["branch"]), far(v["branch_send"]),
        near(v["mixed"]),
        [near(value) for value in v["out_pieces"]],
        near(v["query"]), near(v["keys_values"]), near(v["log_sums"]),
        near(v["query_segments"]), near(v["key_segments"]),
        near(v["cosine"]), near(v["sine"]),
        [near(value) for value in v["qkv_pieces"]],
        near(v["inputs"]), near(v["scale"]), near(v["gain"]), near(v["grad_middle"]),
    ]
    any_space, vmem_space = pl.BlockSpec(memory_space=pl.ANY), pl.BlockSpec(memory_space=pltpu.VMEM)
    line = jax.ShapeDtypeStruct((count,) + piece, BF16)
    dma = pltpu.SemaphoreType.DMA
    low = lambda *shape: pltpu.VMEM(shape, BF16)
    wide = lambda *shape: pltpu.VMEM(shape, F32)
    scratch = [
        [low(rows, feed_part) for _ in range(cuts)],
        [low(rows, feed_part) for _ in range(cuts)],
        low(rows, half), low(rows, half), low(rows, half),
        low(rows, q_width), low(rows, qkv_width),
        low(rows, q_width), wide(rows, q_width), wide(3 * rows, 2 * kv_width),
        low(2, rows, 2 * kv_width), low(2, rows, 2 * kv_width), low(rows, qkv_width),
        low(rows // 2, width), wide(rows // 2, width), low(rows // 2, width),
        low(rows // 2, width), low(rows // 2, width), low(rows // 2, width),
        low(rows // 2, width),
        low(*piece), low(*piece), low(4, *piece), low(*piece), low(2, *piece), low(2, *piece),
        dma((2 * cuts + 5,)), dma((2 * cuts + 5,)), dma((3,)), dma((3,)), dma((2,)), dma((2,)),
        dma((count,)), dma((count,)), dma((count,)), dma((count,)), dma((count,)),
        dma((3,)), dma((2,)),
    ]
    outs = flat_call(
        functools.partial(tail_body, plan),
        operands,
        out_specs=[any_space, any_space, any_space, any_space, vmem_space, vmem_space],
        out_shape=[
            line, line, line, line,
            jax.ShapeDtypeStruct((rows, width), BF16),
            jax.ShapeDtypeStruct((1, width), F32),
        ],
        scratch_shapes=scratch,
        input_output_aliases={0: 0},
        compiler_params=pltpu.CompilerParams(
            collective_id=0, has_side_effects=True, vmem_limit_bytes=60 << 20
        ),
        cost_estimate=pl.CostEstimate(
            flops=400 << 30, bytes_accessed=30 << 20, transcendentals=0
        ),
        name="tail",
    )
    return outs[1], outs[4], outs[5]


def swap(value, axis, size, bit):
    return lax.ppermute(value, axis, [(i, i ^ bit) for i in range(size)])


def shift(value, axis, size, by):
    if abs(by) >= size:
        return jnp.zeros_like(value)
    return lax.ppermute(
        value, axis, [(i, i + by) for i in range(size) if 0 <= i + by < size]
    )


class Lane:
    def __init__(self, move, depth=2):
        self.move, self.depth, self.done = move, depth, []

    def send(self, value):
        if len(self.done) >= self.depth:
            value, self.done[-self.depth] = tie(value, self.done[-self.depth])
        self.done.append(self.move(value))
        return len(self.done) - 1

    def get(self, at):
        return self.done[at]


def shards(
    sizes,
    block_input,
    segment_ids,
    attention_gain,
    query_weight,
    key_weight,
    value_weight,
    out_weight,
    feed_gain,
    gate_weight,
    up_weight,
    down_weight,
    cotangent,
):
    shard_count, ctx_count, tp_count = sizes
    seqs, span, width = block_input.shape
    rows = seqs * span
    seq_length = segment_ids.shape[1]
    half = width // 2
    part = half // 2
    q_width = query_weight.shape[1]
    kv_width = key_weight.shape[1]
    feed_width = gate_weight.shape[1]
    group = q_width // kv_width
    shard, ctx, tp = (lax.axis_index(name) for name in ("fsdp", "ctx", "tp"))
    odd = ctx % 2
    sibling = tp % 2

    own_at = shard * half
    near_at = (1 - shard) * half + odd * part
    far_at = (1 - shard) * half + (1 - odd) * part

    def to_local(value):
        return jnp.concatenate(
            [
                take(value, own_at, half, 1),
                take(value, near_at, part, 1),
                take(value, far_at, part, 1),
            ],
            axis=1,
        )

    def other_half(value):
        return jnp.concatenate(
            [
                take(value, half + odd * part, part, 1),
                take(value, half + (1 - odd) * part, part, 1),
            ],
            axis=1,
        )

    def from_local(value):
        own, other = value[:, :half], other_half(value)
        return jnp.where(
            shard == 0,
            jnp.concatenate([own, other], axis=1),
            jnp.concatenate([other, own], axis=1),
        )

    fsdp_lane = Lane(lambda value: swap(value, "fsdp", shard_count, 1))

    def over_fsdp(value):
        return swap(value, "fsdp", shard_count, 1)

    def over_ctx(value):
        return swap(value, "ctx", ctx_count, 1)

    def near_part(weight, axis):
        return take(weight, odd * part, part, axis)

    def core_half(value):
        return take(value, sibling * (rows // 2), rows // 2, 0)

    def join_cores(mine):
        other = swap(mine, "tp", tp_count, 1)
        return jnp.where(
            sibling == 0,
            jnp.concatenate([mine, other], axis=0),
            jnp.concatenate([other, mine], axis=0),
        )

    def chip_sum(first, second):
        return (second + swap(first, "tp", tp_count, 1).astype(F32)).astype(BF16)

    def finish_sum(chip):
        total = (chip.astype(F32) + swap(chip, "tp", tp_count, 2).astype(F32)).astype(BF16)
        return join_cores(total).astype(F32)

    def tp_sum(first, second):
        if tp_count != 4:
            whole_rows = jnp.where(
                sibling == 0,
                jnp.concatenate([second, first.astype(F32)], axis=0),
                jnp.concatenate([first.astype(F32), second], axis=0),
            )
            return lax.psum(whole_rows, "tp")
        return finish_sum(chip_sum(first, second))

    gains_own = jnp.stack([attention_gain, feed_gain])
    qkv_own = jnp.concatenate([query_weight, key_weight, value_weight], axis=1)
    feed_cuts = 2
    feed_part = feed_width // feed_cuts
    columns = [slice(cut * feed_part, (cut + 1) * feed_part) for cut in range(feed_cuts)]
    grad_rows = to_local(cotangent.reshape(rows, width))
    send_gate = [near_part(gate_weight[:, cut], 0) for cut in columns]
    send_up = [near_part(up_weight[:, cut], 0) for cut in columns]
    send_down = [near_part(down_weight[cut], 1) for cut in columns]
    send_grad = core_half(other_half(grad_rows))

    gains_other = over_fsdp(gains_own)
    near_qkv = over_fsdp(near_part(qkv_own, 0))
    near_out = over_fsdp(near_part(out_weight, 1))

    span_start = ctx * span
    positions = take(doc_positions(segment_ids), span_start, span, 1).reshape(rows)
    query_segments = take(segment_ids, span_start, span, 1)
    cosine, sine = rope_tables(positions)
    blocks_back, base, lead = attention_plan(span, WINDOW)
    key_segments = take(
        jnp.pad(segment_ids, ((0, 0), (blocks_back * span, 0)), constant_values=-1),
        span_start,
        (blocks_back + 1) * span,
        1,
    )

    inputs = to_local(block_input.reshape(rows, width)).astype(F32)
    scale_a = row_scale_of(inputs)
    normed_a = inputs * scale_a
    gains = jnp.concatenate(
        [gains_own, take(gains_other, odd * part, part, 1), take(gains_other, (1 - odd) * part, part, 1)],
        axis=1,
    ).astype(F32)
    gain_a, gain_m = gains[0:1], gains[1:2]
    hidden_a = (normed_a * gain_a).astype(BF16)

    near_qkv, send_gate[0] = tie(near_qkv, send_gate[0])
    near_gate, near_up, far_gate, far_up = ([None] * feed_cuts for _ in range(4))
    near_gate[0] = over_fsdp(send_gate[0])
    far_qkv = over_ctx(near_qkv)
    near_out, send_up[0] = tie(near_out, send_up[0])
    near_up[0] = over_fsdp(send_up[0])
    far_qkv, near_out = tie(far_qkv, near_out)
    far_out = over_ctx(near_out)

    def dot_pieces(matrix, own, near, far):
        return (
            dot_rows(matrix[:, :half], own)
            + dot_rows(matrix[:, half : half + part], near)
            + dot_rows(matrix[:, half + part :], far)
        )

    def back_pieces(matrix, own, near, far):
        return jnp.concatenate(
            [dot_back(matrix, own), dot_back(matrix, near), dot_back(matrix, far)], axis=1
        )

    qkv = dot_pieces(hidden_a, qkv_own, near_qkv, far_qkv)
    key_low = rotate(qkv[:, q_width : q_width + kv_width], cosine, sine).astype(BF16)
    value_low = qkv[:, q_width + kv_width :].astype(BF16)
    keys_values = jnp.concatenate([key_low, value_low], axis=1).reshape(seqs, span, 2 * kv_width)
    query_low = (rotate(qkv[:, :q_width], cosine, sine).astype(BF16) * HD**-0.5).reshape(
        seqs, span, q_width
    )
    earlier = [shift(keys_values, "ctx", ctx_count, back) for back in range(blocks_back, 0, -1)]
    *earlier, near_gate[0], far_out, query_low, send_gate[1] = tie(
        *earlier, near_gate[0], far_out, query_low, send_gate[1]
    )
    near_gate[1] = over_fsdp(send_gate[1])
    far_gate[0] = over_ctx(near_gate[0])
    keys_values = jnp.concatenate(earlier + [keys_values], axis=1)
    mixed, log_sums = attend_forward(
        query_low, keys_values, query_segments, key_segments, base, lead, group
    )
    mixed_low = mixed.reshape(rows, q_width)
    mixed_low, near_up[0], send_up[1] = tie(mixed_low, near_up[0], send_up[1])
    near_up[1] = over_fsdp(send_up[1])
    far_up[0] = over_ctx(near_up[0])

    def out_project(at):
        matrix = take(mixed_low, at * (rows // 2), rows // 2, 0)
        return jnp.concatenate(
            [dot_rows(matrix, out_weight), dot_rows(matrix, near_out), dot_rows(matrix, far_out)],
            axis=1,
        )

    first, second = out_project(1 - sibling).astype(BF16), out_project(sibling)
    if tp_count == 4:
        chip = chip_sum(first, second)
        chip, near_gate[1], far_gate[0], send_down[0] = tie(
            chip, near_gate[1], far_gate[0], send_down[0]
        )
        near_down = [over_fsdp(send_down[0])]
        far_gate[1] = over_ctx(near_gate[1])
        total = (chip.astype(F32) + swap(chip, "tp", tp_count, 2).astype(F32)).astype(BF16)
        total, near_up[1], far_up[0], send_down[1] = tie(
            total, near_up[1], far_up[0], send_down[1]
        )
        near_down.append(over_fsdp(send_down[1]))
        far_up[1] = over_ctx(near_up[1])
        branch_a = join_cores(total).astype(F32)
    else:
        branch_a = tp_sum(first, second)
        near_down = [over_fsdp(value) for value in send_down]
        far_gate[1] = over_ctx(near_gate[1])
        far_up[1] = over_ctx(near_up[1])
    middle = inputs + branch_a

    scale_m = row_scale_of(middle)
    normed_m = middle * scale_m
    hidden_m = (normed_m * gain_m).astype(BF16)
    gate_cuts, up_cuts, act_cuts = [], [], []
    for cut in range(feed_cuts):
        gate_value, up_value, activated = feed_forward(
            hidden_m,
            (gate_weight, near_gate[cut], far_gate[cut]),
            (up_weight, near_up[cut], far_up[cut]),
            cut,
            feed_part,
        )
        gate_cuts.append(gate_value)
        up_cuts.append(up_value)
        act_cuts.append(activated)
    act_cuts[0], near_down[0], send_grad = tie(act_cuts[0], near_down[0], send_grad)
    other_grad = over_fsdp(send_grad)
    far_down = [over_ctx(near_down[0])]
    act_other = [over_fsdp(act_cuts[0])]
    act_cuts[1], near_down[1] = tie(act_cuts[1], near_down[1])
    act_other.append(over_fsdp(act_cuts[1]))
    far_down.append(over_ctx(near_down[1]))
    grad_own, grad_other = grad_rows[:, :half], join_cores(other_grad)
    fsdp_lane.done = list(act_other)

    pieces = CHUNK_ROWS * CHUNK_COLUMNS
    down_count = feed_width * half // pieces
    starts, pool_size = [], 0
    for size in (feed_width * half,) * 3 + (q_width * half,) * 2 + (2 * kv_width * half,):
        starts.append(pool_size)
        pool_size += size // pieces
    pool = None
    for cut in range(feed_cuts):
        pool = outer_sum(
            pool,
            cut * down_count // feed_cuts,
            pool_size,
            act_cuts[cut],
            act_other[cut],
            [grad_own],
            [grad_other],
        )

    grad_gate_cuts, grad_up_cuts = [], []
    for cut in range(feed_cuts):
        grad_gate, grad_up = feed_backward(
            grad_rows,
            (down_weight, near_down[cut], far_down[cut]),
            gate_cuts[cut],
            up_cuts[cut],
            cut,
        )
        grad_gate_cuts.append(grad_gate)
        grad_up_cuts.append(grad_up)

    grad_hidden_m = tp_sum(
        *project(
            sibling,
            list(zip(grad_gate_cuts, grad_up_cuts)),
            [
                (
                    (gate_weight, near_gate[cut], far_gate[cut]),
                    (up_weight, near_up[cut], far_up[cut]),
                )
                for cut in range(feed_cuts)
            ],
            width,
            True,
        )
    )
    feed_gain_part = jnp.sum(grad_hidden_m * normed_m, axis=0)
    grad_middle = norm_back(grad_hidden_m, gain_m, normed_m, scale_m, grad_rows.astype(F32))
    grad_branch = grad_middle.astype(BF16)

    branch_m = tp_sum(
        *project(
            sibling,
            [(value,) for value in act_cuts],
            [((down_weight, near_down[cut], far_down[cut]),) for cut in range(feed_cuts)],
            width,
            False,
        )
    )
    block_out = from_local((middle + branch_m).astype(BF16)).reshape(seqs, span, width)

    fused = (shard_count, ctx_count, tp_count) == (2, 4, 4)
    fused = fused and seqs == 1 and (blocks_back, base) == (2, 0)
    if fused:
        tile = min(LANES, rows)
        log_rows = jnp.swapaxes(log_sums[0, :, : q_width // HD].reshape(rows // tile, tile, -1), 1, 2)
        pool, input_grad, gain_row = tail(
            (
                q_width // HD,
                group,
                lead,
                starts[1],
                tuple(starts),
                pool_size,
            ),
            pool,
            {
                "grad_gate": grad_gate_cuts,
                "grad_up": grad_up_cuts,
                "hidden_m": hidden_m[:, :half],
                "hidden_m_send": other_half(hidden_m),
                "hidden_a": hidden_a[:, :half],
                "hidden_a_send": other_half(hidden_a),
                "branch": grad_branch,
                "branch_send": other_half(grad_branch),
                "mixed": mixed_low,
                "out_pieces": [out_weight, near_out, far_out],
                "query": query_low[0],
                "keys_values": keys_values[0],
                "log_sums": log_rows,
                "query_segments": query_segments.reshape(rows // tile, 1, tile),
                "key_segments": key_segments.reshape(-1, 1),
                "cosine": cosine,
                "sine": sine,
                "qkv_pieces": [qkv_own, near_qkv, far_qkv],
                "inputs": inputs.astype(BF16),
                "scale": scale_a,
                "gain": gain_a,
                "grad_middle": grad_middle,
            },
        )
        attention_gain_part = gain_row[0]
        input_grad = input_grad.reshape(seqs, span, width)
    else:
        gate_at = [fsdp_lane.send(value) for value in grad_gate_cuts]
        up_at = [fsdp_lane.send(value) for value in grad_up_cuts]
        hidden_m_at = fsdp_lane.send(core_half(other_half(hidden_m)))
        hidden_own, hidden_other = hidden_m[:, :half], join_cores(fsdp_lane.get(hidden_m_at))
        for which, (own, at) in enumerate(((grad_gate_cuts, gate_at), (grad_up_cuts, up_at))):
            pool = outer_sum(
                pool,
                starts[1 + which],
                pool_size,
                hidden_own,
                hidden_other,
                own,
                [fsdp_lane.get(i) for i in at],
            )

        grad_mixed = (
            dot_back(grad_branch[:, :half], out_weight)
            + dot_back(grad_branch[:, half : half + part], near_out)
            + dot_back(grad_branch[:, half + part :], far_out)
        ).astype(BF16)
        branch_at = fsdp_lane.send(core_half(other_half(grad_branch)))
        mixed_at = fsdp_lane.send(mixed_low)
        hidden_a_at = fsdp_lane.send(core_half(other_half(hidden_a)))
        grad_query, grad_keys_values = attend_backward(
            query_low,
            keys_values,
            grad_mixed.reshape(seqs, span, q_width),
            jnp.swapaxes(log_sums, 1, 2)[:, : q_width // HD],
            query_segments,
            key_segments,
            base,
            lead,
            group,
        )
        kv_sum = grad_keys_values[:, blocks_back * span :]
        for back in range(1, blocks_back + 1):
            at = (blocks_back - back) * span
            kv_sum = kv_sum + shift(
                grad_keys_values[:, at : at + span].astype(BF16), "ctx", ctx_count, -back
            ).astype(F32)
        kv_sum = kv_sum.reshape(rows, 2 * kv_width)
        grad_qkv = jnp.concatenate(
            [
                rotate(grad_query.reshape(rows, q_width), cosine, -sine),
                rotate(kv_sum[:, :kv_width], cosine, -sine),
                kv_sum[:, kv_width:],
            ],
            axis=1,
        ).astype(BF16)
        qkv_at = fsdp_lane.send(grad_qkv)
        first, second = (
            back_pieces(take(grad_qkv, at * (rows // 2), rows // 2, 0), qkv_own, near_qkv, far_qkv)
            for at in (1 - sibling, sibling)
        )
        grad_hidden_a = tp_sum(first.astype(BF16), second)
        attention_gain_part = jnp.sum(grad_hidden_a * normed_a, axis=0)
        input_grad = norm_back(grad_hidden_a, gain_a, normed_a, scale_a, grad_middle)
        input_grad = from_local(input_grad.astype(BF16)).reshape(seqs, span, width)

        pool = outer_sum(
            pool,
            starts[3],
            pool_size,
            mixed_low,
            fsdp_lane.get(mixed_at),
            [grad_branch[:, :half]],
            [join_cores(fsdp_lane.get(branch_at))],
        )
        qkv_other = fsdp_lane.get(qkv_at)
        hidden_own, hidden_other = hidden_a[:, :half], join_cores(fsdp_lane.get(hidden_a_at))
        for which, cut in ((4, slice(0, q_width)), (5, slice(q_width, None))):
            pool = outer_sum(
                pool,
                starts[which],
                pool_size,
                hidden_own,
                hidden_other,
                [grad_qkv[:, cut]],
                [qkv_other[:, cut]],
            )
        pool = lax.psum(pool.astype(F32), "ctx")

    gain_parts = jnp.stack([attention_gain_part, feed_gain_part])
    gain_other = over_fsdp(other_half(gain_parts))
    gain_sums = lax.psum(gain_parts[:, :half] + gain_other, "ctx")

    down_grad, gate_grad, up_grad, out_grad, query_grad, key_grad, value_grad = widen(
        pool,
        starts,
        [
            down_weight.shape,
            gate_weight.shape,
            up_weight.shape,
            out_weight.shape,
            query_weight.shape,
            key_weight.shape,
            value_weight.shape,
        ],
    )
    return (
        block_out,
        input_grad,
        gain_sums[0],
        query_grad,
        key_grad,
        value_grad,
        out_grad,
        gain_sums[1],
        gate_grad,
        up_grad,
        down_grad,
    )


def solution(mesh):
    sizes = tuple(mesh.shape[name] for name in ("fsdp", "ctx", "tp"))
    in_specs = (
        P("fsdp", "ctx", None),
        P("fsdp", None),
        P("fsdp"),
        P("fsdp", "tp"),
        P("fsdp", "tp"),
        P("fsdp", "tp"),
        P("tp", "fsdp"),
        P("fsdp"),
        P("fsdp", "tp"),
        P("fsdp", "tp"),
        P("tp", "fsdp"),
        P("fsdp", "ctx", None),
    )
    out_specs = (
        P("fsdp", "ctx", None),
        P("fsdp", "ctx", None),
        P("fsdp"),
        P("fsdp", "tp"),
        P("fsdp", "tp"),
        P("fsdp", "tp"),
        P("tp", "fsdp"),
        P("fsdp"),
        P("fsdp", "tp"),
        P("fsdp", "tp"),
        P("tp", "fsdp"),
    )
    return jax.shard_map(
        functools.partial(shards, sizes),
        mesh=mesh,
        in_specs=in_specs,
        out_specs=out_specs,
        check_vma=False,
    )
```

time: 919 us -> 863 us (0.939)
  Pallas kernels: 38.3 us -> 502 us
  matrix products: 181 us -> 7.44 us
  other arithmetic: 179 us -> 47.9 us
  starting transfers between devices: 160 us -> 34.1 us
  waiting for transfers between devices: 253 us -> 194 us
  local copies, waits for them, and re-layouts: 81.2 us -> 56.6 us
    pallas_call x1 -> x10, Pallas kernels: 21 us -> 485 us  [the longest x1 396 us: flat_call(): return pl.pallas_call(unflatten, in_specs=specs, **call)(*arrays)]
    dot_general x73 -> x0, matrix products: 136 us -> none  [the longest x39 77.5 us: dot_back(): lax.dot_general(matrix, other_side, (((1,), (1,)), ((), ())), preferred_e...]
    ppermute x35 -> x0, starting transfers between devices: 112 us -> none  [the longest x10 58.2 us: add(): got_in = got_out = lax.ppermute(sends[0], self.axis, inward + outward)]
    ppermute x35 -> x0, waiting for transfers between devices: 88.2 us -> none  [the longest x5 43.1 us: add(): got_in = lax.ppermute(sends.pop(0), self.axis, inward)]
    convert_element_type x35 -> x6, other arithmetic: 72.5 us -> 7.76 us  [the longest x3 3.65 us: chip_sum(): return (second + swap(first, 'tp', tp_count, 1).astype(F32)).astype(BF16)]
    concatenate x10 -> x1, other arithmetic: 42.3 us -> 1.08 us  [out_project(): jnp.concatenate([dot_rows(matrix, out_weight), dot_rows(matrix, near_out)...]
    dot_general x33 -> x9, matrix products: 44.6 us -> 7.44 us  [dot_rows(): return jnp.dot(matrix, other_side, preferred_element_type=F32)]
    ppermute x46 -> x31, waiting for transfers between devices: 158 us -> 194 us  [swap(): return lax.ppermute(value, axis, [(i, i ^ bit) for i in range(size)])]
  transfers between devices with their start and end apart: 85 -> 33, of which waited for: 24 -> 14; matrix products, arithmetic and copies ran while one was open for 47% -> 7% of each run, Pallas kernels for 4% -> 11%
where the time goes in v2:
time: 863 us; the launch traced here: 853 us
  Pallas kernels  502 us (58%)
  waiting for transfers between devices  194 us (22%)
  local copies, waits for them, and re-layouts  56.6 us (7%)
  other arithmetic  47.9 us (6%)
  starting transfers between devices  34.1 us (4%)
    pallas_call x1, Pallas kernels, flat_call(): return pl.pallas_call(unflatten, in_specs=specs, **call)(*arrays)  396 us
    ppermute x31, waiting for transfers between devices, swap(): return lax.ppermute(value, axis, [(i, i ^ bit) for i in range(size)])  194 us
    pallas_call x1, Pallas kernels, widen(): pl.pallas_call(functools.partial(widen_body, starts), grid=(pool.shape[0]...  27.3 us
    ppermute x31, starting transfers between devices, swap(): return lax.ppermute(value, axis, [(i, i ^ bit) for i in range(size)])  26.1 us
    pallas_call x2, Pallas kernels, project(): pl.pallas_call(functools.partial(project_body, cuts, steps, terms, pieces...  26 us
    unnamed x165, local copies, waits for them, and re-layouts  25.9 us
  transfers between devices with their start and end apart: 33, of which 14 were waited for; matrix products, arithmetic and copies ran while one was open for 7% of the time, Pallas kernels for 11%

profile of v2, /device:TPU:0, one launch (start us, length us, event | category | flops | bytes accessed | tf_op | source)
XLA Modules:
  0.0 852.7 jit_solution(10030628569263530680)
XLA Ops:
  2.1 3.0 collective-permute-start
  5.1 1.9 constant_dynamic-slice_fusion.21
  10.7 1.8 collective-permute-start.1
  14.8 2.4 copy-done.50
  21.5 1.8 fusion.29
  25.1 12.5 %collective-permute-done.1.refs_23_ = bf16[512,768]{1,0:T(8,128)(2,1)} collective-permute-done((bf16[512,768]{1,0:T(8,128)(2,1)}, bf16[512,768]{1,0:T(8,128)(2,1)}, u32[]{:S(2)}, u32[]{:S(2)}) %collective-permute-start.1) | collective-permute-done | bytes 786464 | tf_op jit(solution)/shard_map/ppermute | solution.py:1026
  37.5 1.6 collective-permute-start.2
  44.5 1.7 fusion.15
  46.3 9.6 %collective-permute-done.2.refs_24_ = bf16[512,768]{1,0:T(8,128)(2,1)S(1)} collective-permute-done((bf16[512,768]{1,0:T(8,128)(2,1)}, bf16[512,768]{1,0:T(8,128)(2,1)S(1)}, u32[]{:S(2)}, u32[]{:S(2)}) %collective-permute-start.2) | collective-permute-done | bytes 786464 | tf_op jit(solution)/shard_map/ppermute | solution.py:1026
  59.0 3.5 collective-permute-start.5
  62.5 4.5 collective-permute-start.4
  68.4 20.0 %collective-permute-done.6.refs_1_.refs_5_ = bf16[512,1024]{1,0:T(8,128)(2,1)S(1)} collective-permute-done((bf16[512,1024]{1,0:T(8,128)(2,1)S(1)}, bf16[512,1024]{1,0:T(8,128)(2,1)S(1)}, u32[]{:S(2)}, u32[]{:S(2)}) %collective-permute-start.6) | collective-permute-done | bytes 1048608 | tf_op jit(solution)/shard_map/ppermute | solution.py:1026
  89.6 17.2 %attend_forward.1 = (bf16[1,512,512]{2,1,0:T(8,128)(2,1)S(1)}, f32[1,512,128]{2,1,0:T(8,128)S(1)}) custom-call(bf16[1,512,512]{2,1,0:T(8,128)(2,1)S(1)} %multiply_bitcast_fusion.q_ref, bf16[1,1536,256]{2,1,0:T(8,128)(2,1)S(1)} %get-tuple-element.156.kv_ref, s32[1,512,1]{2,1,0:T(8,128)S(1)} %copy.30.qseg_ref, s32[1,4,1,1152]{3,2,1,0:T(1,128)S(1)} %add_bitcast_fusion.kseg_ref), custom_call_target="tpu_custom_call" | custom-call | flops 21139292160 | bytes 4194304 | tf_op jit(solution)/shard_map/attend_forward/pallas_call | solution.py:189
  109.9 2.4 fusion.60
  112.3 2.4 constant_dynamic-slice_fusion.14
  119.0 1.7 fusion.10
  120.8 18.7 %collective-permute-done.10.refs_1_.refs_11_ = bf16[512,1024]{1,0:T(8,128)(2,1)S(1)} collective-permute-done((bf16[512,1024]{1,0:T(8,128)(2,1)S(1)}, bf16[512,1024]{1,0:T(8,128)(2,1)S(1)}, u32[]{:S(2)}, u32[]{:S(2)}) %collective-permute-start.10) | collective-permute-done | bytes 1048608 | tf_op jit(solution)/shard_map/ppermute | solution.py:1026
  144.2 19.0 %collective-permute-done.12 = bf16[256,2048]{1,0:T(8,128)(2,1)S(1)} collective-permute-done((bf16[256,2048]{1,0:T(8,128)(2,1)S(1)}, bf16[256,2048]{1,0:T(8,128)(2,1)S(1)}, u32[]{:S(2)}, u32[]{:S(2)}) %collective-permute-start.12) | collective-permute-done | bytes 1048608 | tf_op jit(solution)/shard_map/ppermute | solution.py:1026
  165.6 1.7 dynamic-slice_bitcast_fusion.refs_0_
  174.5 1.6 collective-permute-start.18
  176.0 2.8 multiply_reduce_fusion
  178.8 2.8 multiply_convert_fusion.hidden_ref
  181.7 16.9 %collective-permute-done.17.refs_2_.refs_12_ = bf16[512,1024]{1,0:T(8,128)(2,1)S(1)} collective-permute-done((bf16[512,1024]{1,0:T(8,128)(2,1)S(1)}, bf16[512,1024]{1,0:T(8,128)(2,1)S(1)}, u32[]{:S(2)}, u32[]{:S(2)}) %collective-permute-start.17) | collective-permute-done | bytes 1048608 | tf_op jit(solution)/shard_map/ppermute | solution.py:1026
  198.6 21.5 %collective-permute-done.18.refs_5_.refs_15_ = bf16[512,1024]{1,0:T(8,128)(2,1)S(1)} collective-permute-done((bf16[512,1024]{1,0:T(8,128)(2,1)}, bf16[512,1024]{1,0:T(8,128)(2,1)S(1)}, u32[]{:S(2)}, u32[]{:S(2)}) %collective-permute-start.18) | collective-permute-done | bytes 1048608 | tf_op jit(solution)/shard_map/ppermute | solution.py:1026
  220.2 7.9 feed_forward.3
  231.2 7.8 feed_forward.2
  244.1 12.7 %collective-permute-done.21.refs_7_.refs_2_ = bf16[1024,512]{1,0:T(8,128)(2,1)S(1)} collective-permute-done((bf16[1024,512]{1,0:T(8,128)(2,1)S(1)}, bf16[1024,512]{1,0:T(8,128)(2,1)S(1)}, u32[]{:S(2)}, u32[]{:S(2)}) %collective-permute-start.21) | collective-permute-done | bytes 1048608 | tf_op jit(solution)/shard_map/ppermute | solution.py:1026
  256.8 20.6 %collective-permute-done.20.refs_4_.refs_2_ = bf16[1024,512]{1,0:T(8,128)(2,1)S(1)} collective-permute-done((bf16[1024,512]{1,0:T(8,128)(2,1)S(1)}, bf16[1024,512]{1,0:T(8,128)(2,1)S(1)}, u32[]{:S(2)}, u32[]{:S(2)}) %collective-permute-start.20) | collective-permute-done | bytes 1048608 | tf_op jit(solution)/shard_map/ppermute | solution.py:1026
  278.6 9.7 %project.2 = (bf16[256,2048]{1,0:T(8,128)(2,1)S(1)}, f32[256,2048]{1,0:T(8,128)}) custom-call(s32[1]{0:T(128)} %bitcast.17.sibling_ref, bf16[512,1024]{1,0:T(8,128)(2,1)} %get-tuple-element.87.refs_0_.left_ref, bf16[512,1024]{1,0:T(8,128)(2,1)} %get-tuple-element.92.refs_1_.left_ref, bf16[2048,1024]{1,0:T(8,128)(2,1)} %refs_0_.7, ...), custom_call_target="tpu_custom_call" | custom-call | flops 6442450944 | bytes 16777216 | tf_op jit(solution)/shard_map/project/pallas_call | solution.py:409
  289.6 1.6 copy-done.24
  291.2 4.6 feed_backward.3
  297.7 4.5 feed_backward.2
  302.3 16.3 %project.3 = (bf16[256,2048]{1,0:T(8,128)(2,1)S(1)}, f32[256,2048]{1,0:T(8,128)}) custom-call(s32[1]{0:T(128)} %bitcast.17.sibling_ref, bf16[512,1024]{1,0:T(8,128)(2,1)S(1)} %get-tuple-element.100.refs_0_.refs_1_, bf16[512,1024]{1,0:T(8,128)(2,1)S(1)} %get-tuple-element.104.refs_1_.refs_3_, bf16[512,1024]{1,0:T(8,128)(2,1)S(1)} %copy-done.30, ...), custom_call_target="tpu_custom_call" | custom-call | flops 12884901888 | bytes 16777216 | tf_op jit(solution)/shard_map/project/pallas_call | solution.py:409
  320.2 1.7 add_convert_fusion.4
  326.4 7.7 collective-permute-done.26
  334.1 13.9 %collective-permute-done.23 = bf16[256,2048]{1,0:T(8,128)(2,1)S(1)} collective-permute-done((bf16[256,2048]{1,0:T(8,128)(2,1)S(1)}, bf16[256,2048]{1,0:T(8,128)(2,1)S(1)}, u32[]{:S(2)}, u32[]{:S(2)}) %collective-permute-start.23) | collective-permute-done | bytes 1048608 | tf_op jit(solution)/shard_map/ppermute | solution.py:1026
  349.4 19.9 %collective-permute-done.30 = bf16[256,2048]{1,0:T(8,128)(2,1)S(1)} collective-permute-done((bf16[256,2048]{1,0:T(8,128)(2,1)S(1)}, bf16[256,2048]{1,0:T(8,128)(2,1)S(1)}, u32[]{:S(2)}, u32[]{:S(2)}) %collective-permute-start.30) | collective-permute-done | bytes 1048608 | tf_op jit(solution)/shard_map/ppermute | solution.py:1026
  372.8 2.3 slice.155.refs_7_
  379.3 2.0 maximum_select_fusion.5.refs_1_
  381.3 5.3 outer_sum.2.refs_2_
  386.6 5.5 outer_sum.3.refs_0_
  392.1 7.6 fusion.5
  401.9 4.7 fusion.2
  406.6 7.0 fusion.58
  415.2 395.6 %tail.1 = (bf16[29,256,1024]{2,1,0:T(8,128)(2,1)}, bf16[29,256,1024]{2,1,0:T(8,128)(2,1)}, bf16[29,256,1024]{2,1,0:T(8,128)(2,1)}, bf16[29,256,1024]{2,1,0:T(8,1...) custom-call(bf16[29,256,1024]{2,1,0:T(8,128)(2,1)} %outer_sum.3.refs_0_, ...), custom_call_target="tpu_custom_call", output_to_operand_aliasing={{0}: (0, {})} | custom-call | flops 429496729600 | bytes 31457280 | tf_op jit(solution)/shard_map/tail/pallas_call | solution.py:950
  812.8 1.7 maximum_select_fusion.2
  814.4 27.3 %widen.1 = (f32[2048,1024]{1,0:T(8,128)}, f32[1024,2048]{1,0:T(8,128)}, f32[1024,2048]{1,0:T(8,128)}, f32[512,1024]{1,0:T(8,128)}, f32[1024,512]{1,0:T(8,128)}, ...) custom-call(bf16[29,256,1024]{2,1,0:T(8,128)(2,1)} %get-tuple-element.111.pool_ref), custom_call_target="tpu_custom_call" | custom-call | flops 1 | bytes 47185920 | tf_op jit(solution)/shard_map/widen/pallas_call | solution.py:516
  841.8 8.5 psum.7
  (291 shorter events, 81.2 us)
Async XLA Ops:
  2.1 22.9 %collective-permute-start = (bf16[2,1024]{1,0:T(2,128)(2,1)S(1)}, bf16[2,1024]{1,0:T(2,128)(2,1)S(1)}, u32[]{:S(2)}, u32[]{:S(2)}) collective-permute-start(bf16[2,1024]{1,0:T(2,128)(2,1)S(1)} %pad_maximum_fusion.10), channel_id=1, source_target_pairs={{0,16},{16,0},{1,17},{17,1},{2,18},{18,2},{3,19},{19,3},{4,20},{20... | collective-permute-start | bytes 12296 | tf_op jit(solution)/shard_map/ppermute | solution.py:1026
  7.0 34.5 %collective-permute-start.3 = (bf16[512,512]{1,0:T(8,128)(2,1)}, bf16[512,512]{1,0:T(8,128)(2,1)S(1)}, u32[]{:S(2)}, u32[]{:S(2)}) collective-permute-start(bf16[512,512]{1,0:T(8,128)(2,1)} %constant_dynamic-slice_fusion.21), channel_id=1, source_target_pairs={{0,16},{16,0},{1,17},{17,1},{2,18},{18,2},{3,19},{19,3},{4,20},{20... | collective-permute-start | bytes 1572872 | tf_op jit(solution)/shard_map/ppermute | solution.py:1026
  10.7 26.8 %collective-permute-start.1 = (bf16[512,768]{1,0:T(8,128)(2,1)}, bf16[512,768]{1,0:T(8,128)(2,1)}, u32[]{:S(2)}, u32[]{:S(2)}) collective-permute-start(bf16[512,768]{1,0:T(8,128)(2,1)} %constant_dynamic-slice_fusion.23), channel_id=1, source_target_pairs={{0,16},{16,0},{1,17},{17,1},{2,18},{18,2},{3,19},{19,3},{4,20},{20... | collective-permute-start | bytes 2359304 | tf_op jit(solution)/shard_map/ppermute | solution.py:1026
  37.5 18.3 %collective-permute-start.2 = (bf16[512,768]{1,0:T(8,128)(2,1)}, bf16[512,768]{1,0:T(8,128)(2,1)S(1)}, u32[]{:S(2)}, u32[]{:S(2)}) collective-permute-start(bf16[512,768]{1,0:T(8,128)(2,1)} %collective-permute-done.1.refs_23_), channel_id=1, source_target_pairs={{0,4},{4,0},{8,12},{12,8},{1,5},{5,1},{9,13},{13,9},{2,6},{6,2},{1... | collective-permute-start | bytes 2359304 | tf_op jit(solution)/shard_map/ppermute | solution.py:1026
  41.5 25.4 %copy-start.54 = (bf16[512,512]{1,0:T(8,128)(2,1)}, bf16[512,512]{1,0:T(8,128)(2,1)S(1)}, u32[]{:S(2)}) copy-start(bf16[512,512]{1,0:T(8,128)(2,1)S(1)} %collective-permute-done.3.refs_13_) | copy-start | bytes 1572868
  42.5 64.3 %collective-permute-start.8 = (bf16[512,1024]{1,0:T(8,128)(2,1)S(1)}, bf16[512,1024]{1,0:T(8,128)(2,1)S(1)}, u32[]{:S(2)}, u32[]{:S(2)}) collective-permute-start(bf16[512,1024]{1,0:T(8,128)(2,1)S(1)} %copy-done.65), channel_id=1, source_target_pairs={{0,16},{16,0},{1,17},{17,1},{2,18},{18,2},{3,19},{19,3},{4,20},{20... | collective-permute-start | bytes 3145736 | tf_op jit(solution)/shard_map/ppermute | solution.py:1026
  43.1 45.4 %collective-permute-start.6 = (bf16[512,1024]{1,0:T(8,128)(2,1)S(1)}, bf16[512,1024]{1,0:T(8,128)(2,1)S(1)}, u32[]{:S(2)}, u32[]{:S(2)}) collective-permute-start(bf16[512,1024]{1,0:T(8,128)(2,1)S(1)} %copy-done.66), channel_id=1, source_target_pairs={{0,16},{16,0},{1,17},{17,1},{2,18},{18,2},{3,19},{19,3},{4,20},{20... | collective-permute-start | bytes 3145736 | tf_op jit(solution)/shard_map/ppermute | solution.py:1026
  59.0 29.5 %collective-permute-start.5 = (bf16[1,512,256]{2,1,0:T(8,128)(2,1)S(1)}, bf16[1,512,256]{2,1,0:T(8,128)(2,1)S(1)}, u32[]{:S(2)}, u32[]{:S(2)}) collective-permute-start(bf16[1,512,256]{2,1,0:T(8,128)(2,1)S(1)} %maximum_bitcast_fusion), channel_id=1, source_target_pairs={{0,4},{4,8},{8,12},{1,5},{5,9},{9,13},{2,6},{6,10},{10,14},{3,7},{... | collective-permute-start | bytes 786440 | tf_op jit(solution)/shard_map/ppermute | solution.py:1032
  62.5 26.0 %collective-permute-start.4 = (bf16[1,512,256]{2,1,0:T(8,128)(2,1)S(1)}, bf16[1,512,256]{2,1,0:T(8,128)(2,1)S(1)}, u32[]{:S(2)}, u32[]{:S(2)}) collective-permute-start(bf16[1,512,256]{2,1,0:T(8,128)(2,1)S(1)} %maximum_bitcast_fusion), channel_id=1, source_target_pairs={{0,8},{4,12},{1,9},{5,13},{2,10},{6,14},{3,11},{7,15},{16,24},{20,... | collective-permute-start | bytes 786440 | tf_op jit(solution)/shard_map/ppermute | solution.py:1032
  67.0 21.5 %collective-permute-start.7 = (bf16[512,512]{1,0:T(8,128)(2,1)S(1)}, bf16[512,512]{1,0:T(8,128)(2,1)S(1)}, u32[]{:S(2)}, u32[]{:S(2)}) collective-permute-start(bf16[512,512]{1,0:T(8,128)(2,1)S(1)} %collective-permute-done.3.refs_13_), channel_id=1, source_target_pairs={{0,4},{4,0},{8,12},{12,8},{1,5},{5,1},{9,13},{13,9},{2,6},{6,2},{1... | collective-permute-start | bytes 1572872 | tf_op jit(solution)/shard_map/ppermute | solution.py:1026
  68.4 38.3 %copy-start.1 = (bf16[1,512,512]{2,1,0:T(8,128)(2,1)}, bf16[1,512,512]{2,1,0:T(8,128)(2,1)S(1)}, u32[]{:S(2)}) copy-start(bf16[1,512,512]{2,1,0:T(8,128)(2,1)S(1)} %multiply_bitcast_fusion.q_ref) | copy-start | bytes 1572868
  88.4 26.9 %copy-start.4 = (bf16[512,1024]{1,0:T(8,128)(2,1)}, bf16[512,1024]{1,0:T(8,128)(2,1)S(1)}, u32[]{:S(2)}) copy-start(bf16[512,1024]{1,0:T(8,128)(2,1)S(1)} %collective-permute-done.6.refs_1_.refs_5_) | copy-start | bytes 3145732
  106.8 35.9 %copy-start.2 = (bf16[512,1024]{1,0:T(8,128)(2,1)}, bf16[512,1024]{1,0:T(8,128)(2,1)S(1)}, u32[]{:S(2)}) copy-start(bf16[512,1024]{1,0:T(8,128)(2,1)S(1)} %collective-permute-done.8.refs_4_.refs_8_) | copy-start | bytes 3145732
  109.0 10.1 %collective-permute-start.9 = (bf16[256,2048]{1,0:T(8,128)(2,1)}, bf16[256,2048]{1,0:T(8,128)(2,1)}, u32[]{:S(2)}, u32[]{:S(2)}) collective-permute-start(bf16[256,2048]{1,0:T(8,128)(2,1)} %pad_maximum_fusion.2), channel_id=1, source_target_pairs={{0,1},{1,0},{2,3},{3,2},{4,5},{5,4},{6,7},{7,6},{8,9},{9,8},{10,11... | collective-permute-start | bytes 3145736 | tf_op jit(solution)/shard_map/ppermute | solution.py:1026
  114.8 24.7 %collective-permute-start.10 = (bf16[512,1024]{1,0:T(8,128)(2,1)S(1)}, bf16[512,1024]{1,0:T(8,128)(2,1)S(1)}, u32[]{:S(2)}, u32[]{:S(2)}) collective-permute-start(bf16[512,1024]{1,0:T(8,128)(2,1)S(1)} %copy-done.70), channel_id=1, source_target_pairs={{0,16},{16,0},{1,17},{17,1},{2,18},{18,2},{3,19},{19,3},{4,20},{20... | collective-permute-start | bytes 3145736 | tf_op jit(solution)/shard_map/ppermute | solution.py:1026
  115.3 24.4 %collective-permute-start.11 = (bf16[512,1024]{1,0:T(8,128)(2,1)S(1)}, bf16[512,1024]{1,0:T(8,128)(2,1)S(1)}, u32[]{:S(2)}, u32[]{:S(2)}) collective-permute-start(bf16[512,1024]{1,0:T(8,128)(2,1)S(1)} %collective-permute-done.6.refs_1_.refs_5_), channel_id=1, source_target_pairs={{0,4},{4,0},{8,12},{12,8},{1,5},{5,1},{9,13},{13,9},{2,6},{6,2},{1... | collective-permute-start | bytes 3145736 | tf_op jit(solution)/shard_map/ppermute | solution.py:1026
  139.7 23.6 %collective-permute-start.12 = (bf16[256,2048]{1,0:T(8,128)(2,1)S(1)}, bf16[256,2048]{1,0:T(8,128)(2,1)S(1)}, u32[]{:S(2)}, u32[]{:S(2)}) collective-permute-start(bf16[256,2048]{1,0:T(8,128)(2,1)S(1)} %fusion.10), channel_id=1, source_target_pairs={{0,2},{1,3},{2,0},{3,1},{4,6},{5,7},{6,4},{7,5},{8,10},{9,11},{10,... | collective-permute-start | bytes 3145736 | tf_op jit(solution)/shard_map/ppermute | solution.py:1026
  141.2 23.4 %collective-permute-start.13 = (bf16[512,1024]{1,0:T(8,128)(2,1)S(1)}, bf16[512,1024]{1,0:T(8,128)(2,1)}, u32[]{:S(2)}, u32[]{:S(2)}) collective-permute-start(bf16[512,1024]{1,0:T(8,128)(2,1)S(1)} %copy-done.69), channel_id=1, source_target_pairs={{0,16},{16,0},{1,17},{17,1},{2,18},{18,2},{3,19},{19,3},{4,20},{20... | collective-permute-start | bytes 3145736 | tf_op jit(solution)/shard_map/ppermute | solution.py:1026
  142.7 22.9 %collective-permute-start.14 = (bf16[512,1024]{1,0:T(8,128)(2,1)S(1)}, bf16[512,1024]{1,0:T(8,128)(2,1)S(1)}, u32[]{:S(2)}, u32[]{:S(2)}) collective-permute-start(bf16[512,1024]{1,0:T(8,128)(2,1)S(1)} %collective-permute-done.8.refs_4_.refs_8_), channel_id=1, source_target_pairs={{0,4},{4,0},{8,12},{12,8},{1,5},{5,1},{9,13},{13,9},{2,6},{6,2},{1... | collective-permute-start | bytes 3145736 | tf_op jit(solution)/shard_map/ppermute | solution.py:1026
  165.6 10.4 %collective-permute-start.15 = (bf16[256,2048]{1,0:T(8,128)(2,1)}, bf16[256,2048]{1,0:T(8,128)(2,1)}, u32[]{:S(2)}, u32[]{:S(2)}) collective-permute-start(bf16[256,2048]{1,0:T(8,128)(2,1)} %add_convert_fusion.5), channel_id=1, source_target_pairs={{0,1},{1,0},{2,3},{3,2},{4,5},{5,4},{6,7},{7,6},{8,9},{9,8},{10,11... | collective-permute-start | bytes 3145736 | tf_op jit(solution)/shard_map/ppermute | solution.py:1026
  171.9 69.7 %collective-permute-start.16 = (bf16[1024,512]{1,0:T(8,128)(2,1)S(1)}, bf16[1024,512]{1,0:T(8,128)(2,1)S(1)}, u32[]{:S(2)}, u32[]{:S(2)}) collective-permute-start(bf16[1024,512]{1,0:T(8,128)(2,1)S(1)} %copy-done.71), channel_id=1, source_target_pairs={{0,16},{16,0},{1,17},{17,1},{2,18},{18,2},{3,19},{19,3},{4,20},{20... | collective-permute-start | bytes 3145736 | tf_op jit(solution)/shard_map/ppermute | solution.py:1026
  172.6 26.0 %collective-permute-start.17 = (bf16[512,1024]{1,0:T(8,128)(2,1)S(1)}, bf16[512,1024]{1,0:T(8,128)(2,1)S(1)}, u32[]{:S(2)}, u32[]{:S(2)}) collective-permute-start(bf16[512,1024]{1,0:T(8,128)(2,1)S(1)} %copy-done.7), channel_id=1, source_target_pairs={{0,4},{4,0},{8,12},{12,8},{1,5},{5,1},{9,13},{13,9},{2,6},{6,2},{1... | collective-permute-start | bytes 3145736 | tf_op jit(solution)/shard_map/ppermute | solution.py:1026
  173.1 57.6 %collective-permute-start.19 = (bf16[1024,512]{1,0:T(8,128)(2,1)S(1)}, bf16[1024,512]{1,0:T(8,128)(2,1)S(1)}, u32[]{:S(2)}, u32[]{:S(2)}) collective-permute-start(bf16[1024,512]{1,0:T(8,128)(2,1)S(1)} %copy-done.72), channel_id=1, source_target_pairs={{0,16},{16,0},{1,17},{17,1},{2,18},{18,2},{3,19},{19,3},{4,20},{20... | collective-permute-start | bytes 3145736 | tf_op jit(solution)/shard_map/ppermute | solution.py:1026
  174.5 45.7 %collective-permute-start.18 = (bf16[512,1024]{1,0:T(8,128)(2,1)}, bf16[512,1024]{1,0:T(8,128)(2,1)S(1)}, u32[]{:S(2)}, u32[]{:S(2)}) collective-permute-start(bf16[512,1024]{1,0:T(8,128)(2,1)} %collective-permute-done.13.refs_4_.refs_14_), channel_id=1, source_target_pairs={{0,4},{4,0},{8,12},{12,8},{1,5},{5,1},{9,13},{13,9},{2,6},{6,2},{1... | collective-permute-start | bytes 3145736 | tf_op jit(solution)/shard_map/ppermute | solution.py:1026
  181.7 49.5 %copy-start.3 = (bf16[512,1024]{1,0:T(8,128)(2,1)S(1)}, bf16[512,1024]{1,0:T(8,128)(2,1)}, u32[]{:S(2)}) copy-start(bf16[512,1024]{1,0:T(8,128)(2,1)} %copy-done.2) | copy-start | bytes 3145732
  181.7 49.5 %copy-start.5 = (bf16[512,1024]{1,0:T(8,128)(2,1)S(1)}, bf16[512,1024]{1,0:T(8,128)(2,1)}, u32[]{:S(2)}) copy-start(bf16[512,1024]{1,0:T(8,128)(2,1)} %copy-done.4) | copy-start | bytes 3145732
  181.7 49.5 %copy-start.9 = (bf16[512,1024]{1,0:T(8,128)(2,1)S(1)}, bf16[512,1024]{1,0:T(8,128)(2,1)}, u32[]{:S(2)}) copy-start(bf16[512,1024]{1,0:T(8,128)(2,1)} %copy-done.8) | copy-start | bytes 3145732
  181.7 49.5 %copy-start.11 = (bf16[512,1024]{1,0:T(8,128)(2,1)S(1)}, bf16[512,1024]{1,0:T(8,128)(2,1)}, u32[]{:S(2)}) copy-start(bf16[512,1024]{1,0:T(8,128)(2,1)} %copy-done.10) | copy-start | bytes 3145732
  198.6 29.4 %copy-start.12 = (bf16[512,1024]{1,0:T(8,128)(2,1)}, bf16[512,1024]{1,0:T(8,128)(2,1)S(1)}, u32[]{:S(2)}) copy-start(bf16[512,1024]{1,0:T(8,128)(2,1)S(1)} %collective-permute-done.17.refs_2_.refs_12_) | copy-start | bytes 3145732
  230.7 26.1 %collective-permute-start.21 = (bf16[1024,512]{1,0:T(8,128)(2,1)S(1)}, bf16[1024,512]{1,0:T(8,128)(2,1)S(1)}, u32[]{:S(2)}, u32[]{:S(2)}) collective-permute-start(bf16[1024,512]{1,0:T(8,128)(2,1)S(1)} %collective-permute-done.19.refs_6_.refs_1_), channel_id=1, source_target_pairs={{0,4},{4,0},{8,12},{12,8},{1,5},{5,1},{9,13},{13,9},{2,6},{6,2},{1... | collective-permute-start | bytes 3145736 | tf_op jit(solution)/shard_map/ppermute | solution.py:1026
  241.6 35.8 %collective-permute-start.20 = (bf16[1024,512]{1,0:T(8,128)(2,1)S(1)}, bf16[1024,512]{1,0:T(8,128)(2,1)S(1)}, u32[]{:S(2)}, u32[]{:S(2)}) collective-permute-start(bf16[1024,512]{1,0:T(8,128)(2,1)S(1)} %collective-permute-done.16.refs_3_.refs_1_), channel_id=1, source_target_pairs={{0,4},{4,0},{8,12},{12,8},{1,5},{5,1},{9,13},{13,9},{2,6},{6,2},{1... | collective-permute-start | bytes 3145736 | tf_op jit(solution)/shard_map/ppermute | solution.py:1026
  288.4 31.9 %collective-permute-start.22 = (bf16[256,2048]{1,0:T(8,128)(2,1)S(1)}, bf16[256,2048]{1,0:T(8,128)(2,1)}, u32[]{:S(2)}, u32[]{:S(2)}) collective-permute-start(bf16[256,2048]{1,0:T(8,128)(2,1)S(1)} %get-tuple-element.96), channel_id=1, source_target_pairs={{0,1},{1,0},{2,3},{3,2},{4,5},{5,4},{6,7},{7,6},{8,9},{9,8},{10,11... | collective-permute-start | bytes 3145736 | tf_op jit(solution)/shard_map/ppermute | solution.py:1026
  318.7 4.4 collective-permute-start.29
  319.2 14.9 %collective-permute-start.26 = (bf16[256,1024]{1,0:T(8,128)(2,1)S(1)}, bf16[256,1024]{1,0:T(8,128)(2,1)}, u32[]{:S(2)}, u32[]{:S(2)}) collective-permute-start(bf16[256,1024]{1,0:T(8,128)(2,1)S(1)} %fusion.13), channel_id=1, source_target_pairs={{0,16},{16,0},{1,17},{17,1},{2,18},{18,2},{3,19},{19,3},{4,20},{20... | collective-permute-start | bytes 1572872 | tf_op jit(solution)/shard_map/ppermute | solution.py:1026
  321.9 26.1 %collective-permute-start.23 = (bf16[256,2048]{1,0:T(8,128)(2,1)S(1)}, bf16[256,2048]{1,0:T(8,128)(2,1)S(1)}, u32[]{:S(2)}, u32[]{:S(2)}) collective-permute-start(bf16[256,2048]{1,0:T(8,128)(2,1)S(1)} %add_convert_fusion.4), channel_id=1, source_target_pairs={{0,2},{1,3},{2,0},{3,1},{4,6},{5,7},{6,4},{7,5},{8,10},{9,11},{10,... | collective-permute-start | bytes 3145736 | tf_op jit(solution)/shard_map/ppermute | solution.py:1026
  323.4 45.9 %collective-permute-start.30 = (bf16[256,2048]{1,0:T(8,128)(2,1)S(1)}, bf16[256,2048]{1,0:T(8,128)(2,1)S(1)}, u32[]{:S(2)}, u32[]{:S(2)}) collective-permute-start(bf16[256,2048]{1,0:T(8,128)(2,1)S(1)} %add_convert_fusion.2), channel_id=1, source_target_pairs={{0,2},{1,3},{2,0},{3,1},{4,6},{5,7},{6,4},{7,5},{8,10},{9,11},{10,... | collective-permute-start | bytes 3145736 | tf_op jit(solution)/shard_map/ppermute | solution.py:1026
  324.3 62.3 %collective-permute-start.25 = (bf16[512,1024]{1,0:T(8,128)(2,1)}, bf16[512,1024]{1,0:T(8,128)(2,1)}, u32[]{:S(2)}, u32[]{:S(2)}) collective-permute-start(bf16[512,1024]{1,0:T(8,128)(2,1)} %get-tuple-element.92.refs_1_.left_ref), channel_id=1, source_target_pairs={{0,16},{16,0},{1,17},{17,1},{2,18},{18,2},{3,19},{19,3},{4,20},{20... | collective-permute-start | bytes 3145736 | tf_op jit(solution)/shard_map/ppermute | solution.py:1026
  325.4 55.9 %collective-permute-start.28 = (bf16[512,1024]{1,0:T(8,128)(2,1)}, bf16[512,1024]{1,0:T(8,128)(2,1)}, u32[]{:S(2)}, u32[]{:S(2)}) collective-permute-start(bf16[512,1024]{1,0:T(8,128)(2,1)} %get-tuple-element.87.refs_0_.left_ref), channel_id=1, source_target_pairs={{0,16},{16,0},{1,17},{17,1},{2,18},{18,2},{3,19},{19,3},{4,20},{20... | collective-permute-start | bytes 3145736 | tf_op jit(solution)/shard_map/ppermute | solution.py:1026
  334.1 45.1 %collective-permute-start.27 = (bf16[256,1024]{1,0:T(8,128)(2,1)}, bf16[256,1024]{1,0:T(8,128)(2,1)}, u32[]{:S(2)}, u32[]{:S(2)}) collective-permute-start(bf16[256,1024]{1,0:T(8,128)(2,1)} %collective-permute-done.26), channel_id=1, source_target_pairs={{0,1},{1,0},{2,3},{3,2},{4,5},{5,4},{6,7},{7,6},{8,9},{9,8},{10,11... | collective-permute-start | bytes 1572872 | tf_op jit(solution)/shard_map/ppermute | solution.py:1026
  349.4 42.8 %collective-permute-start.24 = (bf16[256,2048]{1,0:T(8,128)(2,1)}, bf16[256,2048]{1,0:T(8,128)(2,1)}, u32[]{:S(2)}, u32[]{:S(2)}) collective-permute-start(bf16[256,2048]{1,0:T(8,128)(2,1)} %add_convert_fusion.3), channel_id=1, source_target_pairs={{0,1},{1,0},{2,3},{3,2},{4,5},{5,4},{6,7},{7,6},{8,9},{9,8},{10,11... | collective-permute-start | bytes 3145736 | tf_op jit(solution)/shard_map/ppermute | solution.py:1026
  370.7 21.5 %collective-permute-start.31 = (bf16[256,2048]{1,0:T(8,128)(2,1)}, bf16[256,2048]{1,0:T(8,128)(2,1)}, u32[]{:S(2)}, u32[]{:S(2)}) collective-permute-start(bf16[256,2048]{1,0:T(8,128)(2,1)} %add_convert_fusion.1), channel_id=1, source_target_pairs={{0,1},{1,0},{2,3},{3,2},{4,5},{5,4},{6,7},{7,6},{8,9},{9,8},{10,11... | collective-permute-start | bytes 3145736 | tf_op jit(solution)/shard_map/ppermute | solution.py:1026
  415.2 395.6 %copy-start.78 = (f32[2048]{0:T(1024)S(1)}, f32[2048]{0:T(1024)}, u32[]{:S(2)}) copy-start(f32[2048]{0:T(1024)} %get-tuple-element.125) | copy-start | bytes 24580
  415.2 397.5 %copy-start.48 = (bf16[1,512,1024]{2,1,0:T(8,128)(2,1)S(1)}, bf16[1,512,1024]{2,1,0:T(8,128)(2,1)}, u32[]{:S(2)}) copy-start(bf16[1,512,1024]{2,1,0:T(8,128)(2,1)} %slice_bitcast_fusion) | copy-start | bytes 3145732
  415.2 397.5 %copy-start.63 = (bf16[1,512,512]{2,1,0:T(8,128)(2,1)S(1)}, bf16[1,512,512]{2,1,0:T(8,128)(2,1)}, u32[]{:S(2)}) copy-start(bf16[1,512,512]{2,1,0:T(8,128)(2,1)} %get-tuple-element.139) | copy-start | bytes 1572868
  415.2 397.5 %copy-start.64 = (bf16[1,512,512]{2,1,0:T(8,128)(2,1)S(1)}, bf16[1,512,512]{2,1,0:T(8,128)(2,1)}, u32[]{:S(2)}) copy-start(bf16[1,512,512]{2,1,0:T(8,128)(2,1)} %get-tuple-element.140) | copy-start | bytes 1572868
  811.6 30.1 %collective-permute-start.32 = (f32[2,1024]{1,0:T(2,128)S(1)}, f32[2,1024]{1,0:T(2,128)S(1)}, u32[]{:S(2)}, u32[]{:S(2)}) collective-permute-start(f32[2,1024]{1,0:T(2,128)S(1)} %pad_maximum_fusion.9), channel_id=1, source_target_pairs={{0,16},{16,0},{1,17},{17,1},{2,18},{18,2},{3,19},{19,3},{4,20},{20... | collective-permute-start | bytes 24584 | tf_op jit(solution)/shard_map/ppermute | solution.py:1026
  814.4 27.3 %copy-start.80 = (f32[1,2048]{1,0:T(1,128)S(1)}, f32[1,2048]{1,0:T(1,128)}, u32[]{:S(2)}) copy-start(f32[1,2048]{1,0:T(1,128)} %get-tuple-element.110) | copy-start | bytes 24580
  814.4 36.5 %copy-start.58 = (bf16[512,2048]{1,0:T(8,128)(2,1)S(1)}, bf16[512,2048]{1,0:T(8,128)(2,1)}, u32[]{:S(2)}) copy-start(bf16[512,2048]{1,0:T(8,128)(2,1)} %get-tuple-element.109) | copy-start | bytes 6291460
  (66 other events, 477.8 us)

commit v3 on v2

--- a/solution.py
+++ b/solution.py
@@ -526,12 +526,9 @@
 
 
 def tail_body(plan, *refs):
-    heads, group, lead, ready, starts, count = plan
+    heads, group, lead, starts, count = plan
     (
-        pool_in, gate_refs, up_refs, hidden_m_ref, hidden_m_send, hidden_a_ref, hidden_a_send,
-        branch_ref, branch_send, mixed_ref, out_refs, query_ref, keys_ref, log_ref,
-        query_seg_ref, key_seg_ref, cosine_ref, sine_ref, qkv_refs, inputs_ref, scale_ref,
-        gain_ref, grad_middle_ref,
+        pool_in, hidden_m_send, hidden_a_send, branch_send, stored,
         pool_ref, sum_ref, near_ref, across_ref, grad_ref, gain_out_ref,
         gate_land, up_land, hidden_m_land, hidden_a_land, branch_land, mixed_land, qkv_land,
         grad_mixed_ref, dq_ref, dkv_ref, kv_send, kv_land, qkv_grad_ref,
@@ -539,7 +536,14 @@
         own_buf, near_buf, part_buf, across_buf, total_buf, piece_buf,
         x_send, x_recv, tp_send, tp_recv, kv_send_sem, kv_recv_sem,
         send_sem, land_sem, cross_send, cross_land, keep_sem, load_sem, piece_sem,
+        loaded, loaded_sem,
     ) = refs
+    (
+        gate_refs, up_refs, hidden_m_ref, hidden_a_ref, branch_ref, mixed_ref, out_refs,
+        query_ref, keys_ref, log_ref, query_seg_ref, key_seg_ref, cosine_ref, sine_ref,
+        qkv_refs, inputs_ref, scale_ref, gain_ref, grad_middle_ref,
+    ) = loaded
+    stored_gate, stored_up, stored_mixed = stored[0], stored[1], stored[5]
     rows, width = inputs_ref.shape
     half, part = width // 2, width // 4
     half_rows = rows // 2
@@ -571,11 +575,11 @@
         )
 
     cuts = len(gate_refs)
-    gate_copies = [x_copy(i, gate_refs[i], gate_land[i]) for i in range(cuts)]
-    up_copies = [x_copy(cuts + i, up_refs[i], up_land[i]) for i in range(cuts)]
+    gate_copies = [x_copy(i, stored_gate[i], gate_land[i]) for i in range(cuts)]
+    up_copies = [x_copy(cuts + i, stored_up[i], up_land[i]) for i in range(cuts)]
     hidden_m_copy = x_copy(2 * cuts, hidden_m_send, hidden_m_land)
     branch_copy = x_copy(2 * cuts + 1, branch_send, branch_land)
-    mixed_copy = x_copy(2 * cuts + 2, mixed_ref, mixed_land)
+    mixed_copy = x_copy(2 * cuts + 2, stored_mixed, mixed_land)
     hidden_a_copy = x_copy(2 * cuts + 3, hidden_a_send, hidden_a_land)
     qkv_copy = x_copy(2 * cuts + 4, qkv_grad_ref, qkv_land)
     queue = gate_copies + [hidden_m_copy] + up_copies
@@ -587,27 +591,36 @@
                 queue[at - 2].wait_send()
             queue[at].start()
 
+    split = CHUNK_ROWS // own_buf.shape[0]
+    count = count * split
+
+    def share(ref, k):
+        size = CHUNK_ROWS // split
+        return ref.at[k // split, pl.ds(pl.multiple_of(lax.rem(k, split) * size, size), size), :]
+
     def to_pair(source, land, k):
         return pltpu.make_async_remote_copy(
-            src_ref=source, dst_ref=land.at[k], send_sem=send_sem.at[k],
+            src_ref=source, dst_ref=share(land, k), send_sem=send_sem.at[k],
             recv_sem=land_sem.at[k], device_id={"ctx": pair}, device_id_type=mesh_id,
         )
 
     def inward_copy(k):
-        return to_pair(pool_ref.at[k], near_ref, k)
+        return to_pair(share(pool_ref, k), near_ref, k)
 
     def outward_copy(k):
         return to_pair(total_buf.at[lax.rem(k, 2)], sum_ref, k)
 
     def cross_copy(k):
         return pltpu.make_async_remote_copy(
-            src_ref=part_buf.at[lax.rem(k, 4)], dst_ref=across_ref.at[k],
+            src_ref=part_buf.at[lax.rem(k, 4)], dst_ref=share(across_ref, k),
             send_sem=cross_send.at[k], recv_sem=cross_land.at[k],
             device_id={"ctx": across}, device_id_type=mesh_id,
         )
 
     def keep_copy(k):
-        return pltpu.make_async_copy(total_buf.at[lax.rem(k, 2)], sum_ref.at[k], keep_sem.at[k])
+        return pltpu.make_async_copy(
+            total_buf.at[lax.rem(k, 2)], share(sum_ref, k), keep_sem.at[k]
+        )
 
     def load(source, buffer, at):
         return pltpu.make_async_copy(source, buffer, load_sem.at[at])
@@ -616,7 +629,7 @@
 
     def inward(k):
         inward_copy(k).wait_recv()
-        loads = [load(pool_ref.at[k], own_buf, 0), load(near_ref.at[k], near_buf, 1)]
+        loads = [load(share(pool_ref, k), own_buf, 0), load(share(near_ref, k), near_buf, 1)]
         for copy in loads:
             copy.start()
         for copy in loads:
@@ -628,7 +641,7 @@
 
     def outward(k, reuse):
         cross_copy(k).wait_recv()
-        copy = load(across_ref.at[k], across_buf, 2)
+        copy = load(share(across_ref, k), across_buf, 2)
         copy.start()
         if reuse:
             keep_copy(k - 2).wait()
@@ -641,7 +654,7 @@
         outward_copy(k).start()
         keep_copy(k).start()
 
-    ahead = 2
+    ahead = 2 * split
 
     def send_piece(k, carry):
         inward_copy(k).wait_send()
@@ -653,6 +666,8 @@
         return carry
 
     def pump(first, last):
+        first, last = first * split, last * split
+
         @pl.when(is_end)
         def _():
             lax.fori_loop(min(first, count), min(last, count), send_piece, 0)
@@ -674,7 +689,7 @@
 
                 lax.fori_loop(k, min(last, count), both, 0)
             k = max(k, count)
-            while k < last:
+            while k < min(last, count + lag):
                 outward(jnp.int32(k - lag), True)
                 k += 1
 
@@ -684,6 +699,16 @@
             inward_copy(jnp.int32(k)).start()
 
     send_next(0, 2)
+    fills = [
+        pltpu.make_async_copy(source, buffer, loaded_sem.at[at])
+        for at, (source, buffer) in enumerate(
+            zip(jax.tree.leaves(stored), jax.tree.leaves(loaded))
+        )
+    ]
+    for fill in fills:
+        fill.start()
+    for fill in fills:
+        fill.wait()
 
     grad_mixed = None
     at = 0
@@ -915,7 +940,7 @@
             )
         ],
     )
-    pump(17, count + lag)
+    pump(17, count // split + lag)
 
     for copy in queue[-2:] + [first_copy, y_copy, total_copy]:
         copy.wait_send()
@@ -934,52 +959,41 @@
     @pl.when(is_end)
     def _():
         def close(k, carry):
-            to_pair(pool_ref.at[k], sum_ref, k).wait_recv()
+            to_pair(share(pool_ref, k), sum_ref, k).wait_recv()
             return carry
 
         lax.fori_loop(0, count, close, 0)
 
 
-def flat_call(body, groups, **call):
-    flat, tree = jax.tree.flatten(groups, is_leaf=lambda x: isinstance(x, tuple) and len(x) == 2 and isinstance(x[1], pl.BlockSpec))
-    arrays, specs = [x[0] for x in flat], [x[1] for x in flat]
+def flat_call(body, operands, **call):
+    flat, tree = jax.tree.flatten(operands)
 
     def unflatten(*refs):
         body(*jax.tree.unflatten(tree, refs[: len(flat)]), *refs[len(flat) :])
 
-    return pl.pallas_call(unflatten, in_specs=specs, **call)(*arrays)
+    in_specs = [pl.BlockSpec(memory_space=pl.ANY)] * len(flat)
+    return pl.pallas_call(unflatten, in_specs=in_specs, **call)(*flat)
 
 
 def tail(plan, pool, v):
-    heads, group, lead, ready, starts, count = plan
+    heads, group, lead, starts, count = plan
     rows, width = v["inputs"].shape
     half = width // 2
     q_width, kv_width = v["query"].shape[1], v["keys_values"].shape[1] // 2
     qkv_width = q_width + 2 * kv_width
     piece = (CHUNK_ROWS, CHUNK_COLUMNS)
+    split = 2
+    step, steps = (CHUNK_ROWS // split, CHUNK_COLUMNS), count * split
     cuts, feed_part = len(v["grad_gate"]), v["grad_gate"][0].shape[1]
 
-    def near(value):
-        return (value, pl.BlockSpec(memory_space=pltpu.VMEM))
-
-    def far(value):
-        return (value, pl.BlockSpec(memory_space=pl.ANY))
-
-    operands = [
-        far(pool),
-        [near(value) for value in v["grad_gate"]],
-        [near(value) for value in v["grad_up"]],
-        near(v["hidden_m"]), far(v["hidden_m_send"]),
-        near(v["hidden_a"]), far(v["hidden_a_send"]),
-        near(v["branch"]), far(v["branch_send"]),
-        near(v["mixed"]),
-        [near(value) for value in v["out_pieces"]],
-        near(v["query"]), near(v["keys_values"]), near(v["log_sums"]),
-        near(v["query_segments"]), near(v["key_segments"]),
-        near(v["cosine"]), near(v["sine"]),
-        [near(value) for value in v["qkv_pieces"]],
-        near(v["inputs"]), near(v["scale"]), near(v["gain"]), near(v["grad_middle"]),
+    stored = [
+        v["grad_gate"], v["grad_up"], v["hidden_m"], v["hidden_a"], v["branch"], v["mixed"],
+        v["out_pieces"], v["query"], v["keys_values"], v["log_sums"], v["query_segments"],
+        v["key_segments"], v["cosine"], v["sine"], v["qkv_pieces"], v["inputs"], v["scale"],
+        v["gain"], v["grad_middle"],
     ]
+    operands = [pool, v["hidden_m_send"], v["hidden_a_send"], v["branch_send"], stored]
+    loaded = jax.tree.map(lambda value: pltpu.VMEM(value.shape, value.dtype), stored)
     any_space, vmem_space = pl.BlockSpec(memory_space=pl.ANY), pl.BlockSpec(memory_space=pltpu.VMEM)
     line = jax.ShapeDtypeStruct((count,) + piece, BF16)
     dma = pltpu.SemaphoreType.DMA
@@ -995,10 +1009,11 @@
         low(rows // 2, width), wide(rows // 2, width), low(rows // 2, width),
         low(rows // 2, width), low(rows // 2, width), low(rows // 2, width),
         low(rows // 2, width),
-        low(*piece), low(*piece), low(4, *piece), low(*piece), low(2, *piece), low(2, *piece),
+        low(*step), low(*step), low(4, *step), low(*step), low(2, *step), low(2, *piece),
         dma((2 * cuts + 5,)), dma((2 * cuts + 5,)), dma((3,)), dma((3,)), dma((2,)), dma((2,)),
-        dma((count,)), dma((count,)), dma((count,)), dma((count,)), dma((count,)),
+        dma((steps,)), dma((steps,)), dma((steps,)), dma((steps,)), dma((steps,)),
         dma((3,)), dma((2,)),
+        loaded, dma((len(jax.tree.leaves(stored)),)),
     ]
     outs = flat_call(
         functools.partial(tail_body, plan),
@@ -1160,7 +1175,8 @@
 
     gains_other = over_fsdp(gains_own)
     near_qkv = over_fsdp(near_part(qkv_own, 0))
-    near_out = over_fsdp(near_part(out_weight, 1))
+    gains_other, send_out = tie(gains_other, near_part(out_weight, 1))
+    near_out = over_fsdp(send_out)
 
     span_start = ctx * span
     positions = take(doc_positions(segment_ids), span_start, span, 1).reshape(rows)
@@ -1213,17 +1229,17 @@
         seqs, span, q_width
     )
     earlier = [shift(keys_values, "ctx", ctx_count, back) for back in range(blocks_back, 0, -1)]
-    *earlier, near_gate[0], far_out, query_low, send_gate[1] = tie(
-        *earlier, near_gate[0], far_out, query_low, send_gate[1]
-    )
-    near_gate[1] = over_fsdp(send_gate[1])
-    far_gate[0] = over_ctx(near_gate[0])
+    *earlier, query_low = tie(*earlier, query_low)
     keys_values = jnp.concatenate(earlier + [keys_values], axis=1)
     mixed, log_sums = attend_forward(
         query_low, keys_values, query_segments, key_segments, base, lead, group
     )
     mixed_low = mixed.reshape(rows, q_width)
-    mixed_low, near_up[0], send_up[1] = tie(mixed_low, near_up[0], send_up[1])
+    mixed_low, far_out, near_gate[0], near_up[0], send_gate[1], send_up[1] = tie(
+        mixed_low, far_out, near_gate[0], near_up[0], send_gate[1], send_up[1]
+    )
+    near_gate[1] = over_fsdp(send_gate[1])
+    far_gate[0] = over_ctx(near_gate[0])
     near_up[1] = over_fsdp(send_up[1])
     far_up[0] = over_ctx(near_up[0])
 
@@ -1237,30 +1253,25 @@
     first, second = out_project(1 - sibling).astype(BF16), out_project(sibling)
     if tp_count == 4:
         chip = chip_sum(first, second)
-        chip, near_gate[1], far_gate[0], send_down[0] = tie(
-            chip, near_gate[1], far_gate[0], send_down[0]
-        )
-        near_down = [over_fsdp(send_down[0])]
-        far_gate[1] = over_ctx(near_gate[1])
         total = (chip.astype(F32) + swap(chip, "tp", tp_count, 2).astype(F32)).astype(BF16)
-        total, near_up[1], far_up[0], send_down[1] = tie(
-            total, near_up[1], far_up[0], send_down[1]
-        )
-        near_down.append(over_fsdp(send_down[1]))
-        far_up[1] = over_ctx(near_up[1])
+        total, near_gate[1], far_gate[0] = tie(total, near_gate[1], far_gate[0])
         branch_a = join_cores(total).astype(F32)
     else:
         branch_a = tp_sum(first, second)
-        near_down = [over_fsdp(value) for value in send_down]
-        far_gate[1] = over_ctx(near_gate[1])
-        far_up[1] = over_ctx(near_up[1])
+    far_gate[1] = over_ctx(near_gate[1])
     middle = inputs + branch_a
 
     scale_m = row_scale_of(middle)
     normed_m = middle * scale_m
     hidden_m = (normed_m * gain_m).astype(BF16)
+    hidden_m, near_up[1], far_up[0], send_down[0] = tie(
+        hidden_m, near_up[1], far_up[0], send_down[0]
+    )
+    near_down = [over_fsdp(send_down[0])]
+    far_up[1] = over_ctx(near_up[1])
     gate_cuts, up_cuts, act_cuts = [], [], []
-    for cut in range(feed_cuts):
+
+    def feed(cut):
         gate_value, up_value, activated = feed_forward(
             hidden_m,
             (gate_weight, near_gate[cut], far_gate[cut]),
@@ -1271,15 +1282,20 @@
         gate_cuts.append(gate_value)
         up_cuts.append(up_value)
         act_cuts.append(activated)
-    act_cuts[0], near_down[0], send_grad = tie(act_cuts[0], near_down[0], send_grad)
+
+    feed(0)
+    act_cuts[0], near_down[0], far_gate[1], send_down[1] = tie(
+        act_cuts[0], near_down[0], far_gate[1], send_down[1]
+    )
+    near_down.append(over_fsdp(send_down[1]))
+    far_down = [over_ctx(near_down[0])]
+    feed(1)
+    act_cuts[1], near_down[1], send_grad, act_cuts[0] = tie(
+        act_cuts[1], near_down[1], send_grad, act_cuts[0]
+    )
     other_grad = over_fsdp(send_grad)
-    far_down = [over_ctx(near_down[0])]
-    act_other = [over_fsdp(act_cuts[0])]
-    act_cuts[1], near_down[1] = tie(act_cuts[1], near_down[1])
-    act_other.append(over_fsdp(act_cuts[1]))
+    act_other = [over_fsdp(act_cuts[0]), over_fsdp(act_cuts[1])]
     far_down.append(over_ctx(near_down[1]))
-    grad_own, grad_other = grad_rows[:, :half], join_cores(other_grad)
-    fsdp_lane.done = list(act_other)
 
     pieces = CHUNK_ROWS * CHUNK_COLUMNS
     down_count = feed_width * half // pieces
@@ -1287,6 +1303,44 @@
     for size in (feed_width * half,) * 3 + (q_width * half,) * 2 + (2 * kv_width * half,):
         starts.append(pool_size)
         pool_size += size // pieces
+    grad_gate_cuts, grad_up_cuts = [], []
+    for cut in range(feed_cuts):
+        grad_gate, grad_up = feed_backward(
+            grad_rows,
+            (down_weight, near_down[cut], far_down[cut]),
+            gate_cuts[cut],
+            up_cuts[cut],
+            cut,
+        )
+        grad_gate_cuts.append(grad_gate)
+        grad_up_cuts.append(grad_up)
+
+    grad_gate_cuts[1], act_other[0], other_grad = tie(
+        grad_gate_cuts[1], act_other[0], other_grad
+    )
+    grad_own, grad_other = grad_rows[:, :half], join_cores(other_grad)
+    first, second = project(
+        sibling,
+        list(zip(grad_gate_cuts, grad_up_cuts)),
+        [
+            (
+                (gate_weight, near_gate[cut], far_gate[cut]),
+                (up_weight, near_up[cut], far_up[cut]),
+            )
+            for cut in range(feed_cuts)
+        ],
+        width,
+        True,
+    )
+    first, second, act_other[1], *act_cuts = tie(first, second, act_other[1], *act_cuts)
+    if tp_count == 4:
+        chip = chip_sum(first, second)
+        total = (chip.astype(F32) + swap(chip, "tp", tp_count, 2).astype(F32)).astype(BF16)
+        grad_hidden_m = join_cores(total).astype(F32)
+    else:
+        total = None
+        grad_hidden_m = tp_sum(first, second)
+    fsdp_lane.done = list(act_other)
     pool = None
     for cut in range(feed_cuts):
         pool = outer_sum(
@@ -1299,47 +1353,23 @@
             [grad_other],
         )
 
-    grad_gate_cuts, grad_up_cuts = [], []
-    for cut in range(feed_cuts):
-        grad_gate, grad_up = feed_backward(
-            grad_rows,
-            (down_weight, near_down[cut], far_down[cut]),
-            gate_cuts[cut],
-            up_cuts[cut],
-            cut,
-        )
-        grad_gate_cuts.append(grad_gate)
-        grad_up_cuts.append(grad_up)
-
-    grad_hidden_m = tp_sum(
-        *project(
-            sibling,
-            list(zip(grad_gate_cuts, grad_up_cuts)),
-            [
-                (
-                    (gate_weight, near_gate[cut], far_gate[cut]),
-                    (up_weight, near_up[cut], far_up[cut]),
-                )
-                for cut in range(feed_cuts)
-            ],
-            width,
-            True,
-        )
-    )
     feed_gain_part = jnp.sum(grad_hidden_m * normed_m, axis=0)
     grad_middle = norm_back(grad_hidden_m, gain_m, normed_m, scale_m, grad_rows.astype(F32))
     grad_branch = grad_middle.astype(BF16)
 
-    branch_m = tp_sum(
-        *project(
-            sibling,
-            [(value,) for value in act_cuts],
-            [((down_weight, near_down[cut], far_down[cut]),) for cut in range(feed_cuts)],
-            width,
-            False,
-        )
-    )
-    block_out = from_local((middle + branch_m).astype(BF16)).reshape(seqs, span, width)
+    first, second = project(
+        sibling,
+        [(value,) for value in act_cuts],
+        [((down_weight, near_down[cut], far_down[cut]),) for cut in range(feed_cuts)],
+        width,
+        False,
+    )
+    if tp_count == 4:
+        chip = chip_sum(first, second)
+        across = swap(chip, "tp", tp_count, 2)
+    else:
+        chip = across = None
+        branch_m = tp_sum(first, second)
 
     fused = (shard_count, ctx_count, tp_count) == (2, 4, 4)
     fused = fused and seqs == 1 and (blocks_back, base) == (2, 0)
@@ -1351,7 +1381,6 @@
                 q_width // HD,
                 group,
                 lead,
-                starts[1],
                 tuple(starts),
                 pool_size,
             ),
@@ -1383,6 +1412,7 @@
         )
         attention_gain_part = gain_row[0]
         input_grad = input_grad.reshape(seqs, span, width)
+        across, pool = tie(across, pool)
     else:
         gate_at = [fsdp_lane.send(value) for value in grad_gate_cuts]
         up_at = [fsdp_lane.send(value) for value in grad_up_cuts]
@@ -1466,6 +1496,11 @@
             )
         pool = lax.psum(pool.astype(F32), "ctx")
 
+    if tp_count == 4:
+        total = (chip.astype(F32) + across.astype(F32)).astype(BF16)
+        branch_m = join_cores(total).astype(F32)
+    block_out = from_local((middle + branch_m).astype(BF16)).reshape(seqs, span, width)
+
     gain_parts = jnp.stack([attention_gain_part, feed_gain_part])
     gain_other = over_fsdp(other_half(gain_parts))
     gain_sums = lax.psum(gain_parts[:, :half] + gain_other, "ctx")

time: 863 us -> 782 us (0.906)
  waiting for transfers between devices: 194 us -> 121 us
    ppermute x31, waiting for transfers between devices: 194 us -> 114 us  [swap(): return lax.ppermute(value, axis, [(i, i ^ bit) for i in range(size)])]
    unnamed x165 -> x167, local copies, waits for them, and re-layouts: 25.9 us -> 23.6 us
  transfers between devices with their start and end apart: 33 -> 33, of which waited for: 14 -> 19; matrix products, arithmetic and copies ran while one was open for 7% -> 9% of each run, Pallas kernels for 11% -> 64%
where the time goes in v3:
time: 782 us; the launch traced here: 771 us
  Pallas kernels  497 us (64%)
  waiting for transfers between devices  121 us (15%)
  local copies, waits for them, and re-layouts  52.2 us (7%)
  other arithmetic  48.6 us (6%)
  starting transfers between devices  35.4 us (5%)
  blocking collectives  8.72 us (1%)
    pallas_call x1, Pallas kernels, flat_call(): return pl.pallas_call(unflatten, in_specs=in_specs, **call)(*flat)  395 us
    ppermute x31, waiting for transfers between devices, swap(): return lax.ppermute(value, axis, [(i, i ^ bit) for i in range(size)])  114 us
    pallas_call x1, Pallas kernels, widen(): pl.pallas_call(functools.partial(widen_body, starts), grid=(pool.shape[0]...  27.9 us
    ppermute x31, starting transfers between devices, swap(): return lax.ppermute(value, axis, [(i, i ^ bit) for i in range(size)])  27.4 us
    pallas_call x2, Pallas kernels, project(): pl.pallas_call(functools.partial(project_body, cuts, steps, terms, pieces...  24.9 us
    unnamed x167, local copies, waits for them, and re-layouts  23.6 us
    pallas_call x1, Pallas kernels, attend_forward(): pl.pallas_call(functools.partial(attend_forward_body, lead, heads, group)...  17.2 us
  transfers between devices with their start and end apart: 33, of which 19 were waited for; matrix products, arithmetic and copies ran while one was open for 9% of the time, Pallas kernels for 64%

profile of v3, /device:TPU:0, one launch (start us, length us, event | category | flops | bytes accessed | tf_op | source)
XLA Modules:
  0.0 770.9 jit_solution(5895660906034303976)
XLA Ops:
  2.1 3.0 collective-permute-start
  12.6 2.4 copy-done.54
  19.3 1.8 fusion.29
  22.8 2.0 collective-permute-start.3
  24.9 3.6 collective-permute-done.1.refs_23_
  32.4 5.8 collective-permute-done.3.refs_13_
  38.5 1.7 collective-permute-start.7
  40.2 1.7 fusion.15
  41.9 3.4 collective-permute-done.2.refs_24_
  47.9 3.5 collective-permute-start.5
  51.4 4.5 collective-permute-start.4
  58.0 5.6 collective-permute-done.4
  64.6 17.2 %attend_forward.1 = (bf16[1,512,512]{2,1,0:T(8,128)(2,1)S(1)}, f32[1,512,128]{2,1,0:T(8,128)S(1)}) custom-call(bf16[1,512,512]{2,1,0:T(8,128)(2,1)S(1)} %multiply_bitcast_fusion.q_ref, bf16[1,1536,256]{2,1,0:T(8,128)(2,1)S(1)} %get-tuple-element.184.kv_ref, s32[1,512,1]{2,1,0:T(8,128)S(1)} %copy.30.qseg_ref, s32[1,4,1,1152]{3,2,1,0:T(1,128)S(1)} %add_bitcast_fusion.kseg_ref), custom_call_target="tpu_custom_call" | custom-call | flops 21139292160 | bytes 4194304 | tf_op jit(solution)/shard_map/attend_forward/pallas_call | solution.py:189
  81.8 2.5 collective-permute-done.7.refs_1_.refs_5_
  91.1 1.7 collective-permute-start.10
  95.0 21.4 %collective-permute-done.10 = bf16[256,2048]{1,0:T(8,128)(2,1)S(1)} collective-permute-done((bf16[256,2048]{1,0:T(8,128)(2,1)S(1)}, bf16[256,2048]{1,0:T(8,128)(2,1)S(1)}, u32[]{:S(2)}, u32[]{:S(2)}) %collective-permute-start.10) | collective-permute-done | bytes 1048608 | tf_op jit(solution)/shard_map/ppermute | solution.py:1041
  118.1 4.4 fusion.60
  126.9 2.8 multiply_reduce_fusion
  129.7 2.5 multiply_convert_fusion.hidden_ref
  132.2 16.7 %collective-permute-done.14.refs_4_.refs_14_ = bf16[512,1024]{1,0:T(8,128)(2,1)} collective-permute-done((bf16[512,1024]{1,0:T(8,128)(2,1)S(1)}, bf16[512,1024]{1,0:T(8,128)(2,1)}, u32[]{:S(2)}, u32[]{:S(2)}) %collective-permute-start.14) | collective-permute-done | bytes 1048608 | tf_op jit(solution)/shard_map/ppermute | solution.py:1041
  148.9 2.3 collective-permute-done.15.refs_5_.refs_9_
  157.5 6.8 feed_forward.2
  164.3 9.4 %collective-permute-done.17.refs_2_.refs_12_ = bf16[512,1024]{1,0:T(8,128)(2,1)} collective-permute-done((bf16[512,1024]{1,0:T(8,128)(2,1)}, bf16[512,1024]{1,0:T(8,128)(2,1)}, u32[]{:S(2)}, u32[]{:S(2)}) %collective-permute-start.17) | collective-permute-done | bytes 1048608 | tf_op jit(solution)/shard_map/ppermute | solution.py:1041
  173.7 1.9 collective-permute-done.16.refs_1_.refs_3_
  180.8 15.3 %collective-permute-done.19.refs_5_.refs_15_ = bf16[512,1024]{1,0:T(8,128)(2,1)S(1)} collective-permute-done((bf16[512,1024]{1,0:T(8,128)(2,1)}, bf16[512,1024]{1,0:T(8,128)(2,1)S(1)}, u32[]{:S(2)}, u32[]{:S(2)}) %collective-permute-start.19) | collective-permute-done | bytes 1048608 | tf_op jit(solution)/shard_map/ppermute | solution.py:1041
  196.1 7.5 feed_forward.3
  210.5 8.0 %collective-permute-done.18.refs_2_.refs_4_ = bf16[1024,512]{1,0:T(8,128)(2,1)S(1)} collective-permute-done((bf16[1024,512]{1,0:T(8,128)(2,1)}, bf16[1024,512]{1,0:T(8,128)(2,1)S(1)}, u32[]{:S(2)}, u32[]{:S(2)}) %collective-permute-start.18) | collective-permute-done | bytes 1048608 | tf_op jit(solution)/shard_map/ppermute | solution.py:1041
  218.6 2.0 copy-done.22
  220.5 4.7 feed_backward.2
  226.2 13.7 %collective-permute-done.21.refs_2_.refs_7_ = bf16[1024,512]{1,0:T(8,128)(2,1)S(1)} collective-permute-done((bf16[1024,512]{1,0:T(8,128)(2,1)S(1)}, bf16[1024,512]{1,0:T(8,128)(2,1)S(1)}, u32[]{:S(2)}, u32[]{:S(2)}) %collective-permute-start.21) | collective-permute-done | bytes 1048608 | tf_op jit(solution)/shard_map/ppermute | solution.py:1041
  240.0 2.0 copy-done.24
  242.0 4.5 feed_backward.3
  247.5 15.3 %project.2 = (bf16[256,2048]{1,0:T(8,128)(2,1)S(1)}, f32[256,2048]{1,0:T(8,128)}) custom-call(s32[1]{0:T(128)} %bitcast.17.sibling_ref, bf16[512,1024]{1,0:T(8,128)(2,1)S(1)} %get-tuple-element.107.refs_0_.refs_4_, bf16[512,1024]{1,0:T(8,128)(2,1)S(1)} %copy-done.29, bf16[512,1024]{1,0:T(8,128)(2,1)S(1)} %get-tuple-element.120.refs_2_.refs_5_, ...), custom_call_target="tpu_custom_call" | custom-call | flops 12884901888 | bytes 16777216 | tf_op jit(solution)/shard_map/project/pallas_call | solution.py:409
  264.8 2.7 collective-permute-done.28
  267.5 2.8 add_convert_fusion.3
  273.1 2.3 slice.155.refs_9_
  280.7 9.6 %project.3 = (bf16[256,2048]{1,0:T(8,128)(2,1)S(1)}, f32[256,2048]{1,0:T(8,128)}) custom-call(s32[1]{0:T(128)} %bitcast.17.sibling_ref, bf16[512,1024]{1,0:T(8,128)(2,1)S(1)} %copy-done.2, bf16[512,1024]{1,0:T(8,128)(2,1)S(1)} %copy-done.4, bf16[2048,1024]{1,0:T(8,128)(2,1)} %refs_5_.1, bf16[1024,512]{1,0:T(8,128)(2,1)} %collective-permute-done.16.refs_1_.refs_3_, ...), custom_call_target="tpu_custom_call" | custom-call | flops 6442450944 | bytes 16777216 | tf_op jit(solution)/shard_map/project/pallas_call | solution.py:409
  290.3 5.5 collective-permute-done.29
  295.9 1.9 add_convert_fusion.2
  298.4 4.1 outer_sum.2.refs_2_
  302.5 4.1 outer_sum.3.refs_0_
  308.8 3.4 fusion.2
  312.2 7.7 fusion.58
  321.6 395.2 %tail.1 = (bf16[29,256,1024]{2,1,0:T(8,128)(2,1)}, bf16[29,256,1024]{2,1,0:T(8,128)(2,1)}, bf16[29,256,1024]{2,1,0:T(8,128)(2,1)}, bf16[29,256,1024]{2,1,0:T(8,1...) custom-call(bf16[29,256,1024]{2,1,0:T(8,128)(2,1)} %outer_sum.3.refs_0_, ...), custom_call_target="tpu_custom_call", output_to_operand_aliasing={{0}: (0, {})} | custom-call | flops 429496729600 | bytes 31457280 | tf_op jit(solution)/shard_map/tail/pallas_call | solution.py:975
  716.8 1.9 add_convert_fusion.1
  718.9 27.9 %widen.1 = (f32[2048,1024]{1,0:T(8,128)}, f32[1024,2048]{1,0:T(8,128)}, f32[1024,2048]{1,0:T(8,128)}, f32[512,1024]{1,0:T(8,128)}, f32[1024,512]{1,0:T(8,128)}, ...) custom-call(bf16[29,256,1024]{2,1,0:T(8,128)(2,1)} %get-tuple-element.139.pool_ref), custom_call_target="tpu_custom_call" | custom-call | flops 1 | bytes 47185920 | tf_op jit(solution)/shard_map/widen/pallas_call | solution.py:516
  746.9 8.3 %fusion.5 = (f32[2048]{0:T(1024)S(1)}, bf16[512,2048]{1,0:T(8,128)(2,1)S(1)}) fusion(bf16[512,2048]{1,0:T(8,128)(2,1)S(1)} %copy-done.35, f32[512]{0:T(512)S(1)} %copy-done.79, bf16[256,2048]{1,0:T(8,128)(2,1)S(1)} %copy-done.40, bf16[256,2048]{1,0:T(8,128)(2,1)S(1)} %copy-done.44, pred[]{:T(512)S(6)} %eq.17, bf16[256,2048]{1,0:T(8,128)(2,1)} %add_convert_fusion.5, ...), kind=kLoop, calls=%fused_computation.10 | loop fusion | flops 38795264 | bytes 10496001 | tf_op jit(solution)/shard_map/reduce_sum | solution.py:1356
  759.7 8.7 %psum.7 = f32[2,1024]{1,0:T(2,128)S(1)} all-reduce(f32[2,1024]{1,0:T(2,128)S(1)} %fusion.37), channel_id=1, replica_groups=mesh['fsdp'=2,'ctx'=4,'tp'=4] {'ctx'}, use_global_device_ids=true, to_apply=%region_6.7 | all-reduce | flops 2048 | bytes 16384 | tf_op jit(solution)/shard_map/psum | solution.py:1506
  (293 shorter events, 81.1 us)
Async XLA Ops:
  2.1 20.7 %collective-permute-start = (bf16[2,1024]{1,0:T(2,128)(2,1)S(1)}, bf16[2,1024]{1,0:T(2,128)(2,1)S(1)}, u32[]{:S(2)}, u32[]{:S(2)}) collective-permute-start(bf16[2,1024]{1,0:T(2,128)(2,1)S(1)} %pad_maximum_fusion.10), channel_id=1, source_target_pairs={{0,16},{16,0},{1,17},{17,1},{2,18},{18,2},{3,19},{19,3},{4,20},{20... | collective-permute-start | bytes 12296 | tf_op jit(solution)/shard_map/ppermute | solution.py:1041
  7.7 20.8 %collective-permute-start.1 = (bf16[512,768]{1,0:T(8,128)(2,1)}, bf16[512,768]{1,0:T(8,128)(2,1)}, u32[]{:S(2)}, u32[]{:S(2)}) collective-permute-start(bf16[512,768]{1,0:T(8,128)(2,1)} %constant_dynamic-slice_fusion.22), channel_id=1, source_target_pairs={{0,16},{16,0},{1,17},{17,1},{2,18},{18,2},{3,19},{19,3},{4,20},{20... | collective-permute-start | bytes 2359304 | tf_op jit(solution)/shard_map/ppermute | solution.py:1041
  22.8 15.3 %collective-permute-start.3 = (bf16[512,512]{1,0:T(8,128)(2,1)}, bf16[512,512]{1,0:T(8,128)(2,1)S(1)}, u32[]{:S(2)}, u32[]{:S(2)}) collective-permute-start(bf16[512,512]{1,0:T(8,128)(2,1)} %constant_dynamic-slice_fusion.25), channel_id=1, source_target_pairs={{0,16},{16,0},{1,17},{17,1},{2,18},{18,2},{3,19},{19,3},{4,20},{20... | collective-permute-start | bytes 1572872 | tf_op jit(solution)/shard_map/ppermute | solution.py:1041
  28.5 16.8 %collective-permute-start.2 = (bf16[512,768]{1,0:T(8,128)(2,1)}, bf16[512,768]{1,0:T(8,128)(2,1)S(1)}, u32[]{:S(2)}, u32[]{:S(2)}) collective-permute-start(bf16[512,768]{1,0:T(8,128)(2,1)} %collective-permute-done.1.refs_23_), channel_id=1, source_target_pairs={{0,4},{4,0},{8,12},{12,8},{1,5},{5,1},{9,13},{13,9},{2,6},{6,2},{1... | collective-permute-start | bytes 2359304 | tf_op jit(solution)/shard_map/ppermute | solution.py:1041
  38.2 49.7 %copy-start.58 = (bf16[512,512]{1,0:T(8,128)(2,1)}, bf16[512,512]{1,0:T(8,128)(2,1)S(1)}, u32[]{:S(2)}) copy-start(bf16[512,512]{1,0:T(8,128)(2,1)S(1)} %collective-permute-done.3.refs_13_) | copy-start | bytes 1572868
  38.2 43.6 %collective-permute-start.8 = (bf16[512,1024]{1,0:T(8,128)(2,1)S(1)}, bf16[512,1024]{1,0:T(8,128)(2,1)}, u32[]{:S(2)}, u32[]{:S(2)}) collective-permute-start(bf16[512,1024]{1,0:T(8,128)(2,1)S(1)} %copy-done.70), channel_id=1, source_target_pairs={{0,16},{16,0},{1,17},{17,1},{2,18},{18,2},{3,19},{19,3},{4,20},{20... | collective-permute-start | bytes 3145736 | tf_op jit(solution)/shard_map/ppermute | solution.py:1041
  38.5 45.8 %collective-permute-start.7 = (bf16[512,1024]{1,0:T(8,128)(2,1)S(1)}, bf16[512,1024]{1,0:T(8,128)(2,1)S(1)}, u32[]{:S(2)}, u32[]{:S(2)}) collective-permute-start(bf16[512,1024]{1,0:T(8,128)(2,1)S(1)} %copy-done.69), channel_id=1, source_target_pairs={{0,16},{16,0},{1,17},{17,1},{2,18},{18,2},{3,19},{19,3},{4,20},{20... | collective-permute-start | bytes 3145736 | tf_op jit(solution)/shard_map/ppermute | solution.py:1041
  47.9 10.1 %collective-permute-start.5 = (bf16[1,512,256]{2,1,0:T(8,128)(2,1)S(1)}, bf16[1,512,256]{2,1,0:T(8,128)(2,1)S(1)}, u32[]{:S(2)}, u32[]{:S(2)}) collective-permute-start(bf16[1,512,256]{2,1,0:T(8,128)(2,1)S(1)} %maximum_bitcast_fusion), channel_id=1, source_target_pairs={{0,4},{4,8},{8,12},{1,5},{5,9},{9,13},{2,6},{6,10},{10,14},{3,7},{... | collective-permute-start | bytes 786440 | tf_op jit(solution)/shard_map/ppermute | solution.py:1047
  51.4 12.2 %collective-permute-start.4 = (bf16[1,512,256]{2,1,0:T(8,128)(2,1)S(1)}, bf16[1,512,256]{2,1,0:T(8,128)(2,1)S(1)}, u32[]{:S(2)}, u32[]{:S(2)}) collective-permute-start(bf16[1,512,256]{2,1,0:T(8,128)(2,1)S(1)} %maximum_bitcast_fusion), channel_id=1, source_target_pairs={{0,8},{4,12},{1,9},{5,13},{2,10},{6,14},{3,11},{7,15},{16,24},{20,... | collective-permute-start | bytes 786440 | tf_op jit(solution)/shard_map/ppermute | solution.py:1047
  56.3 28.1 %collective-permute-start.6 = (bf16[512,512]{1,0:T(8,128)(2,1)S(1)}, bf16[512,512]{1,0:T(8,128)(2,1)S(1)}, u32[]{:S(2)}, u32[]{:S(2)}) collective-permute-start(bf16[512,512]{1,0:T(8,128)(2,1)S(1)} %collective-permute-done.3.refs_13_), channel_id=1, source_target_pairs={{0,4},{4,0},{8,12},{12,8},{1,5},{5,1},{9,13},{13,9},{2,6},{6,2},{1... | collective-permute-start | bytes 1572872 | tf_op jit(solution)/shard_map/ppermute | solution.py:1041
  57.4 24.4 %copy-start.9 = (bf16[1,512,512]{2,1,0:T(8,128)(2,1)}, bf16[1,512,512]{2,1,0:T(8,128)(2,1)S(1)}, u32[]{:S(2)}) copy-start(bf16[1,512,512]{2,1,0:T(8,128)(2,1)S(1)} %multiply_bitcast_fusion.q_ref) | copy-start | bytes 1572868
  64.6 20.0 %copy-start.46 = (bf16[512,1024]{1,0:T(8,128)(2,1)S(1)}, bf16[512,1024]{1,0:T(8,128)(2,1)}, u32[]{:S(2)}) copy-start(bf16[512,1024]{1,0:T(8,128)(2,1)} %refs_12_.1) | copy-start | bytes 3145732
  86.5 3.0 collective-permute-start.9
  91.1 25.3 %collective-permute-start.10 = (bf16[256,2048]{1,0:T(8,128)(2,1)S(1)}, bf16[256,2048]{1,0:T(8,128)(2,1)S(1)}, u32[]{:S(2)}, u32[]{:S(2)}) collective-permute-start(bf16[256,2048]{1,0:T(8,128)(2,1)S(1)} %fusion.10), channel_id=1, source_target_pairs={{0,2},{1,3},{2,0},{3,1},{4,6},{5,7},{6,4},{7,5},{8,10},{9,11},{10,... | collective-permute-start | bytes 3145736 | tf_op jit(solution)/shard_map/ppermute | solution.py:1041
  92.8 25.0 %collective-permute-start.11 = (bf16[512,1024]{1,0:T(8,128)(2,1)S(1)}, bf16[512,1024]{1,0:T(8,128)(2,1)}, u32[]{:S(2)}, u32[]{:S(2)}) collective-permute-start(bf16[512,1024]{1,0:T(8,128)(2,1)S(1)} %copy-done.66), channel_id=1, source_target_pairs={{0,16},{16,0},{1,17},{17,1},{2,18},{18,2},{3,19},{19,3},{4,20},{20... | collective-permute-start | bytes 3145736 | tf_op jit(solution)/shard_map/ppermute | solution.py:1041
  93.4 24.6 %collective-permute-start.12 = (bf16[512,1024]{1,0:T(8,128)(2,1)S(1)}, bf16[512,1024]{1,0:T(8,128)(2,1)S(1)}, u32[]{:S(2)}, u32[]{:S(2)}) collective-permute-start(bf16[512,1024]{1,0:T(8,128)(2,1)S(1)} %collective-permute-done.7.refs_1_.refs_5_), channel_id=1, source_target_pairs={{0,4},{4,0},{8,12},{12,8},{1,5},{5,1},{9,13},{13,9},{2,6},{6,2},{1... | collective-permute-start | bytes 3145736 | tf_op jit(solution)/shard_map/ppermute | solution.py:1041
  118.1 8.9 %collective-permute-start.13 = (bf16[256,2048]{1,0:T(8,128)(2,1)}, bf16[256,2048]{1,0:T(8,128)(2,1)S(1)}, u32[]{:S(2)}, u32[]{:S(2)}) collective-permute-start(bf16[256,2048]{1,0:T(8,128)(2,1)} %add_convert_fusion.5), channel_id=1, source_target_pairs={{0,1},{1,0},{2,3},{3,2},{4,5},{5,4},{6,7},{7,6},{8,9},{9,8},{10,11... | collective-permute-start | bytes 3145736 | tf_op jit(solution)/shard_map/ppermute | solution.py:1041
  123.5 25.4 %collective-permute-start.14 = (bf16[512,1024]{1,0:T(8,128)(2,1)S(1)}, bf16[512,1024]{1,0:T(8,128)(2,1)}, u32[]{:S(2)}, u32[]{:S(2)}) collective-permute-start(bf16[512,1024]{1,0:T(8,128)(2,1)S(1)} %copy-done.65), channel_id=1, source_target_pairs={{0,16},{16,0},{1,17},{17,1},{2,18},{18,2},{3,19},{19,3},{4,20},{20... | collective-permute-start | bytes 3145736 | tf_op jit(solution)/shard_map/ppermute | solution.py:1041
  124.9 26.2 %collective-permute-start.15 = (bf16[512,1024]{1,0:T(8,128)(2,1)}, bf16[512,1024]{1,0:T(8,128)(2,1)S(1)}, u32[]{:S(2)}, u32[]{:S(2)}) collective-permute-start(bf16[512,1024]{1,0:T(8,128)(2,1)} %collective-permute-done.8.refs_4_.refs_8_), channel_id=1, source_target_pairs={{0,4},{4,0},{8,12},{12,8},{1,5},{5,1},{9,13},{13,9},{2,6},{6,2},{1... | collective-permute-start | bytes 3145736 | tf_op jit(solution)/shard_map/ppermute | solution.py:1041
  126.5 47.3 %collective-permute-start.17 = (bf16[512,1024]{1,0:T(8,128)(2,1)}, bf16[512,1024]{1,0:T(8,128)(2,1)}, u32[]{:S(2)}, u32[]{:S(2)}) collective-permute-start(bf16[512,1024]{1,0:T(8,128)(2,1)} %collective-permute-done.11.refs_1_.refs_11_), channel_id=1, source_target_pairs={{0,4},{4,0},{8,12},{12,8},{1,5},{5,1},{9,13},{13,9},{2,6},{6,2},{1... | collective-permute-start | bytes 3145736 | tf_op jit(solution)/shard_map/ppermute | solution.py:1041
  129.7 182.5 %copy-start.78 = (f32[512]{0:T(512)}, f32[512]{0:T(512)S(1)}, u32[]{:S(2)}) copy-start(f32[512]{0:T(512)S(1)} %add_rsqrt_fusion) | copy-start | bytes 6148
  152.1 23.5 %collective-permute-start.16 = (bf16[1024,512]{1,0:T(8,128)(2,1)}, bf16[1024,512]{1,0:T(8,128)(2,1)}, u32[]{:S(2)}, u32[]{:S(2)}) collective-permute-start(bf16[1024,512]{1,0:T(8,128)(2,1)} %constant_dynamic-slice_fusion.14), channel_id=1, source_target_pairs={{0,16},{16,0},{1,17},{17,1},{2,18},{18,2},{3,19},{19,3},{4,20},{20... | collective-permute-start | bytes 3145736 | tf_op jit(solution)/shard_map/ppermute | solution.py:1041
  155.7 20.6 %copy-start.50 = (bf16[512,512]{1,0:T(8,128)(2,1)}, bf16[512,512]{1,0:T(8,128)(2,1)S(1)}, u32[]{:S(2)}) copy-start(bf16[512,512]{1,0:T(8,128)(2,1)S(1)} %get-tuple-element.171) | copy-start | bytes 1572868
  155.7 20.6 %copy-start.52 = (bf16[512,512]{1,0:T(8,128)(2,1)}, bf16[512,512]{1,0:T(8,128)(2,1)S(1)}, u32[]{:S(2)}) copy-start(bf16[512,512]{1,0:T(8,128)(2,1)S(1)} %get-tuple-element.172) | copy-start | bytes 1572868
  155.9 40.2 %collective-permute-start.19 = (bf16[512,1024]{1,0:T(8,128)(2,1)}, bf16[512,1024]{1,0:T(8,128)(2,1)S(1)}, u32[]{:S(2)}, u32[]{:S(2)}) collective-permute-start(bf16[512,1024]{1,0:T(8,128)(2,1)} %collective-permute-done.14.refs_4_.refs_14_), channel_id=1, source_target_pairs={{0,4},{4,0},{8,12},{12,8},{1,5},{5,1},{9,13},{13,9},{2,6},{6,2},{1... | collective-permute-start | bytes 3145736 | tf_op jit(solution)/shard_map/ppermute | solution.py:1041
  164.3 43.5 %copy-start.1 = (bf16[512,1024]{1,0:T(8,128)(2,1)}, bf16[512,1024]{1,0:T(8,128)(2,1)S(1)}, u32[]{:S(2)}) copy-start(bf16[512,1024]{1,0:T(8,128)(2,1)S(1)} %get-tuple-element.125.refs_0_.left_ref) | copy-start | bytes 3145732
  175.7 30.6 %collective-permute-start.20 = (bf16[1024,512]{1,0:T(8,128)(2,1)S(1)}, bf16[1024,512]{1,0:T(8,128)(2,1)S(1)}, u32[]{:S(2)}, u32[]{:S(2)}) collective-permute-start(bf16[1024,512]{1,0:T(8,128)(2,1)S(1)} %constant_dynamic-slice_fusion.13), channel_id=1, source_target_pairs={{0,16},{16,0},{1,17},{17,1},{2,18},{18,2},{3,19},{19,3},{4,20},{20... | collective-permute-start | bytes 3145736 | tf_op jit(solution)/shard_map/ppermute | solution.py:1041
  179.2 39.4 %collective-permute-start.18 = (bf16[1024,512]{1,0:T(8,128)(2,1)}, bf16[1024,512]{1,0:T(8,128)(2,1)S(1)}, u32[]{:S(2)}, u32[]{:S(2)}) collective-permute-start(bf16[1024,512]{1,0:T(8,128)(2,1)} %collective-permute-done.16.refs_1_.refs_3_), channel_id=1, source_target_pairs={{0,4},{4,0},{8,12},{12,8},{1,5},{5,1},{9,13},{13,9},{2,6},{6,2},{1... | collective-permute-start | bytes 3145736 | tf_op jit(solution)/shard_map/ppermute | solution.py:1041
  206.3 33.7 %copy-start.16 = (bf16[1024,512]{1,0:T(8,128)(2,1)}, bf16[1024,512]{1,0:T(8,128)(2,1)S(1)}, u32[]{:S(2)}) copy-start(bf16[1024,512]{1,0:T(8,128)(2,1)S(1)} %collective-permute-done.20.refs_1_.refs_6_) | copy-start | bytes 3145732
  206.3 33.7 %collective-permute-start.21 = (bf16[1024,512]{1,0:T(8,128)(2,1)S(1)}, bf16[1024,512]{1,0:T(8,128)(2,1)S(1)}, u32[]{:S(2)}, u32[]{:S(2)}) collective-permute-start(bf16[1024,512]{1,0:T(8,128)(2,1)S(1)} %collective-permute-done.20.refs_1_.refs_6_), channel_id=1, source_target_pairs={{0,4},{4,0},{8,12},{12,8},{1,5},{5,1},{9,13},{13,9},{2,6},{6,2},{1... | collective-permute-start | bytes 3145736 | tf_op jit(solution)/shard_map/ppermute | solution.py:1041
  207.8 38.6 %collective-permute-start.22 = (bf16[512,1024]{1,0:T(8,128)(2,1)S(1)}, bf16[512,1024]{1,0:T(8,128)(2,1)S(1)}, u32[]{:S(2)}, u32[]{:S(2)}) collective-permute-start(bf16[512,1024]{1,0:T(8,128)(2,1)S(1)} %get-tuple-element.125.refs_0_.left_ref), channel_id=1, source_target_pairs={{0,16},{16,0},{1,17},{17,1},{2,18},{18,2},{3,19},{19,3},{4,20},{20... | collective-permute-start | bytes 3145736 | tf_op jit(solution)/shard_map/ppermute | solution.py:1041
  208.5 38.0 %collective-permute-start.23 = (bf16[256,1024]{1,0:T(8,128)(2,1)S(1)}, bf16[256,1024]{1,0:T(8,128)(2,1)S(1)}, u32[]{:S(2)}, u32[]{:S(2)}) collective-permute-start(bf16[256,1024]{1,0:T(8,128)(2,1)S(1)} %fusion.13), channel_id=1, source_target_pairs={{0,16},{16,0},{1,17},{17,1},{2,18},{18,2},{3,19},{19,3},{4,20},{20... | collective-permute-start | bytes 1572872 | tf_op jit(solution)/shard_map/ppermute | solution.py:1041
  209.9 55.0 %collective-permute-start.24 = (bf16[512,1024]{1,0:T(8,128)(2,1)S(1)}, bf16[512,1024]{1,0:T(8,128)(2,1)S(1)}, u32[]{:S(2)}, u32[]{:S(2)}) collective-permute-start(bf16[512,1024]{1,0:T(8,128)(2,1)S(1)} %get-tuple-element.126.refs_1_.left_ref), channel_id=1, source_target_pairs={{0,16},{16,0},{1,17},{17,1},{2,18},{18,2},{3,19},{19,3},{4,20},{20... | collective-permute-start | bytes 3145736 | tf_op jit(solution)/shard_map/ppermute | solution.py:1041
  220.5 19.4 %copy-start.26 = (f32[512,1024]{1,0:T(8,128)S(1)}, f32[512,1024]{1,0:T(8,128)}, u32[]{:S(2)}) copy-start(f32[512,1024]{1,0:T(8,128)} %copy-done.25) | copy-start | bytes 6291460
  226.2 21.3 %copy-start.27 = (bf16[512,1024]{1,0:T(8,128)(2,1)}, bf16[512,1024]{1,0:T(8,128)(2,1)S(1)}, u32[]{:S(2)}) copy-start(bf16[512,1024]{1,0:T(8,128)(2,1)S(1)} %get-tuple-element.107.refs_0_.refs_4_) | copy-start | bytes 3145732
  264.8 2.7 collective-permute-start.28
  270.3 25.5 %collective-permute-start.29 = (bf16[256,2048]{1,0:T(8,128)(2,1)}, bf16[256,2048]{1,0:T(8,128)(2,1)}, u32[]{:S(2)}, u32[]{:S(2)}) collective-permute-start(bf16[256,2048]{1,0:T(8,128)(2,1)} %add_convert_fusion.3), channel_id=1, source_target_pairs={{0,2},{1,3},{2,0},{3,1},{4,6},{5,7},{6,4},{7,5},{8,10},{9,11},{10,... | collective-permute-start | bytes 3145736 | tf_op jit(solution)/shard_map/ppermute | solution.py:1041
  279.7 18.2 %collective-permute-start.27 = (bf16[256,1024]{1,0:T(8,128)(2,1)S(1)}, bf16[256,1024]{1,0:T(8,128)(2,1)S(1)}, u32[]{:S(2)}, u32[]{:S(2)}) collective-permute-start(bf16[256,1024]{1,0:T(8,128)(2,1)S(1)} %copy-done.74), channel_id=1, source_target_pairs={{0,1},{1,0},{2,3},{3,2},{4,5},{5,4},{6,7},{7,6},{8,9},{9,8},{10,11... | collective-permute-start | bytes 1572872 | tf_op jit(solution)/shard_map/ppermute | solution.py:1041
  290.3 16.3 %collective-permute-start.25 = (bf16[256,2048]{1,0:T(8,128)(2,1)S(1)}, bf16[256,2048]{1,0:T(8,128)(2,1)S(1)}, u32[]{:S(2)}, u32[]{:S(2)}) collective-permute-start(bf16[256,2048]{1,0:T(8,128)(2,1)S(1)} %get-tuple-element.128), channel_id=1, source_target_pairs={{0,1},{1,0},{2,3},{3,2},{4,5},{5,4},{6,7},{7,6},{8,9},{9,8},{10,11... | collective-permute-start | bytes 3145736 | tf_op jit(solution)/shard_map/ppermute | solution.py:1041
  297.8 10.7 %collective-permute-start.30 = (bf16[256,2048]{1,0:T(8,128)(2,1)S(1)}, bf16[256,2048]{1,0:T(8,128)(2,1)S(1)}, u32[]{:S(2)}, u32[]{:S(2)}) collective-permute-start(bf16[256,2048]{1,0:T(8,128)(2,1)S(1)} %add_convert_fusion.2), channel_id=1, source_target_pairs={{0,1},{1,0},{2,3},{3,2},{4,5},{5,4},{6,7},{7,6},{8,9},{9,8},{10,11... | collective-permute-start | bytes 3145736 | tf_op jit(solution)/shard_map/ppermute | solution.py:1041
  307.9 408.9 %collective-permute-start.26 = (bf16[256,2048]{1,0:T(8,128)(2,1)}, bf16[256,2048]{1,0:T(8,128)(2,1)}, u32[]{:S(2)}, u32[]{:S(2)}) collective-permute-start(bf16[256,2048]{1,0:T(8,128)(2,1)} %add_convert_fusion.4), channel_id=1, source_target_pairs={{0,2},{1,3},{2,0},{3,1},{4,6},{5,7},{6,4},{7,5},{8,10},{9,11},{10,... | collective-permute-start | bytes 3145736 | tf_op jit(solution)/shard_map/ppermute | solution.py:1041
  718.7 28.1 %collective-permute-start.31 = (bf16[256,2048]{1,0:T(8,128)(2,1)S(1)}, bf16[256,2048]{1,0:T(8,128)(2,1)S(1)}, u32[]{:S(2)}, u32[]{:S(2)}) collective-permute-start(bf16[256,2048]{1,0:T(8,128)(2,1)S(1)} %add_convert_fusion.1), channel_id=1, source_target_pairs={{0,1},{1,0},{2,3},{3,2},{4,5},{5,4},{6,7},{7,6},{8,9},{9,8},{10,11... | collective-permute-start | bytes 3145736 | tf_op jit(solution)/shard_map/ppermute | solution.py:1041
  718.8 28.0 %copy-start.35 = (bf16[512,2048]{1,0:T(8,128)(2,1)S(1)}, bf16[512,2048]{1,0:T(8,128)(2,1)}, u32[]{:S(2)}) copy-start(bf16[512,2048]{1,0:T(8,128)(2,1)} %copy-done.32) | copy-start | bytes 6291460
  718.8 28.0 %copy-start.38 = (bf16[256,2048]{1,0:T(8,128)(2,1)S(1)}, bf16[256,2048]{1,0:T(8,128)(2,1)}, u32[]{:S(2)}) copy-start(bf16[256,2048]{1,0:T(8,128)(2,1)} %copy-done.36) | copy-start | bytes 3145732
  718.8 28.0 %copy-start.40 = (bf16[256,2048]{1,0:T(8,128)(2,1)S(1)}, bf16[256,2048]{1,0:T(8,128)(2,1)}, u32[]{:S(2)}) copy-start(bf16[256,2048]{1,0:T(8,128)(2,1)} %copy-done.39) | copy-start | bytes 3145732
  718.9 28.0 %copy-start.44 = (bf16[256,2048]{1,0:T(8,128)(2,1)S(1)}, bf16[256,2048]{1,0:T(8,128)(2,1)}, u32[]{:S(2)}) copy-start(bf16[256,2048]{1,0:T(8,128)(2,1)} %copy-done.43) | copy-start | bytes 3145732
  718.9 28.0 %copy-start.79 = (f32[512]{0:T(512)S(1)}, f32[512]{0:T(512)}, u32[]{:S(2)}) copy-start(f32[512]{0:T(512)} %copy-done.78) | copy-start | bytes 6148
  756.0 3.7 collective-permute-start.32
  (67 other events, 322.8 us)

commit v4 on v3

--- a/solution.py
+++ b/solution.py
@@ -528,22 +528,24 @@
 def tail_body(plan, *refs):
     heads, group, lead, starts, count = plan
     (
-        pool_in, hidden_m_send, hidden_a_send, branch_send, stored,
-        pool_ref, sum_ref, near_ref, across_ref, grad_ref, gain_out_ref,
+        pool_in, hidden_m_send, hidden_a_send, feed_chip, stored,
+        pool_ref, sum_ref, near_ref, across_ref, feed_land, grad_ref, gain_out_ref,
         gate_land, up_land, hidden_m_land, hidden_a_land, branch_land, mixed_land, qkv_land,
         grad_mixed_ref, dq_ref, dkv_ref, kv_send, kv_land, qkv_grad_ref,
         first_ref, second_ref, core_land, chip_ref, y_land, total_ref, other_ref,
+        middle_y, middle_total, middle_other, branch_ref, branch_send,
         own_buf, near_buf, part_buf, across_buf, total_buf, piece_buf,
         x_send, x_recv, tp_send, tp_recv, kv_send_sem, kv_recv_sem,
         send_sem, land_sem, cross_send, cross_land, keep_sem, load_sem, piece_sem,
         loaded, loaded_sem,
     ) = refs
     (
-        gate_refs, up_refs, hidden_m_ref, hidden_a_ref, branch_ref, mixed_ref, out_refs,
+        gate_refs, up_refs, hidden_m_ref, hidden_a_ref, mixed_ref, out_refs,
         query_ref, keys_ref, log_ref, query_seg_ref, key_seg_ref, cosine_ref, sine_ref,
         qkv_refs, inputs_ref, scale_ref, gain_ref, grad_middle_ref,
+        middle_chip, cotangent_ref, middle_scale, middle_gain,
     ) = loaded
-    stored_gate, stored_up, stored_mixed = stored[0], stored[1], stored[5]
+    stored_gate, stored_up, stored_mixed = stored[0], stored[1], stored[4]
     rows, width = inputs_ref.shape
     half, part = width // 2, width // 4
     half_rows = rows // 2
@@ -590,6 +592,12 @@
             if at >= 2:
                 queue[at - 2].wait_send()
             queue[at].start()
+
+    def tp_copy(at, source, land, target):
+        return pltpu.make_async_remote_copy(
+            src_ref=source, dst_ref=land, send_sem=tp_send.at[at], recv_sem=tp_recv.at[at],
+            device_id={"tp": target}, device_id_type=mesh_id,
+        )
 
     split = CHUNK_ROWS // own_buf.shape[0]
     count = count * split
@@ -666,7 +674,9 @@
         return carry
 
     def pump(first, last):
-        first, last = first * split, last * split
+        pump_steps(first * split, last * split)
+
+    def pump_steps(first, last):
 
         @pl.when(is_end)
         def _():
@@ -699,6 +709,10 @@
             inward_copy(jnp.int32(k)).start()
 
     send_next(0, 2)
+    middle_y_copy = tp_copy(3, stored[-4], middle_y, across_y)
+    middle_core_copy = tp_copy(4, middle_total, middle_other, core)
+    feed_copy = tp_copy(5, feed_chip, feed_land, across_y)
+    middle_y_copy.start()
     fills = [
         pltpu.make_async_copy(source, buffer, loaded_sem.at[at])
         for at, (source, buffer) in enumerate(
@@ -709,6 +723,43 @@
         fill.start()
     for fill in fills:
         fill.wait()
+    pump_steps(0, 3)
+
+    theirs = pl.multiple_of((1 - sibling) * half_rows, half_rows)
+    mine = pl.multiple_of(sibling * half_rows, half_rows)
+    step_rows = 64
+    odd = lax.rem(ctx, 2)
+    near_send = pl.multiple_of(odd * part, part)
+    far_send = pl.multiple_of((1 - odd) * part, part)
+
+    def middle_rows(source, base):
+        def body(step, total):
+            at = pl.multiple_of(step * step_rows, step_rows)
+            here = pl.ds(pl.multiple_of(base + at, step_rows), step_rows)
+            normed = grad_middle_ref[here, :]
+            hidden = source[pl.ds(at, step_rows), :].astype(F32)
+            grad = hidden * middle_gain[...]
+            mean = jnp.sum(grad * normed, axis=-1, keepdims=True) * (1.0 / width)
+            value = cotangent_ref[here, :].astype(F32) + middle_scale[here, :] * (
+                grad - normed * mean
+            )
+            grad_middle_ref[here, :] = value
+            low = value.astype(BF16)
+            branch_ref[here, :] = low
+            branch_send[here, pl.ds(near_send, part)] = low[:, half : half + part]
+            branch_send[here, pl.ds(far_send, part)] = low[:, half + part :]
+            return total + jnp.sum(hidden * normed, axis=0, keepdims=True)
+
+        return lax.fori_loop(0, half_rows // step_rows, body, jnp.zeros((1, width), F32))
+
+    middle_y_copy.wait_recv()
+    middle_total[...] = (middle_chip[...].astype(F32) + middle_y[...].astype(F32)).astype(BF16)
+    middle_core_copy.start()
+    feed_gain = middle_rows(middle_total, mine)
+    pump_steps(3, 4)
+    middle_core_copy.wait_recv()
+    gain_out_ref[1:2, :] = feed_gain + middle_rows(middle_other, theirs)
+    send_next(2, 3)
 
     grad_mixed = None
     at = 0
@@ -723,6 +774,15 @@
     reach = tile + lead
 
     def attend(step, carry):
+        @pl.when(is_end)
+        def _():
+            send_piece(step + lag + 2, 0)
+
+        @pl.when(is_middle)
+        def _():
+            inward(step + lag + 2)
+            outward(step + 2, True)
+
         start = pl.multiple_of(step * tile, tile)
         distance = (
             lax.broadcasted_iota(jnp.int32, (reach, tile), 1)
@@ -745,8 +805,7 @@
         return carry
 
     lax.fori_loop(0, tiles, attend, 0)
-    pump(0, 2)
-    send_next(2, 3)
+    send_next(3, 4)
 
     for back in (1, 2):
         kv_send[back - 1] = dkv_ref[(2 - back) * rows : (3 - back) * rows, :].astype(BF16)
@@ -763,71 +822,6 @@
         @pl.when(ctx >= back)
         def _():
             kv_copy(back).start()
-
-    pump(2, 3)
-    for back in (1, 2):
-
-        @pl.when(ctx + back < 4)
-        def _():
-            kv_copy(back).wait_recv()
-
-    send_next(3, 4)
-    kv_width = dkv_ref.shape[1] // 2
-    q_width = dq_ref.shape[1]
-    cosine, sine = cosine_ref[...], sine_ref[...]
-    front = lax.rem(lax.broadcasted_iota(jnp.int32, (rows, LANES), 1), HD) < HD // 2
-
-    def unrotate(value):
-        swapped = jnp.where(
-            front, pltpu.roll(value, LANES - HD // 2, 1), pltpu.roll(value, HD // 2, 1)
-        )
-        return (value * cosine - swapped * sine).astype(BF16)
-
-    for at in range(0, q_width, LANES):
-        qkv_grad_ref[:, at : at + LANES] = unrotate(dq_ref[:, at : at + LANES])
-    kv_sum = dkv_ref[2 * rows :, :]
-    for back in range(2):
-        kv_sum = kv_sum + kv_land[back].astype(F32)
-    for at in range(0, kv_width, LANES):
-        qkv_grad_ref[:, q_width + at : q_width + at + LANES] = unrotate(
-            kv_sum[:, at : at + LANES]
-        )
-    qkv_grad_ref[:, q_width + kv_width :] = kv_sum[:, kv_width:].astype(BF16)
-
-    def tp_copy(at, source, land, target):
-        return pltpu.make_async_remote_copy(
-            src_ref=source, dst_ref=land, send_sem=tp_send.at[at], recv_sem=tp_recv.at[at],
-            device_id={"tp": target}, device_id_type=mesh_id,
-        )
-
-    first_copy = tp_copy(0, first_ref, core_land, core)
-    y_copy = tp_copy(1, chip_ref, y_land, across_y)
-    total_copy = tp_copy(2, total_ref, other_ref, core)
-    theirs = pl.multiple_of((1 - sibling) * half_rows, half_rows)
-    mine = pl.multiple_of(sibling * half_rows, half_rows)
-
-    def back_project(start, store):
-        at = 0
-        for piece in qkv_refs:
-            size = piece.shape[0]
-            store(at, size, dot_back(qkv_grad_ref[pl.ds(start, half_rows), :], piece[...]))
-            at += size
-
-    def store_first(at, size, value):
-        first_ref[:, at : at + size] = value.astype(BF16)
-
-    def store_second(at, size, value):
-        second_ref[:, at : at + size] = value
-
-    back_project(theirs, store_first)
-    first_copy.start()
-    back_project(mine, store_second)
-    pump(3, 5)
-    first_copy.wait_recv()
-    chip_ref[...] = (second_ref[...] + core_land[...].astype(F32)).astype(BF16)
-    y_copy.start()
-    pump(5, 6)
-    send_next(4, 5)
 
     def piece_copy(slot, k):
         return pltpu.make_async_copy(piece_buf.at[slot], pool_ref.at[k], piece_sem.at[slot])
@@ -855,19 +849,77 @@
             for block in range(half // CHUNK_ROWS)
         ]
 
+    pump(4, 5)
     for copy in gate_copies + [hidden_m_copy]:
         copy.wait_recv()
     put(starts[1], feed_pieces(gate_refs, gate_land))
-    pump(6, 7)
+    send_next(4, 5)
+    pump(5, 6)
+
+    for back in (1, 2):
+
+        @pl.when(ctx + back < 4)
+        def _():
+            kv_copy(back).wait_recv()
+
+    kv_width = dkv_ref.shape[1] // 2
+    q_width = dq_ref.shape[1]
+    cosine, sine = cosine_ref[...], sine_ref[...]
+    front = lax.rem(lax.broadcasted_iota(jnp.int32, (rows, LANES), 1), HD) < HD // 2
+
+    def unrotate(value):
+        swapped = jnp.where(
+            front, pltpu.roll(value, LANES - HD // 2, 1), pltpu.roll(value, HD // 2, 1)
+        )
+        return (value * cosine - swapped * sine).astype(BF16)
+
+    for at in range(0, q_width, LANES):
+        qkv_grad_ref[:, at : at + LANES] = unrotate(dq_ref[:, at : at + LANES])
+    kv_sum = dkv_ref[2 * rows :, :]
+    for back in range(2):
+        kv_sum = kv_sum + kv_land[back].astype(F32)
+    for at in range(0, kv_width, LANES):
+        qkv_grad_ref[:, q_width + at : q_width + at + LANES] = unrotate(
+            kv_sum[:, at : at + LANES]
+        )
+    qkv_grad_ref[:, q_width + kv_width :] = kv_sum[:, kv_width:].astype(BF16)
+
+    first_copy = tp_copy(0, first_ref, core_land, core)
+    y_copy = tp_copy(1, chip_ref, y_land, across_y)
+    total_copy = tp_copy(2, total_ref, other_ref, core)
+
+    def back_project(start, store):
+        at = 0
+        for piece in qkv_refs:
+            size = piece.shape[0]
+            store(at, size, dot_back(qkv_grad_ref[pl.ds(start, half_rows), :], piece[...]))
+            at += size
+
+    def store_first(at, size, value):
+        first_ref[:, at : at + size] = value.astype(BF16)
+
+    def store_second(at, size, value):
+        second_ref[:, at : at + size] = value
+
+    back_project(theirs, store_first)
+    first_copy.start()
+    back_project(mine, store_second)
+    pump(6, 8)
+    first_copy.wait_recv()
+    chip_ref[...] = (second_ref[...] + core_land[...].astype(F32)).astype(BF16)
+    y_copy.start()
+    send_next(5, 6)
+    pump(8, 10)
+
 
     y_copy.wait_recv()
     total_ref[...] = (chip_ref[...].astype(F32) + y_land[...].astype(F32)).astype(BF16)
     total_copy.start()
+    feed_copy.start()
     gain = gain_ref[...]
     near_at = pl.multiple_of((1 - shard) * half + lax.rem(ctx, 2) * part, part)
     far_at = pl.multiple_of((1 - shard) * half + (1 - lax.rem(ctx, 2)) * part, part)
     own_at = pl.multiple_of(shard * half, half)
-    step_rows = 64
 
     def norm_rows(source, base):
         def body(step, total):
@@ -887,16 +939,14 @@
         return lax.fori_loop(0, half_rows // step_rows, body, jnp.zeros((1, width), F32))
 
     gain_sum = norm_rows(total_ref, mine)
-    pump(7, 8)
-    send_next(5, 6)
+    pump(10, 11)
+    send_next(6, 7)
     total_copy.wait_recv()
-    gain_out_ref[...] = gain_sum + norm_rows(other_ref, theirs)
-    pump(8, 10)
-    send_next(6, 7)
+    gain_out_ref[0:1, :] = gain_sum + norm_rows(other_ref, theirs)
+    pump(11, 12)
     for copy in up_copies:
         copy.wait_recv()
     put(starts[2], feed_pieces(up_refs, up_land))
-    pump(10, 12)
     send_next(7, 8)
     pump(12, 14)
     send_next(8, len(queue))
@@ -942,7 +992,10 @@
     )
     pump(17, count // split + lag)
 
+    feed_copy.wait_recv()
     for copy in queue[-2:] + [first_copy, y_copy, total_copy]:
+        copy.wait_send()
+    for copy in (middle_y_copy, middle_core_copy, feed_copy):
         copy.wait_send()
     for back in (1, 2):
 
@@ -987,12 +1040,13 @@
     cuts, feed_part = len(v["grad_gate"]), v["grad_gate"][0].shape[1]
 
     stored = [
-        v["grad_gate"], v["grad_up"], v["hidden_m"], v["hidden_a"], v["branch"], v["mixed"],
+        v["grad_gate"], v["grad_up"], v["hidden_m"], v["hidden_a"], v["mixed"],
         v["out_pieces"], v["query"], v["keys_values"], v["log_sums"], v["query_segments"],
         v["key_segments"], v["cosine"], v["sine"], v["qkv_pieces"], v["inputs"], v["scale"],
-        v["gain"], v["grad_middle"],
+        v["gain"], v["normed_m"], v["middle_chip"], v["cotangent"], v["middle_scale"],
+        v["middle_gain"],
     ]
-    operands = [pool, v["hidden_m_send"], v["hidden_a_send"], v["branch_send"], stored]
+    operands = [pool, v["hidden_m_send"], v["hidden_a_send"], v["feed_chip"], stored]
     loaded = jax.tree.map(lambda value: pltpu.VMEM(value.shape, value.dtype), stored)
     any_space, vmem_space = pl.BlockSpec(memory_space=pl.ANY), pl.BlockSpec(memory_space=pltpu.VMEM)
     line = jax.ShapeDtypeStruct((count,) + piece, BF16)
@@ -1009,8 +1063,10 @@
         low(rows // 2, width), wide(rows // 2, width), low(rows // 2, width),
         low(rows // 2, width), low(rows // 2, width), low(rows // 2, width),
         low(rows // 2, width),
+        low(rows // 2, width), low(rows // 2, width), low(rows // 2, width),
+        low(rows, width), low(rows, half),
         low(*step), low(*step), low(4, *step), low(*step), low(2, *step), low(2, *piece),
-        dma((2 * cuts + 5,)), dma((2 * cuts + 5,)), dma((3,)), dma((3,)), dma((2,)), dma((2,)),
+        dma((2 * cuts + 5,)), dma((2 * cuts + 5,)), dma((6,)), dma((6,)), dma((2,)), dma((2,)),
         dma((steps,)), dma((steps,)), dma((steps,)), dma((steps,)), dma((steps,)),
         dma((3,)), dma((2,)),
         loaded, dma((len(jax.tree.leaves(stored)),)),
@@ -1018,23 +1074,24 @@
     outs = flat_call(
         functools.partial(tail_body, plan),
         operands,
-        out_specs=[any_space, any_space, any_space, any_space, vmem_space, vmem_space],
+        out_specs=[any_space] * 5 + [vmem_space, vmem_space],
         out_shape=[
             line, line, line, line,
+            jax.ShapeDtypeStruct((rows // 2, width), BF16),
             jax.ShapeDtypeStruct((rows, width), BF16),
-            jax.ShapeDtypeStruct((1, width), F32),
+            jax.ShapeDtypeStruct((2, width), F32),
         ],
         scratch_shapes=scratch,
         input_output_aliases={0: 0},
         compiler_params=pltpu.CompilerParams(
-            collective_id=0, has_side_effects=True, vmem_limit_bytes=60 << 20
+            collective_id=0, has_side_effects=True, vmem_limit_bytes=62 << 20
         ),
         cost_estimate=pl.CostEstimate(
             flops=400 << 30, bytes_accessed=30 << 20, transcendentals=0
         ),
         name="tail",
     )
-    return outs[1], outs[4], outs[5]
+    return outs[1], outs[4], outs[5], outs[6]
 
 
 def swap(value, axis, size, bit):
@@ -1333,12 +1390,11 @@
         True,
     )
     first, second, act_other[1], *act_cuts = tie(first, second, act_other[1], *act_cuts)
-    if tp_count == 4:
-        chip = chip_sum(first, second)
-        total = (chip.astype(F32) + swap(chip, "tp", tp_count, 2).astype(F32)).astype(BF16)
-        grad_hidden_m = join_cores(total).astype(F32)
+    fused = (shard_count, ctx_count, tp_count) == (2, 4, 4)
+    fused = fused and seqs == 1 and (blocks_back, base, span) == (2, 0, 4 * LANES)
+    if fused:
+        middle_chip = chip_sum(first, second)
     else:
-        total = None
         grad_hidden_m = tp_sum(first, second)
     fsdp_lane.done = list(act_other)
     pool = None
@@ -1353,10 +1409,6 @@
             [grad_other],
         )
 
-    feed_gain_part = jnp.sum(grad_hidden_m * normed_m, axis=0)
-    grad_middle = norm_back(grad_hidden_m, gain_m, normed_m, scale_m, grad_rows.astype(F32))
-    grad_branch = grad_middle.astype(BF16)
-
     first, second = project(
         sibling,
         [(value,) for value in act_cuts],
@@ -1364,19 +1416,15 @@
         width,
         False,
     )
-    if tp_count == 4:
-        chip = chip_sum(first, second)
-        across = swap(chip, "tp", tp_count, 2)
+    if fused:
+        feed_chip = chip_sum(first, second)
     else:
-        chip = across = None
         branch_m = tp_sum(first, second)
 
-    fused = (shard_count, ctx_count, tp_count) == (2, 4, 4)
-    fused = fused and seqs == 1 and (blocks_back, base) == (2, 0)
     if fused:
         tile = min(LANES, rows)
         log_rows = jnp.swapaxes(log_sums[0, :, : q_width // HD].reshape(rows // tile, tile, -1), 1, 2)
-        pool, input_grad, gain_row = tail(
+        pool, across, input_grad, gain_rows = tail(
             (
                 q_width // HD,
                 group,
@@ -1392,8 +1440,6 @@
                 "hidden_m_send": other_half(hidden_m),
                 "hidden_a": hidden_a[:, :half],
                 "hidden_a_send": other_half(hidden_a),
-                "branch": grad_branch,
-                "branch_send": other_half(grad_branch),
                 "mixed": mixed_low,
                 "out_pieces": [out_weight, near_out, far_out],
                 "query": query_low[0],
@@ -1407,13 +1453,22 @@
                 "inputs": inputs.astype(BF16),
                 "scale": scale_a,
                 "gain": gain_a,
-                "grad_middle": grad_middle,
+                "normed_m": normed_m,
+                "middle_chip": middle_chip,
+                "cotangent": grad_rows,
+                "middle_scale": scale_m,
+                "middle_gain": gain_m,
+                "feed_chip": feed_chip,
             },
         )
-        attention_gain_part = gain_row[0]
+        attention_gain_part, feed_gain_part = gain_rows[0], gain_rows[1]
         input_grad = input_grad.reshape(seqs, span, width)
-        across, pool = tie(across, pool)
+        total = (feed_chip.astype(F32) + across.astype(F32)).astype(BF16)
+        branch_m = join_cores(total).astype(F32)
     else:
+        feed_gain_part = jnp.sum(grad_hidden_m * normed_m, axis=0)
+        grad_middle = norm_back(grad_hidden_m, gain_m, normed_m, scale_m, grad_rows.astype(F32))
+        grad_branch = grad_middle.astype(BF16)
         gate_at = [fsdp_lane.send(value) for value in grad_gate_cuts]
         up_at = [fsdp_lane.send(value) for value in grad_up_cuts]
         hidden_m_at = fsdp_lane.send(core_half(other_half(hidden_m)))
@@ -1496,9 +1551,6 @@
             )
         pool = lax.psum(pool.astype(F32), "ctx")
 
-    if tp_count == 4:
-        total = (chip.astype(F32) + across.astype(F32)).astype(BF16)
-        branch_m = join_cores(total).astype(F32)
     block_out = from_local((middle + branch_m).astype(BF16)).reshape(seqs, span, width)
 
     gain_parts = jnp.stack([attention_gain_part, feed_gain_part])

time: 782 us -> 736 us (0.941)
  other arithmetic: 48.6 us -> 32.1 us
  Pallas kernels: 497 us -> 481 us
  waiting for transfers between devices: 121 us -> 109 us
    pallas_call x1, Pallas kernels: 395 us -> 379 us  [flat_call(): return pl.pallas_call(unflatten, in_specs=in_specs, **call)(*flat)]
    reduce_sum x2 -> x0, other arithmetic: 11.7 us -> none  [the longest x1 8.3 us: shards(): feed_gain_part = jnp.sum(grad_hidden_m * normed_m, axis=0)]
    ppermute x31 -> x28, waiting for transfers between devices: 114 us -> 103 us  [swap(): return lax.ppermute(value, axis, [(i, i ^ bit) for i in range(size)])]
    unnamed x167 -> x135, local copies, waits for them, and re-layouts: 23.6 us -> 20.2 us
    ppermute x31 -> x28, starting transfers between devices: 27.4 us -> 27.8 us  [swap(): return lax.ppermute(value, axis, [(i, i ^ bit) for i in range(size)])]
  transfers between devices with their start and end apart: 33 -> 30, of which waited for: 19 -> 15; matrix products, arithmetic and copies ran while one was open for 9% -> 8% of each run, Pallas kernels for 64% -> 14%
where the time goes in v4:
time: 736 us; the launch traced here: 725 us
  Pallas kernels  481 us (65%)
  waiting for transfers between devices  109 us (15%)
  local copies, waits for them, and re-layouts  50.6 us (7%)
  starting transfers between devices  35.8 us (5%)
  other arithmetic  32.1 us (4%)
  blocking collectives  8.52 us (1%)
    pallas_call x1, Pallas kernels, flat_call(): return pl.pallas_call(unflatten, in_specs=in_specs, **call)(*flat)  379 us
    ppermute x28, waiting for transfers between devices, swap(): return lax.ppermute(value, axis, [(i, i ^ bit) for i in range(size)])  103 us
    ppermute x28, starting transfers between devices, swap(): return lax.ppermute(value, axis, [(i, i ^ bit) for i in range(size)])  27.8 us
    pallas_call x1, Pallas kernels, widen(): pl.pallas_call(functools.partial(widen_body, starts), grid=(pool.shape[0]...  27.3 us
    pallas_call x2, Pallas kernels, project(): pl.pallas_call(functools.partial(project_body, cuts, steps, terms, pieces...  25 us
    unnamed x135, local copies, waits for them, and re-layouts  20.2 us
    pallas_call x1, Pallas kernels, attend_forward(): pl.pallas_call(functools.partial(attend_forward_body, lead, heads, group)...  17.1 us
  transfers between devices with their start and end apart: 30, of which 15 were waited for; matrix products, arithmetic and copies ran while one was open for 8% of the time, Pallas kernels for 14%

profile of v4, /device:TPU:0, one launch (start us, length us, event | category | flops | bytes accessed | tf_op | source)
XLA Modules:
  0.0 724.7 jit_solution(12076720425818557974)
XLA Ops:
  2.1 3.0 collective-permute-start
  12.0 2.4 dynamic-slice_bitcast_fusion.5
  14.9 2.4 copy-done.37
  21.5 1.8 fusion.23
  25.2 2.0 collective-permute-start.3
  27.3 1.6 collective-permute-start.2
  31.3 7.5 %collective-permute-done.3.refs_12_ = bf16[512,512]{1,0:T(8,128)(2,1)S(1)} collective-permute-done((bf16[512,512]{1,0:T(8,128)(2,1)}, bf16[512,512]{1,0:T(8,128)(2,1)S(1)}, u32[]{:S(2)}, u32[]{:S(2)}) %collective-permute-start.3) | collective-permute-done | bytes 524320 | tf_op jit(solution)/shard_map/ppermute | solution.py:1098
  38.8 1.7 collective-permute-start.8
  40.8 1.7 fusion.9
  42.6 3.4 collective-permute-done.2.refs_23_
  48.6 3.5 collective-permute-start.5
  52.1 4.5 collective-permute-start.4
  58.1 5.3 collective-permute-done.4
  64.3 17.1 %attend_forward.1 = (bf16[1,512,512]{2,1,0:T(8,128)(2,1)S(1)}, f32[1,512,128]{2,1,0:T(8,128)S(1)}) custom-call(bf16[1,512,512]{2,1,0:T(8,128)(2,1)S(1)} %multiply_bitcast_fusion.q_ref, bf16[1,1536,256]{2,1,0:T(8,128)(2,1)S(1)} %get-tuple-element.178.kv_ref, s32[1,512,1]{2,1,0:T(8,128)S(1)} %copy.31.qseg_ref, s32[1,4,1,1152]{3,2,1,0:T(1,128)S(1)} %add_bitcast_fusion.kseg_ref), custom_call_target="tpu_custom_call" | custom-call | flops 21139292160 | bytes 4194304 | tf_op jit(solution)/shard_map/attend_forward/pallas_call | solution.py:189
  81.5 3.5 collective-permute-done.7.refs_1_.refs_5_
  96.3 20.7 %collective-permute-done.10 = bf16[256,2048]{1,0:T(8,128)(2,1)S(1)} collective-permute-done((bf16[256,2048]{1,0:T(8,128)(2,1)S(1)}, bf16[256,2048]{1,0:T(8,128)(2,1)S(1)}, u32[]{:S(2)}, u32[]{:S(2)}) %collective-permute-start.10) | collective-permute-done | bytes 1048608 | tf_op jit(solution)/shard_map/ppermute | solution.py:1098
  119.4 4.4 fusion.49
  125.7 1.7 collective-permute-start.15
  127.7 2.8 multiply_reduce_fusion
  130.5 4.2 multiply_convert_fusion
  134.7 15.5 %collective-permute-done.14.refs_4_.refs_14_ = bf16[512,1024]{1,0:T(8,128)(2,1)} collective-permute-done((bf16[512,1024]{1,0:T(8,128)(2,1)S(1)}, bf16[512,1024]{1,0:T(8,128)(2,1)}, u32[]{:S(2)}, u32[]{:S(2)}) %collective-permute-start.14) | collective-permute-done | bytes 1048608 | tf_op jit(solution)/shard_map/ppermute | solution.py:1098
  150.2 1.7 collective-permute-done.15.refs_5_.refs_9_
  156.9 1.6 collective-permute-start.19
  158.5 6.8 feed_forward.2
  166.7 7.9 %collective-permute-done.17.refs_2_.refs_12_ = bf16[512,1024]{1,0:T(8,128)(2,1)} collective-permute-done((bf16[512,1024]{1,0:T(8,128)(2,1)}, bf16[512,1024]{1,0:T(8,128)(2,1)}, u32[]{:S(2)}, u32[]{:S(2)}) %collective-permute-start.17) | collective-permute-done | bytes 1048608 | tf_op jit(solution)/shard_map/ppermute | solution.py:1098
  174.5 1.9 collective-permute-done.16.refs_1_.refs_3_
  180.2 1.6 collective-permute-start.18
  181.8 15.1 %collective-permute-done.19.refs_5_.refs_15_ = bf16[512,1024]{1,0:T(8,128)(2,1)S(1)} collective-permute-done((bf16[512,1024]{1,0:T(8,128)(2,1)}, bf16[512,1024]{1,0:T(8,128)(2,1)S(1)}, u32[]{:S(2)}, u32[]{:S(2)}) %collective-permute-start.19) | collective-permute-done | bytes 1048608 | tf_op jit(solution)/shard_map/ppermute | solution.py:1098
  196.9 7.9 %feed_forward.3 = (f32[512,1024]{1,0:T(8,128)S(1)}, f32[512,1024]{1,0:T(8,128)S(1)}, bf16[512,1024]{1,0:T(8,128)(2,1)S(1)}) custom-call(bf16[512,2048]{1,0:T(8,128)(2,1)S(1)} %get-tuple-element.97.hidden_ref, bf16[1024,2048]{1,0:T(8,128)(2,1)} %refs_10_.1, bf16[512,1024]{1,0:T(8,128)(2,1)} %collective-permute-done.11.refs_1_.refs_11_, ...), custom_call_target="tpu_custom_call" | custom-call | flops 6442450944 | bytes 8388608 | tf_op jit(solution)/shard_map/feed_forward/pallas_call | solution.py:291
  208.4 1.7 collective-permute-start.21
  212.2 2.4 slice.159.refs_9_
  222.9 1.6 copy-done.16
  224.5 1.6 copy-done.18
  226.1 4.8 feed_backward.2
  230.9 9.9 %collective-permute-done.21.refs_2_.refs_7_ = bf16[1024,512]{1,0:T(8,128)(2,1)} collective-permute-done((bf16[1024,512]{1,0:T(8,128)(2,1)}, bf16[1024,512]{1,0:T(8,128)(2,1)}, u32[]{:S(2)}, u32[]{:S(2)}) %collective-permute-start.21) | collective-permute-done | bytes 1048608 | tf_op jit(solution)/shard_map/ppermute | solution.py:1098
  240.9 4.7 feed_backward.3
  245.6 10.5 %collective-permute-done.23 = bf16[256,1024]{1,0:T(8,128)(2,1)S(1)} collective-permute-done((bf16[256,1024]{1,0:T(8,128)(2,1)S(1)}, bf16[256,1024]{1,0:T(8,128)(2,1)S(1)}, u32[]{:S(2)}, u32[]{:S(2)}) %collective-permute-start.23) | collective-permute-done | bytes 524320 | tf_op jit(solution)/shard_map/ppermute | solution.py:1098
  256.1 15.4 %project.2 = (bf16[256,2048]{1,0:T(8,128)(2,1)S(1)}, f32[256,2048]{1,0:T(8,128)}) custom-call(s32[1]{0:T(128)} %bitcast.17.sibling_ref, bf16[512,1024]{1,0:T(8,128)(2,1)S(1)} %get-tuple-element.106.refs_0_.refs_4_, bf16[512,1024]{1,0:T(8,128)(2,1)S(1)} %get-tuple-element.107.refs_1_.refs_6_, bf16[512,1024]{1,0:T(8,128)(2,1)S(1)} %get-tuple-element.119.refs_2_.refs_5_, ...), custom_call_target="tpu_custom_call" | custom-call | flops 12884901888 | bytes 16777216 | tf_op jit(solution)/shard_map/project/pallas_call | solution.py:409
  271.6 3.8 collective-permute-done.24.left_other_ref
  275.9 9.5 %project.3 = (bf16[256,2048]{1,0:T(8,128)(2,1)S(1)}, f32[256,2048]{1,0:T(8,128)}) custom-call(s32[1]{0:T(128)} %bitcast.17.sibling_ref, bf16[512,1024]{1,0:T(8,128)(2,1)S(1)} %copy-done.4, bf16[512,1024]{1,0:T(8,128)(2,1)S(1)} %copy-done.6, bf16[2048,1024]{1,0:T(8,128)(2,1)} %refs_5_.1, bf16[1024,512]{1,0:T(8,128)(2,1)} %collective-permute-done.16.refs_1_.refs_3_, ...), custom_call_target="tpu_custom_call" | custom-call | flops 6442450944 | bytes 16777216 | tf_op jit(solution)/shard_map/project/pallas_call | solution.py:409
  285.9 4.1 outer_sum.2.refs_2_
  290.0 4.3 outer_sum.3.refs_0_
  297.6 378.6 %tail.1 = (bf16[29,256,1024]{2,1,0:T(8,128)(2,1)}, bf16[29,256,1024]{2,1,0:T(8,128)(2,1)}, bf16[29,256,1024]{2,1,0:T(8,128)(2,1)}, bf16[29,256,1024]{2,1,0:T(8,1...) custom-call(bf16[29,256,1024]{2,1,0:T(8,128)(2,1)} %outer_sum.3.refs, ...), custom_call_target="tpu_custom_call", output_to_operand_aliasing={{0}: (0, {})} | custom-call | flops 429496729600 | bytes 31457280 | tf_op jit(solution)/shard_map/tail/pallas_call | solution.py:1028
  676.2 2.6 add_convert_fusion.1
  679.5 27.3 %widen.1 = (f32[2048,1024]{1,0:T(8,128)}, f32[1024,2048]{1,0:T(8,128)}, f32[1024,2048]{1,0:T(8,128)}, f32[512,1024]{1,0:T(8,128)}, f32[1024,512]{1,0:T(8,128)}, ...) custom-call(bf16[29,256,1024]{2,1,0:T(8,128)(2,1)} %get-tuple-element.137.pool_ref), custom_call_target="tpu_custom_call" | custom-call | flops 1 | bytes 47185920 | tf_op jit(solution)/shard_map/widen/pallas_call | solution.py:516
  706.8 8.5 %psum.7 = f32[2,1024]{1,0:T(2,128)S(1)} all-reduce(f32[2,1024]{1,0:T(2,128)S(1)} %slice_add_fusion), channel_id=1, replica_groups=mesh['fsdp'=2,'ctx'=4,'tp'=4] {'ctx'}, use_global_device_ids=true, to_apply=%region_4.5 | all-reduce | flops 2048 | bytes 16384 | tf_op jit(solution)/shard_map/psum | solution.py:1558
  716.0 4.6 add_convert_fusion
  720.8 1.7 maximum_select_fusion.2
  (250 shorter events, 69.6 us)
Async XLA Ops:
  2.1 23.0 %collective-permute-start = (bf16[2,1024]{1,0:T(2,128)(2,1)S(1)}, bf16[2,1024]{1,0:T(2,128)(2,1)S(1)}, u32[]{:S(2)}, u32[]{:S(2)}) collective-permute-start(bf16[2,1024]{1,0:T(2,128)(2,1)S(1)} %pad_maximum_fusion.9), channel_id=1, source_target_pairs={{0,16},{16,0},{1,17},{17,1},{2,18},{18,2},{3,19},{19,3},{4,20},{20... | collective-permute-start | bytes 12296 | tf_op jit(solution)/shard_map/ppermute | solution.py:1098
  7.7 19.6 %collective-permute-start.1 = (bf16[512,768]{1,0:T(8,128)(2,1)}, bf16[512,768]{1,0:T(8,128)(2,1)}, u32[]{:S(2)}, u32[]{:S(2)}) collective-permute-start(bf16[512,768]{1,0:T(8,128)(2,1)} %constant_dynamic-slice_fusion.22), channel_id=1, source_target_pairs={{0,16},{16,0},{1,17},{17,1},{2,18},{18,2},{3,19},{19,3},{4,20},{20... | collective-permute-start | bytes 2359304 | tf_op jit(solution)/shard_map/ppermute | solution.py:1098
  14.8 14.1 %copy-start.27 = (bf16[512,2048]{1,0:T(8,128)(2,1)}, bf16[512,2048]{1,0:T(8,128)(2,1)S(1)}, u32[]{:S(2)}) copy-start(bf16[512,2048]{1,0:T(8,128)(2,1)S(1)} %get-tuple-element.150.refs_24_) | copy-start | bytes 6291460
  25.2 13.7 %collective-permute-start.3 = (bf16[512,512]{1,0:T(8,128)(2,1)}, bf16[512,512]{1,0:T(8,128)(2,1)S(1)}, u32[]{:S(2)}, u32[]{:S(2)}) collective-permute-start(bf16[512,512]{1,0:T(8,128)(2,1)} %constant_dynamic-slice_fusion.25), channel_id=1, source_target_pairs={{0,16},{16,0},{1,17},{17,1},{2,18},{18,2},{3,19},{19,3},{4,20},{20... | collective-permute-start | bytes 1572872 | tf_op jit(solution)/shard_map/ppermute | solution.py:1098
  27.2 103.3 %copy-start.64 = (f32[1,2048]{1,0:T(1,128)}, f32[1,2048]{1,0:T(1,128)S(1)}, u32[]{:S(2)}) copy-start(f32[1,2048]{1,0:T(1,128)S(1)} %get-tuple-element.183.refs_31_) | copy-start | bytes 24580
  27.3 18.7 %collective-permute-start.2 = (bf16[512,768]{1,0:T(8,128)(2,1)}, bf16[512,768]{1,0:T(8,128)(2,1)S(1)}, u32[]{:S(2)}, u32[]{:S(2)}) collective-permute-start(bf16[512,768]{1,0:T(8,128)(2,1)} %collective-permute-done.1.refs_22_), channel_id=1, source_target_pairs={{0,4},{4,0},{8,12},{12,8},{1,5},{5,1},{9,13},{13,9},{2,6},{6,2},{1... | collective-permute-start | bytes 2359304 | tf_op jit(solution)/shard_map/ppermute | solution.py:1098
  30.3 15.7 %copy-start.30 = (bf16[512,2048]{1,0:T(8,128)(2,1)}, bf16[512,2048]{1,0:T(8,128)(2,1)S(1)}, u32[]{:S(2)}) copy-start(bf16[512,2048]{1,0:T(8,128)(2,1)S(1)} %fusion.2) | copy-start | bytes 6291460
  38.8 49.7 %copy-start.43 = (bf16[512,512]{1,0:T(8,128)(2,1)}, bf16[512,512]{1,0:T(8,128)(2,1)S(1)}, u32[]{:S(2)}) copy-start(bf16[512,512]{1,0:T(8,128)(2,1)S(1)} %collective-permute-done.3.refs_12_) | copy-start | bytes 1572868
  38.8 42.6 %collective-permute-start.8 = (bf16[512,1024]{1,0:T(8,128)(2,1)S(1)}, bf16[512,1024]{1,0:T(8,128)(2,1)}, u32[]{:S(2)}, u32[]{:S(2)}) collective-permute-start(bf16[512,1024]{1,0:T(8,128)(2,1)S(1)} %copy-done.55), channel_id=1, source_target_pairs={{0,16},{16,0},{1,17},{17,1},{2,18},{18,2},{3,19},{19,3},{4,20},{20... | collective-permute-start | bytes 3145736 | tf_op jit(solution)/shard_map/ppermute | solution.py:1098
  40.5 44.5 %collective-permute-start.7 = (bf16[512,1024]{1,0:T(8,128)(2,1)S(1)}, bf16[512,1024]{1,0:T(8,128)(2,1)S(1)}, u32[]{:S(2)}, u32[]{:S(2)}) collective-permute-start(bf16[512,1024]{1,0:T(8,128)(2,1)S(1)} %copy-done.54), channel_id=1, source_target_pairs={{0,16},{16,0},{1,17},{17,1},{2,18},{18,2},{3,19},{19,3},{4,20},{20... | collective-permute-start | bytes 3145736 | tf_op jit(solution)/shard_map/ppermute | solution.py:1098
  48.6 9.5 %collective-permute-start.5 = (bf16[1,512,256]{2,1,0:T(8,128)(2,1)S(1)}, bf16[1,512,256]{2,1,0:T(8,128)(2,1)S(1)}, u32[]{:S(2)}, u32[]{:S(2)}) collective-permute-start(bf16[1,512,256]{2,1,0:T(8,128)(2,1)S(1)} %maximum_bitcast_fusion), channel_id=1, source_target_pairs={{0,4},{4,8},{8,12},{1,5},{5,9},{9,13},{2,6},{6,10},{10,14},{3,7},{... | collective-permute-start | bytes 786440 | tf_op jit(solution)/shard_map/ppermute | solution.py:1104
  52.1 11.3 %collective-permute-start.4 = (bf16[1,512,256]{2,1,0:T(8,128)(2,1)S(1)}, bf16[1,512,256]{2,1,0:T(8,128)(2,1)S(1)}, u32[]{:S(2)}, u32[]{:S(2)}) collective-permute-start(bf16[1,512,256]{2,1,0:T(8,128)(2,1)S(1)} %maximum_bitcast_fusion), channel_id=1, source_target_pairs={{0,8},{4,12},{1,9},{5,13},{2,10},{6,14},{3,11},{7,15},{16,24},{20,... | collective-permute-start | bytes 786440 | tf_op jit(solution)/shard_map/ppermute | solution.py:1104
  57.0 28.0 %collective-permute-start.6 = (bf16[512,512]{1,0:T(8,128)(2,1)S(1)}, bf16[512,512]{1,0:T(8,128)(2,1)S(1)}, u32[]{:S(2)}, u32[]{:S(2)}) collective-permute-start(bf16[512,512]{1,0:T(8,128)(2,1)S(1)} %collective-permute-done.3.refs_12_), channel_id=1, source_target_pairs={{0,4},{4,0},{8,12},{12,8},{1,5},{5,1},{9,13},{13,9},{2,6},{6,2},{1... | collective-permute-start | bytes 1572872 | tf_op jit(solution)/shard_map/ppermute | solution.py:1098
  58.0 23.4 %copy-start.7 = (bf16[1,512,512]{2,1,0:T(8,128)(2,1)}, bf16[1,512,512]{2,1,0:T(8,128)(2,1)S(1)}, u32[]{:S(2)}) copy-start(bf16[1,512,512]{2,1,0:T(8,128)(2,1)S(1)} %multiply_bitcast_fusion.q_ref) | copy-start | bytes 1572868
  64.3 21.0 %copy-start.35 = (bf16[512,1024]{1,0:T(8,128)(2,1)S(1)}, bf16[512,1024]{1,0:T(8,128)(2,1)}, u32[]{:S(2)}) copy-start(bf16[512,1024]{1,0:T(8,128)(2,1)} %refs_11_.1) | copy-start | bytes 3145732
  87.2 3.0 collective-permute-start.9
  91.8 25.3 %collective-permute-start.10 = (bf16[256,2048]{1,0:T(8,128)(2,1)S(1)}, bf16[256,2048]{1,0:T(8,128)(2,1)S(1)}, u32[]{:S(2)}, u32[]{:S(2)}) collective-permute-start(bf16[256,2048]{1,0:T(8,128)(2,1)S(1)} %fusion.4), channel_id=1, source_target_pairs={{0,2},{1,3},{2,0},{3,1},{4,6},{5,7},{6,4},{7,5},{8,10},{9,11},{10,... | collective-permute-start | bytes 3145736 | tf_op jit(solution)/shard_map/ppermute | solution.py:1098
  93.3 25.1 %collective-permute-start.11 = (bf16[512,1024]{1,0:T(8,128)(2,1)S(1)}, bf16[512,1024]{1,0:T(8,128)(2,1)}, u32[]{:S(2)}, u32[]{:S(2)}) collective-permute-start(bf16[512,1024]{1,0:T(8,128)(2,1)S(1)} %copy-done.51), channel_id=1, source_target_pairs={{0,16},{16,0},{1,17},{17,1},{2,18},{18,2},{3,19},{19,3},{4,20},{20... | collective-permute-start | bytes 3145736 | tf_op jit(solution)/shard_map/ppermute | solution.py:1098
  94.7 24.6 %collective-permute-start.12 = (bf16[512,1024]{1,0:T(8,128)(2,1)S(1)}, bf16[512,1024]{1,0:T(8,128)(2,1)S(1)}, u32[]{:S(2)}, u32[]{:S(2)}) collective-permute-start(bf16[512,1024]{1,0:T(8,128)(2,1)S(1)} %collective-permute-done.7.refs_1_.refs_5_), channel_id=1, source_target_pairs={{0,4},{4,0},{8,12},{12,8},{1,5},{5,1},{9,13},{13,9},{2,6},{6,2},{1... | collective-permute-start | bytes 3145736 | tf_op jit(solution)/shard_map/ppermute | solution.py:1098
  119.4 8.4 %collective-permute-start.13 = (bf16[256,2048]{1,0:T(8,128)(2,1)}, bf16[256,2048]{1,0:T(8,128)(2,1)S(1)}, u32[]{:S(2)}, u32[]{:S(2)}) collective-permute-start(bf16[256,2048]{1,0:T(8,128)(2,1)} %add_convert_fusion.4), channel_id=1, source_target_pairs={{0,1},{1,0},{2,3},{3,2},{4,5},{5,4},{6,7},{7,6},{8,9},{9,8},{10,11... | collective-permute-start | bytes 3145736 | tf_op jit(solution)/shard_map/ppermute | solution.py:1098
  124.9 25.4 %collective-permute-start.14 = (bf16[512,1024]{1,0:T(8,128)(2,1)S(1)}, bf16[512,1024]{1,0:T(8,128)(2,1)}, u32[]{:S(2)}, u32[]{:S(2)}) collective-permute-start(bf16[512,1024]{1,0:T(8,128)(2,1)S(1)} %copy-done.50), channel_id=1, source_target_pairs={{0,16},{16,0},{1,17},{17,1},{2,18},{18,2},{3,19},{19,3},{4,20},{20... | collective-permute-start | bytes 3145736 | tf_op jit(solution)/shard_map/ppermute | solution.py:1098
  125.7 26.2 %collective-permute-start.15 = (bf16[512,1024]{1,0:T(8,128)(2,1)}, bf16[512,1024]{1,0:T(8,128)(2,1)S(1)}, u32[]{:S(2)}, u32[]{:S(2)}) collective-permute-start(bf16[512,1024]{1,0:T(8,128)(2,1)} %collective-permute-done.8.refs_4_.refs_8_), channel_id=1, source_target_pairs={{0,4},{4,0},{8,12},{12,8},{1,5},{5,1},{9,13},{13,9},{2,6},{6,2},{1... | collective-permute-start | bytes 3145736 | tf_op jit(solution)/shard_map/ppermute | solution.py:1098
  127.5 47.1 %collective-permute-start.17 = (bf16[512,1024]{1,0:T(8,128)(2,1)}, bf16[512,1024]{1,0:T(8,128)(2,1)}, u32[]{:S(2)}, u32[]{:S(2)}) collective-permute-start(bf16[512,1024]{1,0:T(8,128)(2,1)} %collective-permute-done.11.refs_1_.refs_11_), channel_id=1, source_target_pairs={{0,4},{4,0},{8,12},{12,8},{1,5},{5,1},{9,13},{13,9},{2,6},{6,2},{1... | collective-permute-start | bytes 3145736 | tf_op jit(solution)/shard_map/ppermute | solution.py:1098
  152.9 23.5 %collective-permute-start.16 = (bf16[1024,512]{1,0:T(8,128)(2,1)}, bf16[1024,512]{1,0:T(8,128)(2,1)}, u32[]{:S(2)}, u32[]{:S(2)}) collective-permute-start(bf16[1024,512]{1,0:T(8,128)(2,1)} %constant_dynamic-slice_fusion.14), channel_id=1, source_target_pairs={{0,16},{16,0},{1,17},{17,1},{2,18},{18,2},{3,19},{19,3},{4,20},{20... | collective-permute-start | bytes 3145736 | tf_op jit(solution)/shard_map/ppermute | solution.py:1098
  156.9 20.8 %copy-start.48 = (bf16[512,512]{1,0:T(8,128)(2,1)S(1)}, bf16[512,512]{1,0:T(8,128)(2,1)}, u32[]{:S(2)}) copy-start(bf16[512,512]{1,0:T(8,128)(2,1)} %get-tuple-element.165) | copy-start | bytes 1572868
  156.9 20.8 %copy-start.49 = (bf16[512,512]{1,0:T(8,128)(2,1)S(1)}, bf16[512,512]{1,0:T(8,128)(2,1)}, u32[]{:S(2)}) copy-start(bf16[512,512]{1,0:T(8,128)(2,1)} %get-tuple-element.166) | copy-start | bytes 1572868
  156.9 40.0 %collective-permute-start.19 = (bf16[512,1024]{1,0:T(8,128)(2,1)}, bf16[512,1024]{1,0:T(8,128)(2,1)S(1)}, u32[]{:S(2)}, u32[]{:S(2)}) collective-permute-start(bf16[512,1024]{1,0:T(8,128)(2,1)} %collective-permute-done.14.refs_4_.refs_14_), channel_id=1, source_target_pairs={{0,4},{4,0},{8,12},{12,8},{1,5},{5,1},{9,13},{13,9},{2,6},{6,2},{1... | collective-permute-start | bytes 3145736 | tf_op jit(solution)/shard_map/ppermute | solution.py:1098
  176.5 32.0 %collective-permute-start.20 = (bf16[1024,512]{1,0:T(8,128)(2,1)S(1)}, bf16[1024,512]{1,0:T(8,128)(2,1)}, u32[]{:S(2)}, u32[]{:S(2)}) collective-permute-start(bf16[1024,512]{1,0:T(8,128)(2,1)S(1)} %constant_dynamic-slice_fusion.13), channel_id=1, source_target_pairs={{0,16},{16,0},{1,17},{17,1},{2,18},{18,2},{3,19},{19,3},{4,20},{20... | collective-permute-start | bytes 3145736 | tf_op jit(solution)/shard_map/ppermute | solution.py:1098
  180.2 42.7 %collective-permute-start.18 = (bf16[1024,512]{1,0:T(8,128)(2,1)}, bf16[1024,512]{1,0:T(8,128)(2,1)}, u32[]{:S(2)}, u32[]{:S(2)}) collective-permute-start(bf16[1024,512]{1,0:T(8,128)(2,1)} %collective-permute-done.16.refs_1_.refs_3_), channel_id=1, source_target_pairs={{0,4},{4,0},{8,12},{12,8},{1,5},{5,1},{9,13},{13,9},{2,6},{6,2},{1... | collective-permute-start | bytes 3145736 | tf_op jit(solution)/shard_map/ppermute | solution.py:1098
  208.4 32.5 %collective-permute-start.21 = (bf16[1024,512]{1,0:T(8,128)(2,1)}, bf16[1024,512]{1,0:T(8,128)(2,1)}, u32[]{:S(2)}, u32[]{:S(2)}) collective-permute-start(bf16[1024,512]{1,0:T(8,128)(2,1)} %collective-permute-done.20.refs_1_.refs_6_), channel_id=1, source_target_pairs={{0,4},{4,0},{8,12},{12,8},{1,5},{5,1},{9,13},{13,9},{2,6},{6,2},{1... | collective-permute-start | bytes 3145736 | tf_op jit(solution)/shard_map/ppermute | solution.py:1098
  218.6 37.5 %collective-permute-start.22 = (bf16[512,1024]{1,0:T(8,128)(2,1)}, bf16[512,1024]{1,0:T(8,128)(2,1)S(1)}, u32[]{:S(2)}, u32[]{:S(2)}) collective-permute-start(bf16[512,1024]{1,0:T(8,128)(2,1)} %copy-done.3), channel_id=1, source_target_pairs={{0,16},{16,0},{1,17},{17,1},{2,18},{18,2},{3,19},{19,3},{4,20},{20... | collective-permute-start | bytes 3145736 | tf_op jit(solution)/shard_map/ppermute | solution.py:1098
  220.8 35.3 %collective-permute-start.23 = (bf16[256,1024]{1,0:T(8,128)(2,1)S(1)}, bf16[256,1024]{1,0:T(8,128)(2,1)S(1)}, u32[]{:S(2)}, u32[]{:S(2)}) collective-permute-start(bf16[256,1024]{1,0:T(8,128)(2,1)S(1)} %copy-done.59), channel_id=1, source_target_pairs={{0,16},{16,0},{1,17},{17,1},{2,18},{18,2},{3,19},{19,3},{4,20},{20... | collective-permute-start | bytes 1572872 | tf_op jit(solution)/shard_map/ppermute | solution.py:1098
  221.9 53.5 %collective-permute-start.24 = (bf16[512,1024]{1,0:T(8,128)(2,1)S(1)}, bf16[512,1024]{1,0:T(8,128)(2,1)S(1)}, u32[]{:S(2)}, u32[]{:S(2)}) collective-permute-start(bf16[512,1024]{1,0:T(8,128)(2,1)S(1)} %copy-done.6), channel_id=1, source_target_pairs={{0,16},{16,0},{1,17},{17,1},{2,18},{18,2},{3,19},{19,3},{4,20},{20... | collective-permute-start | bytes 3145736 | tf_op jit(solution)/shard_map/ppermute | solution.py:1098
  226.1 14.8 %copy-start.20 = (f32[512,1024]{1,0:T(8,128)S(1)}, f32[512,1024]{1,0:T(8,128)}, u32[]{:S(2)}) copy-start(f32[512,1024]{1,0:T(8,128)} %copy-done.19) | copy-start | bytes 6291460
  226.1 14.8 %copy-start.22 = (f32[512,1024]{1,0:T(8,128)S(1)}, f32[512,1024]{1,0:T(8,128)}, u32[]{:S(2)}) copy-start(f32[512,1024]{1,0:T(8,128)} %copy-done.21) | copy-start | bytes 6291460
  230.9 25.2 %copy-start.23 = (bf16[512,1024]{1,0:T(8,128)(2,1)}, bf16[512,1024]{1,0:T(8,128)(2,1)S(1)}, u32[]{:S(2)}) copy-start(bf16[512,1024]{1,0:T(8,128)(2,1)S(1)} %get-tuple-element.106.refs_0_.refs_4_) | copy-start | bytes 3145732
  230.9 25.2 %copy-start.24 = (bf16[512,1024]{1,0:T(8,128)(2,1)}, bf16[512,1024]{1,0:T(8,128)(2,1)S(1)}, u32[]{:S(2)}) copy-start(bf16[512,1024]{1,0:T(8,128)(2,1)S(1)} %get-tuple-element.107.refs_1_.refs_6_) | copy-start | bytes 3145732
  245.6 26.0 %copy-start.25 = (bf16[512,1024]{1,0:T(8,128)(2,1)}, bf16[512,1024]{1,0:T(8,128)(2,1)S(1)}, u32[]{:S(2)}) copy-start(bf16[512,1024]{1,0:T(8,128)(2,1)S(1)} %get-tuple-element.119.refs_2_.refs_5_) | copy-start | bytes 3145732
  245.6 26.0 %copy-start.26 = (bf16[512,1024]{1,0:T(8,128)(2,1)}, bf16[512,1024]{1,0:T(8,128)(2,1)S(1)}, u32[]{:S(2)}) copy-start(bf16[512,1024]{1,0:T(8,128)(2,1)S(1)} %get-tuple-element.120.refs_3_.refs_7_) | copy-start | bytes 3145732
  256.1 19.7 %copy-start.4 = (bf16[512,1024]{1,0:T(8,128)(2,1)S(1)}, bf16[512,1024]{1,0:T(8,128)(2,1)}, u32[]{:S(2)}) copy-start(bf16[512,1024]{1,0:T(8,128)(2,1)} %copy-done.3) | copy-start | bytes 3145732
  275.4 10.1 %collective-permute-start.26 = (bf16[256,1024]{1,0:T(8,128)(2,1)S(1)}, bf16[256,1024]{1,0:T(8,128)(2,1)S(1)}, u32[]{:S(2)}, u32[]{:S(2)}) collective-permute-start(bf16[256,1024]{1,0:T(8,128)(2,1)S(1)} %collective-permute-done.23), channel_id=1, source_target_pairs={{0,1},{1,0},{2,3},{3,2},{4,5},{5,4},{6,7},{7,6},{8,9},{9,8},{10,11... | collective-permute-start | bytes 1572872 | tf_op jit(solution)/shard_map/ppermute | solution.py:1098
  275.4 19.0 %collective-permute-start.27 = (bf16[256,2048]{1,0:T(8,128)(2,1)S(1)}, bf16[256,2048]{1,0:T(8,128)(2,1)S(1)}, u32[]{:S(2)}, u32[]{:S(2)}) collective-permute-start(bf16[256,2048]{1,0:T(8,128)(2,1)S(1)} %get-tuple-element.133), channel_id=1, source_target_pairs={{0,1},{1,0},{2,3},{3,2},{4,5},{5,4},{6,7},{7,6},{8,9},{9,8},{10,11... | collective-permute-start | bytes 3145736 | tf_op jit(solution)/shard_map/ppermute | solution.py:1098
  285.4 10.2 %collective-permute-start.25 = (bf16[256,2048]{1,0:T(8,128)(2,1)S(1)}, bf16[256,2048]{1,0:T(8,128)(2,1)S(1)}, u32[]{:S(2)}, u32[]{:S(2)}) collective-permute-start(bf16[256,2048]{1,0:T(8,128)(2,1)S(1)} %get-tuple-element.127), channel_id=1, source_target_pairs={{0,1},{1,0},{2,3},{3,2},{4,5},{5,4},{6,7},{7,6},{8,9},{9,8},{10,11... | collective-permute-start | bytes 3145736 | tf_op jit(solution)/shard_map/ppermute | solution.py:1098
  297.6 378.6 %copy-start.39 = (bf16[256,2048]{1,0:T(8,128)(2,1)S(1)}, bf16[256,2048]{1,0:T(8,128)(2,1)}, u32[]{:S(2)}) copy-start(bf16[256,2048]{1,0:T(8,128)(2,1)} %add_convert_fusion.3.refs_3_) | copy-start | bytes 3145732
  678.8 37.2 %collective-permute-start.28 = (bf16[256,2048]{1,0:T(8,128)(2,1)}, bf16[256,2048]{1,0:T(8,128)(2,1)}, u32[]{:S(2)}, u32[]{:S(2)}) collective-permute-start(bf16[256,2048]{1,0:T(8,128)(2,1)} %add_convert_fusion.1), channel_id=1, source_target_pairs={{0,1},{1,0},{2,3},{3,2},{4,5},{5,4},{6,7},{7,6},{8,9},{9,8},{10,11... | collective-permute-start | bytes 3145736 | tf_op jit(solution)/shard_map/ppermute | solution.py:1098
  678.8 28.0 %collective-permute-start.29 = (f32[2,1024]{1,0:T(2,128)S(1)}, f32[2,1024]{1,0:T(2,128)S(1)}, u32[]{:S(2)}, u32[]{:S(2)}) collective-permute-start(f32[2,1024]{1,0:T(2,128)S(1)} %pad_maximum_fusion.8), channel_id=1, source_target_pairs={{0,16},{16,0},{1,17},{17,1},{2,18},{18,2},{3,19},{19,3},{4,20},{20... | collective-permute-start | bytes 24584 | tf_op jit(solution)/shard_map/ppermute | solution.py:1098
  679.5 36.5 %copy-start.29 = (bf16[512,2048]{1,0:T(8,128)(2,1)S(1)}, bf16[512,2048]{1,0:T(8,128)(2,1)}, u32[]{:S(2)}) copy-start(bf16[512,2048]{1,0:T(8,128)(2,1)} %copy-done.27) | copy-start | bytes 6291460
  679.5 36.5 %copy-start.33 = (bf16[256,2048]{1,0:T(8,128)(2,1)S(1)}, bf16[256,2048]{1,0:T(8,128)(2,1)}, u32[]{:S(2)}) copy-start(bf16[256,2048]{1,0:T(8,128)(2,1)} %copy-done.32) | copy-start | bytes 3145732
  (48 other events, 193.3 us)

commit v5 on v4

--- a/solution.py
+++ b/solution.py
@@ -534,6 +534,7 @@
         grad_mixed_ref, dq_ref, dkv_ref, kv_send, kv_land, qkv_grad_ref,
         first_ref, second_ref, core_land, chip_ref, y_land, total_ref, other_ref,
         middle_y, middle_total, middle_other, branch_ref, branch_send,
+        gains_ref, gain_send, gain_land, gain_mine, gain_all, gain_send_sem, gain_recv_sem,
         own_buf, near_buf, part_buf, across_buf, total_buf, piece_buf,
         x_send, x_recv, tp_send, tp_recv, kv_send_sem, kv_recv_sem,
         send_sem, land_sem, cross_send, cross_land, keep_sem, load_sem, piece_sem,
@@ -562,6 +563,7 @@
 
     kv_land[...] = jnp.zeros_like(kv_land)
     dkv_ref[...] = jnp.zeros_like(dkv_ref)
+    gains_ref[...] = jnp.zeros_like(gains_ref)
 
     barrier = pltpu.get_barrier_semaphore()
     others = [{"fsdp": partner}, {"tp": core}, {"tp": across_y}]
@@ -758,7 +760,7 @@
     feed_gain = middle_rows(middle_total, mine)
     pump_steps(3, 4)
     middle_core_copy.wait_recv()
-    gain_out_ref[1:2, :] = feed_gain + middle_rows(middle_other, theirs)
+    gains_ref[1:2, :] = feed_gain + middle_rows(middle_other, theirs)
     send_next(2, 3)
 
     grad_mixed = None
@@ -942,12 +944,29 @@
     pump(10, 11)
     send_next(6, 7)
     total_copy.wait_recv()
-    gain_out_ref[0:1, :] = gain_sum + norm_rows(other_ref, theirs)
+    gains_ref[0:1, :] = gain_sum + norm_rows(other_ref, theirs)
+    gain_send[:, pl.ds(near_send, part)] = gains_ref[:, half : half + part]
+    gain_send[:, pl.ds(far_send, part)] = gains_ref[:, half + part :]
+    gain_copy = x_copy(2 * cuts + 5, gain_send, gain_land)
+    gain_copy.start()
     pump(11, 12)
     for copy in up_copies:
         copy.wait_recv()
     put(starts[2], feed_pieces(up_refs, up_land))
     send_next(7, 8)
+    gain_copy.wait_recv()
+    gain_mine[...] = gains_ref[:, :half] + gain_land[...]
+    gain_all[ctx] = gain_mine[...]
+
+    def gain_to(by, slot):
+        return pltpu.make_async_remote_copy(
+            src_ref=gain_mine, dst_ref=gain_all.at[slot], send_sem=gain_send_sem.at[by - 1],
+            recv_sem=gain_recv_sem.at[by - 1], device_id={"ctx": lax.rem(ctx + by, 4)},
+            device_id_type=mesh_id,
+        )
+
+    for by in (1, 2, 3):
+        gain_to(by, ctx).start()
     pump(12, 14)
     send_next(8, len(queue))
     branch_copy.wait_recv()
@@ -992,6 +1011,12 @@
     )
     pump(17, count // split + lag)
 
+    for by in (1, 2, 3):
+        gain_to(by, lax.rem(ctx + 4 - by, 4)).wait_recv()
+    gain_out_ref[...] = (gain_all[0] + gain_all[1]) + (gain_all[2] + gain_all[3])
+    for by in (1, 2, 3):
+        gain_to(by, ctx).wait_send()
+    gain_copy.wait_send()
     feed_copy.wait_recv()
     for copy in queue[-2:] + [first_copy, y_copy, total_copy]:
         copy.wait_send()
@@ -1065,8 +1090,10 @@
         low(rows // 2, width),
         low(rows // 2, width), low(rows // 2, width), low(rows // 2, width),
         low(rows, width), low(rows, half),
+        wide(8, width), wide(8, half), wide(8, half), wide(8, half), wide(4, 8, half),
+        dma((3,)), dma((3,)),
         low(*step), low(*step), low(4, *step), low(*step), low(2, *step), low(2, *piece),
-        dma((2 * cuts + 5,)), dma((2 * cuts + 5,)), dma((6,)), dma((6,)), dma((2,)), dma((2,)),
+        dma((2 * cuts + 6,)), dma((2 * cuts + 6,)), dma((6,)), dma((6,)), dma((2,)), dma((2,)),
         dma((steps,)), dma((steps,)), dma((steps,)), dma((steps,)), dma((steps,)),
         dma((3,)), dma((2,)),
         loaded, dma((len(jax.tree.leaves(stored)),)),
@@ -1079,7 +1106,7 @@
             line, line, line, line,
             jax.ShapeDtypeStruct((rows // 2, width), BF16),
             jax.ShapeDtypeStruct((rows, width), BF16),
-            jax.ShapeDtypeStruct((2, width), F32),
+            jax.ShapeDtypeStruct((8, half), F32),
         ],
         scratch_shapes=scratch,
         input_output_aliases={0: 0},
@@ -1372,10 +1399,7 @@
         grad_gate_cuts.append(grad_gate)
         grad_up_cuts.append(grad_up)
 
-    grad_gate_cuts[1], act_other[0], other_grad = tie(
-        grad_gate_cuts[1], act_other[0], other_grad
-    )
-    grad_own, grad_other = grad_rows[:, :half], join_cores(other_grad)
+    grad_gate_cuts[1], act_other[0] = tie(grad_gate_cuts[1], act_other[0])
     first, second = project(
         sibling,
         list(zip(grad_gate_cuts, grad_up_cuts)),
@@ -1389,7 +1413,8 @@
         width,
         True,
     )
-    first, second, act_other[1], *act_cuts = tie(first, second, act_other[1], *act_cuts)
+    first, second, other_grad, *act_cuts = tie(first, second, other_grad, *act_cuts)
+    grad_own, grad_other = grad_rows[:, :half], join_cores(other_grad)
     fused = (shard_count, ctx_count, tp_count) == (2, 4, 4)
     fused = fused and seqs == 1 and (blocks_back, base, span) == (2, 0, 4 * LANES)
     if fused:
@@ -1424,7 +1449,7 @@
     if fused:
         tile = min(LANES, rows)
         log_rows = jnp.swapaxes(log_sums[0, :, : q_width // HD].reshape(rows // tile, tile, -1), 1, 2)
-        pool, across, input_grad, gain_rows = tail(
+        pool, across, input_grad, gain_sums = tail(
             (
                 q_width // HD,
                 group,
@@ -1461,7 +1486,6 @@
                 "feed_chip": feed_chip,
             },
         )
-        attention_gain_part, feed_gain_part = gain_rows[0], gain_rows[1]
         input_grad = input_grad.reshape(seqs, span, width)
         total = (feed_chip.astype(F32) + across.astype(F32)).astype(BF16)
         branch_m = join_cores(total).astype(F32)
@@ -1549,13 +1573,12 @@
                 [grad_qkv[:, cut]],
                 [qkv_other[:, cut]],
             )
+        gain_parts = jnp.stack([attention_gain_part, feed_gain_part])
+        gain_other = over_fsdp(other_half(gain_parts))
+        gain_sums = lax.psum(gain_parts[:, :half] + gain_other, "ctx")
         pool = lax.psum(pool.astype(F32), "ctx")
 
     block_out = from_local((middle + branch_m).astype(BF16)).reshape(seqs, span, width)
-
-    gain_parts = jnp.stack([attention_gain_part, feed_gain_part])
-    gain_other = over_fsdp(other_half(gain_parts))
-    gain_sums = lax.psum(gain_parts[:, :half] + gain_other, "ctx")
 
     down_grad, gate_grad, up_grad, out_grad, query_grad, key_grad, value_grad = widen(
         pool,

time: 736 us -> 714 us (0.970)
  waiting for transfers between devices: 109 us -> 94.5 us
  blocking collectives: 8.52 us -> 0 us
    ppermute x28 -> x27, waiting for transfers between devices: 103 us -> 89.2 us  [swap(): return lax.ppermute(value, axis, [(i, i ^ bit) for i in range(size)])]
    psum x1 -> x0, blocking collectives: 8.52 us -> none  [shards(): gain_sums = lax.psum(gain_parts[:, :half] + gain_other, 'ctx')]
    ppermute x28 -> x27, starting transfers between devices: 27.8 us -> 27.2 us  [swap(): return lax.ppermute(value, axis, [(i, i ^ bit) for i in range(size)])]
    unnamed x135 -> x131, local copies, waits for them, and re-layouts: 20.2 us -> 20.3 us
  transfers between devices with their start and end apart: 30 -> 29, of which waited for: 15 -> 13; matrix products, arithmetic and copies ran while one was open for 8% -> 8% of each run, Pallas kernels for 14% -> 15%
where the time goes in v5:
time: 714 us; the launch traced here: 703 us
  Pallas kernels  483 us (68%)
  waiting for transfers between devices  94.5 us (13%)
  local copies, waits for them, and re-layouts  51.5 us (7%)
  starting transfers between devices  35.2 us (5%)
  other arithmetic  30.3 us (4%)
    pallas_call x1, Pallas kernels, flat_call(): return pl.pallas_call(unflatten, in_specs=in_specs, **call)(*flat)  380 us
    ppermute x27, waiting for transfers between devices, swap(): return lax.ppermute(value, axis, [(i, i ^ bit) for i in range(size)])  89.2 us
    pallas_call x1, Pallas kernels, widen(): pl.pallas_call(functools.partial(widen_body, starts), grid=(pool.shape[0]...  27.3 us
    ppermute x27, starting transfers between devices, swap(): return lax.ppermute(value, axis, [(i, i ^ bit) for i in range(size)])  27.2 us
    pallas_call x2, Pallas kernels, project(): pl.pallas_call(functools.partial(project_body, cuts, steps, terms, pieces...  25.7 us
    unnamed x131, local copies, waits for them, and re-layouts  20.3 us
    pallas_call x1, Pallas kernels, attend_forward(): pl.pallas_call(functools.partial(attend_forward_body, lead, heads, group)...  17.1 us
    pallas_call x2, Pallas kernels, feed_forward(): pl.pallas_call(functools.partial(feed_forward_body, tuple((w.shape[0] for...  14.7 us
  transfers between devices with their start and end apart: 29, of which 13 were waited for; matrix products, arithmetic and copies ran while one was open for 8% of the time, Pallas kernels for 15%

profile of v5, /device:TPU:0, one launch (start us, length us, event | category | flops | bytes accessed | tf_op | source)
XLA Modules:
  0.0 702.8 jit_solution(3376294001809335479)
XLA Ops:
  2.1 3.0 collective-permute-start
  12.0 2.4 dynamic-slice_bitcast_fusion.5
  14.9 2.4 copy-done.37
  21.5 1.8 fusion.23
  25.1 2.0 collective-permute-start.3
  27.3 1.6 collective-permute-start.2
  31.3 7.5 %collective-permute-done.3.refs_12_ = bf16[512,512]{1,0:T(8,128)(2,1)S(1)} collective-permute-done((bf16[512,512]{1,0:T(8,128)(2,1)}, bf16[512,512]{1,0:T(8,128)(2,1)S(1)}, u32[]{:S(2)}, u32[]{:S(2)}) %collective-permute-start.3) | collective-permute-done | bytes 524320 | tf_op jit(solution)/shard_map/ppermute | solution.py:1125
  38.8 1.7 collective-permute-start.8
  40.8 1.7 fusion.9
  42.5 3.4 collective-permute-done.2.refs_23_
  48.6 3.5 collective-permute-start.5
  52.1 4.5 collective-permute-start.4
  58.1 5.3 collective-permute-done.4
  64.4 17.1 %attend_forward.1 = (bf16[1,512,512]{2,1,0:T(8,128)(2,1)S(1)}, f32[1,512,128]{2,1,0:T(8,128)S(1)}) custom-call(bf16[1,512,512]{2,1,0:T(8,128)(2,1)S(1)} %multiply_bitcast_fusion.q_ref, bf16[1,1536,256]{2,1,0:T(8,128)(2,1)S(1)} %get-tuple-element.176.kv_ref, s32[1,512,1]{2,1,0:T(8,128)S(1)} %copy.31.qseg_ref, s32[1,4,1,1152]{3,2,1,0:T(1,128)S(1)} %add_bitcast_fusion.kseg_ref), custom_call_target="tpu_custom_call" | custom-call | flops 21139292160 | bytes 4194304 | tf_op jit(solution)/shard_map/attend_forward/pallas_call | solution.py:189
  81.5 3.5 collective-permute-done.7.refs_1_.refs_5_
  90.2 1.6 fusion.4
  91.7 1.5 collective-permute-start.10
  94.7 1.6 collective-permute-start.12
  96.3 20.7 %collective-permute-done.10 = bf16[256,2048]{1,0:T(8,128)(2,1)S(1)} collective-permute-done((bf16[256,2048]{1,0:T(8,128)(2,1)S(1)}, bf16[256,2048]{1,0:T(8,128)(2,1)S(1)}, u32[]{:S(2)}, u32[]{:S(2)}) %collective-permute-start.10) | collective-permute-done | bytes 1048608 | tf_op jit(solution)/shard_map/ppermute | solution.py:1125
  119.4 4.4 fusion.49
  125.7 1.7 collective-permute-start.15
  127.8 2.8 multiply_reduce_fusion
  130.6 4.1 multiply_convert_fusion
  134.7 15.5 %collective-permute-done.14.refs_4_.refs_14_ = bf16[512,1024]{1,0:T(8,128)(2,1)} collective-permute-done((bf16[512,1024]{1,0:T(8,128)(2,1)S(1)}, bf16[512,1024]{1,0:T(8,128)(2,1)}, u32[]{:S(2)}, u32[]{:S(2)}) %collective-permute-start.14) | collective-permute-done | bytes 1048608 | tf_op jit(solution)/shard_map/ppermute | solution.py:1125
  150.2 1.8 collective-permute-done.15.refs_5_.refs_9_
  156.9 1.6 collective-permute-start.19
  158.5 6.8 feed_forward.2
  166.6 7.9 %collective-permute-done.17.refs_2_.refs_12_ = bf16[512,1024]{1,0:T(8,128)(2,1)} collective-permute-done((bf16[512,1024]{1,0:T(8,128)(2,1)}, bf16[512,1024]{1,0:T(8,128)(2,1)}, u32[]{:S(2)}, u32[]{:S(2)}) %collective-permute-start.17) | collective-permute-done | bytes 1048608 | tf_op jit(solution)/shard_map/ppermute | solution.py:1125
  174.6 1.9 collective-permute-done.16.refs_1_.refs_3_
  180.2 1.6 collective-permute-start.18
  181.8 15.1 %collective-permute-done.19.refs_5_.refs_15_ = bf16[512,1024]{1,0:T(8,128)(2,1)S(1)} collective-permute-done((bf16[512,1024]{1,0:T(8,128)(2,1)}, bf16[512,1024]{1,0:T(8,128)(2,1)S(1)}, u32[]{:S(2)}, u32[]{:S(2)}) %collective-permute-start.19) | collective-permute-done | bytes 1048608 | tf_op jit(solution)/shard_map/ppermute | solution.py:1125
  196.9 7.9 %feed_forward.3 = (f32[512,1024]{1,0:T(8,128)S(1)}, f32[512,1024]{1,0:T(8,128)S(1)}, bf16[512,1024]{1,0:T(8,128)(2,1)S(1)}) custom-call(bf16[512,2048]{1,0:T(8,128)(2,1)S(1)} %get-tuple-element.96.hidden_ref, bf16[1024,2048]{1,0:T(8,128)(2,1)} %refs_10_.1, bf16[512,1024]{1,0:T(8,128)(2,1)} %collective-permute-done.11.refs_1_.refs_11_, ...), custom_call_target="tpu_custom_call" | custom-call | flops 6442450944 | bytes 8388608 | tf_op jit(solution)/shard_map/feed_forward/pallas_call | solution.py:291
  208.5 1.7 collective-permute-start.21
  212.3 2.4 slice.151.refs_9_
  222.9 1.6 copy-done.16
  224.5 1.6 copy-done.18
  226.1 4.8 feed_backward.2
  231.0 10.0 %collective-permute-done.21.refs_2_.refs_7_ = bf16[1024,512]{1,0:T(8,128)(2,1)} collective-permute-done((bf16[1024,512]{1,0:T(8,128)(2,1)}, bf16[1024,512]{1,0:T(8,128)(2,1)}, u32[]{:S(2)}, u32[]{:S(2)}) %collective-permute-start.21) | collective-permute-done | bytes 1048608 | tf_op jit(solution)/shard_map/ppermute | solution.py:1125
  240.9 4.7 feed_backward.3
  245.7 16.1 %project.2 = (bf16[256,2048]{1,0:T(8,128)(2,1)S(1)}, f32[256,2048]{1,0:T(8,128)}) custom-call(s32[1]{0:T(128)} %bitcast.17.sibling_ref, bf16[512,1024]{1,0:T(8,128)(2,1)S(1)} %get-tuple-element.105.refs_0_.refs_4_, bf16[512,1024]{1,0:T(8,128)(2,1)S(1)} %get-tuple-element.106.refs_1_.refs_6_, bf16[512,1024]{1,0:T(8,128)(2,1)S(1)} %get-tuple-element.117.refs_2_.refs_5_, ...), custom_call_target="tpu_custom_call" | custom-call | flops 12884901888 | bytes 16777216 | tf_op jit(solution)/shard_map/project/pallas_call | solution.py:409
  262.4 9.5 %project.3 = (bf16[256,2048]{1,0:T(8,128)(2,1)S(1)}, f32[256,2048]{1,0:T(8,128)}) custom-call(s32[1]{0:T(128)} %bitcast.17.sibling_ref, bf16[512,1024]{1,0:T(8,128)(2,1)S(1)} %copy-done.4, bf16[512,1024]{1,0:T(8,128)(2,1)S(1)} %copy-done.6, bf16[2048,1024]{1,0:T(8,128)(2,1)} %refs_5_.1, bf16[1024,512]{1,0:T(8,128)(2,1)} %collective-permute-done.16.refs_1_.refs_3_, ...), custom_call_target="tpu_custom_call" | custom-call | flops 6442450944 | bytes 16777216 | tf_op jit(solution)/shard_map/project/pallas_call | solution.py:409
  272.6 4.1 outer_sum.2.refs_2_
  276.7 4.3 outer_sum.3.refs_0_
  284.2 380.1 %tail.1 = (bf16[29,256,1024]{2,1,0:T(8,128)(2,1)}, bf16[29,256,1024]{2,1,0:T(8,128)(2,1)}, bf16[29,256,1024]{2,1,0:T(8,128)(2,1)}, bf16[29,256,1024]{2,1,0:T(8,1...) custom-call(bf16[29,256,1024]{2,1,0:T(8,128)(2,1)} %outer_sum.3.refs, ...), custom_call_target="tpu_custom_call", output_to_operand_aliasing={{0}: (0, {})} | custom-call | flops 429496729600 | bytes 31457280 | tf_op jit(solution)/shard_map/tail/pallas_call | solution.py:1053
  664.4 1.6 add_convert_fusion.1
  666.1 27.3 %widen.1 = (f32[2048,1024]{1,0:T(8,128)}, f32[1024,2048]{1,0:T(8,128)}, f32[1024,2048]{1,0:T(8,128)}, f32[512,1024]{1,0:T(8,128)}, f32[1024,512]{1,0:T(8,128)}, ...) custom-call(bf16[29,256,1024]{2,1,0:T(8,128)(2,1)} %get-tuple-element.135.pool_ref), custom_call_target="tpu_custom_call" | custom-call | flops 1 | bytes 47185920 | tf_op jit(solution)/shard_map/widen/pallas_call | solution.py:516
  694.9 3.8 add_convert_fusion
  698.9 1.7 maximum_select_fusion.2
  (240 shorter events, 65.4 us)
Async XLA Ops:
  2.1 23.0 %collective-permute-start = (bf16[2,1024]{1,0:T(2,128)(2,1)S(1)}, bf16[2,1024]{1,0:T(2,128)(2,1)S(1)}, u32[]{:S(2)}, u32[]{:S(2)}) collective-permute-start(bf16[2,1024]{1,0:T(2,128)(2,1)S(1)} %pad_maximum_fusion.8), channel_id=1, source_target_pairs={{0,16},{16,0},{1,17},{17,1},{2,18},{18,2},{3,19},{19,3},{4,20},{20... | collective-permute-start | bytes 12296 | tf_op jit(solution)/shard_map/ppermute | solution.py:1125
  7.7 19.6 %collective-permute-start.1 = (bf16[512,768]{1,0:T(8,128)(2,1)}, bf16[512,768]{1,0:T(8,128)(2,1)}, u32[]{:S(2)}, u32[]{:S(2)}) collective-permute-start(bf16[512,768]{1,0:T(8,128)(2,1)} %constant_dynamic-slice_fusion.20), channel_id=1, source_target_pairs={{0,16},{16,0},{1,17},{17,1},{2,18},{18,2},{3,19},{19,3},{4,20},{20... | collective-permute-start | bytes 2359304 | tf_op jit(solution)/shard_map/ppermute | solution.py:1125
  14.9 14.0 %copy-start.27 = (bf16[512,2048]{1,0:T(8,128)(2,1)}, bf16[512,2048]{1,0:T(8,128)(2,1)S(1)}, u32[]{:S(2)}) copy-start(bf16[512,2048]{1,0:T(8,128)(2,1)S(1)} %get-tuple-element.148.refs_24_) | copy-start | bytes 6291460
  25.1 13.7 %collective-permute-start.3 = (bf16[512,512]{1,0:T(8,128)(2,1)}, bf16[512,512]{1,0:T(8,128)(2,1)S(1)}, u32[]{:S(2)}, u32[]{:S(2)}) collective-permute-start(bf16[512,512]{1,0:T(8,128)(2,1)} %constant_dynamic-slice_fusion.23), channel_id=1, source_target_pairs={{0,16},{16,0},{1,17},{17,1},{2,18},{18,2},{3,19},{19,3},{4,20},{20... | collective-permute-start | bytes 1572872 | tf_op jit(solution)/shard_map/ppermute | solution.py:1125
  27.2 103.3 %copy-start.63 = (f32[1,2048]{1,0:T(1,128)}, f32[1,2048]{1,0:T(1,128)S(1)}, u32[]{:S(2)}) copy-start(f32[1,2048]{1,0:T(1,128)S(1)} %get-tuple-element.181.refs_31_) | copy-start | bytes 24580
  27.3 18.7 %collective-permute-start.2 = (bf16[512,768]{1,0:T(8,128)(2,1)}, bf16[512,768]{1,0:T(8,128)(2,1)S(1)}, u32[]{:S(2)}, u32[]{:S(2)}) collective-permute-start(bf16[512,768]{1,0:T(8,128)(2,1)} %collective-permute-done.1.refs_22_), channel_id=1, source_target_pairs={{0,4},{4,0},{8,12},{12,8},{1,5},{5,1},{9,13},{13,9},{2,6},{6,2},{1... | collective-permute-start | bytes 2359304 | tf_op jit(solution)/shard_map/ppermute | solution.py:1125
  30.3 15.7 %copy-start.30 = (bf16[512,2048]{1,0:T(8,128)(2,1)}, bf16[512,2048]{1,0:T(8,128)(2,1)S(1)}, u32[]{:S(2)}) copy-start(bf16[512,2048]{1,0:T(8,128)(2,1)S(1)} %fusion.2) | copy-start | bytes 6291460
  38.8 49.7 %copy-start.43 = (bf16[512,512]{1,0:T(8,128)(2,1)}, bf16[512,512]{1,0:T(8,128)(2,1)S(1)}, u32[]{:S(2)}) copy-start(bf16[512,512]{1,0:T(8,128)(2,1)S(1)} %collective-permute-done.3.refs_12_) | copy-start | bytes 1572868
  38.8 42.7 %collective-permute-start.8 = (bf16[512,1024]{1,0:T(8,128)(2,1)S(1)}, bf16[512,1024]{1,0:T(8,128)(2,1)}, u32[]{:S(2)}, u32[]{:S(2)}) collective-permute-start(bf16[512,1024]{1,0:T(8,128)(2,1)S(1)} %copy-done.55), channel_id=1, source_target_pairs={{0,16},{16,0},{1,17},{17,1},{2,18},{18,2},{3,19},{19,3},{4,20},{20... | collective-permute-start | bytes 3145736 | tf_op jit(solution)/shard_map/ppermute | solution.py:1125
  40.5 44.5 %collective-permute-start.7 = (bf16[512,1024]{1,0:T(8,128)(2,1)S(1)}, bf16[512,1024]{1,0:T(8,128)(2,1)S(1)}, u32[]{:S(2)}, u32[]{:S(2)}) collective-permute-start(bf16[512,1024]{1,0:T(8,128)(2,1)S(1)} %copy-done.54), channel_id=1, source_target_pairs={{0,16},{16,0},{1,17},{17,1},{2,18},{18,2},{3,19},{19,3},{4,20},{20... | collective-permute-start | bytes 3145736 | tf_op jit(solution)/shard_map/ppermute | solution.py:1125
  48.6 9.5 %collective-permute-start.5 = (bf16[1,512,256]{2,1,0:T(8,128)(2,1)S(1)}, bf16[1,512,256]{2,1,0:T(8,128)(2,1)S(1)}, u32[]{:S(2)}, u32[]{:S(2)}) collective-permute-start(bf16[1,512,256]{2,1,0:T(8,128)(2,1)S(1)} %maximum_bitcast_fusion), channel_id=1, source_target_pairs={{0,4},{4,8},{8,12},{1,5},{5,9},{9,13},{2,6},{6,10},{10,14},{3,7},{... | collective-permute-start | bytes 786440 | tf_op jit(solution)/shard_map/ppermute | solution.py:1131
  52.1 11.3 %collective-permute-start.4 = (bf16[1,512,256]{2,1,0:T(8,128)(2,1)S(1)}, bf16[1,512,256]{2,1,0:T(8,128)(2,1)S(1)}, u32[]{:S(2)}, u32[]{:S(2)}) collective-permute-start(bf16[1,512,256]{2,1,0:T(8,128)(2,1)S(1)} %maximum_bitcast_fusion), channel_id=1, source_target_pairs={{0,8},{4,12},{1,9},{5,13},{2,10},{6,14},{3,11},{7,15},{16,24},{20,... | collective-permute-start | bytes 786440 | tf_op jit(solution)/shard_map/ppermute | solution.py:1131
  57.0 28.0 %collective-permute-start.6 = (bf16[512,512]{1,0:T(8,128)(2,1)S(1)}, bf16[512,512]{1,0:T(8,128)(2,1)S(1)}, u32[]{:S(2)}, u32[]{:S(2)}) collective-permute-start(bf16[512,512]{1,0:T(8,128)(2,1)S(1)} %collective-permute-done.3.refs_12_), channel_id=1, source_target_pairs={{0,4},{4,0},{8,12},{12,8},{1,5},{5,1},{9,13},{13,9},{2,6},{6,2},{1... | collective-permute-start | bytes 1572872 | tf_op jit(solution)/shard_map/ppermute | solution.py:1125
  58.1 23.4 %copy-start.7 = (bf16[1,512,512]{2,1,0:T(8,128)(2,1)}, bf16[1,512,512]{2,1,0:T(8,128)(2,1)S(1)}, u32[]{:S(2)}) copy-start(bf16[1,512,512]{2,1,0:T(8,128)(2,1)S(1)} %multiply_bitcast_fusion.q_ref) | copy-start | bytes 1572868
  64.4 20.9 %copy-start.35 = (bf16[512,1024]{1,0:T(8,128)(2,1)S(1)}, bf16[512,1024]{1,0:T(8,128)(2,1)}, u32[]{:S(2)}) copy-start(bf16[512,1024]{1,0:T(8,128)(2,1)} %refs_11_.1) | copy-start | bytes 3145732
  87.2 3.0 collective-permute-start.9
  91.7 25.3 %collective-permute-start.10 = (bf16[256,2048]{1,0:T(8,128)(2,1)S(1)}, bf16[256,2048]{1,0:T(8,128)(2,1)S(1)}, u32[]{:S(2)}, u32[]{:S(2)}) collective-permute-start(bf16[256,2048]{1,0:T(8,128)(2,1)S(1)} %fusion.4), channel_id=1, source_target_pairs={{0,2},{1,3},{2,0},{3,1},{4,6},{5,7},{6,4},{7,5},{8,10},{9,11},{10,... | collective-permute-start | bytes 3145736 | tf_op jit(solution)/shard_map/ppermute | solution.py:1125
  93.2 25.2 %collective-permute-start.11 = (bf16[512,1024]{1,0:T(8,128)(2,1)S(1)}, bf16[512,1024]{1,0:T(8,128)(2,1)}, u32[]{:S(2)}, u32[]{:S(2)}) collective-permute-start(bf16[512,1024]{1,0:T(8,128)(2,1)S(1)} %copy-done.51), channel_id=1, source_target_pairs={{0,16},{16,0},{1,17},{17,1},{2,18},{18,2},{3,19},{19,3},{4,20},{20... | collective-permute-start | bytes 3145736 | tf_op jit(solution)/shard_map/ppermute | solution.py:1125
  94.7 24.6 %collective-permute-start.12 = (bf16[512,1024]{1,0:T(8,128)(2,1)S(1)}, bf16[512,1024]{1,0:T(8,128)(2,1)S(1)}, u32[]{:S(2)}, u32[]{:S(2)}) collective-permute-start(bf16[512,1024]{1,0:T(8,128)(2,1)S(1)} %collective-permute-done.7.refs_1_.refs_5_), channel_id=1, source_target_pairs={{0,4},{4,0},{8,12},{12,8},{1,5},{5,1},{9,13},{13,9},{2,6},{6,2},{1... | collective-permute-start | bytes 3145736 | tf_op jit(solution)/shard_map/ppermute | solution.py:1125
  119.4 8.4 %collective-permute-start.13 = (bf16[256,2048]{1,0:T(8,128)(2,1)}, bf16[256,2048]{1,0:T(8,128)(2,1)S(1)}, u32[]{:S(2)}, u32[]{:S(2)}) collective-permute-start(bf16[256,2048]{1,0:T(8,128)(2,1)} %add_convert_fusion.4), channel_id=1, source_target_pairs={{0,1},{1,0},{2,3},{3,2},{4,5},{5,4},{6,7},{7,6},{8,9},{9,8},{10,11... | collective-permute-start | bytes 3145736 | tf_op jit(solution)/shard_map/ppermute | solution.py:1125
  124.9 25.4 %collective-permute-start.14 = (bf16[512,1024]{1,0:T(8,128)(2,1)S(1)}, bf16[512,1024]{1,0:T(8,128)(2,1)}, u32[]{:S(2)}, u32[]{:S(2)}) collective-permute-start(bf16[512,1024]{1,0:T(8,128)(2,1)S(1)} %copy-done.50), channel_id=1, source_target_pairs={{0,16},{16,0},{1,17},{17,1},{2,18},{18,2},{3,19},{19,3},{4,20},{20... | collective-permute-start | bytes 3145736 | tf_op jit(solution)/shard_map/ppermute | solution.py:1125
  125.7 26.2 %collective-permute-start.15 = (bf16[512,1024]{1,0:T(8,128)(2,1)}, bf16[512,1024]{1,0:T(8,128)(2,1)S(1)}, u32[]{:S(2)}, u32[]{:S(2)}) collective-permute-start(bf16[512,1024]{1,0:T(8,128)(2,1)} %collective-permute-done.8.refs_4_.refs_8_), channel_id=1, source_target_pairs={{0,4},{4,0},{8,12},{12,8},{1,5},{5,1},{9,13},{13,9},{2,6},{6,2},{1... | collective-permute-start | bytes 3145736 | tf_op jit(solution)/shard_map/ppermute | solution.py:1125
  127.5 47.1 %collective-permute-start.17 = (bf16[512,1024]{1,0:T(8,128)(2,1)}, bf16[512,1024]{1,0:T(8,128)(2,1)}, u32[]{:S(2)}, u32[]{:S(2)}) collective-permute-start(bf16[512,1024]{1,0:T(8,128)(2,1)} %collective-permute-done.11.refs_1_.refs_11_), channel_id=1, source_target_pairs={{0,4},{4,0},{8,12},{12,8},{1,5},{5,1},{9,13},{13,9},{2,6},{6,2},{1... | collective-permute-start | bytes 3145736 | tf_op jit(solution)/shard_map/ppermute | solution.py:1125
  153.0 23.5 %collective-permute-start.16 = (bf16[1024,512]{1,0:T(8,128)(2,1)}, bf16[1024,512]{1,0:T(8,128)(2,1)}, u32[]{:S(2)}, u32[]{:S(2)}) collective-permute-start(bf16[1024,512]{1,0:T(8,128)(2,1)} %constant_dynamic-slice_fusion.12), channel_id=1, source_target_pairs={{0,16},{16,0},{1,17},{17,1},{2,18},{18,2},{3,19},{19,3},{4,20},{20... | collective-permute-start | bytes 3145736 | tf_op jit(solution)/shard_map/ppermute | solution.py:1125
  156.9 20.8 %copy-start.48 = (bf16[512,512]{1,0:T(8,128)(2,1)S(1)}, bf16[512,512]{1,0:T(8,128)(2,1)}, u32[]{:S(2)}) copy-start(bf16[512,512]{1,0:T(8,128)(2,1)} %get-tuple-element.163) | copy-start | bytes 1572868
  156.9 20.8 %copy-start.49 = (bf16[512,512]{1,0:T(8,128)(2,1)S(1)}, bf16[512,512]{1,0:T(8,128)(2,1)}, u32[]{:S(2)}) copy-start(bf16[512,512]{1,0:T(8,128)(2,1)} %get-tuple-element.164) | copy-start | bytes 1572868
  156.9 40.0 %collective-permute-start.19 = (bf16[512,1024]{1,0:T(8,128)(2,1)}, bf16[512,1024]{1,0:T(8,128)(2,1)S(1)}, u32[]{:S(2)}, u32[]{:S(2)}) collective-permute-start(bf16[512,1024]{1,0:T(8,128)(2,1)} %collective-permute-done.14.refs_4_.refs_14_), channel_id=1, source_target_pairs={{0,4},{4,0},{8,12},{12,8},{1,5},{5,1},{9,13},{13,9},{2,6},{6,2},{1... | collective-permute-start | bytes 3145736 | tf_op jit(solution)/shard_map/ppermute | solution.py:1125
  166.6 11.3 %copy-start.15 = (f32[512,1024]{1,0:T(8,128)}, f32[512,1024]{1,0:T(8,128)S(1)}, u32[]{:S(2)}) copy-start(f32[512,1024]{1,0:T(8,128)S(1)} %get-tuple-element.103.refs_3_) | copy-start | bytes 6291460
  176.5 32.0 %collective-permute-start.20 = (bf16[1024,512]{1,0:T(8,128)(2,1)S(1)}, bf16[1024,512]{1,0:T(8,128)(2,1)}, u32[]{:S(2)}, u32[]{:S(2)}) collective-permute-start(bf16[1024,512]{1,0:T(8,128)(2,1)S(1)} %constant_dynamic-slice_fusion.11), channel_id=1, source_target_pairs={{0,16},{16,0},{1,17},{17,1},{2,18},{18,2},{3,19},{19,3},{4,20},{20... | collective-permute-start | bytes 3145736 | tf_op jit(solution)/shard_map/ppermute | solution.py:1125
  180.2 42.7 %collective-permute-start.18 = (bf16[1024,512]{1,0:T(8,128)(2,1)}, bf16[1024,512]{1,0:T(8,128)(2,1)}, u32[]{:S(2)}, u32[]{:S(2)}) collective-permute-start(bf16[1024,512]{1,0:T(8,128)(2,1)} %collective-permute-done.16.refs_1_.refs_3_), channel_id=1, source_target_pairs={{0,4},{4,0},{8,12},{12,8},{1,5},{5,1},{9,13},{13,9},{2,6},{6,2},{1... | collective-permute-start | bytes 3145736 | tf_op jit(solution)/shard_map/ppermute | solution.py:1125
  208.5 32.4 %collective-permute-start.21 = (bf16[1024,512]{1,0:T(8,128)(2,1)}, bf16[1024,512]{1,0:T(8,128)(2,1)}, u32[]{:S(2)}, u32[]{:S(2)}) collective-permute-start(bf16[1024,512]{1,0:T(8,128)(2,1)} %collective-permute-done.20.refs_1_.refs_6_), channel_id=1, source_target_pairs={{0,4},{4,0},{8,12},{12,8},{1,5},{5,1},{9,13},{13,9},{2,6},{6,2},{1... | collective-permute-start | bytes 3145736 | tf_op jit(solution)/shard_map/ppermute | solution.py:1125
  218.6 27.0 %collective-permute-start.22 = (bf16[512,1024]{1,0:T(8,128)(2,1)}, bf16[512,1024]{1,0:T(8,128)(2,1)S(1)}, u32[]{:S(2)}, u32[]{:S(2)}) collective-permute-start(bf16[512,1024]{1,0:T(8,128)(2,1)} %copy-done.3), channel_id=1, source_target_pairs={{0,16},{16,0},{1,17},{17,1},{2,18},{18,2},{3,19},{19,3},{4,20},{20... | collective-permute-start | bytes 3145736 | tf_op jit(solution)/shard_map/ppermute | solution.py:1125
  220.9 41.0 %collective-permute-start.23 = (bf16[256,1024]{1,0:T(8,128)(2,1)}, bf16[256,1024]{1,0:T(8,128)(2,1)S(1)}, u32[]{:S(2)}, u32[]{:S(2)}) collective-permute-start(bf16[256,1024]{1,0:T(8,128)(2,1)} %fusion.7), channel_id=1, source_target_pairs={{0,16},{16,0},{1,17},{17,1},{2,18},{18,2},{3,19},{19,3},{4,20},{20... | collective-permute-start | bytes 1572872 | tf_op jit(solution)/shard_map/ppermute | solution.py:1125
  221.9 54.8 %collective-permute-start.25 = (bf16[512,1024]{1,0:T(8,128)(2,1)S(1)}, bf16[512,1024]{1,0:T(8,128)(2,1)S(1)}, u32[]{:S(2)}, u32[]{:S(2)}) collective-permute-start(bf16[512,1024]{1,0:T(8,128)(2,1)S(1)} %copy-done.6), channel_id=1, source_target_pairs={{0,16},{16,0},{1,17},{17,1},{2,18},{18,2},{3,19},{19,3},{4,20},{20... | collective-permute-start | bytes 3145736 | tf_op jit(solution)/shard_map/ppermute | solution.py:1125
  226.1 14.8 %copy-start.20 = (f32[512,1024]{1,0:T(8,128)S(1)}, f32[512,1024]{1,0:T(8,128)}, u32[]{:S(2)}) copy-start(f32[512,1024]{1,0:T(8,128)} %copy-done.19) | copy-start | bytes 6291460
  226.1 14.8 %copy-start.22 = (f32[512,1024]{1,0:T(8,128)S(1)}, f32[512,1024]{1,0:T(8,128)}, u32[]{:S(2)}) copy-start(f32[512,1024]{1,0:T(8,128)} %copy-done.21) | copy-start | bytes 6291460
  230.9 14.7 %copy-start.23 = (bf16[512,1024]{1,0:T(8,128)(2,1)}, bf16[512,1024]{1,0:T(8,128)(2,1)S(1)}, u32[]{:S(2)}) copy-start(bf16[512,1024]{1,0:T(8,128)(2,1)S(1)} %get-tuple-element.105.refs_0_.refs_4_) | copy-start | bytes 3145732
  230.9 14.7 %copy-start.24 = (bf16[512,1024]{1,0:T(8,128)(2,1)}, bf16[512,1024]{1,0:T(8,128)(2,1)S(1)}, u32[]{:S(2)}) copy-start(bf16[512,1024]{1,0:T(8,128)(2,1)S(1)} %get-tuple-element.106.refs_1_.refs_6_) | copy-start | bytes 3145732
  245.6 16.2 %copy-start.25 = (bf16[512,1024]{1,0:T(8,128)(2,1)}, bf16[512,1024]{1,0:T(8,128)(2,1)S(1)}, u32[]{:S(2)}) copy-start(bf16[512,1024]{1,0:T(8,128)(2,1)S(1)} %get-tuple-element.117.refs_2_.refs_5_) | copy-start | bytes 3145732
  245.7 16.2 %copy-start.26 = (bf16[512,1024]{1,0:T(8,128)(2,1)}, bf16[512,1024]{1,0:T(8,128)(2,1)S(1)}, u32[]{:S(2)}) copy-start(bf16[512,1024]{1,0:T(8,128)(2,1)S(1)} %get-tuple-element.118.refs_3_.refs_7_) | copy-start | bytes 3145732
  245.7 16.8 %copy-start.4 = (bf16[512,1024]{1,0:T(8,128)(2,1)S(1)}, bf16[512,1024]{1,0:T(8,128)(2,1)}, u32[]{:S(2)}) copy-start(bf16[512,1024]{1,0:T(8,128)(2,1)} %copy-done.3) | copy-start | bytes 3145732
  261.9 10.2 %collective-permute-start.26 = (bf16[256,1024]{1,0:T(8,128)(2,1)S(1)}, bf16[256,1024]{1,0:T(8,128)(2,1)S(1)}, u32[]{:S(2)}, u32[]{:S(2)}) collective-permute-start(bf16[256,1024]{1,0:T(8,128)(2,1)S(1)} %collective-permute-done.23), channel_id=1, source_target_pairs={{0,1},{1,0},{2,3},{3,2},{4,5},{5,4},{6,7},{7,6},{8,9},{9,8},{10,11... | collective-permute-start | bytes 1572872 | tf_op jit(solution)/shard_map/ppermute | solution.py:1125
  261.9 19.0 %collective-permute-start.27 = (bf16[256,2048]{1,0:T(8,128)(2,1)S(1)}, bf16[256,2048]{1,0:T(8,128)(2,1)S(1)}, u32[]{:S(2)}, u32[]{:S(2)}) collective-permute-start(bf16[256,2048]{1,0:T(8,128)(2,1)S(1)} %get-tuple-element.131), channel_id=1, source_target_pairs={{0,1},{1,0},{2,3},{3,2},{4,5},{5,4},{6,7},{7,6},{8,9},{9,8},{10,11... | collective-permute-start | bytes 3145736 | tf_op jit(solution)/shard_map/ppermute | solution.py:1125
  272.0 10.2 %collective-permute-start.24 = (bf16[256,2048]{1,0:T(8,128)(2,1)S(1)}, bf16[256,2048]{1,0:T(8,128)(2,1)S(1)}, u32[]{:S(2)}, u32[]{:S(2)}) collective-permute-start(bf16[256,2048]{1,0:T(8,128)(2,1)S(1)} %get-tuple-element.126), channel_id=1, source_target_pairs={{0,1},{1,0},{2,3},{3,2},{4,5},{5,4},{6,7},{7,6},{8,9},{9,8},{10,11... | collective-permute-start | bytes 3145736 | tf_op jit(solution)/shard_map/ppermute | solution.py:1125
  284.2 380.1 %copy-start.39 = (bf16[256,2048]{1,0:T(8,128)(2,1)S(1)}, bf16[256,2048]{1,0:T(8,128)(2,1)}, u32[]{:S(2)}) copy-start(bf16[256,2048]{1,0:T(8,128)(2,1)} %add_convert_fusion.3.refs_3_) | copy-start | bytes 3145732
  666.0 28.9 %collective-permute-start.28 = (bf16[256,2048]{1,0:T(8,128)(2,1)S(1)}, bf16[256,2048]{1,0:T(8,128)(2,1)S(1)}, u32[]{:S(2)}, u32[]{:S(2)}) collective-permute-start(bf16[256,2048]{1,0:T(8,128)(2,1)S(1)} %add_convert_fusion.1), channel_id=1, source_target_pairs={{0,1},{1,0},{2,3},{3,2},{4,5},{5,4},{6,7},{7,6},{8,9},{9,8},{10,11... | collective-permute-start | bytes 3145736 | tf_op jit(solution)/shard_map/ppermute | solution.py:1125
  666.1 28.8 %copy-start.29 = (bf16[512,2048]{1,0:T(8,128)(2,1)S(1)}, bf16[512,2048]{1,0:T(8,128)(2,1)}, u32[]{:S(2)}) copy-start(bf16[512,2048]{1,0:T(8,128)(2,1)} %copy-done.27) | copy-start | bytes 6291460
  666.1 28.8 %copy-start.33 = (bf16[256,2048]{1,0:T(8,128)(2,1)S(1)}, bf16[256,2048]{1,0:T(8,128)(2,1)}, u32[]{:S(2)}) copy-start(bf16[256,2048]{1,0:T(8,128)(2,1)} %copy-done.32) | copy-start | bytes 3145732
  (45 other events, 177.2 us)

commit v6 on v5

--- a/solution.py
+++ b/solution.py
@@ -472,51 +472,56 @@
 
 def widen_body(starts, pool_ref, *out_refs):
     step = pl.program_id(0)
-    value = pool_ref[0].astype(F32)
+    group = pool_ref.shape[0]
     last = len(starts) - 1
     for at, start in enumerate(starts):
-        stop = starts[at + 1] if at < last else pl.num_programs(0)
-
-        @pl.when((step >= start) & (step < stop))
+        stop = starts[at + 1] // group if at < last else pl.num_programs(0)
+
+        @pl.when((step >= start // group) & (step < stop))
         def _():
             if at < last - 1:
-                out_refs[at][...] = value
+                for piece in range(group):
+                    rows = slice(piece * CHUNK_ROWS, (piece + 1) * CHUNK_ROWS)
+                    out_refs[at][rows] = pool_ref[piece].astype(F32)
             elif at == last - 1:
                 half = CHUNK_COLUMNS // 2
-                out_refs[at][:CHUNK_ROWS] = value[:, :half]
-                out_refs[at][CHUNK_ROWS:] = value[:, half:]
+                for side in range(2 * group):
+                    rows = slice(side * CHUNK_ROWS, (side + 1) * CHUNK_ROWS)
+                    columns = slice(side % 2 * half, (side % 2 + 1) * half)
+                    out_refs[at][rows] = pool_ref[side // 2, :, columns].astype(F32)
             else:
                 width = out_refs[at].shape[1]
                 for block in range(CHUNK_COLUMNS // (2 * width)):
                     rows = slice(block * CHUNK_ROWS, (block + 1) * CHUNK_ROWS)
                     left = 2 * block * width
-                    out_refs[at][rows] = value[:, left : left + width]
-                    out_refs[at + 1][rows] = value[:, left + width : left + 2 * width]
-
-
-def widen(pool, starts, shapes):
+                    value = pool_ref[0, :, left : left + 2 * width].astype(F32)
+                    out_refs[at][rows] = value[:, :width]
+                    out_refs[at + 1][rows] = value[:, width:]
+
+
+def widen(pool, starts, shapes, group):
     specs = []
+    steps = pool.shape[0] // group
     for at, shape in enumerate(shapes):
         which = min(at, len(starts) - 1)
-        start = starts[which]
-        stop = starts[which + 1] if which + 1 < len(starts) else pool.shape[0]
-        size = stop - start
-        block = (shape[0] * shape[1] // (size * CHUNK_COLUMNS), CHUNK_COLUMNS)
+        first = starts[which] // group
+        stop = starts[which + 1] // group if which + 1 < len(starts) else steps
+        block = (group * CHUNK_ROWS, CHUNK_COLUMNS)
         if which == len(starts) - 1:
             block = shape
         elif which == len(starts) - 2:
-            block = (2 * CHUNK_ROWS, shape[1])
+            block = (2 * group * CHUNK_ROWS, shape[1])
         down = shape[0] // block[0]
 
-        def place(i, start=start, size=size, down=down):
-            k = jnp.clip(i - start, 0, size - 1)
+        def place(i, first=first, size=stop - first, down=down):
+            k = jnp.clip(i - first, 0, size - 1)
             return lax.rem(k, down), k // down
 
         specs.append(pl.BlockSpec(block, place))
     return pl.pallas_call(
         functools.partial(widen_body, starts),
-        grid=(pool.shape[0],),
-        in_specs=[pl.BlockSpec((1, CHUNK_ROWS, CHUNK_COLUMNS), lambda i: (i, 0, 0))],
+        grid=(steps,),
+        in_specs=[pl.BlockSpec((group, CHUNK_ROWS, CHUNK_COLUMNS), lambda i: (i, 0, 0))],
         out_specs=specs,
         out_shape=[jax.ShapeDtypeStruct(shape, F32) for shape in shapes],
         compiler_params=pltpu.CompilerParams(vmem_limit_bytes=48 << 20),
@@ -1074,7 +1079,7 @@
     operands = [pool, v["hidden_m_send"], v["hidden_a_send"], v["feed_chip"], stored]
     loaded = jax.tree.map(lambda value: pltpu.VMEM(value.shape, value.dtype), stored)
     any_space, vmem_space = pl.BlockSpec(memory_space=pl.ANY), pl.BlockSpec(memory_space=pltpu.VMEM)
-    line = jax.ShapeDtypeStruct((count,) + piece, BF16)
+    line = jax.ShapeDtypeStruct(pool.shape, BF16)
     dma = pltpu.SemaphoreType.DMA
     low = lambda *shape: pltpu.VMEM(shape, BF16)
     wide = lambda *shape: pltpu.VMEM(shape, F32)
@@ -1313,19 +1318,18 @@
         seqs, span, q_width
     )
     earlier = [shift(keys_values, "ctx", ctx_count, back) for back in range(blocks_back, 0, -1)]
-    *earlier, query_low = tie(*earlier, query_low)
+    *earlier, query_low, near_up[0] = tie(*earlier, query_low, near_up[0])
+    far_up[0] = over_ctx(near_up[0])
     keys_values = jnp.concatenate(earlier + [keys_values], axis=1)
     mixed, log_sums = attend_forward(
         query_low, keys_values, query_segments, key_segments, base, lead, group
     )
     mixed_low = mixed.reshape(rows, q_width)
-    mixed_low, far_out, near_gate[0], near_up[0], send_gate[1], send_up[1] = tie(
-        mixed_low, far_out, near_gate[0], near_up[0], send_gate[1], send_up[1]
+    mixed_low, far_out, near_gate[0], send_gate[1] = tie(
+        mixed_low, far_out, near_gate[0], send_gate[1]
     )
     near_gate[1] = over_fsdp(send_gate[1])
     far_gate[0] = over_ctx(near_gate[0])
-    near_up[1] = over_fsdp(send_up[1])
-    far_up[0] = over_ctx(near_up[0])
 
     def out_project(at):
         matrix = take(mixed_low, at * (rows // 2), rows // 2, 0)
@@ -1337,22 +1341,27 @@
     first, second = out_project(1 - sibling).astype(BF16), out_project(sibling)
     if tp_count == 4:
         chip = chip_sum(first, second)
+        chip, near_gate[1], far_up[0], send_up[1] = tie(
+            chip, near_gate[1], far_up[0], send_up[1]
+        )
+        near_up[1] = over_fsdp(send_up[1])
+        far_gate[1] = over_ctx(near_gate[1])
         total = (chip.astype(F32) + swap(chip, "tp", tp_count, 2).astype(F32)).astype(BF16)
-        total, near_gate[1], far_gate[0] = tie(total, near_gate[1], far_gate[0])
+        total, near_up[1], far_gate[0], send_down[0] = tie(
+            total, near_up[1], far_gate[0], send_down[0]
+        )
         branch_a = join_cores(total).astype(F32)
     else:
         branch_a = tp_sum(first, second)
-    far_gate[1] = over_ctx(near_gate[1])
+        near_up[1] = over_fsdp(send_up[1])
+        far_gate[1] = over_ctx(near_gate[1])
+    near_down = [over_fsdp(send_down[0])]
+    far_up[1] = over_ctx(near_up[1])
     middle = inputs + branch_a
 
     scale_m = row_scale_of(middle)
     normed_m = middle * scale_m
     hidden_m = (normed_m * gain_m).astype(BF16)
-    hidden_m, near_up[1], far_up[0], send_down[0] = tie(
-        hidden_m, near_up[1], far_up[0], send_down[0]
-    )
-    near_down = [over_fsdp(send_down[0])]
-    far_up[1] = over_ctx(near_up[1])
     gate_cuts, up_cuts, act_cuts = [], [], []
 
     def feed(cut):
@@ -1387,6 +1396,9 @@
     for size in (feed_width * half,) * 3 + (q_width * half,) * 2 + (2 * kv_width * half,):
         starts.append(pool_size)
         pool_size += size // pieces
+    piece_count = pool_size
+    widen_group = 1 if any(start % 2 for start in starts) else 2
+    pool_size += -pool_size % widen_group
     grad_gate_cuts, grad_up_cuts = [], []
     for cut in range(feed_cuts):
         grad_gate, grad_up = feed_backward(
@@ -1455,7 +1467,7 @@
                 group,
                 lead,
                 tuple(starts),
-                pool_size,
+                piece_count,
             ),
             pool,
             {
@@ -1592,6 +1604,7 @@
             key_weight.shape,
             value_weight.shape,
         ],
+        widen_group,
     )
     return (
         block_out,

time: 714 us -> 706 us (0.989)
    dynamic_slice x14 -> x15, local copies, waits for them, and re-layouts: 13.4 us -> 14.4 us  [take(): return lax.dynamic_slice_in_dim(array, start, size, axis)]
    unnamed x131 -> x139, local copies, waits for them, and re-layouts: 20.3 us -> 21.1 us
  transfers between devices with their start and end apart: 29 -> 29, of which waited for: 13 -> 12; matrix products, arithmetic and copies ran while one was open for 8% -> 8% of each run, Pallas kernels for 15% -> 14%
where the time goes in v6:
time: 706 us; the launch traced here: 695 us
  Pallas kernels  477 us (68%)
  waiting for transfers between devices  94.4 us (13%)
  local copies, waits for them, and re-layouts  52.1 us (7%)
  starting transfers between devices  33.7 us (5%)
  other arithmetic  30 us (4%)
    pallas_call x1, Pallas kernels, flat_call(): return pl.pallas_call(unflatten, in_specs=in_specs, **call)(*flat)  381 us
    ppermute x27, waiting for transfers between devices, swap(): return lax.ppermute(value, axis, [(i, i ^ bit) for i in range(size)])  94.4 us
    ppermute x27, starting transfers between devices, swap(): return lax.ppermute(value, axis, [(i, i ^ bit) for i in range(size)])  25.7 us
    pallas_call x2, Pallas kernels, project(): pl.pallas_call(functools.partial(project_body, cuts, steps, terms, pieces...  25.7 us
    unnamed x139, local copies, waits for them, and re-layouts  21.1 us
    pallas_call x1, Pallas kernels, widen(): pl.pallas_call(functools.partial(widen_body, starts), grid=(steps,), in_s...  21 us
    pallas_call x1, Pallas kernels, attend_forward(): pl.pallas_call(functools.partial(attend_forward_body, lead, heads, group)...  17.1 us
    dynamic_slice x15, local copies, waits for them, and re-layouts, take(): return lax.dynamic_slice_in_dim(array, start, size, axis)  14.4 us
  transfers between devices with their start and end apart: 29, of which 12 were waited for; matrix products, arithmetic and copies ran while one was open for 8% of the time, Pallas kernels for 14%

profile of v6, /device:TPU:0, one launch (start us, length us, event | category | flops | bytes accessed | tf_op | source)
XLA Modules:
  0.0 695.1 jit_solution(9966885947659399858)
XLA Ops:
  2.1 3.0 collective-permute-start
  10.1 1.4 dynamic-slice_bitcast_fusion.1
  12.0 2.4 dynamic-slice_bitcast_fusion.5
  14.9 2.4 copy-done.42
  20.8 1.8 fusion.50
  25.0 2.0 collective-permute-start.3
  27.1 1.6 collective-permute-start.2
  31.2 7.5 %collective-permute-done.3.refs_12_ = bf16[512,512]{1,0:T(8,128)(2,1)S(1)} collective-permute-done((bf16[512,512]{1,0:T(8,128)(2,1)}, bf16[512,512]{1,0:T(8,128)(2,1)S(1)}, u32[]{:S(2)}, u32[]{:S(2)}) %collective-permute-start.3) | collective-permute-done | bytes 524320 | tf_op jit(solution)/shard_map/ppermute | solution.py:1130
  38.7 1.7 collective-permute-start.6
  40.7 1.7 fusion.9
  42.4 3.4 collective-permute-done.2.refs_23_
  48.4 3.5 collective-permute-start.5
  51.9 4.5 collective-permute-start.4
  57.9 6.9 collective-permute-done.6.refs_4_.refs_8_
  65.9 17.1 %attend_forward.1 = (bf16[1,512,512]{2,1,0:T(8,128)(2,1)S(1)}, f32[1,512,128]{2,1,0:T(8,128)S(1)}) custom-call(bf16[1,512,512]{2,1,0:T(8,128)(2,1)S(1)} %multiply_bitcast_fusion.q_ref, bf16[1,1536,256]{2,1,0:T(8,128)(2,1)S(1)} %get-tuple-element.176.kv_ref, s32[1,512,1]{2,1,0:T(8,128)S(1)} %copy.31.qseg_ref, s32[1,4,1,1152]{3,2,1,0:T(1,128)S(1)} %add_bitcast_fusion.kseg_ref), custom_call_target="tpu_custom_call" | custom-call | flops 21139292160 | bytes 4194304 | tf_op jit(solution)/shard_map/attend_forward/pallas_call | solution.py:189
  83.1 1.8 collective-permute-done.8.refs_1_.refs_5_
  87.0 1.4 constant_dynamic-slice_fusion.13
  88.5 2.0 collective-permute-start.11
  93.7 1.7 fusion.4
  95.4 18.9 %collective-permute-done.11.refs_5_.refs_9_ = bf16[512,1024]{1,0:T(8,128)(2,1)S(1)} collective-permute-done((bf16[512,1024]{1,0:T(8,128)(2,1)S(1)}, bf16[512,1024]{1,0:T(8,128)(2,1)S(1)}, u32[]{:S(2)}, u32[]{:S(2)}) %collective-permute-start.11) | collective-permute-done | bytes 1048608 | tf_op jit(solution)/shard_map/ppermute | solution.py:1130
  115.8 1.5 collective-permute-start.12
  119.6 1.8 fusion.49
  122.5 17.7 %collective-permute-done.12 = bf16[256,2048]{1,0:T(8,128)(2,1)S(1)} collective-permute-done((bf16[256,2048]{1,0:T(8,128)(2,1)S(1)}, bf16[256,2048]{1,0:T(8,128)(2,1)S(1)}, u32[]{:S(2)}, u32[]{:S(2)}) %collective-permute-start.12) | collective-permute-done | bytes 1048608 | tf_op jit(solution)/shard_map/ppermute | solution.py:1130
  140.2 1.5 add_convert_fusion.4
  142.9 1.4 dynamic-slice_bitcast_fusion.refs_0_
  145.7 1.4 collective-permute-start.17
  148.8 2.8 multiply_reduce_fusion
  151.6 4.2 multiply_convert_fusion
  155.9 6.7 feed_forward.2
  164.0 7.7 %collective-permute-done.17.refs_2_.refs_12_ = bf16[512,1024]{1,0:T(8,128)(2,1)S(1)} collective-permute-done((bf16[512,1024]{1,0:T(8,128)(2,1)S(1)}, bf16[512,1024]{1,0:T(8,128)(2,1)S(1)}, u32[]{:S(2)}, u32[]{:S(2)}) %collective-permute-start.17) | collective-permute-done | bytes 1048608 | tf_op jit(solution)/shard_map/ppermute | solution.py:1130
  177.0 17.2 %collective-permute-done.19.refs_5_.refs_15_ = bf16[512,1024]{1,0:T(8,128)(2,1)S(1)} collective-permute-done((bf16[512,1024]{1,0:T(8,128)(2,1)}, bf16[512,1024]{1,0:T(8,128)(2,1)S(1)}, u32[]{:S(2)}, u32[]{:S(2)}) %collective-permute-start.19) | collective-permute-done | bytes 1048608 | tf_op jit(solution)/shard_map/ppermute | solution.py:1130
  194.2 7.2 %feed_forward.3 = (f32[512,1024]{1,0:T(8,128)S(1)}, f32[512,1024]{1,0:T(8,128)S(1)}, bf16[512,1024]{1,0:T(8,128)(2,1)S(1)}) custom-call(bf16[512,2048]{1,0:T(8,128)(2,1)S(1)} %get-tuple-element.143.hidden_ref, bf16[1024,2048]{1,0:T(8,128)(2,1)} %refs_10_.1, bf16[512,1024]{1,0:T(8,128)(2,1)S(1)} %copy-done.15, ...), custom_call_target="tpu_custom_call" | custom-call | flops 6442450944 | bytes 8388608 | tf_op jit(solution)/shard_map/feed_forward/pallas_call | solution.py:291
  208.5 2.4 slice.151.refs_9_
  219.2 1.6 copy-done.21
  220.8 1.6 copy-done.23
  222.4 4.8 feed_backward.2
  227.3 11.5 %collective-permute-done.21.refs_2_.refs_7_ = bf16[1024,512]{1,0:T(8,128)(2,1)} collective-permute-done((bf16[1024,512]{1,0:T(8,128)(2,1)}, bf16[1024,512]{1,0:T(8,128)(2,1)}, u32[]{:S(2)}, u32[]{:S(2)}) %collective-permute-start.21) | collective-permute-done | bytes 1048608 | tf_op jit(solution)/shard_map/ppermute | solution.py:1130
  238.8 4.7 feed_backward.3
  243.6 16.1 %project.2 = (bf16[256,2048]{1,0:T(8,128)(2,1)S(1)}, f32[256,2048]{1,0:T(8,128)}) custom-call(s32[1]{0:T(128)} %bitcast.17.sibling_ref, bf16[512,1024]{1,0:T(8,128)(2,1)S(1)} %get-tuple-element.105.refs_0_.refs_4_, bf16[512,1024]{1,0:T(8,128)(2,1)S(1)} %get-tuple-element.106.refs_1_.refs_6_, bf16[512,1024]{1,0:T(8,128)(2,1)S(1)} %get-tuple-element.117.refs_2_.refs_5_, ...), custom_call_target="tpu_custom_call" | custom-call | flops 12884901888 | bytes 16777216 | tf_op jit(solution)/shard_map/project/pallas_call | solution.py:409
  260.3 9.5 %project.3 = (bf16[256,2048]{1,0:T(8,128)(2,1)S(1)}, f32[256,2048]{1,0:T(8,128)}) custom-call(s32[1]{0:T(128)} %bitcast.17.sibling_ref, bf16[512,1024]{1,0:T(8,128)(2,1)S(1)} %copy-done.4, bf16[512,1024]{1,0:T(8,128)(2,1)S(1)} %copy-done.6, bf16[2048,1024]{1,0:T(8,128)(2,1)} %refs_5_.1, bf16[1024,512]{1,0:T(8,128)(2,1)} %collective-permute-done.16.refs_1_.refs_3_, ...), custom_call_target="tpu_custom_call" | custom-call | flops 6442450944 | bytes 16777216 | tf_op jit(solution)/shard_map/project/pallas_call | solution.py:409
  270.5 4.1 outer_sum.2.refs_2_
  274.6 4.1 outer_sum.3.refs_0_
  282.0 381.1 %tail.1 = (bf16[30,256,1024]{2,1,0:T(8,128)(2,1)}, bf16[30,256,1024]{2,1,0:T(8,128)(2,1)}, bf16[30,256,1024]{2,1,0:T(8,128)(2,1)}, bf16[30,256,1024]{2,1,0:T(8,1...) custom-call(bf16[30,256,1024]{2,1,0:T(8,128)(2,1)} %outer_sum.3.refs, ...), custom_call_target="tpu_custom_call", output_to_operand_aliasing={{0}: (0, {})} | custom-call | flops 429496729600 | bytes 31457280 | tf_op jit(solution)/shard_map/tail/pallas_call | solution.py:1058
  663.1 1.6 add_convert_fusion.1
  664.8 21.0 %widen.1 = (f32[2048,1024]{1,0:T(8,128)}, f32[1024,2048]{1,0:T(8,128)}, f32[1024,2048]{1,0:T(8,128)}, f32[512,1024]{1,0:T(8,128)}, f32[1024,512]{1,0:T(8,128)}, ...) custom-call(bf16[30,256,1024]{2,1,0:T(8,128)(2,1)} %get-tuple-element.135.pool_ref), custom_call_target="tpu_custom_call" | custom-call | flops 1 | bytes 47185920 | tf_op jit(solution)/shard_map/widen/pallas_call | solution.py:521
  685.8 1.4 fusion.55
  687.2 3.9 add_convert_fusion
  691.4 1.7 maximum_select_fusion.2
  (249 shorter events, 63.9 us)
Async XLA Ops:
  2.1 22.9 %collective-permute-start = (bf16[2,1024]{1,0:T(2,128)(2,1)S(1)}, bf16[2,1024]{1,0:T(2,128)(2,1)S(1)}, u32[]{:S(2)}, u32[]{:S(2)}) collective-permute-start(bf16[2,1024]{1,0:T(2,128)(2,1)S(1)} %pad_maximum_fusion.8), channel_id=1, source_target_pairs={{0,16},{16,0},{1,17},{17,1},{2,18},{18,2},{3,19},{19,3},{4,20},{20... | collective-permute-start | bytes 12296 | tf_op jit(solution)/shard_map/ppermute | solution.py:1130
  7.7 19.4 %collective-permute-start.1 = (bf16[512,768]{1,0:T(8,128)(2,1)}, bf16[512,768]{1,0:T(8,128)(2,1)}, u32[]{:S(2)}, u32[]{:S(2)}) collective-permute-start(bf16[512,768]{1,0:T(8,128)(2,1)} %constant_dynamic-slice_fusion.20), channel_id=1, source_target_pairs={{0,16},{16,0},{1,17},{17,1},{2,18},{18,2},{3,19},{19,3},{4,20},{20... | collective-permute-start | bytes 2359304 | tf_op jit(solution)/shard_map/ppermute | solution.py:1130
  25.0 13.7 %collective-permute-start.3 = (bf16[512,512]{1,0:T(8,128)(2,1)}, bf16[512,512]{1,0:T(8,128)(2,1)S(1)}, u32[]{:S(2)}, u32[]{:S(2)}) collective-permute-start(bf16[512,512]{1,0:T(8,128)(2,1)} %constant_dynamic-slice_fusion.23), channel_id=1, source_target_pairs={{0,16},{16,0},{1,17},{17,1},{2,18},{18,2},{3,19},{19,3},{4,20},{20... | collective-permute-start | bytes 1572872 | tf_op jit(solution)/shard_map/ppermute | solution.py:1130
  27.1 124.5 %copy-start.67 = (f32[1,2048]{1,0:T(1,128)}, f32[1,2048]{1,0:T(1,128)S(1)}, u32[]{:S(2)}) copy-start(f32[1,2048]{1,0:T(1,128)S(1)} %get-tuple-element.181.refs_31_) | copy-start | bytes 24580
  27.1 18.7 %collective-permute-start.2 = (bf16[512,768]{1,0:T(8,128)(2,1)}, bf16[512,768]{1,0:T(8,128)(2,1)S(1)}, u32[]{:S(2)}, u32[]{:S(2)}) collective-permute-start(bf16[512,768]{1,0:T(8,128)(2,1)} %collective-permute-done.1.refs_22_), channel_id=1, source_target_pairs={{0,4},{4,0},{8,12},{12,8},{1,5},{5,1},{9,13},{13,9},{2,6},{6,2},{1... | collective-permute-start | bytes 2359304 | tf_op jit(solution)/shard_map/ppermute | solution.py:1130
  38.7 46.2 %copy-start.49 = (bf16[512,512]{1,0:T(8,128)(2,1)}, bf16[512,512]{1,0:T(8,128)(2,1)S(1)}, u32[]{:S(2)}) copy-start(bf16[512,512]{1,0:T(8,128)(2,1)S(1)} %collective-permute-done.3.refs_12_) | copy-start | bytes 1572868
  38.7 26.1 %collective-permute-start.6 = (bf16[512,1024]{1,0:T(8,128)(2,1)S(1)}, bf16[512,1024]{1,0:T(8,128)(2,1)S(1)}, u32[]{:S(2)}, u32[]{:S(2)}) collective-permute-start(bf16[512,1024]{1,0:T(8,128)(2,1)S(1)} %copy-done.61), channel_id=1, source_target_pairs={{0,16},{16,0},{1,17},{17,1},{2,18},{18,2},{3,19},{19,3},{4,20},{20... | collective-permute-start | bytes 3145736 | tf_op jit(solution)/shard_map/ppermute | solution.py:1130
  40.4 44.5 %collective-permute-start.8 = (bf16[512,1024]{1,0:T(8,128)(2,1)S(1)}, bf16[512,1024]{1,0:T(8,128)(2,1)S(1)}, u32[]{:S(2)}, u32[]{:S(2)}) collective-permute-start(bf16[512,1024]{1,0:T(8,128)(2,1)S(1)} %copy-done.60), channel_id=1, source_target_pairs={{0,16},{16,0},{1,17},{17,1},{2,18},{18,2},{3,19},{19,3},{4,20},{20... | collective-permute-start | bytes 3145736 | tf_op jit(solution)/shard_map/ppermute | solution.py:1130
  48.4 16.4 %collective-permute-start.5 = (bf16[1,512,256]{2,1,0:T(8,128)(2,1)S(1)}, bf16[1,512,256]{2,1,0:T(8,128)(2,1)S(1)}, u32[]{:S(2)}, u32[]{:S(2)}) collective-permute-start(bf16[1,512,256]{2,1,0:T(8,128)(2,1)S(1)} %maximum_bitcast_fusion), channel_id=1, source_target_pairs={{0,4},{4,8},{8,12},{1,5},{5,9},{9,13},{2,6},{6,10},{10,14},{3,7},{... | collective-permute-start | bytes 786440 | tf_op jit(solution)/shard_map/ppermute | solution.py:1136
  51.9 12.9 %collective-permute-start.4 = (bf16[1,512,256]{2,1,0:T(8,128)(2,1)S(1)}, bf16[1,512,256]{2,1,0:T(8,128)(2,1)S(1)}, u32[]{:S(2)}, u32[]{:S(2)}) collective-permute-start(bf16[1,512,256]{2,1,0:T(8,128)(2,1)S(1)} %maximum_bitcast_fusion), channel_id=1, source_target_pairs={{0,8},{4,12},{1,9},{5,13},{2,10},{6,14},{3,11},{7,15},{16,24},{20,... | collective-permute-start | bytes 786440 | tf_op jit(solution)/shard_map/ppermute | solution.py:1136
  56.4 28.4 %collective-permute-start.7 = (bf16[512,512]{1,0:T(8,128)(2,1)S(1)}, bf16[512,512]{1,0:T(8,128)(2,1)S(1)}, u32[]{:S(2)}, u32[]{:S(2)}) collective-permute-start(bf16[512,512]{1,0:T(8,128)(2,1)S(1)} %collective-permute-done.3.refs_12_), channel_id=1, source_target_pairs={{0,4},{4,0},{8,12},{12,8},{1,5},{5,1},{9,13},{13,9},{2,6},{6,2},{1... | collective-permute-start | bytes 1572872 | tf_op jit(solution)/shard_map/ppermute | solution.py:1130
  57.9 25.1 %copy-start.7 = (bf16[1,512,512]{2,1,0:T(8,128)(2,1)}, bf16[1,512,512]{2,1,0:T(8,128)(2,1)S(1)}, u32[]{:S(2)}) copy-start(bf16[1,512,512]{2,1,0:T(8,128)(2,1)S(1)} %multiply_bitcast_fusion.q_ref) | copy-start | bytes 1572868
  64.8 23.7 %copy-start.8 = (bf16[512,1024]{1,0:T(8,128)(2,1)}, bf16[512,1024]{1,0:T(8,128)(2,1)S(1)}, u32[]{:S(2)}) copy-start(bf16[512,1024]{1,0:T(8,128)(2,1)S(1)} %collective-permute-done.6.refs_4_.refs_8_) | copy-start | bytes 3145732
  65.9 19.3 %copy-start.40 = (bf16[512,1024]{1,0:T(8,128)(2,1)S(1)}, bf16[512,1024]{1,0:T(8,128)(2,1)}, u32[]{:S(2)}) copy-start(bf16[512,1024]{1,0:T(8,128)(2,1)} %refs_11_.1) | copy-start | bytes 3145732
  84.9 32.5 %copy-start.10 = (bf16[512,1024]{1,0:T(8,128)(2,1)}, bf16[512,1024]{1,0:T(8,128)(2,1)S(1)}, u32[]{:S(2)}) copy-start(bf16[512,1024]{1,0:T(8,128)(2,1)S(1)} %collective-permute-done.8.refs_1_.refs_5_) | copy-start | bytes 3145732
  87.0 6.7 collective-permute-start.9
  88.5 25.8 %collective-permute-start.11 = (bf16[512,1024]{1,0:T(8,128)(2,1)S(1)}, bf16[512,1024]{1,0:T(8,128)(2,1)S(1)}, u32[]{:S(2)}, u32[]{:S(2)}) collective-permute-start(bf16[512,1024]{1,0:T(8,128)(2,1)S(1)} %collective-permute-done.6.refs_4_.refs_8_), channel_id=1, source_target_pairs={{0,4},{4,0},{8,12},{12,8},{1,5},{5,1},{9,13},{13,9},{2,6},{6,2},{1... | collective-permute-start | bytes 3145736 | tf_op jit(solution)/shard_map/ppermute | solution.py:1130
  90.5 25.3 %collective-permute-start.10 = (bf16[512,1024]{1,0:T(8,128)(2,1)S(1)}, bf16[512,1024]{1,0:T(8,128)(2,1)S(1)}, u32[]{:S(2)}, u32[]{:S(2)}) collective-permute-start(bf16[512,1024]{1,0:T(8,128)(2,1)S(1)} %copy-done.59), channel_id=1, source_target_pairs={{0,16},{16,0},{1,17},{17,1},{2,18},{18,2},{3,19},{19,3},{4,20},{20... | collective-permute-start | bytes 3145736 | tf_op jit(solution)/shard_map/ppermute | solution.py:1130
  93.7 25.9 %copy-start.44 = (bf16[2048,1024]{1,0:T(8,128)(2,1)S(1)}, bf16[2048,1024]{1,0:T(8,128)(2,1)}, u32[]{:S(2)}) copy-start(bf16[2048,1024]{1,0:T(8,128)(2,1)} %refs_5_.1) | copy-start | bytes 12582916
  115.8 24.4 %collective-permute-start.12 = (bf16[256,2048]{1,0:T(8,128)(2,1)S(1)}, bf16[256,2048]{1,0:T(8,128)(2,1)S(1)}, u32[]{:S(2)}, u32[]{:S(2)}) collective-permute-start(bf16[256,2048]{1,0:T(8,128)(2,1)S(1)} %fusion.4), channel_id=1, source_target_pairs={{0,2},{1,3},{2,0},{3,1},{4,6},{5,7},{6,4},{7,5},{8,10},{9,11},{10,... | collective-permute-start | bytes 3145736 | tf_op jit(solution)/shard_map/ppermute | solution.py:1130
  117.3 24.4 %collective-permute-start.14 = (bf16[512,1024]{1,0:T(8,128)(2,1)S(1)}, bf16[512,1024]{1,0:T(8,128)(2,1)S(1)}, u32[]{:S(2)}, u32[]{:S(2)}) collective-permute-start(bf16[512,1024]{1,0:T(8,128)(2,1)S(1)} %collective-permute-done.8.refs_1_.refs_5_), channel_id=1, source_target_pairs={{0,4},{4,0},{8,12},{12,8},{1,5},{5,1},{9,13},{13,9},{2,6},{6,2},{1... | collective-permute-start | bytes 3145736 | tf_op jit(solution)/shard_map/ppermute | solution.py:1130
  118.6 24.3 %collective-permute-start.13 = (bf16[512,1024]{1,0:T(8,128)(2,1)S(1)}, bf16[512,1024]{1,0:T(8,128)(2,1)}, u32[]{:S(2)}, u32[]{:S(2)}) collective-permute-start(bf16[512,1024]{1,0:T(8,128)(2,1)S(1)} %constant_dynamic-slice_fusion.13), channel_id=1, source_target_pairs={{0,16},{16,0},{1,17},{17,1},{2,18},{18,2},{3,19},{19,3},{4,20},{20... | collective-permute-start | bytes 3145736 | tf_op jit(solution)/shard_map/ppermute | solution.py:1130
  142.9 5.9 collective-permute-start.15
  145.7 26.0 %collective-permute-start.17 = (bf16[512,1024]{1,0:T(8,128)(2,1)S(1)}, bf16[512,1024]{1,0:T(8,128)(2,1)S(1)}, u32[]{:S(2)}, u32[]{:S(2)}) collective-permute-start(bf16[512,1024]{1,0:T(8,128)(2,1)S(1)} %copy-done.15), channel_id=1, source_target_pairs={{0,4},{4,0},{8,12},{12,8},{1,5},{5,1},{9,13},{13,9},{2,6},{6,2},{1... | collective-permute-start | bytes 3145736 | tf_op jit(solution)/shard_map/ppermute | solution.py:1130
  147.1 25.6 %collective-permute-start.16 = (bf16[1024,512]{1,0:T(8,128)(2,1)}, bf16[1024,512]{1,0:T(8,128)(2,1)}, u32[]{:S(2)}, u32[]{:S(2)}) collective-permute-start(bf16[1024,512]{1,0:T(8,128)(2,1)} %constant_dynamic-slice_fusion.12), channel_id=1, source_target_pairs={{0,16},{16,0},{1,17},{17,1},{2,18},{18,2},{3,19},{19,3},{4,20},{20... | collective-permute-start | bytes 3145736 | tf_op jit(solution)/shard_map/ppermute | solution.py:1130
  148.2 46.0 %collective-permute-start.19 = (bf16[512,1024]{1,0:T(8,128)(2,1)}, bf16[512,1024]{1,0:T(8,128)(2,1)S(1)}, u32[]{:S(2)}, u32[]{:S(2)}) collective-permute-start(bf16[512,1024]{1,0:T(8,128)(2,1)} %collective-permute-done.13.refs_4_.refs_14_), channel_id=1, source_target_pairs={{0,4},{4,0},{8,12},{12,8},{1,5},{5,1},{9,13},{13,9},{2,6},{6,2},{1... | collective-permute-start | bytes 3145736 | tf_op jit(solution)/shard_map/ppermute | solution.py:1130
  155.9 17.8 %copy-start.55 = (bf16[512,512]{1,0:T(8,128)(2,1)S(1)}, bf16[512,512]{1,0:T(8,128)(2,1)}, u32[]{:S(2)}) copy-start(bf16[512,512]{1,0:T(8,128)(2,1)} %get-tuple-element.163) | copy-start | bytes 1572868
  155.9 17.8 %copy-start.56 = (bf16[512,512]{1,0:T(8,128)(2,1)S(1)}, bf16[512,512]{1,0:T(8,128)(2,1)}, u32[]{:S(2)}) copy-start(bf16[512,512]{1,0:T(8,128)(2,1)} %get-tuple-element.164) | copy-start | bytes 1572868
  171.7 22.5 %copy-start.18 = (bf16[512,1024]{1,0:T(8,128)(2,1)}, bf16[512,1024]{1,0:T(8,128)(2,1)S(1)}, u32[]{:S(2)}) copy-start(bf16[512,1024]{1,0:T(8,128)(2,1)S(1)} %collective-permute-done.17.refs_2_.refs_12_) | copy-start | bytes 3145732
  172.7 32.3 %collective-permute-start.20 = (bf16[1024,512]{1,0:T(8,128)(2,1)S(1)}, bf16[1024,512]{1,0:T(8,128)(2,1)}, u32[]{:S(2)}, u32[]{:S(2)}) collective-permute-start(bf16[1024,512]{1,0:T(8,128)(2,1)S(1)} %constant_dynamic-slice_fusion.11), channel_id=1, source_target_pairs={{0,16},{16,0},{1,17},{17,1},{2,18},{18,2},{3,19},{19,3},{4,20},{20... | collective-permute-start | bytes 3145736 | tf_op jit(solution)/shard_map/ppermute | solution.py:1130
  176.3 42.9 %collective-permute-start.18 = (bf16[1024,512]{1,0:T(8,128)(2,1)}, bf16[1024,512]{1,0:T(8,128)(2,1)}, u32[]{:S(2)}, u32[]{:S(2)}) collective-permute-start(bf16[1024,512]{1,0:T(8,128)(2,1)} %collective-permute-done.16.refs_1_.refs_3_), channel_id=1, source_target_pairs={{0,4},{4,0},{8,12},{12,8},{1,5},{5,1},{9,13},{13,9},{2,6},{6,2},{1... | collective-permute-start | bytes 3145736 | tf_op jit(solution)/shard_map/ppermute | solution.py:1130
  205.0 33.8 %collective-permute-start.21 = (bf16[1024,512]{1,0:T(8,128)(2,1)}, bf16[1024,512]{1,0:T(8,128)(2,1)}, u32[]{:S(2)}, u32[]{:S(2)}) collective-permute-start(bf16[1024,512]{1,0:T(8,128)(2,1)} %collective-permute-done.20.refs_1_.refs_6_), channel_id=1, source_target_pairs={{0,4},{4,0},{8,12},{12,8},{1,5},{5,1},{9,13},{13,9},{2,6},{6,2},{1... | collective-permute-start | bytes 3145736 | tf_op jit(solution)/shard_map/ppermute | solution.py:1130
  214.9 28.7 %collective-permute-start.22 = (bf16[512,1024]{1,0:T(8,128)(2,1)}, bf16[512,1024]{1,0:T(8,128)(2,1)S(1)}, u32[]{:S(2)}, u32[]{:S(2)}) collective-permute-start(bf16[512,1024]{1,0:T(8,128)(2,1)} %copy-done.3), channel_id=1, source_target_pairs={{0,16},{16,0},{1,17},{17,1},{2,18},{18,2},{3,19},{19,3},{4,20},{20... | collective-permute-start | bytes 3145736 | tf_op jit(solution)/shard_map/ppermute | solution.py:1130
  217.2 42.6 %collective-permute-start.23 = (bf16[256,1024]{1,0:T(8,128)(2,1)}, bf16[256,1024]{1,0:T(8,128)(2,1)S(1)}, u32[]{:S(2)}, u32[]{:S(2)}) collective-permute-start(bf16[256,1024]{1,0:T(8,128)(2,1)} %fusion.7), channel_id=1, source_target_pairs={{0,16},{16,0},{1,17},{17,1},{2,18},{18,2},{3,19},{19,3},{4,20},{20... | collective-permute-start | bytes 1572872 | tf_op jit(solution)/shard_map/ppermute | solution.py:1130
  218.1 56.4 %collective-permute-start.25 = (bf16[512,1024]{1,0:T(8,128)(2,1)S(1)}, bf16[512,1024]{1,0:T(8,128)(2,1)S(1)}, u32[]{:S(2)}, u32[]{:S(2)}) collective-permute-start(bf16[512,1024]{1,0:T(8,128)(2,1)S(1)} %copy-done.6), channel_id=1, source_target_pairs={{0,16},{16,0},{1,17},{17,1},{2,18},{18,2},{3,19},{19,3},{4,20},{20... | collective-permute-start | bytes 3145736 | tf_op jit(solution)/shard_map/ppermute | solution.py:1130
  222.4 16.4 %copy-start.25 = (f32[512,1024]{1,0:T(8,128)S(1)}, f32[512,1024]{1,0:T(8,128)}, u32[]{:S(2)}) copy-start(f32[512,1024]{1,0:T(8,128)} %copy-done.24) | copy-start | bytes 6291460
  222.4 16.4 %copy-start.27 = (f32[512,1024]{1,0:T(8,128)S(1)}, f32[512,1024]{1,0:T(8,128)}, u32[]{:S(2)}) copy-start(f32[512,1024]{1,0:T(8,128)} %copy-done.26) | copy-start | bytes 6291460
  227.2 16.3 %copy-start.28 = (bf16[512,1024]{1,0:T(8,128)(2,1)}, bf16[512,1024]{1,0:T(8,128)(2,1)S(1)}, u32[]{:S(2)}) copy-start(bf16[512,1024]{1,0:T(8,128)(2,1)S(1)} %get-tuple-element.105.refs_0_.refs_4_) | copy-start | bytes 3145732
  227.3 16.3 %copy-start.29 = (bf16[512,1024]{1,0:T(8,128)(2,1)}, bf16[512,1024]{1,0:T(8,128)(2,1)S(1)}, u32[]{:S(2)}) copy-start(bf16[512,1024]{1,0:T(8,128)(2,1)S(1)} %get-tuple-element.106.refs_1_.refs_6_) | copy-start | bytes 3145732
  243.5 16.2 %copy-start.30 = (bf16[512,1024]{1,0:T(8,128)(2,1)}, bf16[512,1024]{1,0:T(8,128)(2,1)S(1)}, u32[]{:S(2)}) copy-start(bf16[512,1024]{1,0:T(8,128)(2,1)S(1)} %get-tuple-element.117.refs_2_.refs_5_) | copy-start | bytes 3145732
  243.6 16.8 %copy-start.4 = (bf16[512,1024]{1,0:T(8,128)(2,1)S(1)}, bf16[512,1024]{1,0:T(8,128)(2,1)}, u32[]{:S(2)}) copy-start(bf16[512,1024]{1,0:T(8,128)(2,1)} %copy-done.3) | copy-start | bytes 3145732
  259.8 10.2 %collective-permute-start.26 = (bf16[256,1024]{1,0:T(8,128)(2,1)S(1)}, bf16[256,1024]{1,0:T(8,128)(2,1)S(1)}, u32[]{:S(2)}, u32[]{:S(2)}) collective-permute-start(bf16[256,1024]{1,0:T(8,128)(2,1)S(1)} %collective-permute-done.23), channel_id=1, source_target_pairs={{0,1},{1,0},{2,3},{3,2},{4,5},{5,4},{6,7},{7,6},{8,9},{9,8},{10,11... | collective-permute-start | bytes 1572872 | tf_op jit(solution)/shard_map/ppermute | solution.py:1130
  259.8 18.8 %collective-permute-start.27 = (bf16[256,2048]{1,0:T(8,128)(2,1)S(1)}, bf16[256,2048]{1,0:T(8,128)(2,1)S(1)}, u32[]{:S(2)}, u32[]{:S(2)}) collective-permute-start(bf16[256,2048]{1,0:T(8,128)(2,1)S(1)} %get-tuple-element.131), channel_id=1, source_target_pairs={{0,1},{1,0},{2,3},{3,2},{4,5},{5,4},{6,7},{7,6},{8,9},{9,8},{10,11... | collective-permute-start | bytes 3145736 | tf_op jit(solution)/shard_map/ppermute | solution.py:1130
  269.9 10.1 %collective-permute-start.24 = (bf16[256,2048]{1,0:T(8,128)(2,1)S(1)}, bf16[256,2048]{1,0:T(8,128)(2,1)S(1)}, u32[]{:S(2)}, u32[]{:S(2)}) collective-permute-start(bf16[256,2048]{1,0:T(8,128)(2,1)S(1)} %get-tuple-element.126), channel_id=1, source_target_pairs={{0,1},{1,0},{2,3},{3,2},{4,5},{5,4},{6,7},{7,6},{8,9},{9,8},{10,11... | collective-permute-start | bytes 3145736 | tf_op jit(solution)/shard_map/ppermute | solution.py:1130
  282.0 381.1 %copy-start.45 = (bf16[256,2048]{1,0:T(8,128)(2,1)S(1)}, bf16[256,2048]{1,0:T(8,128)(2,1)}, u32[]{:S(2)}) copy-start(bf16[256,2048]{1,0:T(8,128)(2,1)} %add_convert_fusion.3.refs_3_) | copy-start | bytes 3145732
  664.7 22.5 %collective-permute-start.28 = (bf16[256,2048]{1,0:T(8,128)(2,1)S(1)}, bf16[256,2048]{1,0:T(8,128)(2,1)S(1)}, u32[]{:S(2)}, u32[]{:S(2)}) collective-permute-start(bf16[256,2048]{1,0:T(8,128)(2,1)S(1)} %add_convert_fusion.1), channel_id=1, source_target_pairs={{0,1},{1,0},{2,3},{3,2},{4,5},{5,4},{6,7},{7,6},{8,9},{9,8},{10,11... | collective-permute-start | bytes 3145736 | tf_op jit(solution)/shard_map/ppermute | solution.py:1130
  664.8 22.4 %copy-start.34 = (bf16[512,2048]{1,0:T(8,128)(2,1)S(1)}, bf16[512,2048]{1,0:T(8,128)(2,1)}, u32[]{:S(2)}) copy-start(bf16[512,2048]{1,0:T(8,128)(2,1)} %copy-done.32) | copy-start | bytes 6291460
  664.8 22.4 %copy-start.38 = (bf16[256,2048]{1,0:T(8,128)(2,1)S(1)}, bf16[256,2048]{1,0:T(8,128)(2,1)}, u32[]{:S(2)}) copy-start(bf16[256,2048]{1,0:T(8,128)(2,1)} %copy-done.37) | copy-start | bytes 3145732
  (49 other events, 232.4 us)
